TPU v7x, 32 devices: a whole 2x2x4 slice. The times are simulated.
32 devices in a mesh: seq: 8 (over y, x, core), head: 4 (over z).
Axes of the slice: x: 2, y: 2, z: 4, core: 2. Of those that a mesh axis runs over, the one named last changes fastest.
Arguments:
- query_act: bfloat16 [2048, 1536], P('seq', 'head'), may hold values from -0.59765625 to 0.59765625
- key_act: bfloat16 [2048, 1536], P('seq', 'head'), may hold values from -0.59765625 to 0.59765625
- value_act: bfloat16 [2048, 1536], P('seq', 'head'), may hold values from -0.59765625 to 0.59765625
- grad_output: bfloat16 [2048, 1536], P('seq', 'head'), may hold values from -1.0546875 to 1.0546875
- log_decay: float32 [2048, 12], P('seq', 'head'), may hold values from -1 to 0
- w_query: bfloat16 [6144, 1536], P(None, 'head'), may hold values from -0.109375 to 0.109375
- w_key: bfloat16 [6144, 1536], P(None, 'head'), may hold values from -0.109375 to 0.109375
Outputs:
- grad_input: bfloat16 [6144, 2048], P('head', 'seq')
All inputs are finite; a program needn't handle non-finite values.
Results may differ from a plain program's by a relative error of at most 0.015.
Values may be sent and summed in bfloat16 or wider, within the bound.
No kernel may reach another device: no remote copies, remote signals or barrier semaphores. Data moves between devices by JAX's collectives and lax.ppermute only.
A program may use at most 128 MiB of HBM per device.

v0:
```python
import jax
import jax.numpy as jnp
from jax import lax
from jax.sharding import PartitionSpec as P


def entering(value, axis, join, neutral):
    count, mine = (lax.axis_size(axis), lax.axis_index(axis))
    pieces = jax.tree.map(lambda part: lax.all_gather(part, axis), value)
    pieces = jax.tree.map(lambda part: part[::-1], pieces)
    mine = count - 1 - mine
    subtotal = jax.tree.map(
        lambda part, zero: jnp.full_like(part, 0) + jnp.asarray(zero, part.dtype), value, neutral
    )

    def turn(position, subtotal):
        longer = join(subtotal, jax.tree.map(lambda part: part[position], pieces))
        return jax.tree.map(lambda new, old: jnp.where(position < mine, new, old), longer, subtotal)

    return lax.fori_loop(0, count - 1, turn, subtotal)


def chain_combine(earlier, later):
    return (earlier[0] * later[0], later[0][:, None, None] * earlier[1] + later[1])


def shards(query_act, key_act, value_act, grad_output, log_decay, w_query, w_key):
    f32 = jnp.float32
    bf16 = jnp.bfloat16
    span = query_act.shape[0]
    nheads = log_decay.shape[1]
    width = query_act.shape[1] // nheads
    queries = query_act.reshape(span, nheads, width)
    keys_blk = key_act.reshape(span, nheads, width)
    values_blk = value_act.reshape(span, nheads, width)
    grads_blk = grad_output.reshape(span, nheads, width)
    cumlog = jnp.cumsum(log_decay, axis=0)
    last_log = cumlog[-1]
    decay_total = jnp.exp(last_log)
    key_weighted = (keys_blk * jnp.exp(last_log[None, :] - cumlog)[:, :, None]).astype(bf16)
    query_weighted = (queries * jnp.exp(cumlog)[:, :, None]).astype(bf16)
    local_state = jnp.einsum("thd,the->hde", key_weighted, values_blk, preferred_element_type=f32)
    local_grad = jnp.einsum("thd,the->hde", query_weighted, grads_blk, preferred_element_type=f32)
    identity = (jnp.ones_like(decay_total), jnp.zeros_like(local_state))
    totals = lax.all_gather(last_log[None, :], "seq", axis=0, tiled=True)
    my_index = lax.axis_index("seq")
    block_all = jnp.arange(totals.shape[0])
    masked = jnp.where((block_all < my_index)[:, None], totals, 0.0)
    from_here = jnp.cumsum(masked[::-1], axis=0)[::-1]
    between = jnp.concatenate([from_here[1:], jnp.zeros_like(from_here[:1])], axis=0)
    pieces = lax.all_gather(local_state[None], "seq", axis=0, tiled=True)
    row_count = pieces.shape[0]
    block_ids = jnp.arange(row_count)
    factor = jnp.where((block_ids < my_index)[:, None], jnp.exp(jnp.minimum(between, 0.0)), 0.0)
    state_in = jnp.sum(factor[:, :, None, None] * pieces, axis=0)
    grad_in = entering((decay_total, local_grad), "seq", chain_combine, identity)[1]
    positions = jnp.arange(span)
    causal_mask = positions[:, None] >= positions[None, :]
    log_gap = cumlog[:, None, :] - cumlog[None, :, :]
    decay_mat = jnp.where(causal_mask[:, :, None], jnp.exp(jnp.minimum(log_gap, 0.0)), 0.0)
    dot_scores = jnp.einsum("the,she->tsh", grads_blk, values_blk, preferred_element_type=f32)
    weighted = (dot_scores * decay_mat).astype(bf16)
    dq_local = jnp.einsum("tsh,shd->thd", weighted, keys_blk, preferred_element_type=f32)
    dk_local = jnp.einsum("tsh,thd->shd", weighted, queries, preferred_element_type=f32)
    dq_carry = (
        jnp.einsum("the,hde->thd", grads_blk, state_in.astype(bf16), preferred_element_type=f32)
        * jnp.exp(cumlog)[:, :, None]
    )
    dk_carry = (
        jnp.einsum("the,hde->thd", values_blk, grad_in.astype(bf16), preferred_element_type=f32)
        * jnp.exp(last_log[None, :] - cumlog)[:, :, None]
    )
    dq_flat = (dq_local + dq_carry).astype(bf16).reshape(span, nheads * width)
    dk_flat = (dk_local + dk_carry).astype(bf16).reshape(span, nheads * width)
    dims = (((1,), (1,)), ((), ()))
    term = lax.dot_general(w_query, dq_flat, dims, preferred_element_type=f32)
    summed = lax.psum_scatter(
        (term + lax.dot_general(w_key, dk_flat, dims, preferred_element_type=f32)).astype(
            jnp.bfloat16
        ),
        "head",
        scatter_dimension=0,
        tiled=True,
    ).astype(jnp.float32)
    return summed.astype(bf16)


def solution(mesh):
    placed = (
        P("seq", "head"),
        P("seq", "head"),
        P("seq", "head"),
        P("seq", "head"),
        P("seq", "head"),
        P(None, "head"),
        P(None, "head"),
    )
    return jax.shard_map(
        shards, mesh=mesh, in_specs=placed, out_specs=P("head", "seq"), check_vma=False
    )
```

profile of v0, /device:TPU:0, one launch (start us, length us, event | category | flops | bytes accessed | tf_op | source)
XLA Modules:
  0.0 147.0 jit_solution(3241556248433468925)
XLA Ops:
  6.5 0.0 all-gather.9.cloned.1.call-start
  6.5 0.7 reshape.52
  7.2 0.9 reduce-window.6
  8.1 0.1 slice.20
  8.2 0.1 copy.101
  8.4 0.1 copy.102
  8.5 0.1 add_bitcast_fusion
  8.5 0.2 exponential_reduce_fusion
  8.7 0.1 subtract_exponential_fusion
  8.8 1.1 copy.109
  9.9 1.1 copy.98
  11.0 0.9 fusion.12
  11.9 0.0 all-gather.9.cloned.1.call-update
  11.9 0.0 all-gather.7.cloned.1.call-start
  11.9 1.1 copy.103
  13.0 1.1 copy.97
  14.1 0.9 fusion.11
  15.0 0.0 all-gather.7.cloned.1.call-update
  15.0 0.0 reduce-scatter.2.cloned.1.call-start
  15.1 10.2 %all-gather.3 = f32[8,1,3]{2,1,0:T(1,128)S(1)} all-gather(f32[1,1,3]{2,1,0:T(1,128)S(1)} %bitcast.108), channel_id=1, replica_groups=mesh['seq'=8,'head'=4] {'seq'}, dimensions={0}, use_global_device_ids=true | all-gather | bytes 108 | tf_op jit(solution)/shard_map/all_gather | solution.py:9
  25.3 0.1 copy.111
  25.4 0.1 rev.11
  25.5 0.1 copy.113
  25.6 8.7 %all-gather.2 = f32[8,1,3]{2,1,0:T(1,128)S(1)} all-gather(f32[1,1,3]{2,1,0:T(1,128)S(1)} %bitcast.105), channel_id=1, replica_groups=mesh['seq'=8,'head'=4] {'seq'}, dimensions={0}, use_global_device_ids=true | all-gather | bytes 108 | tf_op jit(solution)/shard_map/all_gather | solution.py:45
  34.3 0.1 copy.105
  34.4 0.1 rev.10
  34.5 0.2 reduce_window_sum.28
  34.6 0.1 slice.19
  34.7 0.1 copy.106
  34.8 0.4 fusion.4
  35.2 0.2 convolution_bitcast_fusion.1
  35.4 5.0 %all-gather.9.cloned.1.call-done = f32[24,128,128]{2,1,0:T(8,128)} async-done(((f32[3,128,128]{2,1,0:T(8,128)}), f32[24,128,128]{2,1,0:T(8,128)}) %all-gather.9.cloned.1.call-update) | async-done | bytes 1572880 | tf_op jit(solution)/shard_map/all_gather | solution.py:9
  40.4 1.5 %rev.12 = f32[8,3,128,128]{3,2,1,0:T(8,128)S(1)} reverse(f32[8,3,128,128]{3,2,1,0:T(8,128)} %bitcast.98), dimensions={0} | reverse | bytes 3145728 | tf_op jit(solution)/shard_map/rev | solution.py:10
  41.9 1.0 while.14
  42.0 0.1 fusion.35
  42.1 0.1 fusion.35
  42.3 0.1 fusion.35
  42.4 0.1 fusion.35
  42.5 0.1 fusion.35
  42.7 0.1 fusion.35
  42.8 0.1 fusion.35
  42.9 0.2 fusion.5
  43.1 0.3 fusion.9
  43.4 24.6 %all-gather.7.cloned.1.call-done = f32[24,128,128]{2,1,0:T(8,128)} async-done(((f32[3,128,128]{2,1,0:T(8,128)}), f32[24,128,128]{2,1,0:T(8,128)}) %all-gather.7.cloned.1.call-update) | async-done | bytes 1572880 | tf_op jit(solution)/shard_map/all_gather | solution.py:51
  68.0 1.6 %multiply_reduce_fusion = bf16[3,128,128]{2,1,0:T(8,128)(2,1)S(1)} fusion(f32[8,3,128,128]{3,2,1,0:T(8,128)} %bitcast.97, f32[8,3]{1,0:T(8,128)S(1)} %copy.106), kind=kLoop, calls=%fused_computation.6 | loop fusion | flops 737280 | bytes 1671264 | tf_op jit(solution)/shard_map/reduce_sum | solution.py:55
  69.6 0.0 slice-start
  69.6 0.2 fusion.10
  69.8 0.0 slice-start.1
  69.8 4.3 %fusion.18 = f32[256,6144]{1,0:T(8,128)S(1)} fusion(bf16[256,384]{0,1:T(8,128)(2,1)S(1)} %bitcast.100, bf16[6144,384]{1,0:T(8,128)(2,1)} %param.14), kind=kOutput, calls=%fused_computation.38 | convolution fusion | flops 1207959552 | bytes 11206656 | tf_op jit(solution)/shard_map/dot_general | solution.py:76
  74.2 0.0 slice-done
  74.2 0.0 slice-done.1
  74.2 3.5 %fusion.2 = bf16[6144,256]{0,1:T(8,128)(2,1)} fusion(f32[256,6144]{1,0:T(8,128)S(1)} %fusion.18, bf16[256,384]{0,1:T(8,128)(2,1)S(1)} %bitcast.99, bf16[6144,384]{1,0:T(8,128)(2,1)S(1)} %bitcast.86), kind=kOutput, calls=%fused_computation.5 | convolution fusion | flops 1211105280 | bytes 14352384 | tf_op jit(solution)/shard_map/dot_general | solution.py:78
  77.7 0.0 reduce-scatter.2.cloned.1.call-update
  77.7 60.4 %reduce-scatter.2.cloned.1.call-done = bf16[1536,256]{0,1:T(8,128)(2,1)} async-done(((bf16[6144,256]{0,1:T(8,128)(2,1)}), bf16[1536,256]{0,1:T(8,128)(2,1)}) %reduce-scatter.2.cloned.1.call-update) | async-done | bytes 786448 | tf_op jit(solution)/shard_map/reduce_scatter | solution.py:77
  138.2 2.3 %copy.115 = bf16[1536,256]{1,0:T(8,128)(2,1)} copy(bf16[1536,256]{0,1:T(8,128)(2,1)} %reduce-scatter.2.cloned.1.call-done) | data formatting | bytes 1572864 | tf_op jit(solution)/shard_map/reduce_scatter | solution.py:77
  (16 shorter events, 0.2 us)
Async XLA Ops:
  6.5 33.9 %all-gather.9.cloned.1.call-start = ((), (), s32[]{:S(2)}) async-start(), calls=%async_computation.3 | async-start | bytes 1769472 | tf_op jit(solution)/shard_map/all_gather | solution.py:9
  11.9 56.2 %all-gather.7.cloned.1.call-start = ((), (), s32[]{:S(2)}) async-start(), calls=%async_computation.2 | async-start | bytes 1769472 | tf_op jit(solution)/shard_map/all_gather | solution.py:51
  15.0 123.2 %reduce-scatter.2.cloned.1.call-start = ((), (), s32[]{:S(2)}) async-start(), calls=%async_computation.1 | async-start | bytes 3932160 | tf_op jit(solution)/shard_map/reduce_scatter | solution.py:77
  69.6 4.6 %slice-start = ((s8[4718592]{0:T(1024)(128)(4,1)}), s8[4194304]{0:T(1024)(128)(4,1)S(1)}, s32[]{:S(2)}) async-start(s8[4718592]{0:T(1024)(128)(4,1)} %bitcast.85), calls=%async_computation.4 | async-start | bytes 8388608
  69.8 4.4 %slice-start.1 = ((s8[4718592]{0:T(1024)(128)(4,1)}), s8[524288]{0:T(1024)(128)(4,1)S(1)}, s32[]{:S(2)}) async-start(s8[4718592]{0:T(1024)(128)(4,1)} %bitcast.85), calls=%async_computation.5 | async-start | bytes 1048576
Sparse Core Ops, SparseCore 0:
  12.0 28.3 all-gather.8
  42.3 25.6 all-gather.6
  77.9 60.2 reduce-scatter.1
where the time goes:
time: 147 us
  waiting for transfers between devices  90 us (61%)
  blocking collectives  18.9 us (13%)
  between operations  13.3 us (9%)
  matrix products  10.9 us (7%)
  local copies, waits for them, and re-layouts  9.93 us (7%)
  other arithmetic  3.6 us (2%)
    reduce_scatter x1, waiting for transfers between devices, shards(): lax.psum_scatter((term + lax.dot_general(w_key, dk_flat, dims, preferred_...  60.4 us
    all_gather x1, waiting for transfers between devices, shards(): pieces = lax.all_gather(local_state[None], 'seq', axis=0, tiled=True)  24.6 us
    all_gather x1, blocking collectives, entering(): pieces = jax.tree.map(lambda part: lax.all_gather(part, axis), value)  10.2 us
    all_gather x1, blocking collectives, shards(): totals = lax.all_gather(last_log[None, :], 'seq', axis=0, tiled=True)  8.71 us
    all_gather x1, waiting for transfers between devices, entering(): pieces = jax.tree.map(lambda part: lax.all_gather(part, axis), value)  4.99 us
    unnamed x10, local copies, waits for them, and re-layouts  4.37 us
    dot_general x1, matrix products, shards(): term = lax.dot_general(w_query, dq_flat, dims, preferred_element_type=f32)  4.32 us
    dot_general x1, matrix products, shards(): lax.dot_general(w_key, dk_flat, dims, preferred_element_type=f32)  3.51 us
  transfers between devices with their start and end apart: 3, of which 3 were waited for; matrix products, arithmetic and copies ran while one was open for 5% of the time, Pallas kernels for 0%

commit v1 on v0

v1 whole, which is shorter than its diff:
```python
import jax
import jax.numpy as jnp
from jax import lax
from jax.sharding import PartitionSpec as P

F32 = jnp.float32
BF16 = jnp.bfloat16


def scan_blocks(state, grad, last_log):
    count, mine = lax.axis_size("seq"), lax.axis_index("seq")
    nheads, width = state.shape[0], state.shape[1]
    shape = state.shape
    rows = nheads * width
    before = jnp.zeros_like(last_log)
    after = jnp.zeros_like(last_log)
    total = last_log
    state_in = jnp.zeros(shape, F32)
    grad_in = jnp.zeros(shape, F32)
    hop = 1
    while hop < count:
        pairs = [(i, i ^ hop) for i in range(count)]
        upper = (mine // hop) % 2 == 1
        if 2 * hop < count:
            high = total.astype(BF16)
            low = (total - high.astype(F32)).astype(BF16)
            tail = jnp.zeros((16, width), BF16).at[0, :nheads].set(high).at[1, :nheads].set(low)
            sent = jnp.concatenate(
                [state.astype(BF16).reshape(rows, width), grad.astype(BF16).reshape(rows, width), tail]
            )
            got = lax.ppermute(sent, "seq", pairs)
            got_state = got[:rows].astype(F32).reshape(shape)
            got_grad = got[rows : 2 * rows].astype(F32).reshape(shape)
            tail = got[2 * rows :].astype(F32)
            got_total = tail[0, :nheads] + tail[1, :nheads]
        else:
            sent = jnp.where(upper, grad, state).astype(BF16).reshape(rows, width)
            got_state = got_grad = lax.ppermute(sent, "seq", pairs).astype(F32).reshape(shape)
            got_total = total
        state_in = jnp.where(upper, state_in + jnp.exp(before)[:, None, None] * got_state, state_in)
        grad_in = jnp.where(upper, grad_in, grad_in + jnp.exp(after)[:, None, None] * got_grad)
        mine_decay = jnp.exp(total)[:, None, None]
        other_decay = jnp.exp(got_total)[:, None, None]
        state, grad = (
            jnp.where(upper, mine_decay * got_state + state, other_decay * state + got_state),
            jnp.where(upper, got_grad + other_decay * grad, grad + mine_decay * got_grad),
        )
        before = jnp.where(upper, before + got_total, before)
        after = jnp.where(upper, after, after + got_total)
        total = total + got_total
        hop *= 2
    return state_in, grad_in


def share_order(count):
    bits = []
    hop = 2
    while hop < count:
        bits.append(hop)
        hop *= 2
    return bits, bits[::-1]


def gather_shares(piece):
    count = lax.axis_size("seq")
    even, odd = share_order(count)
    held = piece
    for hop_even, hop_odd in zip(even, odd):
        pairs = [(i, i ^ (hop_odd if i % 2 else hop_even)) for i in range(count)]
        held = jnp.concatenate([held, lax.ppermute(held, "seq", pairs)])
    return jnp.concatenate([held, lax.ppermute(held, "seq", [(i, i ^ 1) for i in range(count)])])


def share_places(count):
    even, odd = share_order(count)
    tables = []
    for first, second in ((even, odd), (odd, even)):
        def spread(order):
            out = [0]
            for hop in order:
                out = out + [d ^ hop for d in out]
            return out
        order = spread(first) + [d ^ 1 for d in spread(second)]
        place = [0] * count
        for position, delta in enumerate(order):
            place[delta] = position
        tables.append(place)
    return tables


def shards(query_act, key_act, value_act, grad_output, log_decay, w_query, w_key):
    span = query_act.shape[0]
    nheads = log_decay.shape[1]
    width = query_act.shape[1] // nheads
    nseq, nhead = lax.axis_size("seq"), lax.axis_size("head")
    my_seq, my_head = lax.axis_index("seq"), lax.axis_index("head")
    chunk = w_query.shape[0] // nhead
    share = chunk // nseq

    pieces = []
    sources = []
    for k in range(1, nhead):
        if nhead & (nhead - 1) == 0:
            pairs = [(i, i ^ k) for i in range(nhead)]
            target = source = my_head ^ k
        else:
            pairs = [(i, (i + k) % nhead) for i in range(nhead)]
            target, source = (my_head + k) % nhead, (my_head + nhead - k) % nhead
        start = target * chunk + my_seq * share
        sent = jnp.concatenate(
            [lax.dynamic_slice_in_dim(w, start, share, 0) for w in (w_query, w_key)], axis=1
        )
        pieces.append(lax.ppermute(sent, "head", pairs))
        sources.append(source)

    queries = query_act.reshape(span, nheads, width)
    keys_blk = key_act.reshape(span, nheads, width)
    values_blk = value_act.reshape(span, nheads, width)
    grads_blk = grad_output.reshape(span, nheads, width)
    cumlog = jnp.cumsum(log_decay, axis=0)
    last_log = cumlog[-1]
    key_weighted = (keys_blk * jnp.exp(last_log[None, :] - cumlog)[:, :, None]).astype(BF16)
    query_weighted = (queries * jnp.exp(cumlog)[:, :, None]).astype(BF16)
    local_state = jnp.einsum("thd,the->hde", key_weighted, values_blk, preferred_element_type=F32)
    local_grad = jnp.einsum("thd,the->hde", query_weighted, grads_blk, preferred_element_type=F32)
    state_in, grad_in = scan_blocks(local_state, local_grad, last_log)

    positions = jnp.arange(span)
    causal_mask = positions[:, None] >= positions[None, :]
    log_gap = cumlog[:, None, :] - cumlog[None, :, :]
    decay_mat = jnp.where(causal_mask[:, :, None], jnp.exp(jnp.minimum(log_gap, 0.0)), 0.0)
    dot_scores = jnp.einsum("the,she->tsh", grads_blk, values_blk, preferred_element_type=F32)
    weighted = (dot_scores * decay_mat).astype(BF16)
    dq_local = jnp.einsum("tsh,shd->thd", weighted, keys_blk, preferred_element_type=F32)
    dk_local = jnp.einsum("tsh,thd->shd", weighted, queries, preferred_element_type=F32)
    dq_carry = (
        jnp.einsum("the,hde->thd", grads_blk, state_in.astype(BF16), preferred_element_type=F32)
        * jnp.exp(cumlog)[:, :, None]
    )
    dk_carry = (
        jnp.einsum("the,hde->thd", values_blk, grad_in.astype(BF16), preferred_element_type=F32)
        * jnp.exp(last_log[None, :] - cumlog)[:, :, None]
    )
    dq_flat = (dq_local + dq_carry).astype(BF16).reshape(span, nheads * width)
    dk_flat = (dk_local + dk_carry).astype(BF16).reshape(span, nheads * width)
    both = jnp.concatenate([dq_flat, dk_flat], axis=1)

    if nhead == 4:
        p1 = lax.ppermute(both, "head", [(0, 1), (1, 0), (2, 3), (3, 2)])
        p2 = lax.ppermute(both, "head", [(1, 2), (2, 1)])
        p3 = lax.ppermute(p2, "head", [(2, 3), (1, 0)])
        p4 = lax.ppermute(p1, "head", [(1, 2), (2, 1)])
        p5 = lax.ppermute(p4, "head", [(2, 3), (1, 0)])
        inner = (my_head == 1) | (my_head == 2)
        others = [p1, jnp.where(inner, p4, p3), jnp.where(inner, p2, p5)]
    else:
        gathered = lax.all_gather(both, "head")
        others = [gathered[source] for source in sources]

    dims = (((1,), (1,)), ((), ()))
    start = my_head * chunk
    total = lax.dot_general(
        lax.dynamic_slice_in_dim(w_query, start, chunk, 0), dq_flat, dims, preferred_element_type=F32
    ) + lax.dot_general(
        lax.dynamic_slice_in_dim(w_key, start, chunk, 0), dk_flat, dims, preferred_element_type=F32
    )
    remote = 0.0
    for piece, grads in zip(pieces, others):
        remote = remote + lax.dot_general(gather_shares(piece), grads, dims, preferred_element_type=F32)
    even, odd = share_places(nseq)
    deltas = jnp.arange(nseq) ^ my_seq
    place = jnp.where(my_seq % 2 == 1, jnp.array(odd)[deltas], jnp.array(even)[deltas])
    remote = remote.reshape(nseq, share, span)[place].reshape(chunk, span)
    return (total + remote).astype(BF16)


def solution(mesh):
    placed = (
        P("seq", "head"),
        P("seq", "head"),
        P("seq", "head"),
        P("seq", "head"),
        P("seq", "head"),
        P(None, "head"),
        P(None, "head"),
    )
    return jax.shard_map(
        shards, mesh=mesh, in_specs=placed, out_specs=P("head", "seq"), check_vma=False
    )
```

time: 147 us -> 104 us (0.71)
  waiting for transfers between devices: 90 us -> 40.1 us
  starting transfers between devices: 0.09 us -> 28.3 us
  blocking collectives: 18.9 us -> 0 us
  between operations: 13.3 us -> 0.5 us
  other arithmetic: 3.6 us -> 9.27 us
  local copies, waits for them, and re-layouts: 9.93 us -> 12.4 us
  matrix products: 10.9 us -> 12.7 us
    reduce_scatter x1 -> x0, waiting for transfers between devices: 60.4 us -> none  [shards(): lax.psum_scatter((term + lax.dot_general(w_key, dk_flat, dims, preferred_...]
    ppermute x0 -> x20, waiting for transfers between devices: none -> 40.1 us  [the longest x3 11.4 us: shards(): pieces.append(lax.ppermute(sent, 'head', pairs))]
    all_gather x2 -> x0, waiting for transfers between devices: 29.6 us -> none  [the longest x1 24.6 us: shards(): pieces = lax.all_gather(local_state[None], 'seq', axis=0, tiled=True)]
    ppermute x0 -> x20, starting transfers between devices: none -> 28.3 us  [the longest x6 7.91 us: gather_shares(): held = jnp.concatenate([held, lax.ppermute(held, 'seq', pairs)])]
    all_gather x2 -> x0, blocking collectives: 18.9 us -> none  [the longest x1 10.2 us: entering(): pieces = jax.tree.map(lambda part: lax.all_gather(part, axis), value)]
    concatenate x0 -> x12, other arithmetic: none -> 5.6 us  [the longest x6 2.59 us: gather_shares(): held = jnp.concatenate([held, lax.ppermute(held, 'seq', pairs)])]
    gather x0 -> x3, local copies, waits for them, and re-layouts: none -> 3.34 us  [the longest x1 2.05 us: shards(): remote = remote.reshape(nseq, share, span)[place].reshape(chunk, span)]
    dot_general x6 -> x9, matrix products: 8.72 us -> 11.9 us  [the longest x3 6.31 us: shards(): lax.dot_general(gather_shares(piece), grads, dims, preferred_element_type...]
  transfers between devices with their start and end apart: 3 -> 20, of which waited for: 3 -> 7; matrix products, arithmetic and copies ran while one was open for 5% -> 17% of each run, Pallas kernels for 0% -> 0%
where the time goes in v1:
time: 104 us; the launch traced here: 103 us
  waiting for transfers between devices  40.1 us (39%)
  starting transfers between devices  28.3 us (27%)
  matrix products  12.7 us (12%)
  local copies, waits for them, and re-layouts  12.4 us (12%)
  other arithmetic  9.27 us (9%)
    ppermute x3, waiting for transfers between devices, shards(): pieces.append(lax.ppermute(sent, 'head', pairs))  11.4 us
    ppermute x1, waiting for transfers between devices, shards(): p3 = lax.ppermute(p2, 'head', [(2, 3), (1, 0)])  9.75 us
    ppermute x6, starting transfers between devices, gather_shares(): held = jnp.concatenate([held, lax.ppermute(held, 'seq', pairs)])  7.91 us
    ppermute x1, waiting for transfers between devices, shards(): p1 = lax.ppermute(both, 'head', [(0, 1), (1, 0), (2, 3), (3, 2)])  6.61 us
    dot_general x3, matrix products, shards(): lax.dot_general(gather_shares(piece), grads, dims, preferred_element_type...  6.31 us
    ppermute x1, waiting for transfers between devices, shards(): p5 = lax.ppermute(p4, 'head', [(2, 3), (1, 0)])  6.29 us
    ppermute x6, waiting for transfers between devices, gather_shares(): held = jnp.concatenate([held, lax.ppermute(held, 'seq', pairs)])  6.05 us
    unnamed x35, local copies, waits for them, and re-layouts  5.6 us
  transfers between devices with their start and end apart: 20, of which 7 were waited for; matrix products, arithmetic and copies ran while one was open for 17% of the time, Pallas kernels for 0%

profile of v1, /device:TPU:0, one launch (start us, length us, event | category | flops | bytes accessed | tf_op | source)
XLA Modules:
  0.0 103.2 jit_solution(3342816755828021148)
XLA Ops:
  0.0 1.1 %copy.69 = bf16[256,384]{0,1:T(8,128)(2,1)S(1)} copy(bf16[256,384]{1,0:T(8,128)(2,1)} %param.19) | data formatting | bytes 393216 | tf_op args[2]
  1.1 0.7 reshape.322
  1.8 0.9 reduce-window.6
  3.1 0.2 subtract_convert_fusion.1
  3.3 1.1 %copy.70 = bf16[256,384]{0,1:T(8,128)(2,1)S(1)} copy(bf16[256,384]{1,0:T(8,128)(2,1)} %param.20) | data formatting | bytes 393216 | tf_op args[3]
  4.4 1.1 %copy.78 = bf16[256,384]{0,1:T(8,128)(2,1)S(1)} copy(bf16[256,384]{1,0:T(8,128)(2,1)} %param.17) | data formatting | bytes 393216 | tf_op args[0]
  5.5 0.2 fusion.89
  5.8 1.1 %copy.75 = bf16[256,384]{0,1:T(8,128)(2,1)S(1)} copy(bf16[256,384]{1,0:T(8,128)(2,1)} %param.18) | data formatting | bytes 393216 | tf_op args[1]
  6.9 0.2 fusion.90
  7.3 0.3 scatter.15
  7.5 0.7 pad_maximum_fusion.10
  8.2 0.5 collective-permute-start
  8.7 1.3 %constant_dynamic-slice_fusion = (bf16[192,384]{1,0:T(8,128)(2,1)S(1)}, bf16[192,384]{1,0:T(8,128)(2,1)S(1)}, bf16[192,384]{1,0:T(8,128)(2,1)S(1)}, bf16[192,384...) fusion(bf16[6144,384]{1,0:T(8,128)(2,1)} %param.23, s32[]{:T(128)S(6)} %select_n.223, ...), kind=kLoop, calls=%fused_computation.117 | loop fusion | bytes 1769484 | tf_op jit(solution)/shard_map/dynamic_slice | solution.py:111
  10.0 0.7 pad_maximum_fusion.7
  10.8 2.6 %collective-permute-start.3 = (bf16[192,768]{1,0:T(8,128)(2,1)}, bf16[192,768]{1,0:T(8,128)(2,1)S(1)}, u32[]{:S(2)}, u32[]{:S(2)}) collective-permute-start(bf16[192,768]{1,0:T(8,128)(2,1)} %pad_maximum_fusion.7), channel_id=1, source_target_pairs={{0,1},{1,0},{2,3},{3,2},{4,5},{5,4},{6,7},{7,6},{8,9},{9,8},{10,11... | collective-permute-start | bytes 884744 | tf_op jit(solution)/shard_map/ppermute | solution.py:113
  13.4 2.7 %collective-permute-start.8 = (bf16[192,768]{1,0:T(8,128)(2,1)S(1)}, bf16[192,768]{1,0:T(8,128)(2,1)S(1)}, u32[]{:S(2)}, u32[]{:S(2)}) collective-permute-start(bf16[192,768]{1,0:T(8,128)(2,1)S(1)} %pad_maximum_fusion.8), channel_id=1, source_target_pairs={{0,2},{1,3},{2,0},{3,1},{4,6},{5,7},{6,4},{7,5},{8,10},{9,11},{10,... | collective-permute-start | bytes 884744 | tf_op jit(solution)/shard_map/ppermute | solution.py:113
  16.0 0.7 pad_maximum_fusion.9
  16.8 0.4 fusion.24
  17.2 0.8 slice_convert_fusion.2
  18.0 0.2 subtract_convert_fusion
  18.2 0.3 scatter.19
  18.5 1.0 slice_convert_fusion.1
  19.8 0.2 fusion.85
  20.0 1.8 %collective-permute-start.1 = (bf16[784,128]{1,0:T(8,128)(2,1)S(1)}, bf16[784,128]{1,0:T(8,128)(2,1)S(1)}, u32[]{:S(2)}, u32[]{:S(2)}) collective-permute-start(bf16[784,128]{1,0:T(8,128)(2,1)S(1)} %pad_maximum_fusion.11), channel_id=1, source_target_pairs={{0,8},{4,12},{8,0},{12,4},{16,24},{20,28},{24,16},{28,20},{1,9},{5... | collective-permute-start | bytes 602120 | tf_op jit(solution)/shard_map/ppermute | solution.py:31
  21.7 0.2 convolution_bitcast_fusion.1
  22.0 5.2 %collective-permute-done.3 = bf16[192,768]{1,0:T(8,128)(2,1)S(1)} collective-permute-done((bf16[192,768]{1,0:T(8,128)(2,1)}, bf16[192,768]{1,0:T(8,128)(2,1)S(1)}, u32[]{:S(2)}, u32[]{:S(2)}) %collective-permute-start.3) | collective-permute-done | bytes 294944 | tf_op jit(solution)/shard_map/ppermute | solution.py:113
  27.2 1.7 %collective-permute-start.4 = (bf16[192,768]{1,0:T(8,128)(2,1)S(1)}, bf16[192,768]{1,0:T(8,128)(2,1)S(1)}, u32[]{:S(2)}, u32[]{:S(2)}) collective-permute-start(bf16[192,768]{1,0:T(8,128)(2,1)S(1)} %collective-permute-done.3), channel_id=1, source_target_pairs={{0,8},{4,20},{8,0},{12,28},{16,24},{20,4},{24,16},{28,12},{1,9},{5... | collective-permute-start | bytes 884744 | tf_op jit(solution)/shard_map/ppermute | solution.py:70
  28.9 0.2 fusion.44
  29.1 1.6 %collective-permute-start.2 = (bf16[384,128]{1,0:T(8,128)(2,1)S(1)}, bf16[384,128]{1,0:T(8,128)(2,1)S(1)}, u32[]{:S(2)}, u32[]{:S(2)}) collective-permute-start(bf16[384,128]{1,0:T(8,128)(2,1)S(1)} %bitcast.128), channel_id=1, source_target_pairs={{0,16},{4,20},{8,24},{12,28},{16,0},{20,4},{24,8},{28,12},{1,17},{... | collective-permute-start | bytes 294920 | tf_op jit(solution)/shard_map/ppermute | solution.py:38
  30.7 6.1 %collective-permute-done.8 = bf16[192,768]{1,0:T(8,128)(2,1)S(1)} collective-permute-done((bf16[192,768]{1,0:T(8,128)(2,1)S(1)}, bf16[192,768]{1,0:T(8,128)(2,1)S(1)}, u32[]{:S(2)}, u32[]{:S(2)}) %collective-permute-start.8) | collective-permute-done | bytes 294944 | tf_op jit(solution)/shard_map/ppermute | solution.py:113
  36.9 1.5 %collective-permute-start.9 = (bf16[192,768]{1,0:T(8,128)(2,1)S(1)}, bf16[192,768]{1,0:T(8,128)(2,1)S(1)}, u32[]{:S(2)}, u32[]{:S(2)}) collective-permute-start(bf16[192,768]{1,0:T(8,128)(2,1)S(1)} %collective-permute-done.8), channel_id=1, source_target_pairs={{0,8},{4,20},{8,0},{12,28},{16,24},{20,4},{24,16},{28,12},{1,9},{5... | collective-permute-start | bytes 884744 | tf_op jit(solution)/shard_map/ppermute | solution.py:70
  38.4 0.5 collective-permute-start.16
  38.9 0.3 fusion.35
  39.2 1.6 %collective-permute-start.5 = (bf16[384,768]{1,0:T(8,128)(2,1)S(1)}, bf16[384,768]{1,0:T(8,128)(2,1)S(1)}, u32[]{:S(2)}, u32[]{:S(2)}) collective-permute-start(bf16[384,768]{1,0:T(8,128)(2,1)S(1)} %pad_maximum_fusion.3), channel_id=1, source_target_pairs={{0,16},{4,12},{8,24},{12,4},{16,0},{20,28},{24,8},{28,20},{1,17},{... | collective-permute-start | bytes 1769480 | tf_op jit(solution)/shard_map/ppermute | solution.py:70
  40.8 0.3 fusion.25
  41.1 5.6 %collective-permute-done.9 = bf16[192,768]{1,0:T(8,128)(2,1)S(1)} collective-permute-done((bf16[192,768]{1,0:T(8,128)(2,1)S(1)}, bf16[192,768]{1,0:T(8,128)(2,1)S(1)}, u32[]{:S(2)}, u32[]{:S(2)}) %collective-permute-start.9) | collective-permute-done | bytes 294944 | tf_op jit(solution)/shard_map/ppermute | solution.py:70
  46.7 1.7 %collective-permute-start.10 = (bf16[384,768]{1,0:T(8,128)(2,1)S(1)}, bf16[384,768]{1,0:T(8,128)(2,1)S(1)}, u32[]{:S(2)}, u32[]{:S(2)}) collective-permute-start(bf16[384,768]{1,0:T(8,128)(2,1)S(1)} %pad_maximum_fusion.4), channel_id=1, source_target_pairs={{0,16},{4,12},{8,24},{12,4},{16,0},{20,28},{24,8},{28,20},{1,17},{... | collective-permute-start | bytes 1769480 | tf_op jit(solution)/shard_map/ppermute | solution.py:70
  48.4 0.3 fusion.34
  48.7 0.5 collective-permute-done.5
  49.2 1.2 %pad_maximum_fusion = bf16[768,768]{1,0:T(8,128)(2,1)} fusion(bf16[384,768]{1,0:T(8,128)(2,1)S(1)} %collective-permute-done.5, bf16[192,768]{1,0:T(8,128)(2,1)S(1)} %collective-permute-done.4, bf16[192,768]{1,0:T(8,128)(2,1)S(1)} %collective-permute-done.3), kind=kLoop, calls=%fused_computation.41 | loop fusion | flops 3538944 | bytes 2359296 | tf_op jit(solution)/shard_map/concatenate | solution.py:70
  50.4 3.4 %collective-permute-start.6 = (bf16[768,768]{1,0:T(8,128)(2,1)}, bf16[768,768]{1,0:T(8,128)(2,1)}, u32[]{:S(2)}, u32[]{:S(2)}) collective-permute-start(bf16[768,768]{1,0:T(8,128)(2,1)} %pad_maximum_fusion), channel_id=1, source_target_pairs={{0,4},{4,0},{8,12},{12,8},{16,20},{20,16},{24,28},{28,24},{1,5},{5... | collective-permute-start | bytes 3538952 | tf_op jit(solution)/shard_map/ppermute | solution.py:71
  53.8 0.7 copy-done.4
  54.5 0.9 collective-permute-start.17
  55.4 0.8 pad_maximum_fusion.6
  56.2 3.4 %collective-permute-start.7 = (bf16[256,768]{0,1:T(8,128)(2,1)}, bf16[256,768]{0,1:T(8,128)(2,1)}, u32[]{:S(2)}, u32[]{:S(2)}) collective-permute-start(bf16[256,768]{0,1:T(8,128)(2,1)} %pad_maximum_fusion.6), channel_id=1, source_target_pairs={{0,1},{1,0},{2,3},{3,2},{4,5},{5,4},{6,7},{7,6},{8,9},{9,8},{10,11... | collective-permute-start | bytes 1179656 | tf_op jit(solution)/shard_map/ppermute | solution.py:149
  59.6 1.2 %pad_maximum_fusion.1 = bf16[768,768]{1,0:T(8,128)(2,1)} fusion(bf16[384,768]{1,0:T(8,128)(2,1)S(1)} %collective-permute-done.10, bf16[192,768]{1,0:T(8,128)(2,1)S(1)} %collective-permute-done.9, bf16[192,768]{1,0:T(8,128)(2,1)S(1)} %collective-permute-done.8), kind=kLoop, calls=%fused_computation.42 | loop fusion | flops 3538944 | bytes 2359296 | tf_op jit(solution)/shard_map/concatenate | solution.py:70
  60.8 0.4 collective-permute-start.11
  61.2 0.6 gather_fusion
  61.9 0.6 gather_fusion.1
  62.5 0.7 collective-permute-start.13
  63.2 6.6 %collective-permute-done.7 = bf16[256,768]{0,1:T(8,128)(2,1)} collective-permute-done((bf16[256,768]{0,1:T(8,128)(2,1)}, bf16[256,768]{0,1:T(8,128)(2,1)}, u32[]{:S(2)}, u32[]{:S(2)}) %collective-permute-start.7) | collective-permute-done | bytes 393248 | tf_op jit(solution)/shard_map/ppermute | solution.py:149
  69.8 0.7 collective-permute-start.12
  70.6 0.1 collective-permute-start.18
  70.8 0.6 copy-done.13
  71.4 1.3 %collective-permute-start.14 = (bf16[256,768]{0,1:T(8,128)(2,1)S(1)}, bf16[256,768]{0,1:T(8,128)(2,1)S(1)}, u32[]{:S(2)}, u32[]{:S(2)}) collective-permute-start(bf16[256,768]{0,1:T(8,128)(2,1)S(1)} %collective-permute-done.13), channel_id=1, source_target_pairs={{2,3},{1,0},{6,7},{5,4},{10,11},{9,8},{14,15},{13,12},{18,19},{17,... | collective-permute-start | bytes 1179656 | tf_op jit(solution)/shard_map/ppermute | solution.py:151
  72.7 1.8 %fusion.32 = f32[1536,256]{1,0:T(8,128)S(1)} fusion(bf16[256,384]{0,1:T(8,128)(2,1)S(1)} %bitcast.111, bf16[6144,384]{1,0:T(8,128)(2,1)} %param.22, s32[]{:T(128)S(6)} %select_n.192), kind=kOutput, calls=%fused_computation.45 | convolution fusion | flops 301989888 | bytes 2949124 | tf_op jit(solution)/shard_map/dot_general | solution.py:162
  74.5 1.4 %collective-permute-start.19 = (bf16[256,768]{0,1:T(8,128)(2,1)S(1)}, bf16[256,768]{0,1:T(8,128)(2,1)S(1)}, u32[]{:S(2)}, u32[]{:S(2)}) collective-permute-start(bf16[256,768]{0,1:T(8,128)(2,1)S(1)} %collective-permute-done.12), channel_id=1, source_target_pairs={{2,3},{1,0},{6,7},{5,4},{10,11},{9,8},{14,15},{13,12},{18,19},{17,... | collective-permute-start | bytes 1179656 | tf_op jit(solution)/shard_map/ppermute | solution.py:153
  76.0 2.1 %fusion = f32[1536,256]{1,0:T(8,128)S(1)} fusion(bf16[256,768]{0,1:T(8,128)(2,1)} %collective-permute-done.7, bf16[768,768]{1,0:T(8,128)(2,1)} %collective-permute-done.6, bf16[384,768]{1,0:T(8,128)(2,1)S(1)} %copy-done.10, bf16[192,768]{1,0:T(8,128)(2,1)S(1)} %copy-done.3, bf16[192,768]{1,0:T(8,128)(2,1)S(1)} %collective-permute-done.3), kind=kOutput, calls=%fused_computation.6 | convolution fusion | flops 613416960 | bytes 4325376 | tf_op jit(solution)/shard_map/dot_general | solution.py:169
  78.2 9.8 %collective-permute-done.14 = bf16[256,768]{0,1:T(8,128)(2,1)S(1)} collective-permute-done((bf16[256,768]{0,1:T(8,128)(2,1)S(1)}, bf16[256,768]{0,1:T(8,128)(2,1)S(1)}, u32[]{:S(2)}, u32[]{:S(2)}) %collective-permute-start.14) | collective-permute-done | bytes 393248 | tf_op jit(solution)/shard_map/ppermute | solution.py:151
  87.9 2.1 %convolution_add_fusion.1 = f32[1536,256]{1,0:T(8,128)S(1)} fusion(f32[1536,256]{1,0:T(8,128)S(1)} %fusion, bf16[768,768]{1,0:T(8,128)(2,1)} %collective-permute-done.11, bf16[384,768]{1,0:T(8,128)(2,1)S(1)} %copy-done.12, bf16[192,768]{1,0:T(8,128)(2,1)S(1)} %copy-done.8, bf16[192,768]{1,0:T(8,128)(2,1)S(1)} %collective-permute-done.8, ...), kind=kOutput, calls=%fused_computation.4 | convolution fusion | flops 614006784 | bytes 6291457 | tf_op jit(solution)/shard_map/dot_general | solution.py:169
  90.0 6.3 %collective-permute-done.19 = bf16[256,768]{0,1:T(8,128)(2,1)S(1)} collective-permute-done((bf16[256,768]{0,1:T(8,128)(2,1)S(1)}, bf16[256,768]{0,1:T(8,128)(2,1)S(1)}, u32[]{:S(2)}, u32[]{:S(2)}) %collective-permute-start.19) | collective-permute-done | bytes 393248 | tf_op jit(solution)/shard_map/ppermute | solution.py:153
  96.3 2.0 %convolution_add_fusion = f32[1536,256]{1,0:T(8,128)} fusion(f32[1536,256]{1,0:T(8,128)S(1)} %convolution_add_fusion.1, bf16[768,768]{1,0:T(8,128)(2,1)S(1)} %collective-permute-done.18, bf16[384,768]{1,0:T(8,128)(2,1)S(1)} %copy-done.14, bf16[192,768]{1,0:T(8,128)(2,1)S(1)} %copy-done.6, bf16[192,768]{1,0:T(8,128)(2,1)S(1)} %collective-permute-done.15, ...), kind=kOutput, calls=%fused_computation.3 | convolution fusion | flops 614006784 | bytes 6291457 | tf_op jit(solution)/shard_map/dot_general | solution.py:169
  98.4 2.1 %gather_fusion.2 = f32[8,192,256]{2,1,0:T(8,128)S(1)} fusion(f32[8,192,256]{2,1,0:T(8,128)} %bitcast.117, s32[1024]{0:T(1024)S(1)} %pad_clamp_fusion), kind=kCustom, calls=%fused_computation.2 | custom fusion | bytes 3145760 | tf_op jit(solution)/shard_map/gather | solution.py:173
  100.5 2.7 %fusion.22 = bf16[1536,256]{1,0:T(8,128)(2,1)} fusion(f32[8,192,256]{2,1,0:T(8,128)S(1)} %gather_fusion.2, f32[1536,256]{1,0:T(8,128)S(1)} %fusion.32, bf16[256,384]{0,1:T(8,128)(2,1)S(1)} %bitcast.104, bf16[6144,384]{1,0:T(8,128)(2,1)} %param.23, s32[]{:T(128)S(6)} %select_n.192), kind=kOutput, calls=%fused_computation.29 | convolution fusion | flops 303169536 | bytes 5308420 | tf_op jit(solution)/shard_map/dot_general | solution.py:164
  (73 shorter events, 1.5 us)
Async XLA Ops:
  8.2 9.0 %collective-permute-start = (bf16[784,128]{0,1:T(8,128)(2,1)}, bf16[784,128]{0,1:T(8,128)(2,1)}, u32[]{:S(2)}, u32[]{:S(2)}) collective-permute-start(bf16[784,128]{0,1:T(8,128)(2,1)} %pad_maximum_fusion.10), channel_id=1, source_target_pairs={{0,4},{4,0},{8,12},{12,8},{16,20},{20,16},{24,28},{28,24},{1,5},{5... | collective-permute-start | bytes 602120 | tf_op jit(solution)/shard_map/ppermute | solution.py:31
  10.8 16.4 %collective-permute-start.3 = (bf16[192,768]{1,0:T(8,128)(2,1)}, bf16[192,768]{1,0:T(8,128)(2,1)S(1)}, u32[]{:S(2)}, u32[]{:S(2)}) collective-permute-start(bf16[192,768]{1,0:T(8,128)(2,1)} %pad_maximum_fusion.7), channel_id=1, source_target_pairs={{0,1},{1,0},{2,3},{3,2},{4,5},{5,4},{6,7},{7,6},{8,9},{9,8},{10,11... | collective-permute-start | bytes 884744 | tf_op jit(solution)/shard_map/ppermute | solution.py:113
  13.4 23.5 %collective-permute-start.8 = (bf16[192,768]{1,0:T(8,128)(2,1)S(1)}, bf16[192,768]{1,0:T(8,128)(2,1)S(1)}, u32[]{:S(2)}, u32[]{:S(2)}) collective-permute-start(bf16[192,768]{1,0:T(8,128)(2,1)S(1)} %pad_maximum_fusion.8), channel_id=1, source_target_pairs={{0,2},{1,3},{2,0},{3,1},{4,6},{5,7},{6,4},{7,5},{8,10},{9,11},{10,... | collective-permute-start | bytes 884744 | tf_op jit(solution)/shard_map/ppermute | solution.py:113
  16.8 21.6 %collective-permute-start.15 = (bf16[192,768]{1,0:T(8,128)(2,1)}, bf16[192,768]{1,0:T(8,128)(2,1)S(1)}, u32[]{:S(2)}, u32[]{:S(2)}) collective-permute-start(bf16[192,768]{1,0:T(8,128)(2,1)} %pad_maximum_fusion.9), channel_id=1, source_target_pairs={{0,3},{1,2},{2,1},{3,0},{4,7},{5,6},{6,5},{7,4},{8,11},{9,10},{10,... | collective-permute-start | bytes 884744 | tf_op jit(solution)/shard_map/ppermute | solution.py:113
  20.0 8.9 %collective-permute-start.1 = (bf16[784,128]{1,0:T(8,128)(2,1)S(1)}, bf16[784,128]{1,0:T(8,128)(2,1)S(1)}, u32[]{:S(2)}, u32[]{:S(2)}) collective-permute-start(bf16[784,128]{1,0:T(8,128)(2,1)S(1)} %pad_maximum_fusion.11), channel_id=1, source_target_pairs={{0,8},{4,12},{8,0},{12,4},{16,24},{20,28},{24,16},{28,20},{1,9},{5... | collective-permute-start | bytes 602120 | tf_op jit(solution)/shard_map/ppermute | solution.py:31
  27.2 12.0 %collective-permute-start.4 = (bf16[192,768]{1,0:T(8,128)(2,1)S(1)}, bf16[192,768]{1,0:T(8,128)(2,1)S(1)}, u32[]{:S(2)}, u32[]{:S(2)}) collective-permute-start(bf16[192,768]{1,0:T(8,128)(2,1)S(1)} %collective-permute-done.3), channel_id=1, source_target_pairs={{0,8},{4,20},{8,0},{12,28},{16,24},{20,4},{24,16},{28,12},{1,9},{5... | collective-permute-start | bytes 884744 | tf_op jit(solution)/shard_map/ppermute | solution.py:70
  29.1 9.8 %collective-permute-start.2 = (bf16[384,128]{1,0:T(8,128)(2,1)S(1)}, bf16[384,128]{1,0:T(8,128)(2,1)S(1)}, u32[]{:S(2)}, u32[]{:S(2)}) collective-permute-start(bf16[384,128]{1,0:T(8,128)(2,1)S(1)} %bitcast.128), channel_id=1, source_target_pairs={{0,16},{4,20},{8,24},{12,28},{16,0},{20,4},{24,8},{28,12},{1,17},{... | collective-permute-start | bytes 294920 | tf_op jit(solution)/shard_map/ppermute | solution.py:38
  36.9 9.8 %collective-permute-start.9 = (bf16[192,768]{1,0:T(8,128)(2,1)S(1)}, bf16[192,768]{1,0:T(8,128)(2,1)S(1)}, u32[]{:S(2)}, u32[]{:S(2)}) collective-permute-start(bf16[192,768]{1,0:T(8,128)(2,1)S(1)} %collective-permute-done.8), channel_id=1, source_target_pairs={{0,8},{4,20},{8,0},{12,28},{16,24},{20,4},{24,16},{28,12},{1,9},{5... | collective-permute-start | bytes 884744 | tf_op jit(solution)/shard_map/ppermute | solution.py:70
  38.4 15.4 %collective-permute-start.16 = (bf16[192,768]{1,0:T(8,128)(2,1)S(1)}, bf16[192,768]{1,0:T(8,128)(2,1)S(1)}, u32[]{:S(2)}, u32[]{:S(2)}) collective-permute-start(bf16[192,768]{1,0:T(8,128)(2,1)S(1)} %collective-permute-done.15), channel_id=1, source_target_pairs={{0,8},{4,20},{8,0},{12,28},{16,24},{20,4},{24,16},{28,12},{1,9},{5... | collective-permute-start | bytes 884744 | tf_op jit(solution)/shard_map/ppermute | solution.py:70
  39.2 11.2 %copy-start.2 = (bf16[192,768]{1,0:T(8,128)(2,1)}, bf16[192,768]{1,0:T(8,128)(2,1)S(1)}, u32[]{:S(2)}) copy-start(bf16[192,768]{1,0:T(8,128)(2,1)S(1)} %collective-permute-done.4) | copy-start | bytes 884740
  39.2 9.9 %collective-permute-start.5 = (bf16[384,768]{1,0:T(8,128)(2,1)S(1)}, bf16[384,768]{1,0:T(8,128)(2,1)S(1)}, u32[]{:S(2)}, u32[]{:S(2)}) collective-permute-start(bf16[384,768]{1,0:T(8,128)(2,1)S(1)} %pad_maximum_fusion.3), channel_id=1, source_target_pairs={{0,16},{4,12},{8,24},{12,4},{16,0},{20,28},{24,8},{28,20},{1,17},{... | collective-permute-start | bytes 1769480 | tf_op jit(solution)/shard_map/ppermute | solution.py:70
  46.7 13.0 %copy-start.7 = (bf16[192,768]{1,0:T(8,128)(2,1)}, bf16[192,768]{1,0:T(8,128)(2,1)S(1)}, u32[]{:S(2)}) copy-start(bf16[192,768]{1,0:T(8,128)(2,1)S(1)} %collective-permute-done.9) | copy-start | bytes 884740
  46.7 12.9 %collective-permute-start.10 = (bf16[384,768]{1,0:T(8,128)(2,1)S(1)}, bf16[384,768]{1,0:T(8,128)(2,1)S(1)}, u32[]{:S(2)}, u32[]{:S(2)}) collective-permute-start(bf16[384,768]{1,0:T(8,128)(2,1)S(1)} %pad_maximum_fusion.4), channel_id=1, source_target_pairs={{0,16},{4,12},{8,24},{12,4},{16,0},{20,28},{24,8},{28,20},{1,17},{... | collective-permute-start | bytes 1769480 | tf_op jit(solution)/shard_map/ppermute | solution.py:70
  49.2 11.6 %copy-start.9 = (bf16[384,768]{1,0:T(8,128)(2,1)}, bf16[384,768]{1,0:T(8,128)(2,1)S(1)}, u32[]{:S(2)}) copy-start(bf16[384,768]{1,0:T(8,128)(2,1)S(1)} %collective-permute-done.5) | copy-start | bytes 1769476
  50.4 10.8 %copy-start.1 = (s32[8]{0:T(128)S(1)}, s32[8]{0:T(128)}, u32[]{:S(2)}) copy-start(s32[8]{0:T(128)} %constant.177.clone) | copy-start | bytes 100
  50.4 11.5 %copy-start = (s32[8]{0:T(128)S(1)}, s32[8]{0:T(128)}, u32[]{:S(2)}) copy-start(s32[8]{0:T(128)} %constant.178.clone) | copy-start | bytes 100
  50.4 25.6 %collective-permute-start.6 = (bf16[768,768]{1,0:T(8,128)(2,1)}, bf16[768,768]{1,0:T(8,128)(2,1)}, u32[]{:S(2)}, u32[]{:S(2)}) collective-permute-start(bf16[768,768]{1,0:T(8,128)(2,1)} %pad_maximum_fusion), channel_id=1, source_target_pairs={{0,4},{4,0},{8,12},{12,8},{16,20},{20,16},{24,28},{28,24},{1,5},{5... | collective-permute-start | bytes 3538952 | tf_op jit(solution)/shard_map/ppermute | solution.py:71
  53.8 0.7 copy-start.4
  54.5 16.0 %copy-start.5 = (bf16[192,768]{1,0:T(8,128)(2,1)S(1)}, bf16[192,768]{1,0:T(8,128)(2,1)}, u32[]{:S(2)}) copy-start(bf16[192,768]{1,0:T(8,128)(2,1)} %copy-done.4) | copy-start | bytes 884740
  54.5 16.0 %collective-permute-start.17 = (bf16[384,768]{1,0:T(8,128)(2,1)S(1)}, bf16[384,768]{1,0:T(8,128)(2,1)S(1)}, u32[]{:S(2)}, u32[]{:S(2)}) collective-permute-start(bf16[384,768]{1,0:T(8,128)(2,1)S(1)} %pad_maximum_fusion.5), channel_id=1, source_target_pairs={{0,16},{4,12},{8,24},{12,4},{16,0},{20,28},{24,8},{28,20},{1,17},{... | collective-permute-start | bytes 1769480 | tf_op jit(solution)/shard_map/ppermute | solution.py:70
  56.2 13.6 %collective-permute-start.7 = (bf16[256,768]{0,1:T(8,128)(2,1)}, bf16[256,768]{0,1:T(8,128)(2,1)}, u32[]{:S(2)}, u32[]{:S(2)}) collective-permute-start(bf16[256,768]{0,1:T(8,128)(2,1)} %pad_maximum_fusion.6), channel_id=1, source_target_pairs={{0,1},{1,0},{2,3},{3,2},{4,5},{5,4},{6,7},{7,6},{8,9},{9,8},{10,11... | collective-permute-start | bytes 1179656 | tf_op jit(solution)/shard_map/ppermute | solution.py:149
  59.6 1.6 %copy-start.11 = (bf16[384,768]{1,0:T(8,128)(2,1)}, bf16[384,768]{1,0:T(8,128)(2,1)S(1)}, u32[]{:S(2)}) copy-start(bf16[384,768]{1,0:T(8,128)(2,1)S(1)} %collective-permute-done.10) | copy-start | bytes 1769476
  60.8 27.1 %collective-permute-start.11 = (bf16[768,768]{1,0:T(8,128)(2,1)}, bf16[768,768]{1,0:T(8,128)(2,1)}, u32[]{:S(2)}, u32[]{:S(2)}) collective-permute-start(bf16[768,768]{1,0:T(8,128)(2,1)} %pad_maximum_fusion.1), channel_id=1, source_target_pairs={{0,4},{4,0},{8,12},{12,8},{16,20},{20,16},{24,28},{28,24},{1,5},{5... | collective-permute-start | bytes 3538952 | tf_op jit(solution)/shard_map/ppermute | solution.py:71
  62.5 8.3 %collective-permute-start.13 = (bf16[256,768]{0,1:T(8,128)(2,1)}, bf16[256,768]{0,1:T(8,128)(2,1)S(1)}, u32[]{:S(2)}, u32[]{:S(2)}) collective-permute-start(bf16[256,768]{0,1:T(8,128)(2,1)} %pad_maximum_fusion.6), channel_id=1, source_target_pairs={{1,2},{2,1},{5,6},{6,5},{9,10},{10,9},{13,14},{14,13},{17,18},{18,... | collective-permute-start | bytes 1179656 | tf_op jit(solution)/shard_map/ppermute | solution.py:150
  63.2 12.8 %copy-start.3 = (bf16[192,768]{1,0:T(8,128)(2,1)S(1)}, bf16[192,768]{1,0:T(8,128)(2,1)}, u32[]{:S(2)}) copy-start(bf16[192,768]{1,0:T(8,128)(2,1)} %copy-done.2) | copy-start | bytes 884740
  63.2 12.8 %copy-start.10 = (bf16[384,768]{1,0:T(8,128)(2,1)S(1)}, bf16[384,768]{1,0:T(8,128)(2,1)}, u32[]{:S(2)}) copy-start(bf16[384,768]{1,0:T(8,128)(2,1)} %copy-done.9) | copy-start | bytes 1769476
  69.8 4.7 %collective-permute-start.12 = (bf16[256,768]{0,1:T(8,128)(2,1)}, bf16[256,768]{0,1:T(8,128)(2,1)S(1)}, u32[]{:S(2)}, u32[]{:S(2)}) collective-permute-start(bf16[256,768]{0,1:T(8,128)(2,1)} %collective-permute-done.7), channel_id=1, source_target_pairs={{1,2},{2,1},{5,6},{6,5},{9,10},{10,9},{13,14},{14,13},{17,18},{18,... | collective-permute-start | bytes 1179656 | tf_op jit(solution)/shard_map/ppermute | solution.py:152
  70.5 0.8 copy-start.13
  70.6 25.7 %collective-permute-start.18 = (bf16[768,768]{1,0:T(8,128)(2,1)S(1)}, bf16[768,768]{1,0:T(8,128)(2,1)S(1)}, u32[]{:S(2)}, u32[]{:S(2)}) collective-permute-start(bf16[768,768]{1,0:T(8,128)(2,1)S(1)} %pad_maximum_fusion.2), channel_id=1, source_target_pairs={{0,4},{4,0},{8,12},{12,8},{16,20},{20,16},{24,28},{28,24},{1,5},{5... | collective-permute-start | bytes 3538952 | tf_op jit(solution)/shard_map/ppermute | solution.py:71
  71.4 16.5 %collective-permute-start.14 = (bf16[256,768]{0,1:T(8,128)(2,1)S(1)}, bf16[256,768]{0,1:T(8,128)(2,1)S(1)}, u32[]{:S(2)}, u32[]{:S(2)}) collective-permute-start(bf16[256,768]{0,1:T(8,128)(2,1)S(1)} %collective-permute-done.13), channel_id=1, source_target_pairs={{2,3},{1,0},{6,7},{5,4},{10,11},{9,8},{14,15},{13,12},{18,19},{17,... | collective-permute-start | bytes 1179656 | tf_op jit(solution)/shard_map/ppermute | solution.py:151
  74.5 13.4 %copy-start.8 = (bf16[192,768]{1,0:T(8,128)(2,1)S(1)}, bf16[192,768]{1,0:T(8,128)(2,1)}, u32[]{:S(2)}) copy-start(bf16[192,768]{1,0:T(8,128)(2,1)} %copy-done.7) | copy-start | bytes 884740
  74.5 13.4 %copy-start.12 = (bf16[384,768]{1,0:T(8,128)(2,1)S(1)}, bf16[384,768]{1,0:T(8,128)(2,1)}, u32[]{:S(2)}) copy-start(bf16[384,768]{1,0:T(8,128)(2,1)} %copy-done.11) | copy-start | bytes 1769476
  74.5 21.8 %collective-permute-start.19 = (bf16[256,768]{0,1:T(8,128)(2,1)S(1)}, bf16[256,768]{0,1:T(8,128)(2,1)S(1)}, u32[]{:S(2)}, u32[]{:S(2)}) collective-permute-start(bf16[256,768]{0,1:T(8,128)(2,1)S(1)} %collective-permute-done.12), channel_id=1, source_target_pairs={{2,3},{1,0},{6,7},{5,4},{10,11},{9,8},{14,15},{13,12},{18,19},{17,... | collective-permute-start | bytes 1179656 | tf_op jit(solution)/shard_map/ppermute | solution.py:153
  78.1 18.2 %copy-start.6 = (bf16[192,768]{1,0:T(8,128)(2,1)S(1)}, bf16[192,768]{1,0:T(8,128)(2,1)}, u32[]{:S(2)}) copy-start(bf16[192,768]{1,0:T(8,128)(2,1)} %copy-done.4) | copy-start | bytes 884740
  78.2 18.2 %copy-start.14 = (bf16[384,768]{1,0:T(8,128)(2,1)S(1)}, bf16[384,768]{1,0:T(8,128)(2,1)}, u32[]{:S(2)}) copy-start(bf16[384,768]{1,0:T(8,128)(2,1)} %copy-done.13) | copy-start | bytes 1769476

commit v2 on v0

v2 whole, which is shorter than its diff:
```python
import functools

import jax
import jax.numpy as jnp
from jax import lax
from jax.experimental import pallas as pl
from jax.experimental.pallas import tpu as pltpu
from jax.sharding import PartitionSpec as P

F32 = jnp.float32
BF16 = jnp.bfloat16
VMEM_BYTES = 40 * 1024 * 1024


def contract(a, b, left, right):
    return lax.dot_general(a, b, (((left,), (right,)), ((), ())), preferred_element_type=F32)


def call(kernel, out_shape, flops, nbytes, *args, aliases=None, **spec):
    return pl.pallas_call(
        kernel,
        out_shape=out_shape,
        cost_estimate=pl.CostEstimate(flops=flops, bytes_accessed=nbytes, transcendentals=0),
        compiler_params=pltpu.CompilerParams(vmem_limit_bytes=VMEM_BYTES),
        input_output_aliases=aliases or {},
        **spec,
    )(*args)


def whole(shape):
    return pl.BlockSpec(shape, lambda *_: (0,) * len(shape))


def thirds(x):
    high = x.astype(BF16)
    rest = x - high.astype(F32)
    middle = rest.astype(BF16)
    return high, middle, (rest - middle.astype(F32)).astype(BF16)


def triangle(span):
    rows = lax.broadcasted_iota(jnp.int32, (span, span), 0)
    cols = lax.broadcasted_iota(jnp.int32, (span, span), 1)
    return rows >= cols


def upper_half(hop):
    return ((lax.axis_index("seq") // hop) % 2).astype(F32)


def states_kernel(nheads, width, decay_ref, q_ref, k_ref, v_ref, g_ref, sent_ref, held_ref, logs_ref):
    span = q_ref.shape[0]
    tri = triangle(span).astype(F32).astype(BF16)
    cum = sum(contract(tri, part, 1, 0) for part in thirds(decay_ref[...]))
    rows = nheads * width
    row = lax.broadcasted_iota(jnp.int32, (8, width), 0)
    totals = jnp.zeros((8, width), F32)
    for h in range(nheads):
        cols = slice(h * width, (h + 1) * width)
        cum_h = cum[:, h : h + 1]
        last = cum[span - 1 : span, h : h + 1]
        key_w = (k_ref[:, cols].astype(F32) * jnp.exp(last - cum_h)).astype(BF16)
        query_w = (q_ref[:, cols].astype(F32) * jnp.exp(cum_h)).astype(BF16)
        state = contract(key_w, v_ref[:, cols], 0, 0)
        grad = contract(query_w, g_ref[:, cols], 0, 0)
        held_ref[h * width : (h + 1) * width, :] = state
        held_ref[rows + h * width : rows + (h + 1) * width, :] = grad
        sent_ref[h * width : (h + 1) * width, :] = state.astype(BF16)
        sent_ref[rows + h * width : rows + (h + 1) * width, :] = grad.astype(BF16)
        totals = jnp.where(row == h, jnp.broadcast_to(last, (8, width)), totals)
    high = totals.astype(BF16).astype(F32)
    sent_ref[2 * rows :, :] = jnp.concatenate([high, totals - high]).astype(BF16)
    logs_ref[0:8, :] = totals
    logs_ref[8:24, :] = jnp.zeros((16, width), F32)


def step_kernel(nheads, width, hop, first, final_next, got_ref, held_ref, logs_ref, *refs):
    if first:
        sent_ref, held_out, logs_out, enter_out = refs
    else:
        enter_ref, sent_ref, held_out, logs_out, enter_out = refs
    rows = nheads * width
    up = upper_half(hop)
    low = 1.0 - up
    tail = got_ref[2 * rows :, :].astype(F32)
    got_total = tail[0:8] + tail[8:16]
    total, before, after = logs_ref[0:8, :], logs_ref[8:16, :], logs_ref[16:24, :]
    own_decay, got_decay = jnp.exp(total), jnp.exp(got_total)
    from_before, from_after = up * jnp.exp(before), low * jnp.exp(after)
    total = total + got_total
    logs_out[0:8, :] = total
    logs_out[8:16, :] = before + up * got_total
    logs_out[16:24, :] = after + low * got_total
    if final_next:
        next_up = upper_half(2 * hop) > 0.5
    else:
        high = total.astype(BF16).astype(F32)
        sent_ref[2 * rows :, :] = jnp.concatenate([high, total - high]).astype(BF16)
    for h in range(nheads):
        one = slice(h * width, (h + 1) * width)
        two = slice(rows + h * width, rows + (h + 1) * width)
        got_state, got_grad = got_ref[one, :].astype(F32), got_ref[two, :].astype(F32)
        own, got = own_decay[h : h + 1, :], got_decay[h : h + 1, :]
        state = (up + low * got) * held_ref[one, :] + (up * own + low) * got_state
        grad = (low + up * got) * held_ref[two, :] + (low * own + up) * got_grad
        state_in = from_before[h : h + 1, :] * got_state
        grad_in = from_after[h : h + 1, :] * got_grad
        if not first:
            state_in = enter_ref[one, :] + state_in
            grad_in = enter_ref[two, :] + grad_in
        enter_out[one, :] = state_in
        enter_out[two, :] = grad_in
        held_out[one, :] = state
        held_out[two, :] = grad
        if final_next:
            sent_ref[one, :] = jnp.where(next_up, grad, state).astype(BF16)
        else:
            sent_ref[one, :] = state.astype(BF16)
            sent_ref[two, :] = grad.astype(BF16)


def local_kernel(nheads, width, decay_ref, q_ref, k_ref, v_ref, g_ref, out_ref):
    span = q_ref.shape[0]
    rows = nheads * width
    causal = triangle(span)
    tri = causal.astype(F32).astype(BF16)
    parts = thirds(decay_ref[...])
    cum = sum(contract(tri, part, 1, 0) for part in parts)
    cum_rows = sum(contract(part, tri, 0, 1) for part in parts)
    for h in range(nheads):
        cols = slice(h * width, (h + 1) * width)
        gap = cum[:, h : h + 1] - cum_rows[h : h + 1, :]
        decay = jnp.where(causal, jnp.exp(jnp.minimum(gap, 0.0)), 0.0)
        weighted = (contract(g_ref[:, cols], v_ref[:, cols], 1, 1) * decay).astype(BF16)
        out_ref[h * width : (h + 1) * width, :] = contract(k_ref[:, cols], weighted, 0, 1)
        out_ref[rows + h * width : rows + (h + 1) * width, :] = contract(
            q_ref[:, cols], weighted, 0, 0
        )


def carry_kernel(nheads, width, hop, decay_ref, v_ref, g_ref, got_ref, logs_ref, enter_ref, local_ref, out_ref):
    span = v_ref.shape[0]
    rows = nheads * width
    tri = triangle(span).astype(F32).astype(BF16)
    cum_rows = sum(contract(part, tri, 0, 1) for part in thirds(decay_ref[...]))
    up = upper_half(hop)
    low = 1.0 - up
    from_before = up * jnp.exp(logs_ref[8:16, :])
    from_after = low * jnp.exp(logs_ref[16:24, :])
    for h in range(nheads):
        cols = slice(h * width, (h + 1) * width)
        two = slice(rows + h * width, rows + (h + 1) * width)
        got = got_ref[cols, :].astype(F32)
        state_in = (enter_ref[cols, :] + from_before[h : h + 1, :] * got).astype(BF16)
        grad_in = (enter_ref[two, :] + from_after[h : h + 1, :] * got).astype(BF16)
        cum_h = cum_rows[h : h + 1, :]
        last = cum_h[:, span - 1 : span]
        dq = local_ref[cols, :] + contract(state_in, g_ref[:, cols], 1, 1) * jnp.exp(cum_h)
        dk = local_ref[two, :] + contract(grad_in, v_ref[:, cols], 1, 1) * jnp.exp(last - cum_h)
        out_ref[cols, :] = dq.astype(BF16)
        out_ref[two, :] = dk.astype(BF16)


def scan_blocks(sent, held, logs, nheads, width):
    count = lax.axis_size("seq")
    rows = nheads * width
    hop, enter = 1, None
    while True:
        got = lax.ppermute(sent, "seq", [(i, i ^ hop) for i in range(count)])
        if 2 * hop >= count:
            return got, logs, enter, hop
        final_next = 4 * hop >= count
        out_shape = (
            jax.ShapeDtypeStruct((rows if final_next else 2 * rows + 16, width), BF16),
            jax.ShapeDtypeStruct((2 * rows, width), F32),
            jax.ShapeDtypeStruct((24, width), F32),
            jax.ShapeDtypeStruct((2 * rows, width), F32),
        )
        args = [got, held, logs] + ([] if enter is None else [enter])
        sent, held, logs, enter = call(
            functools.partial(step_kernel, nheads, width, hop, enter is None, final_next),
            out_shape, 10 * rows * width, 16 * rows * width, *args,
        )
        hop *= 2


def share_order(count):
    bits = []
    hop = 2
    while hop < count:
        bits.append(hop)
        hop *= 2
    return bits, bits[::-1]


def gather_shares(piece):
    count = lax.axis_size("seq")
    even, odd = share_order(count)
    held = piece
    for hop_even, hop_odd in zip(even, odd):
        pairs = [(i, i ^ (hop_odd if i % 2 else hop_even)) for i in range(count)]
        held = jnp.concatenate([held, lax.ppermute(held, "seq", pairs)])
    return held, lax.ppermute(held, "seq", [(i, i ^ 1) for i in range(count)])


def share_deltas(count):
    even, odd = share_order(count)

    def spread(order):
        out = [0]
        for hop in order:
            out = out + [d ^ hop for d in out]
        return out

    return tuple(
        spread(first) + [d ^ 1 for d in spread(second)] for first, second in ((even, odd), (odd, even))
    )


def pack_kernel(share, npieces, starts_ref, wq_ref, wk_ref, *refs):
    outs, sems = refs[:npieces], refs[npieces]
    copies = []
    wide = wq_ref.shape[1]
    for i in range(npieces):
        rows = pl.ds(pl.multiple_of(starts_ref[i], 16), share)
        for j, src in enumerate((wq_ref, wk_ref)):
            copies.append(
                pltpu.make_async_copy(
                    src.at[rows, :], outs[i].at[:, pl.ds(j * wide, wide)], sems.at[i, j]
                )
            )
    for copy in copies:
        copy.start()
    for copy in copies:
        copy.wait()


def pack_weights(w_query, w_key, starts, share):
    npieces = len(starts)
    wide = w_query.shape[1]
    if share % 16:
        return [
            jnp.concatenate([lax.dynamic_slice_in_dim(w, s, share, 0) for w in (w_query, w_key)], axis=1)
            for s in starts
        ]
    return call(
        functools.partial(pack_kernel, share, npieces),
        [jax.ShapeDtypeStruct((share, 2 * wide), BF16)] * npieces,
        0, npieces * share * wide * 8,
        jnp.stack(starts).astype(jnp.int32), w_query, w_key,
        in_specs=[pl.BlockSpec(memory_space=pltpu.SMEM)] + [pl.BlockSpec(memory_space=pl.ANY)] * 2,
        out_specs=[pl.BlockSpec(memory_space=pl.ANY)] * npieces,
        scratch_shapes=[pltpu.SemaphoreType.DMA((npieces, 2))],
    )


def own_kernel(table_ref, wq_ref, wk_ref, grads_ref, out_ref):
    wide = wq_ref.shape[1]
    out_ref[...] = contract(wq_ref[...], grads_ref[:wide, :], 1, 0) + contract(
        wk_ref[...], grads_ref[wide:, :], 1, 0
    )


def add_kernel(blocks, nother, last, table_ref, held_ref, got_ref, *refs):
    others, refs = refs[:nother], refs[nother:]
    total_ref, out_ref, grads = refs
    step = pl.program_id(0)
    half = pl.num_programs(0) // 2

    @pl.when(step == 0)
    def _():
        if nother == 1:
            grads[...] = others[0][...]
        else:
            grads[...] = jnp.where(table_ref[2 * blocks] == 1, others[1][...], others[0][...])

    def finish(weights):
        total = total_ref[...] + contract(weights, grads[...], 1, 0)
        if last:
            per = blocks // pl.num_programs(0)
            share = out_ref.shape[0] // blocks
            for i in range(per):
                place = table_ref[blocks + step * per + i]
                out_ref[pl.ds(pl.multiple_of(place * share, 8), share), :] = total[
                    i * share : (i + 1) * share, :
                ].astype(BF16)
        else:
            out_ref[...] = total

    @pl.when(step < half)
    def _():
        finish(held_ref[...])

    @pl.when(step >= half)
    def _():
        finish(got_ref[...])


def own_product(table, w_query, w_key, grads, blocks):
    span = grads.shape[1]
    wide = w_query.shape[1]
    share = w_query.shape[0] // (lax.axis_size("head") * blocks)
    chunk = share * blocks
    grid_spec = pltpu.PrefetchScalarGridSpec(
        num_scalar_prefetch=1,
        grid=(blocks,),
        in_specs=[pl.BlockSpec((share, wide), lambda j, t: (t[j], 0))] * 2 + [whole(grads.shape)],
        out_specs=pl.BlockSpec((share, span), lambda j, t: (j, 0)),
    )
    return call(
        own_kernel, jax.ShapeDtypeStruct((chunk, span), F32),
        4 * chunk * span * wide, chunk * wide * 4 + chunk * span * 4,
        table, w_query, w_key, grads, grid_spec=grid_spec,
    )


def add_product(table, held, got, others, total, blocks, last):
    chunk, span = total.shape
    deep = held.shape[1]
    steps = 4
    rows = chunk // steps
    half = steps // 2
    grid_spec = pltpu.PrefetchScalarGridSpec(
        num_scalar_prefetch=1,
        grid=(steps,),
        in_specs=[
            pl.BlockSpec((rows, deep), lambda j, t: (jnp.minimum(j, half - 1), 0)),
            pl.BlockSpec((rows, deep), lambda j, t: (jnp.maximum(j - half, 0), 0)),
        ]
        + [whole(others[0].shape)] * len(others)
        + [pl.BlockSpec((rows, span), lambda j, t: (j, 0))],
        out_specs=whole(total.shape) if last else pl.BlockSpec((rows, span), lambda j, t: (j, 0)),
        scratch_shapes=[pltpu.VMEM(others[0].shape, BF16)],
    )
    return call(
        functools.partial(add_kernel, blocks, len(others), last),
        jax.ShapeDtypeStruct((chunk, span), BF16 if last else F32),
        2 * chunk * span * deep, chunk * deep * 2 + chunk * span * 6,
        table, held, got, *others, total, grid_spec=grid_spec,
    )


def shards(query_act, key_act, value_act, grad_output, log_decay, w_query, w_key):
    span = query_act.shape[0]
    nheads = log_decay.shape[1]
    width = query_act.shape[1] // nheads
    nseq, nhead = lax.axis_size("seq"), lax.axis_size("head")
    my_seq, my_head = lax.axis_index("seq"), lax.axis_index("head")
    chunk = w_query.shape[0] // nhead
    share = chunk // nseq
    rows = nheads * width

    starts, sources, routes = [], [], []
    for k in range(1, nhead):
        if nhead & (nhead - 1) == 0:
            routes.append([(i, i ^ k) for i in range(nhead)])
            target = source = my_head ^ k
        else:
            routes.append([(i, (i + k) % nhead) for i in range(nhead)])
            target, source = (my_head + k) % nhead, (my_head + nhead - k) % nhead
        starts.append(target * chunk + my_seq * share)
        sources.append(source)
    packed = pack_weights(w_query, w_key, starts, share)
    pieces = [lax.ppermute(p, "head", route) for p, route in zip(packed, routes)]

    sent, held, logs = call(
        functools.partial(states_kernel, nheads, width),
        (
            jax.ShapeDtypeStruct((2 * rows + 16, width), BF16),
            jax.ShapeDtypeStruct((2 * rows, width), F32),
            jax.ShapeDtypeStruct((24, width), F32),
        ),
        4 * span * rows * width, 8 * span * rows,
        log_decay, query_act, key_act, value_act, grad_output,
    )
    got, logs, enter, hop = scan_blocks(sent, held, logs, nheads, width)
    local = call(
        functools.partial(local_kernel, nheads, width),
        jax.ShapeDtypeStruct((2 * rows, span), F32),
        6 * span * span * rows, 16 * span * rows,
        log_decay, query_act, key_act, value_act, grad_output,
    )
    both = call(
        functools.partial(carry_kernel, nheads, width, hop),
        jax.ShapeDtypeStruct((2 * rows, span), BF16),
        4 * span * rows * width, 16 * span * rows,
        log_decay, value_act, grad_output, got, logs, enter, local,
    )

    if nhead == 4:
        p1 = lax.ppermute(both, "head", [(0, 1), (1, 0), (2, 3), (3, 2)])
        p2 = lax.ppermute(both, "head", [(1, 2), (2, 1)])
        p3 = lax.ppermute(p2, "head", [(2, 3), (1, 0)])
        p4 = lax.ppermute(p1, "head", [(1, 2), (2, 1)])
        p5 = lax.ppermute(p4, "head", [(2, 3), (1, 0)])
        inner = (my_head == 1) | (my_head == 2)
        others = [(p1,), (p3, p4), (p5, p2)]
    else:
        gathered = lax.all_gather(both, "head")
        inner = my_head < 0
        others = [(gathered[source],) for source in sources]

    even, odd = share_deltas(nseq)
    deltas = jnp.where(my_seq % 2 == 1, jnp.array(odd, jnp.int32), jnp.array(even, jnp.int32))
    places = deltas ^ my_seq
    table = jnp.concatenate([places + my_head * nseq, places, inner.astype(jnp.int32)[None]])
    total = own_product(table, w_query, w_key, both, nseq)
    for i, (piece, grads) in enumerate(zip(pieces, others)):
        held, got = gather_shares(piece)
        total = add_product(table, held, got, grads, total, nseq, i == nhead - 2)
    return total


def solution(mesh):
    placed = (
        P("seq", "head"),
        P("seq", "head"),
        P("seq", "head"),
        P("seq", "head"),
        P("seq", "head"),
        P(None, "head"),
        P(None, "head"),
    )
    return jax.shard_map(
        shards, mesh=mesh, in_specs=placed, out_specs=P("head", "seq"), check_vma=False
    )
```

time: 147 us -> 114 us (0.78)
  the two profiles are of different devices: /device:TPU:0 before, /device:TPU:16 now
where the time goes in v2:
time: 114 us; the launch traced here: 113 us
  waiting for transfers between devices  54.4 us (48%)
  starting transfers between devices  25.1 us (22%)
  Pallas kernels  19.3 us (17%)
  local copies, waits for them, and re-layouts  13 us (11%)
  other arithmetic  1.24 us (1%)
    ppermute x3, waiting for transfers between devices, shards(): lax.ppermute(p, 'head', route)  19.7 us
    pallas_call x10, Pallas kernels, call(): pl.pallas_call(kernel, out_shape=out_shape, cost_estimate=pl.CostEstimate...  19.3 us
    ppermute x6, waiting for transfers between devices, gather_shares(): held = jnp.concatenate([held, lax.ppermute(held, 'seq', pairs)])  17.7 us
    unnamed x29, local copies, waits for them, and re-layouts  12 us
    ppermute x6, starting transfers between devices, gather_shares(): held = jnp.concatenate([held, lax.ppermute(held, 'seq', pairs)])  8.21 us
    ppermute x1, waiting for transfers between devices, shards(): p2 = lax.ppermute(both, 'head', [(1, 2), (2, 1)])  8.03 us
    ppermute x1, waiting for transfers between devices, shards(): p4 = lax.ppermute(p1, 'head', [(1, 2), (2, 1)])  5.99 us
    ppermute x3, starting transfers between devices, shards(): lax.ppermute(p, 'head', route)  3.62 us
  transfers between devices with their start and end apart: 20, of which 9 were waited for; matrix products, arithmetic and copies ran while one was open for 4% of the time, Pallas kernels for 12%

profile of v2, /device:TPU:16, one launch (start us, length us, event | category | flops | bytes accessed | tf_op | source)
XLA Modules:
  0.0 113.3 jit_solution(17640874719889312212)
XLA Ops:
  0.0 0.1 pad_add_fusion.1.starts_ref
  0.1 2.3 %copy-done = bf16[6144,384]{1,0:T(8,128)(2,1)S(1)} copy-done((bf16[6144,384]{1,0:T(8,128)(2,1)S(1)}, bf16[6144,384]{1,0:T(8,128)(2,1)}, u32[]{:S(2)}) %copy-start) | copy-done | bytes 4718616
  2.4 2.3 %copy-done.2 = bf16[6144,384]{1,0:T(8,128)(2,1)S(1)} copy-done((bf16[6144,384]{1,0:T(8,128)(2,1)S(1)}, bf16[6144,384]{1,0:T(8,128)(2,1)}, u32[]{:S(2)}) %copy-start.2) | copy-done | bytes 4718616
  4.8 0.0 copy-start.7
  4.8 0.7 shard_map.91
  5.5 1.6 %collective-permute-start.16 = (bf16[192,768]{1,0:T(8,128)(2,1)S(1)}, bf16[192,768]{1,0:T(8,128)(2,1)}, u32[]{:S(2)}, u32[]{:S(2)}) collective-permute-start(bf16[192,768]{1,0:T(8,128)(2,1)S(1)} %get-tuple-element.30), channel_id=1, source_target_pairs={{0,1},{1,0},{2,3},{3,2},{4,5},{5,4},{6,7},{7,6},{8,9},{9,8},{10,11... | collective-permute-start | bytes 884744 | tf_op jit(solution)/shard_map/ppermute | solution.py:364
  7.1 0.1 copy.12.decay_ref
  7.3 0.8 shard_map.92
  8.1 0.1 collective-permute-start.4
  8.2 0.4 collective-permute-start.11
  8.6 1.6 %collective-permute-start = (bf16[192,768]{1,0:T(8,128)(2,1)S(1)}, bf16[192,768]{1,0:T(8,128)(2,1)S(1)}, u32[]{:S(2)}, u32[]{:S(2)}) collective-permute-start(bf16[192,768]{1,0:T(8,128)(2,1)S(1)} %get-tuple-element.18), channel_id=1, source_target_pairs={{0,3},{1,2},{2,1},{3,0},{4,7},{5,6},{6,5},{7,4},{8,11},{9,10},{10,... | collective-permute-start | bytes 884744 | tf_op jit(solution)/shard_map/ppermute | solution.py:364
  10.2 1.0 shard_map.95.local_ref
  11.2 0.0 collective-permute-done.4.got_ref
  11.2 0.1 shard_map.93
  11.3 1.6 %collective-permute-start.5 = (bf16[784,128]{1,0:T(8,128)(2,1)S(1)}, bf16[784,128]{1,0:T(8,128)(2,1)S(1)}, u32[]{:S(2)}, u32[]{:S(2)}) collective-permute-start(bf16[784,128]{1,0:T(8,128)(2,1)S(1)} %get-tuple-element.22), channel_id=1, source_target_pairs={{0,8},{4,12},{8,0},{12,4},{16,24},{20,28},{24,16},{28,20},{1,9},{5... | collective-permute-start | bytes 602120 | tf_op jit(solution)/shard_map/ppermute | solution.py:169
  12.9 3.6 %collective-permute-done.16 = bf16[192,768]{1,0:T(8,128)(2,1)} collective-permute-done((bf16[192,768]{1,0:T(8,128)(2,1)S(1)}, bf16[192,768]{1,0:T(8,128)(2,1)}, u32[]{:S(2)}, u32[]{:S(2)}) %collective-permute-start.16) | collective-permute-done | bytes 294944 | tf_op jit(solution)/shard_map/ppermute | solution.py:364
  16.4 1.5 %collective-permute-start.17 = (bf16[192,768]{1,0:T(8,128)(2,1)}, bf16[192,768]{1,0:T(8,128)(2,1)S(1)}, u32[]{:S(2)}, u32[]{:S(2)}) collective-permute-start(bf16[192,768]{1,0:T(8,128)(2,1)} %collective-permute-done.16), channel_id=1, source_target_pairs={{0,8},{4,20},{8,0},{12,28},{16,24},{20,4},{24,16},{28,12},{1,9},{5... | collective-permute-start | bytes 884744 | tf_op jit(solution)/shard_map/ppermute | solution.py:202
  17.9 1.0 constant_dynamic-update-slice_fusion.8
  19.0 9.7 %collective-permute-done.11 = bf16[192,768]{1,0:T(8,128)(2,1)S(1)} collective-permute-done((bf16[192,768]{1,0:T(8,128)(2,1)S(1)}, bf16[192,768]{1,0:T(8,128)(2,1)S(1)}, u32[]{:S(2)}, u32[]{:S(2)}) %collective-permute-start.11) | collective-permute-done | bytes 294944 | tf_op jit(solution)/shard_map/ppermute | solution.py:364
  28.6 1.5 %collective-permute-start.12 = (bf16[192,768]{1,0:T(8,128)(2,1)S(1)}, bf16[192,768]{1,0:T(8,128)(2,1)S(1)}, u32[]{:S(2)}, u32[]{:S(2)}) collective-permute-start(bf16[192,768]{1,0:T(8,128)(2,1)S(1)} %collective-permute-done.11), channel_id=1, source_target_pairs={{0,8},{4,20},{8,0},{12,28},{16,24},{20,4},{24,16},{28,12},{1,9},{5... | collective-permute-start | bytes 884744 | tf_op jit(solution)/shard_map/ppermute | solution.py:202
  30.1 6.4 %collective-permute-done = bf16[192,768]{1,0:T(8,128)(2,1)S(1)} collective-permute-done((bf16[192,768]{1,0:T(8,128)(2,1)S(1)}, bf16[192,768]{1,0:T(8,128)(2,1)S(1)}, u32[]{:S(2)}, u32[]{:S(2)}) %collective-permute-start) | collective-permute-done | bytes 294944 | tf_op jit(solution)/shard_map/ppermute | solution.py:364
  36.5 1.5 %collective-permute-start.1 = (bf16[192,768]{1,0:T(8,128)(2,1)S(1)}, bf16[192,768]{1,0:T(8,128)(2,1)S(1)}, u32[]{:S(2)}, u32[]{:S(2)}) collective-permute-start(bf16[192,768]{1,0:T(8,128)(2,1)S(1)} %collective-permute-done), channel_id=1, source_target_pairs={{0,8},{4,20},{8,0},{12,28},{16,24},{20,4},{24,16},{28,12},{1,9},{5... | collective-permute-start | bytes 884744 | tf_op jit(solution)/shard_map/ppermute | solution.py:202
  38.0 0.0 collective-permute-done.5.got_ref
  38.0 0.8 shard_map.94
  38.9 1.5 %collective-permute-start.6 = (bf16[384,128]{1,0:T(8,128)(2,1)S(1)}, bf16[384,128]{1,0:T(8,128)(2,1)S(1)}, u32[]{:S(2)}, u32[]{:S(2)}) collective-permute-start(bf16[384,128]{1,0:T(8,128)(2,1)S(1)} %get-tuple-element.26), channel_id=1, source_target_pairs={{0,16},{4,20},{8,24},{12,28},{16,0},{20,4},{24,8},{28,12},{1,17},{... | collective-permute-start | bytes 294920 | tf_op jit(solution)/shard_map/ppermute | solution.py:169
  40.4 0.7 constant_dynamic-update-slice_fusion.2
  41.1 3.0 %collective-permute-done.6.got_ref = bf16[384,128]{1,0:T(8,128)(2,1)S(1)} collective-permute-done((bf16[384,128]{1,0:T(8,128)(2,1)S(1)}, bf16[384,128]{1,0:T(8,128)(2,1)S(1)}, u32[]{:S(2)}, u32[]{:S(2)}) %collective-permute-start.6) | collective-permute-done | bytes 98336 | tf_op jit(solution)/shard_map/ppermute | solution.py:169
  44.1 0.4 shard_map.96.grads_ref
  44.5 0.1 collective-permute-start.7
  44.6 0.0 collective-permute-done.17
  44.6 1.0 pad_maximum_fusion.2
  45.6 1.6 %collective-permute-start.18 = (bf16[384,768]{1,0:T(8,128)(2,1)S(1)}, bf16[384,768]{1,0:T(8,128)(2,1)S(1)}, u32[]{:S(2)}, u32[]{:S(2)}) collective-permute-start(bf16[384,768]{1,0:T(8,128)(2,1)S(1)} %pad_maximum_fusion.2), channel_id=1, source_target_pairs={{0,16},{4,12},{8,24},{12,4},{16,0},{20,28},{24,8},{28,20},{1,17},{... | collective-permute-start | bytes 1769480 | tf_op jit(solution)/shard_map/ppermute | solution.py:202
  47.2 0.0 collective-permute-done.12
  47.2 0.6 collective-permute-start.13
  47.8 0.0 collective-permute-done.1
  47.9 1.6 %collective-permute-start.2 = (bf16[384,768]{1,0:T(8,128)(2,1)S(1)}, bf16[384,768]{1,0:T(8,128)(2,1)S(1)}, u32[]{:S(2)}, u32[]{:S(2)}) collective-permute-start(bf16[384,768]{1,0:T(8,128)(2,1)S(1)} %pad_maximum_fusion), channel_id=1, source_target_pairs={{0,16},{4,12},{8,24},{12,4},{16,0},{20,28},{24,8},{28,20},{1,17},{... | collective-permute-start | bytes 1769480 | tf_op jit(solution)/shard_map/ppermute | solution.py:202
  49.5 0.7 constant_dynamic-update-slice_fusion.1
  50.2 5.3 %collective-permute-done.18 = bf16[384,768]{1,0:T(8,128)(2,1)S(1)} collective-permute-done((bf16[384,768]{1,0:T(8,128)(2,1)S(1)}, bf16[384,768]{1,0:T(8,128)(2,1)S(1)}, u32[]{:S(2)}, u32[]{:S(2)}) %collective-permute-start.18) | collective-permute-done | bytes 589856 | tf_op jit(solution)/shard_map/ppermute | solution.py:202
  55.6 0.0 copy-start.9
  55.6 0.0 copy-start.10
  55.6 0.1 collective-permute-start.19
  55.7 6.2 %collective-permute-done.13 = bf16[384,768]{1,0:T(8,128)(2,1)S(1)} collective-permute-done((bf16[384,768]{1,0:T(8,128)(2,1)S(1)}, bf16[384,768]{1,0:T(8,128)(2,1)S(1)}, u32[]{:S(2)}, u32[]{:S(2)}) %collective-permute-start.13) | collective-permute-done | bytes 589856 | tf_op jit(solution)/shard_map/ppermute | solution.py:202
  61.9 0.1 collective-permute-start.14
  62.0 6.2 %collective-permute-done.2 = bf16[384,768]{1,0:T(8,128)(2,1)S(1)} collective-permute-done((bf16[384,768]{1,0:T(8,128)(2,1)S(1)}, bf16[384,768]{1,0:T(8,128)(2,1)S(1)}, u32[]{:S(2)}, u32[]{:S(2)}) %collective-permute-start.2) | collective-permute-done | bytes 589856 | tf_op jit(solution)/shard_map/ppermute | solution.py:202
  68.2 0.9 constant_dynamic-update-slice_fusion.held_ref
  69.1 0.0 collective-permute-start.3
  69.1 2.3 %collective-permute-start.10 = (bf16[768,256]{1,0:T(8,128)(2,1)S(1)}, bf16[768,256]{1,0:T(8,128)(2,1)}, u32[]{:S(2)}, u32[]{:S(2)}) collective-permute-start(bf16[768,256]{1,0:T(8,128)(2,1)S(1)} %shard_map.96.grads_ref), channel_id=1, source_target_pairs={{1,2},{2,1},{5,6},{6,5},{9,10},{10,9},{13,14},{14,13},{17,18},{18,... | collective-permute-start | bytes 1179656 | tf_op jit(solution)/shard_map/ppermute | solution.py:392
  71.4 0.0 collective-permute-done.7.refs_0_
  71.4 3.5 %collective-permute-start.8 = (bf16[768,256]{1,0:T(8,128)(2,1)S(1)}, bf16[768,256]{1,0:T(8,128)(2,1)}, u32[]{:S(2)}, u32[]{:S(2)}) collective-permute-start(bf16[768,256]{1,0:T(8,128)(2,1)S(1)} %collective-permute-done.7.refs_0_), channel_id=1, source_target_pairs={{1,2},{2,1},{5,6},{6,5},{9,10},{10,9},{13,14},{14,13},{17,18},{18,... | collective-permute-start | bytes 1179656 | tf_op jit(solution)/shard_map/ppermute | solution.py:394
  74.9 8.0 %collective-permute-done.10.refs_1_ = bf16[768,256]{1,0:T(8,128)(2,1)} collective-permute-done((bf16[768,256]{1,0:T(8,128)(2,1)S(1)}, bf16[768,256]{1,0:T(8,128)(2,1)}, u32[]{:S(2)}, u32[]{:S(2)}) %collective-permute-start.10) | collective-permute-done | bytes 393248 | tf_op jit(solution)/shard_map/ppermute | solution.py:392
  83.0 2.0 %collective-permute-start.15 = (bf16[768,256]{1,0:T(8,128)(2,1)}, bf16[768,256]{1,0:T(8,128)(2,1)}, u32[]{:S(2)}, u32[]{:S(2)}) collective-permute-start(bf16[768,256]{1,0:T(8,128)(2,1)} %collective-permute-done.10.refs_1_), channel_id=1, source_target_pairs={{2,3},{1,0},{6,7},{5,4},{10,11},{9,8},{14,15},{13,12},{18,19},{17,... | collective-permute-start | bytes 1179656 | tf_op jit(solution)/shard_map/ppermute | solution.py:393
  85.0 6.0 %collective-permute-done.8.refs_1_ = bf16[768,256]{1,0:T(8,128)(2,1)} collective-permute-done((bf16[768,256]{1,0:T(8,128)(2,1)S(1)}, bf16[768,256]{1,0:T(8,128)(2,1)}, u32[]{:S(2)}, u32[]{:S(2)}) %collective-permute-start.8) | collective-permute-done | bytes 393248 | tf_op jit(solution)/shard_map/ppermute | solution.py:394
  91.0 2.0 %collective-permute-start.9 = (bf16[768,256]{1,0:T(8,128)(2,1)}, bf16[768,256]{1,0:T(8,128)(2,1)}, u32[]{:S(2)}, u32[]{:S(2)}) collective-permute-start(bf16[768,256]{1,0:T(8,128)(2,1)} %collective-permute-done.8.refs_1_), channel_id=1, source_target_pairs={{2,3},{1,0},{6,7},{5,4},{10,11},{9,8},{14,15},{13,12},{18,19},{17,... | collective-permute-start | bytes 1179656 | tf_op jit(solution)/shard_map/ppermute | solution.py:395
  93.1 0.1 pad_add_fusion.table_ref
  93.2 2.3 %copy-done.1 = bf16[6144,384]{1,0:T(8,128)(2,1)S(1)} copy-done((bf16[6144,384]{1,0:T(8,128)(2,1)S(1)}, bf16[6144,384]{1,0:T(8,128)(2,1)}, u32[]{:S(2)}) %copy-start.1) | copy-done | bytes 4718616
  95.5 2.3 %copy-done.3 = bf16[6144,384]{1,0:T(8,128)(2,1)S(1)} copy-done((bf16[6144,384]{1,0:T(8,128)(2,1)S(1)}, bf16[6144,384]{1,0:T(8,128)(2,1)}, u32[]{:S(2)}) %copy-start.3) | copy-done | bytes 4718616
  97.8 2.6 %shard_map.97.refs_1_ = f32[1536,256]{1,0:T(8,128)S(1)} custom-call(s32[17]{0:T(128)S(1)} %pad_add_fusion.table_ref, bf16[6144,384]{1,0:T(8,128)(2,1)S(1)} %copy-done.1, bf16[6144,384]{1,0:T(8,128)(2,1)S(1)} %copy-done.3, bf16[768,256]{1,0:T(8,128)(2,1)S(1)} %shard_map.96.grads_ref), custom_call_target="tpu_custom_call" | custom-call | flops 603979776 | bytes 3932160 | tf_op jit(solution)/shard_map/pallas_call | solution.py:20
  100.4 0.0 collective-permute-done.19.got_ref
  100.5 3.7 %shard_map.98.refs_2_ = f32[1536,256]{1,0:T(8,128)S(1)} custom-call(s32[17]{0:T(128)S(1)} %pad_add_fusion.table_ref, bf16[768,768]{1,0:T(8,128)(2,1)S(1)} %constant_dynamic-update-slice_fusion.6.held_ref, bf16[768,768]{1,0:T(8,128)(2,1)} %collective-permute-done.19.got_ref, bf16[768,256]{1,0:T(8,128)(2,1)S(1)} %collective-permute-done.7.refs_0_, ...), custom_call_target="tpu_custom_call" | custom-call | flops 603979776 | bytes 4718592 | tf_op jit(solution)/shard_map/pallas_call | solution.py:20
  104.2 0.0 collective-permute-done.15.refs_0_
  104.2 0.0 collective-permute-done.14.got_ref
  104.2 4.0 %shard_map.99.refs_2_ = f32[1536,256]{1,0:T(8,128)S(1)} custom-call(s32[17]{0:T(128)S(1)} %pad_add_fusion.table_ref, bf16[768,768]{1,0:T(8,128)(2,1)S(1)} %constant_dynamic-update-slice_fusion.3.held_ref, bf16[768,768]{1,0:T(8,128)(2,1)} %collective-permute-done.14.got_ref, bf16[768,256]{1,0:T(8,128)(2,1)} %collective-permute-done.15.refs_0_, ...), custom_call_target="tpu_custom_call" | custom-call | flops 603979776 | bytes 4718592 | tf_op jit(solution)/shard_map/pallas_call | solution.py:20
  108.2 0.0 collective-permute-done.9.refs_0_
  108.2 5.1 %shard_map.100 = bf16[1536,256]{1,0:T(8,128)(2,1)} custom-call(s32[17]{0:T(128)S(1)} %pad_add_fusion.table_ref, bf16[768,768]{1,0:T(8,128)(2,1)} %constant_dynamic-update-slice_fusion.held_ref, bf16[768,768]{1,0:T(8,128)(2,1)} %collective-permute-done.3.got_ref, bf16[768,256]{1,0:T(8,128)(2,1)} %collective-permute-done.9.refs_0_, ...), custom_call_target="tpu_custom_call" | custom-call | flops 603979776 | bytes 4718592 | tf_op jit(solution)/shard_map/pallas_call | solution.py:20
  (24 shorter events, 0.3 us)
Async XLA Ops:
  0.1 2.3 %copy-start = (bf16[6144,384]{1,0:T(8,128)(2,1)S(1)}, bf16[6144,384]{1,0:T(8,128)(2,1)}, u32[]{:S(2)}) copy-start(bf16[6144,384]{1,0:T(8,128)(2,1)} %wq_ref.3) | copy-start | bytes 14155780
  2.4 2.3 %copy-start.2 = (bf16[6144,384]{1,0:T(8,128)(2,1)S(1)}, bf16[6144,384]{1,0:T(8,128)(2,1)}, u32[]{:S(2)}) copy-start(bf16[6144,384]{1,0:T(8,128)(2,1)} %wk_ref.3) | copy-start | bytes 14155780
  4.8 2.4 %copy-start.8 = (f32[256,3]{0,1:T(4,128)S(1)}, f32[256,3]{0,1:T(4,128)}, u32[]{:S(2)}) copy-start(f32[256,3]{0,1:T(4,128)} %param.13) | copy-start | bytes 9220
  4.8 2.5 %copy-start.4 = (bf16[256,384]{1,0:T(8,128)(2,1)S(1)}, bf16[256,384]{1,0:T(8,128)(2,1)}, u32[]{:S(2)}) copy-start(bf16[256,384]{1,0:T(8,128)(2,1)} %v_ref.5) | copy-start | bytes 589828
  4.8 2.5 %copy-start.5 = (bf16[256,384]{1,0:T(8,128)(2,1)S(1)}, bf16[256,384]{1,0:T(8,128)(2,1)}, u32[]{:S(2)}) copy-start(bf16[256,384]{1,0:T(8,128)(2,1)} %g_ref.5) | copy-start | bytes 589828
  4.8 2.5 %copy-start.6 = (bf16[256,384]{1,0:T(8,128)(2,1)S(1)}, bf16[256,384]{1,0:T(8,128)(2,1)}, u32[]{:S(2)}) copy-start(bf16[256,384]{1,0:T(8,128)(2,1)} %q_ref.3) | copy-start | bytes 589828
  4.8 2.5 %copy-start.7 = (bf16[256,384]{1,0:T(8,128)(2,1)S(1)}, bf16[256,384]{1,0:T(8,128)(2,1)}, u32[]{:S(2)}) copy-start(bf16[256,384]{1,0:T(8,128)(2,1)} %k_ref.3) | copy-start | bytes 589828
  5.5 10.9 %collective-permute-start.16 = (bf16[192,768]{1,0:T(8,128)(2,1)S(1)}, bf16[192,768]{1,0:T(8,128)(2,1)}, u32[]{:S(2)}, u32[]{:S(2)}) collective-permute-start(bf16[192,768]{1,0:T(8,128)(2,1)S(1)} %get-tuple-element.30), channel_id=1, source_target_pairs={{0,1},{1,0},{2,3},{3,2},{4,5},{5,4},{6,7},{7,6},{8,9},{9,8},{10,11... | collective-permute-start | bytes 884744 | tf_op jit(solution)/shard_map/ppermute | solution.py:364
  8.1 3.0 %collective-permute-start.4 = (bf16[784,128]{1,0:T(8,128)(2,1)S(1)}, bf16[784,128]{1,0:T(8,128)(2,1)S(1)}, u32[]{:S(2)}, u32[]{:S(2)}) collective-permute-start(bf16[784,128]{1,0:T(8,128)(2,1)S(1)} %get-tuple-element.19), channel_id=1, source_target_pairs={{0,4},{4,0},{8,12},{12,8},{16,20},{20,16},{24,28},{28,24},{1,5},{5... | collective-permute-start | bytes 602120 | tf_op jit(solution)/shard_map/ppermute | solution.py:169
  8.2 20.4 %collective-permute-start.11 = (bf16[192,768]{1,0:T(8,128)(2,1)S(1)}, bf16[192,768]{1,0:T(8,128)(2,1)S(1)}, u32[]{:S(2)}, u32[]{:S(2)}) collective-permute-start(bf16[192,768]{1,0:T(8,128)(2,1)S(1)} %get-tuple-element.29), channel_id=1, source_target_pairs={{0,2},{1,3},{2,0},{3,1},{4,6},{5,7},{6,4},{7,5},{8,10},{9,11},{10,... | collective-permute-start | bytes 884744 | tf_op jit(solution)/shard_map/ppermute | solution.py:364
  8.6 27.9 %collective-permute-start = (bf16[192,768]{1,0:T(8,128)(2,1)S(1)}, bf16[192,768]{1,0:T(8,128)(2,1)S(1)}, u32[]{:S(2)}, u32[]{:S(2)}) collective-permute-start(bf16[192,768]{1,0:T(8,128)(2,1)S(1)} %get-tuple-element.18), channel_id=1, source_target_pairs={{0,3},{1,2},{2,1},{3,0},{4,7},{5,6},{6,5},{7,4},{8,11},{9,10},{10,... | collective-permute-start | bytes 884744 | tf_op jit(solution)/shard_map/ppermute | solution.py:364
  11.3 26.7 %collective-permute-start.5 = (bf16[784,128]{1,0:T(8,128)(2,1)S(1)}, bf16[784,128]{1,0:T(8,128)(2,1)S(1)}, u32[]{:S(2)}, u32[]{:S(2)}) collective-permute-start(bf16[784,128]{1,0:T(8,128)(2,1)S(1)} %get-tuple-element.22), channel_id=1, source_target_pairs={{0,8},{4,12},{8,0},{12,4},{16,24},{20,28},{24,16},{28,20},{1,9},{5... | collective-permute-start | bytes 602120 | tf_op jit(solution)/shard_map/ppermute | solution.py:169
  16.4 28.1 %collective-permute-start.17 = (bf16[192,768]{1,0:T(8,128)(2,1)}, bf16[192,768]{1,0:T(8,128)(2,1)S(1)}, u32[]{:S(2)}, u32[]{:S(2)}) collective-permute-start(bf16[192,768]{1,0:T(8,128)(2,1)} %collective-permute-done.16), channel_id=1, source_target_pairs={{0,8},{4,20},{8,0},{12,28},{16,24},{20,4},{24,16},{28,12},{1,9},{5... | collective-permute-start | bytes 884744 | tf_op jit(solution)/shard_map/ppermute | solution.py:202
  28.6 18.6 %collective-permute-start.12 = (bf16[192,768]{1,0:T(8,128)(2,1)S(1)}, bf16[192,768]{1,0:T(8,128)(2,1)S(1)}, u32[]{:S(2)}, u32[]{:S(2)}) collective-permute-start(bf16[192,768]{1,0:T(8,128)(2,1)S(1)} %collective-permute-done.11), channel_id=1, source_target_pairs={{0,8},{4,20},{8,0},{12,28},{16,24},{20,4},{24,16},{28,12},{1,9},{5... | collective-permute-start | bytes 884744 | tf_op jit(solution)/shard_map/ppermute | solution.py:202
  36.5 11.3 %collective-permute-start.1 = (bf16[192,768]{1,0:T(8,128)(2,1)S(1)}, bf16[192,768]{1,0:T(8,128)(2,1)S(1)}, u32[]{:S(2)}, u32[]{:S(2)}) collective-permute-start(bf16[192,768]{1,0:T(8,128)(2,1)S(1)} %collective-permute-done), channel_id=1, source_target_pairs={{0,8},{4,20},{8,0},{12,28},{16,24},{20,4},{24,16},{28,12},{1,9},{5... | collective-permute-start | bytes 884744 | tf_op jit(solution)/shard_map/ppermute | solution.py:202
  38.9 5.2 %collective-permute-start.6 = (bf16[384,128]{1,0:T(8,128)(2,1)S(1)}, bf16[384,128]{1,0:T(8,128)(2,1)S(1)}, u32[]{:S(2)}, u32[]{:S(2)}) collective-permute-start(bf16[384,128]{1,0:T(8,128)(2,1)S(1)} %get-tuple-element.26), channel_id=1, source_target_pairs={{0,16},{4,20},{8,24},{12,28},{16,0},{20,4},{24,8},{28,12},{1,17},{... | collective-permute-start | bytes 294920 | tf_op jit(solution)/shard_map/ppermute | solution.py:169
  44.5 26.9 %collective-permute-start.7 = (bf16[768,256]{1,0:T(8,128)(2,1)S(1)}, bf16[768,256]{1,0:T(8,128)(2,1)S(1)}, u32[]{:S(2)}, u32[]{:S(2)}) collective-permute-start(bf16[768,256]{1,0:T(8,128)(2,1)S(1)} %shard_map.96.grads_ref), channel_id=1, source_target_pairs={{0,1},{1,0},{2,3},{3,2},{4,5},{5,4},{6,7},{7,6},{8,9},{9,8},{10,11... | collective-permute-start | bytes 1179656 | tf_op jit(solution)/shard_map/ppermute | solution.py:391
  45.6 9.9 %collective-permute-start.18 = (bf16[384,768]{1,0:T(8,128)(2,1)S(1)}, bf16[384,768]{1,0:T(8,128)(2,1)S(1)}, u32[]{:S(2)}, u32[]{:S(2)}) collective-permute-start(bf16[384,768]{1,0:T(8,128)(2,1)S(1)} %pad_maximum_fusion.2), channel_id=1, source_target_pairs={{0,16},{4,12},{8,24},{12,4},{16,0},{20,28},{24,8},{28,20},{1,17},{... | collective-permute-start | bytes 1769480 | tf_op jit(solution)/shard_map/ppermute | solution.py:202
  47.2 14.6 %collective-permute-start.13 = (bf16[384,768]{1,0:T(8,128)(2,1)S(1)}, bf16[384,768]{1,0:T(8,128)(2,1)S(1)}, u32[]{:S(2)}, u32[]{:S(2)}) collective-permute-start(bf16[384,768]{1,0:T(8,128)(2,1)S(1)} %pad_maximum_fusion.1), channel_id=1, source_target_pairs={{0,16},{4,12},{8,24},{12,4},{16,0},{20,28},{24,8},{28,20},{1,17},{... | collective-permute-start | bytes 1769480 | tf_op jit(solution)/shard_map/ppermute | solution.py:202
  47.9 20.3 %collective-permute-start.2 = (bf16[384,768]{1,0:T(8,128)(2,1)S(1)}, bf16[384,768]{1,0:T(8,128)(2,1)S(1)}, u32[]{:S(2)}, u32[]{:S(2)}) collective-permute-start(bf16[384,768]{1,0:T(8,128)(2,1)S(1)} %pad_maximum_fusion), channel_id=1, source_target_pairs={{0,16},{4,12},{8,24},{12,4},{16,0},{20,28},{24,8},{28,20},{1,17},{... | collective-permute-start | bytes 1769480 | tf_op jit(solution)/shard_map/ppermute | solution.py:202
  55.6 37.5 %copy-start.9 = (s32[8]{0:T(128)S(1)}, s32[8]{0:T(128)}, u32[]{:S(2)}) copy-start(s32[8]{0:T(128)} %constant.35.clone) | copy-start | bytes 100
  55.6 37.5 %copy-start.10 = (s32[8]{0:T(128)S(1)}, s32[8]{0:T(128)}, u32[]{:S(2)}) copy-start(s32[8]{0:T(128)} %constant.36.clone) | copy-start | bytes 100
  55.6 44.8 %collective-permute-start.19 = (bf16[768,768]{1,0:T(8,128)(2,1)S(1)}, bf16[768,768]{1,0:T(8,128)(2,1)}, u32[]{:S(2)}, u32[]{:S(2)}) collective-permute-start(bf16[768,768]{1,0:T(8,128)(2,1)S(1)} %constant_dynamic-update-slice_fusion.6.held_ref), channel_id=1, source_target_pairs={{0,4},{4,0},{8,12},{12,8},{16,20},{20,16},{24,28},{28,24},{1,5},{5... | collective-permute-start | bytes 3538952 | tf_op jit(solution)/shard_map/ppermute | solution.py:203
  61.9 42.3 %collective-permute-start.14 = (bf16[768,768]{1,0:T(8,128)(2,1)S(1)}, bf16[768,768]{1,0:T(8,128)(2,1)}, u32[]{:S(2)}, u32[]{:S(2)}) collective-permute-start(bf16[768,768]{1,0:T(8,128)(2,1)S(1)} %constant_dynamic-update-slice_fusion.3.held_ref), channel_id=1, source_target_pairs={{0,4},{4,0},{8,12},{12,8},{16,20},{20,16},{24,28},{28,24},{1,5},{5... | collective-permute-start | bytes 3538952 | tf_op jit(solution)/shard_map/ppermute | solution.py:203
  69.1 39.2 %collective-permute-start.3 = (bf16[768,768]{1,0:T(8,128)(2,1)}, bf16[768,768]{1,0:T(8,128)(2,1)}, u32[]{:S(2)}, u32[]{:S(2)}) collective-permute-start(bf16[768,768]{1,0:T(8,128)(2,1)} %constant_dynamic-update-slice_fusion.held_ref), channel_id=1, source_target_pairs={{0,4},{4,0},{8,12},{12,8},{16,20},{20,16},{24,28},{28,24},{1,5},{5... | collective-permute-start | bytes 3538952 | tf_op jit(solution)/shard_map/ppermute | solution.py:203
  69.1 13.9 %collective-permute-start.10 = (bf16[768,256]{1,0:T(8,128)(2,1)S(1)}, bf16[768,256]{1,0:T(8,128)(2,1)}, u32[]{:S(2)}, u32[]{:S(2)}) collective-permute-start(bf16[768,256]{1,0:T(8,128)(2,1)S(1)} %shard_map.96.grads_ref), channel_id=1, source_target_pairs={{1,2},{2,1},{5,6},{6,5},{9,10},{10,9},{13,14},{14,13},{17,18},{18,... | collective-permute-start | bytes 1179656 | tf_op jit(solution)/shard_map/ppermute | solution.py:392
  71.4 19.6 %collective-permute-start.8 = (bf16[768,256]{1,0:T(8,128)(2,1)S(1)}, bf16[768,256]{1,0:T(8,128)(2,1)}, u32[]{:S(2)}, u32[]{:S(2)}) collective-permute-start(bf16[768,256]{1,0:T(8,128)(2,1)S(1)} %collective-permute-done.7.refs_0_), channel_id=1, source_target_pairs={{1,2},{2,1},{5,6},{6,5},{9,10},{10,9},{13,14},{14,13},{17,18},{18,... | collective-permute-start | bytes 1179656 | tf_op jit(solution)/shard_map/ppermute | solution.py:394
  83.0 21.2 %collective-permute-start.15 = (bf16[768,256]{1,0:T(8,128)(2,1)}, bf16[768,256]{1,0:T(8,128)(2,1)}, u32[]{:S(2)}, u32[]{:S(2)}) collective-permute-start(bf16[768,256]{1,0:T(8,128)(2,1)} %collective-permute-done.10.refs_1_), channel_id=1, source_target_pairs={{2,3},{1,0},{6,7},{5,4},{10,11},{9,8},{14,15},{13,12},{18,19},{17,... | collective-permute-start | bytes 1179656 | tf_op jit(solution)/shard_map/ppermute | solution.py:393
  91.0 17.2 %collective-permute-start.9 = (bf16[768,256]{1,0:T(8,128)(2,1)}, bf16[768,256]{1,0:T(8,128)(2,1)}, u32[]{:S(2)}, u32[]{:S(2)}) collective-permute-start(bf16[768,256]{1,0:T(8,128)(2,1)} %collective-permute-done.8.refs_1_), channel_id=1, source_target_pairs={{2,3},{1,0},{6,7},{5,4},{10,11},{9,8},{14,15},{13,12},{18,19},{17,... | collective-permute-start | bytes 1179656 | tf_op jit(solution)/shard_map/ppermute | solution.py:395
  93.2 2.3 %copy-start.1 = (bf16[6144,384]{1,0:T(8,128)(2,1)S(1)}, bf16[6144,384]{1,0:T(8,128)(2,1)}, u32[]{:S(2)}) copy-start(bf16[6144,384]{1,0:T(8,128)(2,1)} %wq_ref.3) | copy-start | bytes 14155780
  95.5 2.3 %copy-start.3 = (bf16[6144,384]{1,0:T(8,128)(2,1)S(1)}, bf16[6144,384]{1,0:T(8,128)(2,1)}, u32[]{:S(2)}) copy-start(bf16[6144,384]{1,0:T(8,128)(2,1)} %wk_ref.3) | copy-start | bytes 14155780

commit v3 on v2

v3 whole, which is shorter than its diff:
```python
import functools

import jax
import jax.numpy as jnp
from jax import lax
from jax.experimental import pallas as pl
from jax.experimental.pallas import tpu as pltpu
from jax.sharding import PartitionSpec as P

F32 = jnp.float32
BF16 = jnp.bfloat16
VMEM_BYTES = 40 * 1024 * 1024
PACKSPACE = pltpu.VMEM
WAIT1 = int(1.0e15 * 20e-6)
WAIT2 = int(1.0e15 * 40e-6)


def contract(a, b, left, right):
    return lax.dot_general(a, b, (((left,), (right,)), ((), ())), preferred_element_type=F32)


def call(kernel, out_shape, flops, nbytes, *args, aliases=None, vmem=VMEM_BYTES, **spec):
    return pl.pallas_call(
        kernel,
        out_shape=out_shape,
        cost_estimate=pl.CostEstimate(flops=flops, bytes_accessed=nbytes, transcendentals=0),
        compiler_params=pltpu.CompilerParams(vmem_limit_bytes=vmem),
        input_output_aliases=aliases or {},
        **spec,
    )(*args)


def gate_kernel(count, *refs):
    del count, refs


def gate(passed, tokens=(), flops=0):
    return call(
        functools.partial(gate_kernel, len(passed)),
        [jax.ShapeDtypeStruct(x.shape, x.dtype) for x in passed],
        flops, 0, *passed, *tokens,
        aliases={i: i for i in range(len(passed))},
        in_specs=[pl.BlockSpec(memory_space=pl.ANY)] * (len(passed) + len(tokens)),
        out_specs=[pl.BlockSpec(memory_space=pl.ANY)] * len(passed),
    )


def whole(shape):
    return pl.BlockSpec(shape, lambda *_: (0,) * len(shape))


def thirds(x):
    high = x.astype(BF16)
    rest = x - high.astype(F32)
    middle = rest.astype(BF16)
    return high, middle, (rest - middle.astype(F32)).astype(BF16)


def triangle(span):
    rows = lax.broadcasted_iota(jnp.int32, (span, span), 0)
    cols = lax.broadcasted_iota(jnp.int32, (span, span), 1)
    return rows >= cols


def upper_half(hop):
    return ((lax.axis_index("seq") // hop) % 2).astype(F32)


def states_kernel(nheads, width, decay_ref, q_ref, k_ref, v_ref, g_ref, sent_ref, held_ref, logs_ref):
    span = q_ref.shape[0]
    tri = triangle(span).astype(F32).astype(BF16)
    cum = sum(contract(tri, part, 1, 1) for part in thirds(decay_ref[...]))
    rows = nheads * width
    row = lax.broadcasted_iota(jnp.int32, (8, width), 0)
    totals = jnp.zeros((8, width), F32)
    for h in range(nheads):
        cols = slice(h * width, (h + 1) * width)
        cum_h = cum[:, h : h + 1]
        last = cum[span - 1 : span, h : h + 1]
        key_w = (k_ref[:, cols].astype(F32) * jnp.exp(last - cum_h)).astype(BF16)
        query_w = (q_ref[:, cols].astype(F32) * jnp.exp(cum_h)).astype(BF16)
        state = contract(key_w, v_ref[:, cols], 0, 0)
        grad = contract(query_w, g_ref[:, cols], 0, 0)
        held_ref[h * width : (h + 1) * width, :] = state
        held_ref[rows + h * width : rows + (h + 1) * width, :] = grad
        sent_ref[h * width : (h + 1) * width, :] = state.astype(BF16)
        sent_ref[rows + h * width : rows + (h + 1) * width, :] = grad.astype(BF16)
        totals = jnp.where(row == h, jnp.broadcast_to(last, (8, width)), totals)
    high = totals.astype(BF16).astype(F32)
    sent_ref[2 * rows :, :] = jnp.concatenate([high, totals - high]).astype(BF16)
    logs_ref[0:8, :] = totals
    logs_ref[8:24, :] = jnp.zeros((16, width), F32)


def step_kernel(nheads, width, hop, first, final_next, got_ref, held_ref, logs_ref, *refs):
    if first:
        sent_ref, held_out, logs_out, enter_out = refs
    else:
        enter_ref, sent_ref, held_out, logs_out, enter_out = refs
    rows = nheads * width
    up = upper_half(hop)
    low = 1.0 - up
    tail = got_ref[2 * rows :, :].astype(F32)
    got_total = tail[0:8] + tail[8:16]
    total, before, after = logs_ref[0:8, :], logs_ref[8:16, :], logs_ref[16:24, :]
    own_decay, got_decay = jnp.exp(total), jnp.exp(got_total)
    from_before, from_after = up * jnp.exp(before), low * jnp.exp(after)
    total = total + got_total
    logs_out[0:8, :] = total
    logs_out[8:16, :] = before + up * got_total
    logs_out[16:24, :] = after + low * got_total
    if final_next:
        next_up = upper_half(2 * hop) > 0.5
    else:
        high = total.astype(BF16).astype(F32)
        sent_ref[2 * rows :, :] = jnp.concatenate([high, total - high]).astype(BF16)
    for h in range(nheads):
        one = slice(h * width, (h + 1) * width)
        two = slice(rows + h * width, rows + (h + 1) * width)
        got_state, got_grad = got_ref[one, :].astype(F32), got_ref[two, :].astype(F32)
        own, got = own_decay[h : h + 1, :], got_decay[h : h + 1, :]
        state = (up + low * got) * held_ref[one, :] + (up * own + low) * got_state
        grad = (low + up * got) * held_ref[two, :] + (low * own + up) * got_grad
        state_in = from_before[h : h + 1, :] * got_state
        grad_in = from_after[h : h + 1, :] * got_grad
        if not first:
            state_in = enter_ref[one, :] + state_in
            grad_in = enter_ref[two, :] + grad_in
        enter_out[one, :] = state_in
        enter_out[two, :] = grad_in
        held_out[one, :] = state
        held_out[two, :] = grad
        if final_next:
            sent_ref[one, :] = jnp.where(next_up, grad, state).astype(BF16)
        else:
            sent_ref[one, :] = state.astype(BF16)
            sent_ref[two, :] = grad.astype(BF16)


def local_kernel(nheads, width, decay_ref, q_ref, k_ref, v_ref, g_ref, out_ref):
    span = q_ref.shape[0]
    rows = nheads * width
    causal = triangle(span)
    tri = causal.astype(F32).astype(BF16)
    parts = thirds(decay_ref[...])
    cum = sum(contract(tri, part, 1, 1) for part in parts)
    cum_rows = sum(contract(part, tri, 1, 1) for part in parts)
    for h in range(nheads):
        cols = slice(h * width, (h + 1) * width)
        gap = cum[:, h : h + 1] - cum_rows[h : h + 1, :]
        decay = jnp.where(causal, jnp.exp(jnp.minimum(gap, 0.0)), 0.0)
        weighted = (contract(g_ref[:, cols], v_ref[:, cols], 1, 1) * decay).astype(BF16)
        out_ref[h * width : (h + 1) * width, :] = contract(k_ref[:, cols], weighted, 0, 1)
        out_ref[rows + h * width : rows + (h + 1) * width, :] = contract(
            q_ref[:, cols], weighted, 0, 0
        )


def carry_kernel(nheads, width, hop, decay_ref, v_ref, g_ref, got_ref, logs_ref, enter_ref, local_ref, out_ref):
    span = v_ref.shape[0]
    rows = nheads * width
    tri = triangle(span).astype(F32).astype(BF16)
    cum_rows = sum(contract(part, tri, 1, 1) for part in thirds(decay_ref[...]))
    up = upper_half(hop)
    low = 1.0 - up
    from_before = up * jnp.exp(logs_ref[8:16, :])
    from_after = low * jnp.exp(logs_ref[16:24, :])
    for h in range(nheads):
        cols = slice(h * width, (h + 1) * width)
        two = slice(rows + h * width, rows + (h + 1) * width)
        got = got_ref[cols, :].astype(F32)
        state_in = (enter_ref[cols, :] + from_before[h : h + 1, :] * got).astype(BF16)
        grad_in = (enter_ref[two, :] + from_after[h : h + 1, :] * got).astype(BF16)
        cum_h = cum_rows[h : h + 1, :]
        last = cum_h[:, span - 1 : span]
        dq = local_ref[cols, :] + contract(state_in, g_ref[:, cols], 1, 1) * jnp.exp(cum_h)
        dk = local_ref[two, :] + contract(grad_in, v_ref[:, cols], 1, 1) * jnp.exp(last - cum_h)
        out_ref[cols, :] = dq.astype(BF16)
        out_ref[two, :] = dk.astype(BF16)


def share_order(count):
    bits = []
    hop = 2
    while hop < count:
        bits.append(hop)
        hop *= 2
    return bits, bits[::-1]


def share_hop(held, number):
    count = lax.axis_size("seq")
    even, odd = share_order(count)
    even, odd = even + [1], odd + [1]
    pairs = [(i, i ^ (odd[number] if i % 2 else even[number])) for i in range(count)]
    return lax.ppermute(held, "seq", pairs)


def share_deltas(count):
    even, odd = share_order(count)

    def spread(order):
        out = [0]
        for hop in order:
            out = out + [d ^ hop for d in out]
        return out

    return tuple(
        spread(first) + [d ^ 1 for d in spread(second)] for first, second in ((even, odd), (odd, even))
    )


def pack_kernel(share, shifts, wq_ref, wk_ref, *refs):
    count, nseq = lax.axis_size("head"), lax.axis_size("seq")
    mine, my_seq = lax.axis_index("head"), lax.axis_index("seq")
    outs, sems = refs[: len(shifts)], refs[len(shifts)]
    copies = []
    for i, shift in enumerate(shifts):
        block = lax.rem(mine + shift, count) * nseq + my_seq
        rows = pl.ds(pl.multiple_of(block * share, 16), share)
        for j, src in enumerate((wq_ref, wk_ref)):
            copies.append(
                pltpu.make_async_copy(
                    src.at[rows, :], outs[i].at[pl.ds(j * share, share), :], sems.at[i, j]
                )
            )
    for copy in copies:
        copy.start()
    for copy in copies:
        copy.wait()


def pack_weights(w_query, w_key, shifts, share):
    wide = w_query.shape[1]
    if share % 16:
        count, nseq = lax.axis_size("head"), lax.axis_size("seq")
        blocks = [(lax.axis_index("head") + k) % count * nseq + lax.axis_index("seq") for k in shifts]
        return [
            jnp.concatenate(
                [lax.dynamic_slice_in_dim(w, block * share, share, 0) for w in (w_query, w_key)]
            )
            for block in blocks
        ]
    return call(
        functools.partial(pack_kernel, share, shifts),
        [jax.ShapeDtypeStruct((2 * share, wide), BF16)] * len(shifts),
        0, len(shifts) * share * wide * 8,
        w_query, w_key,
        in_specs=[pl.BlockSpec(memory_space=pl.ANY)] * 2,
        out_specs=[pl.BlockSpec(memory_space=PACKSPACE)] * len(shifts),
        scratch_shapes=[pltpu.SemaphoreType.DMA((len(shifts), 2))],
        vmem=58 * 1024 * 1024,
    )


def own_kernel(table_ref, wq_ref, wk_ref, grads_ref, out_ref):
    wide = wq_ref.shape[1]
    out_ref[...] = contract(wq_ref[...], grads_ref[:wide, :], 1, 0) + contract(
        wk_ref[...], grads_ref[wide:, :], 1, 0
    )


def add_kernel(blocks, nother, last, table_ref, held_ref, got_ref, *refs):
    others, refs = refs[:nother], refs[nother:]
    total_ref, out_ref, grads = refs
    step = pl.program_id(0)
    half = pl.num_programs(0) // 2

    @pl.when(step == 0)
    def _():
        if nother == 1:
            grads[...] = others[0][...]
        else:
            grads[...] = jnp.where(table_ref[2 * blocks] == 1, others[1][...], others[0][...])

    def finish(weights):
        wide = weights.shape[1]
        per = blocks // pl.num_programs(0)
        share = weights.shape[0] // (2 * per)
        left, right = grads[:wide, :], grads[wide:, :]
        parts = []
        for i in range(per):
            start = 2 * i * share
            parts.append(
                contract(weights[start : start + share], left, 1, 0)
                + contract(weights[start + share : start + 2 * share], right, 1, 0)
            )
        total = total_ref[...] + jnp.concatenate(parts)
        if last:
            for i in range(per):
                place = table_ref[blocks + step * per + i]
                out_ref[pl.ds(pl.multiple_of(place * share, 8), share), :] = total[
                    i * share : (i + 1) * share, :
                ].astype(BF16)
        else:
            out_ref[...] = total

    @pl.when(step < half)
    def _():
        finish(held_ref[...])

    @pl.when(step >= half)
    def _():
        finish(got_ref[...])


def own_product(table, w_query, w_key, grads, blocks):
    span = grads.shape[1]
    wide = w_query.shape[1]
    share = w_query.shape[0] // (lax.axis_size("head") * blocks)
    chunk = share * blocks
    grid_spec = pltpu.PrefetchScalarGridSpec(
        num_scalar_prefetch=1,
        grid=(blocks,),
        in_specs=[pl.BlockSpec((share, wide), lambda j, t: (t[j], 0))] * 2 + [whole(grads.shape)],
        out_specs=pl.BlockSpec((share, span), lambda j, t: (j, 0)),
    )
    return call(
        own_kernel, jax.ShapeDtypeStruct((chunk, span), F32),
        4 * chunk * span * wide, chunk * wide * 4 + chunk * span * 4,
        table, w_query, w_key, grads, grid_spec=grid_spec,
    )


def add_product(table, held, got, others, total, blocks, last):
    chunk, span = total.shape
    wide = held.shape[1]
    steps = 4
    rows = chunk // steps
    half = steps // 2
    grid_spec = pltpu.PrefetchScalarGridSpec(
        num_scalar_prefetch=1,
        grid=(steps,),
        in_specs=[
            pl.BlockSpec((2 * rows, wide), lambda j, t: (jnp.minimum(j, half - 1), 0)),
            pl.BlockSpec((2 * rows, wide), lambda j, t: (jnp.maximum(j - half, 0), 0)),
        ]
        + [whole(others[0].shape)] * len(others)
        + [pl.BlockSpec((rows, span), lambda j, t: (j, 0))],
        out_specs=whole(total.shape) if last else pl.BlockSpec((rows, span), lambda j, t: (j, 0)),
        scratch_shapes=[pltpu.VMEM(others[0].shape, BF16)],
    )
    return call(
        functools.partial(add_kernel, blocks, len(others), last),
        jax.ShapeDtypeStruct((chunk, span), BF16 if last else F32),
        4 * chunk * span * wide, chunk * wide * 4 + chunk * span * 6,
        table, held, got, *others, total, grid_spec=grid_spec,
    )


def shards(query_act, key_act, value_act, grad_output, log_decay, w_query, w_key):
    span = query_act.shape[0]
    nheads = log_decay.shape[1]
    width = query_act.shape[1] // nheads
    nseq, nhead = lax.axis_size("seq"), lax.axis_size("head")
    my_seq, my_head = lax.axis_index("seq"), lax.axis_index("head")
    chunk = w_query.shape[0] // nhead
    share = chunk // nseq
    rows = nheads * width

    shifts = [1, nhead - 1] + list(range(2, nhead - 1))
    ring = {k: [(i, (i + k) % nhead) for i in range(nhead)] for k in shifts}
    packed = pack_weights(w_query, w_key, shifts, share)
    pieces = [lax.ppermute(p, "head", ring[k]) for p, k in zip(packed, shifts)]

    decay = gate([log_decay.T], packed)[0]
    sent, held, logs = call(
        functools.partial(states_kernel, nheads, width),
        (
            jax.ShapeDtypeStruct((2 * rows + 16, width), BF16),
            jax.ShapeDtypeStruct((2 * rows, width), F32),
            jax.ShapeDtypeStruct((24, width), F32),
        ),
        4 * span * rows * width, 8 * span * rows,
        decay, query_act, key_act, value_act, grad_output,
    )
    nhops = len(share_order(nseq)[0]) + 1
    holds = [[p] for p in pieces]
    progress = [0] * len(pieces)

    def advance(which):
        for i in which:
            if progress[i] < nhops:
                held = holds[i][0] if progress[i] == 0 else jnp.concatenate(holds[i])
                holds[i] = [held, share_hop(held, progress[i])]
                progress[i] += 1

    hop, enter = 1, None
    while True:
        if 2 * hop >= nseq:
            early = range(min(2, len(holds)))
            sent, *firsts = gate([sent] + [holds[i][0] for i in early])
            for i in early:
                holds[i][0] = firsts[i]
            advance(early)
        got = lax.ppermute(sent, "seq", [(i, i ^ hop) for i in range(nseq)])
        if 2 * hop >= nseq:
            break
        final_next = 4 * hop >= nseq
        out_shape = (
            jax.ShapeDtypeStruct((rows if final_next else 2 * rows + 16, width), BF16),
            jax.ShapeDtypeStruct((2 * rows, width), F32),
            jax.ShapeDtypeStruct((24, width), F32),
            jax.ShapeDtypeStruct((2 * rows, width), F32),
        )
        args = [got, held, logs] + ([] if enter is None else [enter])
        sent, held, logs, enter = call(
            functools.partial(step_kernel, nheads, width, hop, enter is None, final_next),
            out_shape, 10 * rows * width, 16 * rows * width, *args,
        )
        hop *= 2
    local = call(
        functools.partial(local_kernel, nheads, width),
        jax.ShapeDtypeStruct((2 * rows, span), F32),
        6 * span * span * rows, 16 * span * rows,
        decay, query_act, key_act, value_act, grad_output,
    )
    both = call(
        functools.partial(carry_kernel, nheads, width, hop),
        jax.ShapeDtypeStruct((2 * rows, span), BF16),
        4 * span * rows * width, 16 * span * rows,
        decay, value_act, grad_output, got, logs, enter, local,
    )

    even, odd = share_deltas(nseq)
    deltas = jnp.where(my_seq % 2 == 1, jnp.array(odd, jnp.int32), jnp.array(even, jnp.int32))
    places = deltas ^ my_seq
    table = jnp.concatenate([places + my_head * nseq, places, (my_head >= 2).astype(jnp.int32)[None]])
    total = own_product(table, w_query, w_key, both, nseq)

    if nhead == 4:
        p1 = lax.ppermute(both, "head", ring[1])
        p3 = lax.ppermute(both, "head", ring[3])
        holds[0][1], holds[1][1] = gate([holds[0][1], holds[1][1]], [both])
        advance([0, 1])
        (holds[2][0],) = gate([holds[2][0]], [holds[0][0], holds[1][0]])
        advance([2])
        holds[0][1], holds[1][1], holds[2][1], p1, p3 = gate(
            [holds[0][1], holds[1][1], holds[2][1], p1, p3], [total]
        )
        advance([0, 1, 2])
        up = lax.ppermute(p1, "head", [(1, 2), (2, 3)])
        down = lax.ppermute(p3, "head", [(2, 1), (1, 0)])
        others = [(p1,), (p3,), (down, up)]
    else:
        gathered = lax.all_gather(both, "head")
        others = [(gathered[(my_head + nhead - k) % nhead],) for k in shifts]

    while min(progress) < nhops:
        advance(range(len(pieces)))
    for i, grads in enumerate(others):
        total = add_product(table, holds[i][0], holds[i][1], grads, total, nseq, i == nhead - 2)
    return total


def solution(mesh):
    placed = (
        P("seq", "head"),
        P("seq", "head"),
        P("seq", "head"),
        P("seq", "head"),
        P("seq", "head"),
        P(None, "head"),
        P(None, "head"),
    )
    return jax.shard_map(
        shards, mesh=mesh, in_specs=placed, out_specs=P("head", "seq"), check_vma=False
    )
```

time: 114 us -> 87.5 us (0.77)
  the two profiles are of different devices: /device:TPU:16 before, /device:TPU:0 now
where the time goes in v3:
time: 87.5 us; the launch traced here: 87.1 us
  waiting for transfers between devices  36.9 us (42%)
  starting transfers between devices  23.3 us (27%)
  Pallas kernels  15.5 us (18%)
  local copies, waits for them, and re-layouts  11 us (13%)
    pallas_call x15, Pallas kernels, call(): pl.pallas_call(kernel, out_shape=out_shape, cost_estimate=pl.CostEstimate...  15.5 us
    unnamed x32, local copies, waits for them, and re-layouts  10.8 us
    ppermute x3, waiting for transfers between devices, shards(): got = lax.ppermute(sent, 'seq', [(i, i ^ hop) for i in range(nseq)])  8.65 us
    ppermute x9, starting transfers between devices, share_hop(): return lax.ppermute(held, 'seq', pairs)  7.82 us
    ppermute x9, waiting for transfers between devices, share_hop(): return lax.ppermute(held, 'seq', pairs)  7.55 us
    ppermute x1, waiting for transfers between devices, shards(): down = lax.ppermute(p3, 'head', [(2, 1), (1, 0)])  7.11 us
    ppermute x1, waiting for transfers between devices, shards(): p3 = lax.ppermute(both, 'head', ring[3])  6.91 us
    ppermute x3, starting transfers between devices, shards(): pieces = [lax.ppermute(p, 'head', ring[k]) for p, k in zip(packed, shifts)]  5.84 us
  transfers between devices with their start and end apart: 19, of which 7 were waited for; matrix products, arithmetic and copies ran while one was open for 3% of the time, Pallas kernels for 11%

profile of v3, /device:TPU:0, one launch (start us, length us, event | category | flops | bytes accessed | tf_op | source)
XLA Modules:
  0.0 87.1 jit_solution(1780143213306661005)
XLA Ops:
  0.0 0.7 copy.41
  0.7 2.3 %shard_map.91 = (bf16[384,384]{1,0:T(8,128)(2,1)}, bf16[384,384]{1,0:T(8,128)(2,1)}, bf16[384,384]{1,0:T(8,128)(2,1)}) custom-call(bf16[6144,384]{1,0:T(8,128)(2,1)} %wq_ref.3, bf16[6144,384]{1,0:T(8,128)(2,1)} %wk_ref.3), custom_call_target="tpu_custom_call" | custom-call | bytes 1769472 | tf_op jit(solution)/shard_map/pallas_call | solution.py:23
  3.0 1.0 %copy-done.8 = bf16[384,384]{1,0:T(8,128)(2,1)S(1)} copy-done((bf16[384,384]{1,0:T(8,128)(2,1)S(1)}, bf16[384,384]{1,0:T(8,128)(2,1)}, u32[]{:S(2)}) %copy-start.8) | copy-done | bytes 294936
  4.0 1.0 %copy-done.10 = bf16[384,384]{1,0:T(8,128)(2,1)S(1)} copy-done((bf16[384,384]{1,0:T(8,128)(2,1)S(1)}, bf16[384,384]{1,0:T(8,128)(2,1)}, u32[]{:S(2)}) %copy-start.10) | copy-done | bytes 294936
  4.9 0.0 copy-done.6
  5.0 0.0 copy-done.7
  5.0 0.9 shard_map.93
  5.8 0.5 collective-permute-start.1
  6.4 2.6 %collective-permute-start.3 = (bf16[384,384]{1,0:T(8,128)(2,1)S(1)}, bf16[384,384]{1,0:T(8,128)(2,1)S(1)}, u32[]{:S(2)}, u32[]{:S(2)}) collective-permute-start(bf16[384,384]{1,0:T(8,128)(2,1)S(1)} %copy-done.11), channel_id=1, source_target_pairs={{0,1},{1,2},{2,3},{3,0},{4,5},{5,6},{6,7},{7,4},{8,9},{9,10},{10,1... | collective-permute-start | bytes 884744 | tf_op jit(solution)/shard_map/ppermute | solution.py:364
  9.0 2.1 %collective-permute-start.4 = (bf16[384,384]{1,0:T(8,128)(2,1)}, bf16[384,384]{1,0:T(8,128)(2,1)S(1)}, u32[]{:S(2)}, u32[]{:S(2)}) collective-permute-start(bf16[384,384]{1,0:T(8,128)(2,1)} %get-tuple-element.30.refs_2_), channel_id=1, source_target_pairs={{0,3},{1,0},{2,1},{3,2},{4,7},{5,4},{6,5},{7,6},{8,11},{9,8},{10,9... | collective-permute-start | bytes 884744 | tf_op jit(solution)/shard_map/ppermute | solution.py:364
  11.1 0.0 collective-permute-done.1.got_ref
  11.1 0.1 shard_map.94
  11.2 1.7 %collective-permute-start.2 = (bf16[784,128]{1,0:T(8,128)(2,1)S(1)}, bf16[784,128]{1,0:T(8,128)(2,1)S(1)}, u32[]{:S(2)}, u32[]{:S(2)}) collective-permute-start(bf16[784,128]{1,0:T(8,128)(2,1)S(1)} %get-tuple-element.34), channel_id=1, source_target_pairs={{0,8},{4,12},{8,0},{12,4},{16,24},{20,28},{24,16},{28,20},{1,9},{5... | collective-permute-start | bytes 602120 | tf_op jit(solution)/shard_map/ppermute | solution.py:396
  12.9 5.3 %collective-permute-done.2.got_ref = bf16[784,128]{1,0:T(8,128)(2,1)S(1)} collective-permute-done((bf16[784,128]{1,0:T(8,128)(2,1)S(1)}, bf16[784,128]{1,0:T(8,128)(2,1)S(1)}, u32[]{:S(2)}, u32[]{:S(2)}) %collective-permute-start.2) | collective-permute-done | bytes 200736 | tf_op jit(solution)/shard_map/ppermute | solution.py:396
  18.3 0.8 shard_map.95
  19.1 0.0 collective-permute-done.3.refs_1_
  19.1 5.5 %collective-permute-done.4.refs_2_ = bf16[384,384]{1,0:T(8,128)(2,1)S(1)} collective-permute-done((bf16[384,384]{1,0:T(8,128)(2,1)}, bf16[384,384]{1,0:T(8,128)(2,1)S(1)}, u32[]{:S(2)}, u32[]{:S(2)}) %collective-permute-start.4) | collective-permute-done | bytes 294944 | tf_op jit(solution)/shard_map/ppermute | solution.py:364
  24.6 1.5 %collective-permute-start.5 = (bf16[384,384]{1,0:T(8,128)(2,1)S(1)}, bf16[384,384]{1,0:T(8,128)(2,1)S(1)}, u32[]{:S(2)}, u32[]{:S(2)}) collective-permute-start(bf16[384,384]{1,0:T(8,128)(2,1)S(1)} %get-tuple-element.39), channel_id=1, source_target_pairs={{0,8},{4,20},{8,0},{12,28},{16,24},{20,4},{24,16},{28,12},{1,9},{5... | collective-permute-start | bytes 884744 | tf_op jit(solution)/shard_map/ppermute | solution.py:196
  26.1 0.5 collective-permute-start.6
  26.6 1.1 %collective-permute-start = (bf16[384,384]{1,0:T(8,128)(2,1)S(1)}, bf16[384,384]{1,0:T(8,128)(2,1)S(1)}, u32[]{:S(2)}, u32[]{:S(2)}) collective-permute-start(bf16[384,384]{1,0:T(8,128)(2,1)S(1)} %copy-done.9), channel_id=1, source_target_pairs={{0,2},{1,3},{2,0},{3,1},{4,6},{5,7},{6,4},{7,5},{8,10},{9,11},{10,... | collective-permute-start | bytes 884744 | tf_op jit(solution)/shard_map/ppermute | solution.py:364
  27.7 1.0 %shard_map.97.local_ref = f32[768,256]{1,0:T(8,128)S(1)} custom-call(f32[3,256]{1,0:T(4,128)S(1)} %shard_map.92.decay_ref, bf16[256,384]{1,0:T(8,128)(2,1)S(1)} %copy-done.6, bf16[256,384]{1,0:T(8,128)(2,1)S(1)} %copy-done.7, bf16[256,384]{1,0:T(8,128)(2,1)S(1)} %copy-done.4, bf16[256,384]{1,0:T(8,128)(2,1)S(1)} %copy-done.5), custom_call_target="tpu_custom_call" | custom-call | flops 150994944 | bytes 1572864 | tf_op jit(solution)/shard_map/pallas_call | solution.py:23
  28.8 1.6 %collective-permute-start.7 = (bf16[384,128]{1,0:T(8,128)(2,1)S(1)}, bf16[384,128]{1,0:T(8,128)(2,1)S(1)}, u32[]{:S(2)}, u32[]{:S(2)}) collective-permute-start(bf16[384,128]{1,0:T(8,128)(2,1)S(1)} %get-tuple-element.41), channel_id=1, source_target_pairs={{0,16},{4,20},{8,24},{12,28},{16,0},{20,4},{24,8},{28,12},{1,17},{... | collective-permute-start | bytes 294920 | tf_op jit(solution)/shard_map/ppermute | solution.py:396
  30.3 0.9 %constant_dynamic-update-slice_fusion.6 = (bf16[1536,384]{1,0:T(8,128)(2,1)S(1)}, bf16[768,384]{1,0:T(8,128)(2,1)}, bf16[768,384]{1,0:T(8,128)(2,1)}, bf16[1536,384]{1,0:T(8,128)(2,1)S(1)}) fusion(bf16[384,384]{1,0:T(8,128)(2,1)S(1)} %get-tuple-element.40, bf16[384,384]{1,0:T(8,128)(2,1)S(1)} %get-tuple-element.39), kind=kLoop, calls=%fused_computation.8 | loop fusion | bytes 1769472
  31.2 3.3 %collective-permute-done.7.got_ref = bf16[384,128]{1,0:T(8,128)(2,1)S(1)} collective-permute-done((bf16[384,128]{1,0:T(8,128)(2,1)S(1)}, bf16[384,128]{1,0:T(8,128)(2,1)S(1)}, u32[]{:S(2)}, u32[]{:S(2)}) %collective-permute-start.7) | collective-permute-done | bytes 98336 | tf_op jit(solution)/shard_map/ppermute | solution.py:396
  34.6 0.4 shard_map.98.refs_2_.grads_ref
  35.0 0.0 collective-permute-done.5.refs_0_
  35.0 0.0 collective-permute-done.6.refs_1_
  35.0 0.8 constant_dynamic-update-slice_fusion.5
  35.8 1.0 %copy-done.2 = bf16[1536,384]{1,0:T(8,128)(2,1)} copy-done((bf16[1536,384]{1,0:T(8,128)(2,1)}, bf16[1536,384]{1,0:T(8,128)(2,1)S(1)}, u32[]{:S(2)}) %copy-start.2) | copy-done | bytes 1179672
  36.9 1.5 %collective-permute-start.9 = (bf16[768,384]{1,0:T(8,128)(2,1)}, bf16[768,384]{1,0:T(8,128)(2,1)S(1)}, u32[]{:S(2)}, u32[]{:S(2)}) collective-permute-start(bf16[768,384]{1,0:T(8,128)(2,1)} %get-tuple-element.58.refs_2_), channel_id=1, source_target_pairs={{0,16},{4,12},{8,24},{12,4},{16,0},{20,28},{24,8},{28,20},{1,17},{... | collective-permute-start | bytes 1769480 | tf_op jit(solution)/shard_map/ppermute | solution.py:196
  38.4 0.8 constant_dynamic-update-slice_fusion.8
  39.2 0.5 collective-permute-start.8
  39.7 1.6 %collective-permute-start.11 = (bf16[768,256]{1,0:T(8,128)(2,1)S(1)}, bf16[768,256]{1,0:T(8,128)(2,1)S(1)}, u32[]{:S(2)}, u32[]{:S(2)}) collective-permute-start(bf16[768,256]{1,0:T(8,128)(2,1)S(1)} %shard_map.98.refs_2_.grads_ref), channel_id=1, source_target_pairs={{0,1},{1,2},{2,3},{3,0},{4,5},{5,6},{6,7},{7,4},{8,9},{9,10},{10,1... | collective-permute-start | bytes 1179656 | tf_op jit(solution)/shard_map/ppermute | solution.py:432
  41.2 2.3 %collective-permute-start.12 = (bf16[768,256]{1,0:T(8,128)(2,1)S(1)}, bf16[768,256]{1,0:T(8,128)(2,1)S(1)}, u32[]{:S(2)}, u32[]{:S(2)}) collective-permute-start(bf16[768,256]{1,0:T(8,128)(2,1)S(1)} %shard_map.98.refs_2_.grads_ref), channel_id=1, source_target_pairs={{0,3},{1,0},{2,1},{3,2},{4,7},{5,4},{6,5},{7,6},{8,11},{9,8},{10,9... | collective-permute-start | bytes 1179656 | tf_op jit(solution)/shard_map/ppermute | solution.py:433
  43.5 0.0 collective-permute-done.refs_0_
  43.5 1.5 %collective-permute-start.10 = (bf16[384,384]{1,0:T(8,128)(2,1)S(1)}, bf16[384,384]{1,0:T(8,128)(2,1)S(1)}, u32[]{:S(2)}, u32[]{:S(2)}) collective-permute-start(bf16[384,384]{1,0:T(8,128)(2,1)S(1)} %shard_map.100), channel_id=1, source_target_pairs={{0,8},{4,20},{8,0},{12,28},{16,24},{20,4},{24,16},{28,12},{1,9},{5... | collective-permute-start | bytes 884744 | tf_op jit(solution)/shard_map/ppermute | solution.py:196
  45.0 0.1 pad_add_fusion.table_ref
  45.1 2.3 %copy-done = bf16[6144,384]{1,0:T(8,128)(2,1)S(1)} copy-done((bf16[6144,384]{1,0:T(8,128)(2,1)S(1)}, bf16[6144,384]{1,0:T(8,128)(2,1)}, u32[]{:S(2)}) %copy-start) | copy-done | bytes 4718616
  47.4 2.3 %copy-done.1 = bf16[6144,384]{1,0:T(8,128)(2,1)S(1)} copy-done((bf16[6144,384]{1,0:T(8,128)(2,1)S(1)}, bf16[6144,384]{1,0:T(8,128)(2,1)}, u32[]{:S(2)}) %copy-start.1) | copy-done | bytes 4718616
  49.8 2.6 %shard_map.101.refs_5_.refs_1_ = f32[1536,256]{1,0:T(8,128)S(1)} custom-call(s32[17]{0:T(128)S(1)} %pad_add_fusion.table_ref, bf16[6144,384]{1,0:T(8,128)(2,1)S(1)} %copy-done, bf16[6144,384]{1,0:T(8,128)(2,1)S(1)} %copy-done.1, bf16[768,256]{1,0:T(8,128)(2,1)S(1)} %shard_map.98.refs_2_.grads_ref), custom_call_target="tpu_custom_call" | custom-call | flops 603979776 | bytes 3932160 | tf_op jit(solution)/shard_map/pallas_call | solution.py:23
  52.4 1.1 %collective-permute-done.11.refs_3_ = bf16[768,256]{1,0:T(8,128)(2,1)S(1)} collective-permute-done((bf16[768,256]{1,0:T(8,128)(2,1)S(1)}, bf16[768,256]{1,0:T(8,128)(2,1)S(1)}, u32[]{:S(2)}, u32[]{:S(2)}) %collective-permute-start.11) | collective-permute-done | bytes 393248 | tf_op jit(solution)/shard_map/ppermute | solution.py:432
  53.5 6.9 %collective-permute-done.12.refs_4_ = bf16[768,256]{1,0:T(8,128)(2,1)S(1)} collective-permute-done((bf16[768,256]{1,0:T(8,128)(2,1)S(1)}, bf16[768,256]{1,0:T(8,128)(2,1)S(1)}, u32[]{:S(2)}, u32[]{:S(2)}) %collective-permute-start.12) | collective-permute-done | bytes 393248 | tf_op jit(solution)/shard_map/ppermute | solution.py:433
  60.4 0.0 collective-permute-done.10.refs_2_
  60.4 0.0 collective-permute-done.9.refs_1_
  60.4 0.0 collective-permute-done.8.refs_0_
  60.4 0.1 pad_maximum_fusion.1
  60.5 1.6 %collective-permute-start.13 = (bf16[768,384]{1,0:T(8,128)(2,1)S(1)}, bf16[768,384]{1,0:T(8,128)(2,1)S(1)}, u32[]{:S(2)}, u32[]{:S(2)}) collective-permute-start(bf16[768,384]{1,0:T(8,128)(2,1)S(1)} %pad_maximum_fusion.1), channel_id=1, source_target_pairs={{0,16},{4,12},{8,24},{12,4},{16,0},{20,28},{24,8},{28,20},{1,17},{... | collective-permute-start | bytes 1769480 | tf_op jit(solution)/shard_map/ppermute | solution.py:196
  62.1 0.1 constant_dynamic-update-slice_fusion.7.held_ref
  62.2 0.1 collective-permute-start.18
  62.3 0.1 constant_dynamic-update-slice_fusion.4.held_ref
  62.4 0.5 collective-permute-start.17
  62.9 7.5 %collective-permute-done.13 = bf16[768,384]{1,0:T(8,128)(2,1)S(1)} collective-permute-done((bf16[768,384]{1,0:T(8,128)(2,1)S(1)}, bf16[768,384]{1,0:T(8,128)(2,1)S(1)}, u32[]{:S(2)}, u32[]{:S(2)}) %collective-permute-start.13) | collective-permute-done | bytes 589856 | tf_op jit(solution)/shard_map/ppermute | solution.py:196
  70.5 0.1 pad_maximum_fusion.held_ref
  70.6 0.1 collective-permute-start.14
  70.7 1.3 %collective-permute-start.15 = (bf16[768,256]{1,0:T(8,128)(2,1)S(1)}, bf16[768,256]{1,0:T(8,128)(2,1)S(1)}, u32[]{:S(2)}, u32[]{:S(2)}) collective-permute-start(bf16[768,256]{1,0:T(8,128)(2,1)S(1)} %get-tuple-element.47.refs_0_), channel_id=1, source_target_pairs={{2,1},{1,0},{6,5},{5,4},{10,9},{9,8},{14,13},{13,12},{18,17},{17,1... | collective-permute-start | bytes 1179656 | tf_op jit(solution)/shard_map/ppermute | solution.py:443
  72.0 0.7 collective-permute-start.16
  72.6 0.0 collective-permute-done.18.got_ref
  72.7 2.1 %shard_map.103.refs_1_ = f32[1536,256]{1,0:T(8,128)S(1)} custom-call(s32[17]{0:T(128)S(1)} %pad_add_fusion.table_ref, bf16[1536,384]{1,0:T(8,128)(2,1)S(1)} %constant_dynamic-update-slice_fusion.7.held_ref, bf16[1536,384]{1,0:T(8,128)(2,1)S(1)} %collective-permute-done.18.got_ref, bf16[768,256]{1,0:T(8,128)(2,1)S(1)} %get-tuple-element.48.refs_0_, ...), custom_call_target="tpu_custom_call" | custom-call | flops 603979776 | bytes 4718592 | tf_op jit(solution)/shard_map/pallas_call | solution.py:23
  74.8 0.0 collective-permute-done.17.got_ref
  74.8 2.1 %shard_map.104.refs_2_ = f32[1536,256]{1,0:T(8,128)S(1)} custom-call(s32[17]{0:T(128)S(1)} %pad_add_fusion.table_ref, bf16[1536,384]{1,0:T(8,128)(2,1)S(1)} %constant_dynamic-update-slice_fusion.4.held_ref, bf16[1536,384]{1,0:T(8,128)(2,1)S(1)} %collective-permute-done.17.got_ref, bf16[768,256]{1,0:T(8,128)(2,1)S(1)} %get-tuple-element.47.refs_0_, ...), custom_call_target="tpu_custom_call" | custom-call | flops 603979776 | bytes 4718592 | tf_op jit(solution)/shard_map/pallas_call | solution.py:23
  76.9 7.1 %collective-permute-done.15.refs_0_ = bf16[768,256]{1,0:T(8,128)(2,1)S(1)} collective-permute-done((bf16[768,256]{1,0:T(8,128)(2,1)S(1)}, bf16[768,256]{1,0:T(8,128)(2,1)S(1)}, u32[]{:S(2)}, u32[]{:S(2)}) %collective-permute-start.15) | collective-permute-done | bytes 393248 | tf_op jit(solution)/shard_map/ppermute | solution.py:443
  84.1 0.0 collective-permute-done.16.refs_1_
  84.1 0.0 collective-permute-done.14.got_ref
  84.1 3.1 %shard_map.105 = bf16[1536,256]{1,0:T(8,128)(2,1)} custom-call(s32[17]{0:T(128)S(1)} %pad_add_fusion.table_ref, bf16[1536,384]{1,0:T(8,128)(2,1)S(1)} %pad_maximum_fusion.held_ref, bf16[1536,384]{1,0:T(8,128)(2,1)S(1)} %collective-permute-done.14.got_ref, bf16[768,256]{1,0:T(8,128)(2,1)S(1)} %collective-permute-done.15.refs_0_, ...), custom_call_target="tpu_custom_call" | custom-call | flops 603979776 | bytes 4718592 | tf_op jit(solution)/shard_map/pallas_call | solution.py:23
  (27 shorter events, 0.1 us)
Async XLA Ops:
  0.7 4.3 %copy-start.4 = (bf16[256,384]{1,0:T(8,128)(2,1)S(1)}, bf16[256,384]{1,0:T(8,128)(2,1)}, u32[]{:S(2)}) copy-start(bf16[256,384]{1,0:T(8,128)(2,1)} %v_ref.5) | copy-start | bytes 589828
  0.7 4.3 %copy-start.5 = (bf16[256,384]{1,0:T(8,128)(2,1)S(1)}, bf16[256,384]{1,0:T(8,128)(2,1)}, u32[]{:S(2)}) copy-start(bf16[256,384]{1,0:T(8,128)(2,1)} %g_ref.5) | copy-start | bytes 589828
  0.7 4.3 %copy-start.6 = (bf16[256,384]{1,0:T(8,128)(2,1)S(1)}, bf16[256,384]{1,0:T(8,128)(2,1)}, u32[]{:S(2)}) copy-start(bf16[256,384]{1,0:T(8,128)(2,1)} %q_ref.3) | copy-start | bytes 589828
  0.7 4.3 %copy-start.7 = (bf16[256,384]{1,0:T(8,128)(2,1)S(1)}, bf16[256,384]{1,0:T(8,128)(2,1)}, u32[]{:S(2)}) copy-start(bf16[256,384]{1,0:T(8,128)(2,1)} %k_ref.3) | copy-start | bytes 589828
  3.0 1.0 %copy-start.8 = (bf16[384,384]{1,0:T(8,128)(2,1)S(1)}, bf16[384,384]{1,0:T(8,128)(2,1)}, u32[]{:S(2)}) copy-start(bf16[384,384]{1,0:T(8,128)(2,1)} %get-tuple-element.28.refs_3_) | copy-start | bytes 884740
  4.0 1.0 %copy-start.10 = (bf16[384,384]{1,0:T(8,128)(2,1)S(1)}, bf16[384,384]{1,0:T(8,128)(2,1)}, u32[]{:S(2)}) copy-start(bf16[384,384]{1,0:T(8,128)(2,1)} %get-tuple-element.29.refs_1_) | copy-start | bytes 884740
  4.9 1.4 %copy-start.11 = (bf16[384,384]{1,0:T(8,128)(2,1)S(1)}, bf16[384,384]{1,0:T(8,128)(2,1)}, u32[]{:S(2)}) copy-start(bf16[384,384]{1,0:T(8,128)(2,1)} %get-tuple-element.29.refs_1_) | copy-start | bytes 884740
  5.8 20.8 %copy-start.9 = (bf16[384,384]{1,0:T(8,128)(2,1)S(1)}, bf16[384,384]{1,0:T(8,128)(2,1)}, u32[]{:S(2)}) copy-start(bf16[384,384]{1,0:T(8,128)(2,1)} %get-tuple-element.28.refs_3_) | copy-start | bytes 884740
  5.8 5.3 %collective-permute-start.1 = (bf16[784,128]{1,0:T(8,128)(2,1)S(1)}, bf16[784,128]{1,0:T(8,128)(2,1)S(1)}, u32[]{:S(2)}, u32[]{:S(2)}) collective-permute-start(bf16[784,128]{1,0:T(8,128)(2,1)S(1)} %get-tuple-element.31), channel_id=1, source_target_pairs={{0,4},{4,0},{8,12},{12,8},{16,20},{20,16},{24,28},{28,24},{1,5},{5... | collective-permute-start | bytes 602120 | tf_op jit(solution)/shard_map/ppermute | solution.py:396
  6.4 12.7 %collective-permute-start.3 = (bf16[384,384]{1,0:T(8,128)(2,1)S(1)}, bf16[384,384]{1,0:T(8,128)(2,1)S(1)}, u32[]{:S(2)}, u32[]{:S(2)}) collective-permute-start(bf16[384,384]{1,0:T(8,128)(2,1)S(1)} %copy-done.11), channel_id=1, source_target_pairs={{0,1},{1,2},{2,3},{3,0},{4,5},{5,6},{6,7},{7,4},{8,9},{9,10},{10,1... | collective-permute-start | bytes 884744 | tf_op jit(solution)/shard_map/ppermute | solution.py:364
  9.0 15.6 %collective-permute-start.4 = (bf16[384,384]{1,0:T(8,128)(2,1)}, bf16[384,384]{1,0:T(8,128)(2,1)S(1)}, u32[]{:S(2)}, u32[]{:S(2)}) collective-permute-start(bf16[384,384]{1,0:T(8,128)(2,1)} %get-tuple-element.30.refs_2_), channel_id=1, source_target_pairs={{0,3},{1,0},{2,1},{3,2},{4,7},{5,4},{6,5},{7,6},{8,11},{9,8},{10,9... | collective-permute-start | bytes 884744 | tf_op jit(solution)/shard_map/ppermute | solution.py:364
  11.2 7.0 %collective-permute-start.2 = (bf16[784,128]{1,0:T(8,128)(2,1)S(1)}, bf16[784,128]{1,0:T(8,128)(2,1)S(1)}, u32[]{:S(2)}, u32[]{:S(2)}) collective-permute-start(bf16[784,128]{1,0:T(8,128)(2,1)S(1)} %get-tuple-element.34), channel_id=1, source_target_pairs={{0,8},{4,12},{8,0},{12,4},{16,24},{20,28},{24,16},{28,20},{1,9},{5... | collective-permute-start | bytes 602120 | tf_op jit(solution)/shard_map/ppermute | solution.py:396
  24.6 10.4 %collective-permute-start.5 = (bf16[384,384]{1,0:T(8,128)(2,1)S(1)}, bf16[384,384]{1,0:T(8,128)(2,1)S(1)}, u32[]{:S(2)}, u32[]{:S(2)}) collective-permute-start(bf16[384,384]{1,0:T(8,128)(2,1)S(1)} %get-tuple-element.39), channel_id=1, source_target_pairs={{0,8},{4,20},{8,0},{12,28},{16,24},{20,4},{24,16},{28,12},{1,9},{5... | collective-permute-start | bytes 884744 | tf_op jit(solution)/shard_map/ppermute | solution.py:196
  26.1 8.9 %collective-permute-start.6 = (bf16[384,384]{1,0:T(8,128)(2,1)S(1)}, bf16[384,384]{1,0:T(8,128)(2,1)S(1)}, u32[]{:S(2)}, u32[]{:S(2)}) collective-permute-start(bf16[384,384]{1,0:T(8,128)(2,1)S(1)} %get-tuple-element.40), channel_id=1, source_target_pairs={{0,8},{4,20},{8,0},{12,28},{16,24},{20,4},{24,16},{28,12},{1,9},{5... | collective-permute-start | bytes 884744 | tf_op jit(solution)/shard_map/ppermute | solution.py:196
  26.6 16.9 %collective-permute-start = (bf16[384,384]{1,0:T(8,128)(2,1)S(1)}, bf16[384,384]{1,0:T(8,128)(2,1)S(1)}, u32[]{:S(2)}, u32[]{:S(2)}) collective-permute-start(bf16[384,384]{1,0:T(8,128)(2,1)S(1)} %copy-done.9), channel_id=1, source_target_pairs={{0,2},{1,3},{2,0},{3,1},{4,6},{5,7},{6,4},{7,5},{8,10},{9,11},{10,... | collective-permute-start | bytes 884744 | tf_op jit(solution)/shard_map/ppermute | solution.py:364
  28.8 5.8 %collective-permute-start.7 = (bf16[384,128]{1,0:T(8,128)(2,1)S(1)}, bf16[384,128]{1,0:T(8,128)(2,1)S(1)}, u32[]{:S(2)}, u32[]{:S(2)}) collective-permute-start(bf16[384,128]{1,0:T(8,128)(2,1)S(1)} %get-tuple-element.41), channel_id=1, source_target_pairs={{0,16},{4,20},{8,24},{12,28},{16,0},{20,4},{24,8},{28,12},{1,17},{... | collective-permute-start | bytes 294920 | tf_op jit(solution)/shard_map/ppermute | solution.py:396
  35.8 1.0 %copy-start.2 = (bf16[1536,384]{1,0:T(8,128)(2,1)}, bf16[1536,384]{1,0:T(8,128)(2,1)S(1)}, u32[]{:S(2)}) copy-start(bf16[1536,384]{1,0:T(8,128)(2,1)S(1)} %get-tuple-element.57) | copy-start | bytes 3538948
  36.9 23.6 %collective-permute-start.9 = (bf16[768,384]{1,0:T(8,128)(2,1)}, bf16[768,384]{1,0:T(8,128)(2,1)S(1)}, u32[]{:S(2)}, u32[]{:S(2)}) collective-permute-start(bf16[768,384]{1,0:T(8,128)(2,1)} %get-tuple-element.58.refs_2_), channel_id=1, source_target_pairs={{0,16},{4,12},{8,24},{12,4},{16,0},{20,28},{24,8},{28,20},{1,17},{... | collective-permute-start | bytes 1769480 | tf_op jit(solution)/shard_map/ppermute | solution.py:196
  38.4 6.6 %copy-start.12 = (s32[8]{0:T(128)S(1)}, s32[8]{0:T(128)}, u32[]{:S(2)}) copy-start(s32[8]{0:T(128)} %constant.29.clone) | copy-start | bytes 100
  38.4 6.6 %copy-start.13 = (s32[8]{0:T(128)S(1)}, s32[8]{0:T(128)}, u32[]{:S(2)}) copy-start(s32[8]{0:T(128)} %constant.30.clone) | copy-start | bytes 100
  39.2 21.2 %collective-permute-start.8 = (bf16[768,384]{1,0:T(8,128)(2,1)}, bf16[768,384]{1,0:T(8,128)(2,1)S(1)}, u32[]{:S(2)}, u32[]{:S(2)}) collective-permute-start(bf16[768,384]{1,0:T(8,128)(2,1)} %get-tuple-element.54.refs_1_), channel_id=1, source_target_pairs={{0,16},{4,12},{8,24},{12,4},{16,0},{20,28},{24,8},{28,20},{1,17},{... | collective-permute-start | bytes 1769480 | tf_op jit(solution)/shard_map/ppermute | solution.py:196
  39.7 13.8 %collective-permute-start.11 = (bf16[768,256]{1,0:T(8,128)(2,1)S(1)}, bf16[768,256]{1,0:T(8,128)(2,1)S(1)}, u32[]{:S(2)}, u32[]{:S(2)}) collective-permute-start(bf16[768,256]{1,0:T(8,128)(2,1)S(1)} %shard_map.98.refs_2_.grads_ref), channel_id=1, source_target_pairs={{0,1},{1,2},{2,3},{3,0},{4,5},{5,6},{6,7},{7,4},{8,9},{9,10},{10,1... | collective-permute-start | bytes 1179656 | tf_op jit(solution)/shard_map/ppermute | solution.py:432
  41.2 19.2 %collective-permute-start.12 = (bf16[768,256]{1,0:T(8,128)(2,1)S(1)}, bf16[768,256]{1,0:T(8,128)(2,1)S(1)}, u32[]{:S(2)}, u32[]{:S(2)}) collective-permute-start(bf16[768,256]{1,0:T(8,128)(2,1)S(1)} %shard_map.98.refs_2_.grads_ref), channel_id=1, source_target_pairs={{0,3},{1,0},{2,1},{3,2},{4,7},{5,4},{6,5},{7,6},{8,11},{9,8},{10,9... | collective-permute-start | bytes 1179656 | tf_op jit(solution)/shard_map/ppermute | solution.py:433
  43.5 16.9 %collective-permute-start.10 = (bf16[384,384]{1,0:T(8,128)(2,1)S(1)}, bf16[384,384]{1,0:T(8,128)(2,1)S(1)}, u32[]{:S(2)}, u32[]{:S(2)}) collective-permute-start(bf16[384,384]{1,0:T(8,128)(2,1)S(1)} %shard_map.100), channel_id=1, source_target_pairs={{0,8},{4,20},{8,0},{12,28},{16,24},{20,4},{24,16},{28,12},{1,9},{5... | collective-permute-start | bytes 884744 | tf_op jit(solution)/shard_map/ppermute | solution.py:196
  45.1 2.3 %copy-start = (bf16[6144,384]{1,0:T(8,128)(2,1)S(1)}, bf16[6144,384]{1,0:T(8,128)(2,1)}, u32[]{:S(2)}) copy-start(bf16[6144,384]{1,0:T(8,128)(2,1)} %wq_ref.3) | copy-start | bytes 14155780
  47.4 2.3 %copy-start.1 = (bf16[6144,384]{1,0:T(8,128)(2,1)S(1)}, bf16[6144,384]{1,0:T(8,128)(2,1)}, u32[]{:S(2)}) copy-start(bf16[6144,384]{1,0:T(8,128)(2,1)} %wk_ref.3) | copy-start | bytes 14155780
  60.4 1.8 %copy-start.3 = (bf16[1536,384]{1,0:T(8,128)(2,1)S(1)}, bf16[1536,384]{1,0:T(8,128)(2,1)}, u32[]{:S(2)}) copy-start(bf16[1536,384]{1,0:T(8,128)(2,1)} %copy-done.2) | copy-start | bytes 3538948
  60.5 9.9 %collective-permute-start.13 = (bf16[768,384]{1,0:T(8,128)(2,1)S(1)}, bf16[768,384]{1,0:T(8,128)(2,1)S(1)}, u32[]{:S(2)}, u32[]{:S(2)}) collective-permute-start(bf16[768,384]{1,0:T(8,128)(2,1)S(1)} %pad_maximum_fusion.1), channel_id=1, source_target_pairs={{0,16},{4,12},{8,24},{12,4},{16,0},{20,28},{24,8},{28,20},{1,17},{... | collective-permute-start | bytes 1769480 | tf_op jit(solution)/shard_map/ppermute | solution.py:196
  62.2 10.5 %collective-permute-start.18 = (bf16[1536,384]{1,0:T(8,128)(2,1)S(1)}, bf16[1536,384]{1,0:T(8,128)(2,1)S(1)}, u32[]{:S(2)}, u32[]{:S(2)}) collective-permute-start(bf16[1536,384]{1,0:T(8,128)(2,1)S(1)} %constant_dynamic-update-slice_fusion.7.held_ref), channel_id=1, source_target_pairs={{0,4},{4,0},{8,12},{12,8},{16,20},{20,16},{24,28},{28,24},{1,5},{5... | collective-permute-start | bytes 3538952 | tf_op jit(solution)/shard_map/ppermute | solution.py:196
  62.4 12.4 %collective-permute-start.17 = (bf16[1536,384]{1,0:T(8,128)(2,1)S(1)}, bf16[1536,384]{1,0:T(8,128)(2,1)S(1)}, u32[]{:S(2)}, u32[]{:S(2)}) collective-permute-start(bf16[1536,384]{1,0:T(8,128)(2,1)S(1)} %constant_dynamic-update-slice_fusion.4.held_ref), channel_id=1, source_target_pairs={{0,4},{4,0},{8,12},{12,8},{16,20},{20,16},{24,28},{28,24},{1,5},{5... | collective-permute-start | bytes 3538952 | tf_op jit(solution)/shard_map/ppermute | solution.py:196
  70.6 13.5 %collective-permute-start.14 = (bf16[1536,384]{1,0:T(8,128)(2,1)S(1)}, bf16[1536,384]{1,0:T(8,128)(2,1)S(1)}, u32[]{:S(2)}, u32[]{:S(2)}) collective-permute-start(bf16[1536,384]{1,0:T(8,128)(2,1)S(1)} %pad_maximum_fusion.held_ref), channel_id=1, source_target_pairs={{0,4},{4,0},{8,12},{12,8},{16,20},{20,16},{24,28},{28,24},{1,5},{5... | collective-permute-start | bytes 3538952 | tf_op jit(solution)/shard_map/ppermute | solution.py:196
  70.7 13.4 %collective-permute-start.15 = (bf16[768,256]{1,0:T(8,128)(2,1)S(1)}, bf16[768,256]{1,0:T(8,128)(2,1)S(1)}, u32[]{:S(2)}, u32[]{:S(2)}) collective-permute-start(bf16[768,256]{1,0:T(8,128)(2,1)S(1)} %get-tuple-element.47.refs_0_), channel_id=1, source_target_pairs={{2,1},{1,0},{6,5},{5,4},{10,9},{9,8},{14,13},{13,12},{18,17},{17,1... | collective-permute-start | bytes 1179656 | tf_op jit(solution)/shard_map/ppermute | solution.py:443
  72.0 12.1 %collective-permute-start.16 = (bf16[768,256]{1,0:T(8,128)(2,1)S(1)}, bf16[768,256]{1,0:T(8,128)(2,1)S(1)}, u32[]{:S(2)}, u32[]{:S(2)}) collective-permute-start(bf16[768,256]{1,0:T(8,128)(2,1)S(1)} %get-tuple-element.48.refs_0_), channel_id=1, source_target_pairs={{1,2},{2,3},{5,6},{6,7},{9,10},{10,11},{13,14},{14,15},{17,18},{18... | collective-permute-start | bytes 1179656 | tf_op jit(solution)/shard_map/ppermute | solution.py:442

commit v4 on v3

--- a/solution.py
+++ b/solution.py
@@ -9,10 +9,8 @@
 
 F32 = jnp.float32
 BF16 = jnp.bfloat16
-VMEM_BYTES = 40 * 1024 * 1024
-PACKSPACE = pltpu.VMEM
-WAIT1 = int(1.0e15 * 20e-6)
-WAIT2 = int(1.0e15 * 40e-6)
+VMEM_BYTES = 16 * 1024 * 1024
+EARLYC = False
 
 
 def contract(a, b, left, right):
@@ -66,7 +64,7 @@
     return ((lax.axis_index("seq") // hop) % 2).astype(F32)
 
 
-def states_kernel(nheads, width, decay_ref, q_ref, k_ref, v_ref, g_ref, sent_ref, held_ref, logs_ref):
+def states_kernel(nheads, width, decay_ref, q_ref, k_ref, v_ref, g_ref, token_ref, sent_ref, held_ref, logs_ref):
     span = q_ref.shape[0]
     tri = triangle(span).astype(F32).astype(BF16)
     cum = sum(contract(tri, part, 1, 1) for part in thirds(decay_ref[...]))
@@ -243,108 +241,90 @@
         ]
     return call(
         functools.partial(pack_kernel, share, shifts),
-        [jax.ShapeDtypeStruct((2 * share, wide), BF16)] * len(shifts),
+        [
+            jax.ShapeDtypeStruct((2 * share + (16 if i == 2 else 0), wide), BF16)
+            for i in range(len(shifts))
+        ],
         0, len(shifts) * share * wide * 8,
-        w_query, w_key,
+        *(pltpu.with_memory_space_constraint(w, pltpu.HBM) for w in (w_query, w_key)),
         in_specs=[pl.BlockSpec(memory_space=pl.ANY)] * 2,
-        out_specs=[pl.BlockSpec(memory_space=PACKSPACE)] * len(shifts),
+        out_specs=[pl.BlockSpec(memory_space=pltpu.VMEM)] * len(shifts),
         scratch_shapes=[pltpu.SemaphoreType.DMA((len(shifts), 2))],
-        vmem=58 * 1024 * 1024,
-    )
-
-
-def own_kernel(table_ref, wq_ref, wk_ref, grads_ref, out_ref):
-    wide = wq_ref.shape[1]
-    out_ref[...] = contract(wq_ref[...], grads_ref[:wide, :], 1, 0) + contract(
-        wk_ref[...], grads_ref[wide:, :], 1, 0
-    )
-
-
-def add_kernel(blocks, nother, last, table_ref, held_ref, got_ref, *refs):
-    others, refs = refs[:nother], refs[nother:]
-    total_ref, out_ref, grads = refs
-    step = pl.program_id(0)
-    half = pl.num_programs(0) // 2
-
-    @pl.when(step == 0)
-    def _():
-        if nother == 1:
-            grads[...] = others[0][...]
-        else:
-            grads[...] = jnp.where(table_ref[2 * blocks] == 1, others[1][...], others[0][...])
-
-    def finish(weights):
-        wide = weights.shape[1]
-        per = blocks // pl.num_programs(0)
-        share = weights.shape[0] // (2 * per)
-        left, right = grads[:wide, :], grads[wide:, :]
-        parts = []
-        for i in range(per):
-            start = 2 * i * share
-            parts.append(
-                contract(weights[start : start + share], left, 1, 0)
-                + contract(weights[start + share : start + 2 * share], right, 1, 0)
-            )
-        total = total_ref[...] + jnp.concatenate(parts)
-        if last:
-            for i in range(per):
-                place = table_ref[blocks + step * per + i]
-                out_ref[pl.ds(pl.multiple_of(place * share, 8), share), :] = total[
-                    i * share : (i + 1) * share, :
-                ].astype(BF16)
-        else:
-            out_ref[...] = total
-
-    @pl.when(step < half)
-    def _():
-        finish(held_ref[...])
-
-    @pl.when(step >= half)
-    def _():
-        finish(got_ref[...])
-
-
-def own_product(table, w_query, w_key, grads, blocks):
-    span = grads.shape[1]
+    )
+
+
+def row_block(weights, grads):
+    share, wide = weights.shape[0] // 2, weights.shape[1]
+    return contract(weights[:share], grads[:wide], 1, 0) + contract(weights[share:], grads[wide:], 1, 0)
+
+
+def own_kernel(wq_ref, wk_ref, grads_ref, out_ref, near_q, near_k, sems):
+    chunk, wide = near_q.shape
+    rows = pl.ds(pl.multiple_of(lax.axis_index("head") * chunk, 16), chunk)
+    copies = [
+        pltpu.make_async_copy(src.at[rows, :], dst, sems.at[i])
+        for i, (src, dst) in enumerate(((wq_ref, near_q), (wk_ref, near_k)))
+    ]
+    for copy in copies:
+        copy.start()
+    for copy in copies:
+        copy.wait()
+    out_ref[...] = contract(near_q[...], grads_ref[:wide, :], 1, 0) + contract(
+        near_k[...], grads_ref[wide:, :], 1, 0
+    )
+
+
+def own_product(w_query, w_key, grads, chunk):
     wide = w_query.shape[1]
-    share = w_query.shape[0] // (lax.axis_size("head") * blocks)
-    chunk = share * blocks
-    grid_spec = pltpu.PrefetchScalarGridSpec(
-        num_scalar_prefetch=1,
-        grid=(blocks,),
-        in_specs=[pl.BlockSpec((share, wide), lambda j, t: (t[j], 0))] * 2 + [whole(grads.shape)],
-        out_specs=pl.BlockSpec((share, span), lambda j, t: (j, 0)),
-    )
     return call(
-        own_kernel, jax.ShapeDtypeStruct((chunk, span), F32),
-        4 * chunk * span * wide, chunk * wide * 4 + chunk * span * 4,
-        table, w_query, w_key, grads, grid_spec=grid_spec,
-    )
-
-
-def add_product(table, held, got, others, total, blocks, last):
+        own_kernel, jax.ShapeDtypeStruct((chunk, grads.shape[1]), F32),
+        4 * chunk * grads.shape[1] * wide, chunk * wide * 4,
+        *(pltpu.with_memory_space_constraint(w, pltpu.HBM) for w in (w_query, w_key)), grads,
+        in_specs=[pl.BlockSpec(memory_space=pl.ANY)] * 2 + [pl.BlockSpec(memory_space=pltpu.VMEM)],
+        out_specs=pl.BlockSpec(memory_space=pltpu.VMEM),
+        scratch_shapes=[pltpu.VMEM((chunk, wide), BF16)] * 2 + [pltpu.SemaphoreType.DMA((2,))],
+    )
+
+
+def add_kernel(counts, last, table_ref, total_ref, *refs):
+    out_ref, refs = refs[-1], list(refs[:-1])
+    groups = []
+    for nblocks, nother in counts:
+        blocks, refs = refs[:nblocks], refs[nblocks:]
+        others, refs = refs[:nother], refs[nother:]
+        grads = others[0][...]
+        if nother == 2:
+            grads = jnp.where(table_ref[0] == 1, others[1][...], grads)
+        groups.append((blocks, grads))
+    share = groups[0][0][0].shape[0]
+    nshares = table_ref.shape[0] - 1
+    share = out_ref.shape[0] // nshares
+    for j in range(nshares):
+        rows = pl.ds(pl.multiple_of(table_ref[1 + j] * share, 8), share)
+        total = total_ref[rows, :]
+        for blocks, grads in groups:
+            at = 2 * share * j
+            for block in blocks:
+                if at < block.shape[0]:
+                    total = total + row_block(block[at : at + 2 * share], grads)
+                    break
+                at -= block.shape[0]
+        out_ref[rows, :] = total.astype(out_ref.dtype)
+
+
+def add_product(table, total, terms, last):
     chunk, span = total.shape
-    wide = held.shape[1]
-    steps = 4
-    rows = chunk // steps
-    half = steps // 2
-    grid_spec = pltpu.PrefetchScalarGridSpec(
-        num_scalar_prefetch=1,
-        grid=(steps,),
-        in_specs=[
-            pl.BlockSpec((2 * rows, wide), lambda j, t: (jnp.minimum(j, half - 1), 0)),
-            pl.BlockSpec((2 * rows, wide), lambda j, t: (jnp.maximum(j - half, 0), 0)),
-        ]
-        + [whole(others[0].shape)] * len(others)
-        + [pl.BlockSpec((rows, span), lambda j, t: (j, 0))],
-        out_specs=whole(total.shape) if last else pl.BlockSpec((rows, span), lambda j, t: (j, 0)),
-        scratch_shapes=[pltpu.VMEM(others[0].shape, BF16)],
-    )
+    counts = tuple((len(blocks), len(others)) for blocks, others in terms)
+    args = [x for blocks, others in terms for x in (*blocks, *others)]
     return call(
-        functools.partial(add_kernel, blocks, len(others), last),
+        functools.partial(add_kernel, counts, last),
         jax.ShapeDtypeStruct((chunk, span), BF16 if last else F32),
-        4 * chunk * span * wide, chunk * wide * 4 + chunk * span * 6,
-        table, held, got, *others, total, grid_spec=grid_spec,
+        2 * len(terms) * chunk * span * args[-1].shape[0], chunk * span * 8,
+        table, total, *args,
+        in_specs=[pl.BlockSpec(memory_space=pltpu.SMEM)]
+        + [pl.BlockSpec(memory_space=pltpu.VMEM)] * (1 + len(args)),
+        out_specs=pl.BlockSpec(memory_space=pltpu.VMEM),
+        vmem=24 * 1024 * 1024,
     )
 
 
@@ -361,9 +341,9 @@
     shifts = [1, nhead - 1] + list(range(2, nhead - 1))
     ring = {k: [(i, (i + k) % nhead) for i in range(nhead)] for k in shifts}
     packed = pack_weights(w_query, w_key, shifts, share)
-    pieces = [lax.ppermute(p, "head", ring[k]) for p, k in zip(packed, shifts)]
-
-    decay = gate([log_decay.T], packed)[0]
+    pieces = [lax.ppermute(p, "head", ring[k])[: 2 * share] for p, k in zip(packed, shifts)]
+
+    decay = log_decay.T
     sent, held, logs = call(
         functools.partial(states_kernel, nheads, width),
         (
@@ -372,7 +352,8 @@
             jax.ShapeDtypeStruct((24, width), F32),
         ),
         4 * span * rows * width, 8 * span * rows,
-        decay, query_act, key_act, value_act, grad_output,
+        decay, query_act, key_act, value_act, grad_output, packed[0],
+        in_specs=[pl.BlockSpec(memory_space=pltpu.VMEM)] * 5 + [pl.BlockSpec(memory_space=pl.ANY)],
     )
     nhops = len(share_order(nseq)[0]) + 1
     holds = [[p] for p in pieces]
@@ -385,11 +366,17 @@
                 holds[i] = [held, share_hop(held, progress[i])]
                 progress[i] += 1
 
+    local = call(
+        functools.partial(local_kernel, nheads, width),
+        jax.ShapeDtypeStruct((2 * rows, span), F32),
+        6 * span * span * rows, 16 * span * rows,
+        decay, query_act, key_act, value_act, grad_output,
+    )
     hop, enter = 1, None
     while True:
         if 2 * hop >= nseq:
             early = range(min(2, len(holds)))
-            sent, *firsts = gate([sent] + [holds[i][0] for i in early])
+            sent, *firsts = gate([sent] + [holds[i][0] for i in early], [local])
             for i in early:
                 holds[i][0] = firsts[i]
             advance(early)
@@ -409,12 +396,6 @@
             out_shape, 10 * rows * width, 16 * rows * width, *args,
         )
         hop *= 2
-    local = call(
-        functools.partial(local_kernel, nheads, width),
-        jax.ShapeDtypeStruct((2 * rows, span), F32),
-        6 * span * span * rows, 16 * span * rows,
-        decay, query_act, key_act, value_act, grad_output,
-    )
     both = call(
         functools.partial(carry_kernel, nheads, width, hop),
         jax.ShapeDtypeStruct((2 * rows, span), BF16),
@@ -424,16 +405,19 @@
 
     even, odd = share_deltas(nseq)
     deltas = jnp.where(my_seq % 2 == 1, jnp.array(odd, jnp.int32), jnp.array(even, jnp.int32))
-    places = deltas ^ my_seq
-    table = jnp.concatenate([places + my_head * nseq, places, (my_head >= 2).astype(jnp.int32)[None]])
-    total = own_product(table, w_query, w_key, both, nseq)
-
-    if nhead == 4:
+    table = jnp.concatenate([(my_head >= 2).astype(jnp.int32)[None], deltas ^ my_seq])
+    total = own_product(w_query, w_key, both, chunk)
+
+    if nhead == 4 and nhops == 3:
         p1 = lax.ppermute(both, "head", ring[1])
         p3 = lax.ppermute(both, "head", ring[3])
-        holds[0][1], holds[1][1] = gate([holds[0][1], holds[1][1]], [both])
+        if EARLYC:
+            holds[0][1], holds[1][1], holds[2][0] = gate([holds[0][1], holds[1][1], holds[2][0]], [both])
+        else:
+            holds[0][1], holds[1][1] = gate([holds[0][1], holds[1][1]], [both])
         advance([0, 1])
-        (holds[2][0],) = gate([holds[2][0]], [holds[0][0], holds[1][0]])
+        if not EARLYC:
+            (holds[2][0],) = gate([holds[2][0]], [holds[0][0], holds[1][0]])
         advance([2])
         holds[0][1], holds[1][1], holds[2][1], p1, p3 = gate(
             [holds[0][1], holds[1][1], holds[2][1], p1, p3], [total]
@@ -441,15 +425,18 @@
         advance([0, 1, 2])
         up = lax.ppermute(p1, "head", [(1, 2), (2, 3)])
         down = lax.ppermute(p3, "head", [(2, 1), (1, 0)])
-        others = [(p1,), (p3,), (down, up)]
-    else:
-        gathered = lax.all_gather(both, "head")
-        others = [(gathered[(my_head + nhead - k) % nhead],) for k in shifts]
-
+        total = add_product(table, total, [(holds[0], (p1,)), (holds[1], (p3,))], False)
+        holds[2][1], up, down = gate([holds[2][1], up, down], [total])
+        near, far = holds[2]
+        blocks = [near, far] + [share_hop(x, 2) for x in (near, far)]
+        return add_product(table, total, [(blocks, (down, up))], True)
+
+    gathered = lax.all_gather(both, "head")
     while min(progress) < nhops:
         advance(range(len(pieces)))
-    for i, grads in enumerate(others):
-        total = add_product(table, holds[i][0], holds[i][1], grads, total, nseq, i == nhead - 2)
+    for i, k in enumerate(shifts):
+        grads = gathered[(my_head + nhead - k) % nhead]
+        total = add_product(table, total, [(holds[i], (grads,))], i == nhead - 2)
     return total
 
 

time: 87.5 us -> 78.4 us (0.90)
  local copies, waits for them, and re-layouts: 11 us -> 4.5 us
  Pallas kernels: 15.5 us -> 13.8 us
    unnamed x32 -> x16, local copies, waits for them, and re-layouts: 10.8 us -> 1.92 us
    ppermute x9 -> x10, waiting for transfers between devices: 7.55 us -> 2.39 us  [share_hop(): return lax.ppermute(held, 'seq', pairs)]
    ppermute x1, waiting for transfers between devices: 1.13 us -> 5.47 us  [shards(): p1 = lax.ppermute(both, 'head', ring[1])]
    concatenate x2 -> x3, local copies, waits for them, and re-layouts: 0.19 us -> 2.55 us  [advance(): held = holds[i][0] if progress[i] == 0 else jnp.concatenate(holds[i])]
    pallas_call x15 -> x14, Pallas kernels: 15.5 us -> 13.8 us  [call(): pl.pallas_call(kernel, out_shape=out_shape, cost_estimate=pl.CostEstimate...]
    ppermute x3, waiting for transfers between devices: 8.65 us -> 7.6 us  [shards(): got = lax.ppermute(sent, 'seq', [(i, i ^ hop) for i in range(nseq)])]
    ppermute x9 -> x10, starting transfers between devices: 7.82 us -> 7.72 us  [share_hop(): return lax.ppermute(held, 'seq', pairs)]
  transfers between devices with their start and end apart: 19 -> 20, of which waited for: 7 -> 9; matrix products, arithmetic and copies ran while one was open for 3% -> 5% of each run, Pallas kernels for 11% -> 12%
where the time goes in v4:
time: 78.4 us; the launch traced here: 78.2 us
  waiting for transfers between devices  36.3 us (46%)
  starting transfers between devices  23.3 us (30%)
  Pallas kernels  13.8 us (18%)
  local copies, waits for them, and re-layouts  4.5 us (6%)
    pallas_call x14, Pallas kernels, call(): pl.pallas_call(kernel, out_shape=out_shape, cost_estimate=pl.CostEstimate...  13.8 us
    ppermute x10, starting transfers between devices, share_hop(): return lax.ppermute(held, 'seq', pairs)  7.72 us
    ppermute x1, waiting for transfers between devices, shards(): p3 = lax.ppermute(both, 'head', ring[3])  7.72 us
    ppermute x3, waiting for transfers between devices, shards(): got = lax.ppermute(sent, 'seq', [(i, i ^ hop) for i in range(nseq)])  7.6 us
    ppermute x1, waiting for transfers between devices, shards(): down = lax.ppermute(p3, 'head', [(2, 1), (1, 0)])  7.49 us
    ppermute x3, starting transfers between devices, shards(): lax.ppermute(p, 'head', ring[k])[:2 * share]  6.04 us
    ppermute x3, waiting for transfers between devices, shards(): lax.ppermute(p, 'head', ring[k])[:2 * share]  5.58 us
    ppermute x1, waiting for transfers between devices, shards(): p1 = lax.ppermute(both, 'head', ring[1])  5.47 us
  transfers between devices with their start and end apart: 20, of which 9 were waited for; matrix products, arithmetic and copies ran while one was open for 5% of the time, Pallas kernels for 12%

profile of v4, /device:TPU:0, one launch (start us, length us, event | category | flops | bytes accessed | tf_op | source)
XLA Modules:
  0.0 78.2 jit_solution(4463478694685714568)
XLA Ops:
  0.0 0.0 copy-start.4
  0.0 1.4 %shard_map.91 = (bf16[384,384]{1,0:T(8,128)(2,1)S(1)}, bf16[384,384]{1,0:T(8,128)(2,1)S(1)}, bf16[400,384]{1,0:T(8,128)(2,1)S(1)}) custom-call(bf16[6144,384]{1,0:T(8,128)(2,1)} %wq_ref.3, bf16[6144,384]{1,0:T(8,128)(2,1)} %wk_ref.3), custom_call_target="tpu_custom_call" | custom-call | bytes 1769472 | tf_op jit(solution)/shard_map/pallas_call | solution.py:21
  1.4 0.0 copy-done.4
  1.4 0.0 copy-done
  1.4 0.0 copy-done.1
  1.4 0.1 copy-done.2
  1.5 0.1 copy-done.3
  1.6 0.9 %shard_map.92 = (bf16[784,128]{1,0:T(8,128)(2,1)S(1)}, f32[768,128]{1,0:T(8,128)S(1)}, f32[24,128]{1,0:T(8,128)S(1)}) custom-call(f32[3,256]{1,0:T(4,128)S(1)} %bitcast.2, bf16[256,384]{1,0:T(8,128)(2,1)S(1)} %copy-done.2, bf16[256,384]{1,0:T(8,128)(2,1)S(1)} %copy-done.3, bf16[256,384]{1,0:T(8,128)(2,1)S(1)} %copy-done, bf16[256,384]{1,0:T(8,128)(2,1)S(1)} %copy-done.1, ...), custom_call_target="tpu_custom_call" | custom-call | flops 50331648 | bytes 786432 | tf_op jit(solution)/shard_map/pallas_call | solution.py:21
  2.5 0.5 collective-permute-start
  3.0 2.6 %collective-permute-start.2 = (bf16[384,384]{1,0:T(8,128)(2,1)S(1)}, bf16[384,384]{1,0:T(8,128)(2,1)S(1)}, u32[]{:S(2)}, u32[]{:S(2)}) collective-permute-start(bf16[384,384]{1,0:T(8,128)(2,1)S(1)} %get-tuple-element.31.token_ref), channel_id=1, source_target_pairs={{0,1},{1,2},{2,3},{3,0},{4,5},{5,6},{6,7},{7,4},{8,9},{9,10},{10,1... | collective-permute-start | bytes 884744 | tf_op jit(solution)/shard_map/ppermute | solution.py:344
  5.6 2.1 %collective-permute-start.3 = (bf16[384,384]{1,0:T(8,128)(2,1)S(1)}, bf16[384,384]{1,0:T(8,128)(2,1)S(1)}, u32[]{:S(2)}, u32[]{:S(2)}) collective-permute-start(bf16[384,384]{1,0:T(8,128)(2,1)S(1)} %get-tuple-element.40), channel_id=1, source_target_pairs={{0,3},{1,0},{2,1},{3,2},{4,7},{5,4},{6,5},{7,6},{8,11},{9,8},{10,9... | collective-permute-start | bytes 884744 | tf_op jit(solution)/shard_map/ppermute | solution.py:344
  7.7 0.0 collective-permute-done.got_ref
  7.7 0.1 shard_map.93
  7.8 1.7 %collective-permute-start.1 = (bf16[784,128]{1,0:T(8,128)(2,1)S(1)}, bf16[784,128]{1,0:T(8,128)(2,1)S(1)}, u32[]{:S(2)}, u32[]{:S(2)}) collective-permute-start(bf16[784,128]{1,0:T(8,128)(2,1)S(1)} %get-tuple-element.35), channel_id=1, source_target_pairs={{0,8},{4,12},{8,0},{12,4},{16,24},{20,28},{24,16},{28,20},{1,9},{5... | collective-permute-start | bytes 602120 | tf_op jit(solution)/shard_map/ppermute | solution.py:383
  9.5 1.0 %shard_map.95.refs_3_.local_ref = f32[768,256]{1,0:T(8,128)S(1)} custom-call(f32[3,256]{1,0:T(4,128)S(1)} %bitcast.3, bf16[256,384]{1,0:T(8,128)(2,1)S(1)} %copy-done.2, bf16[256,384]{1,0:T(8,128)(2,1)S(1)} %copy-done.3, bf16[256,384]{1,0:T(8,128)(2,1)S(1)} %copy-done, bf16[256,384]{1,0:T(8,128)(2,1)S(1)} %copy-done.1), custom_call_target="tpu_custom_call" | custom-call | flops 150994944 | bytes 1572864 | tf_op jit(solution)/shard_map/pallas_call | solution.py:21
  10.6 4.3 %collective-permute-done.1.got_ref = bf16[784,128]{1,0:T(8,128)(2,1)S(1)} collective-permute-done((bf16[784,128]{1,0:T(8,128)(2,1)S(1)}, bf16[784,128]{1,0:T(8,128)(2,1)S(1)}, u32[]{:S(2)}, u32[]{:S(2)}) %collective-permute-start.1) | collective-permute-done | bytes 200736 | tf_op jit(solution)/shard_map/ppermute | solution.py:383
  14.9 0.8 %shard_map.94 = (bf16[384,128]{1,0:T(8,128)(2,1)S(1)}, f32[768,128]{1,0:T(8,128)}, f32[24,128]{1,0:T(8,128)S(1)}, f32[768,128]{1,0:T(8,128)S(1)}) custom-call(bf16[784,128]{1,0:T(8,128)(2,1)S(1)} %collective-permute-done.1.got_ref, f32[768,128]{1,0:T(8,128)S(1)} %get-tuple-element.36.held_ref, f32[24,128]{1,0:T(8,128)S(1)} %get-tuple-element.37.logs_ref, ...), custom_call_target="tpu_custom_call" | custom-call | flops 491520 | bytes 786432 | tf_op jit(solution)/shard_map/pallas_call | solution.py:21
  15.7 0.0 collective-permute-done.2.refs_1_
  15.7 5.3 %collective-permute-done.3.refs_2_ = bf16[384,384]{1,0:T(8,128)(2,1)S(1)} collective-permute-done((bf16[384,384]{1,0:T(8,128)(2,1)S(1)}, bf16[384,384]{1,0:T(8,128)(2,1)S(1)}, u32[]{:S(2)}, u32[]{:S(2)}) %collective-permute-start.3) | collective-permute-done | bytes 294944 | tf_op jit(solution)/shard_map/ppermute | solution.py:344
  21.0 1.5 %collective-permute-start.5 = (bf16[384,384]{1,0:T(8,128)(2,1)S(1)}, bf16[384,384]{1,0:T(8,128)(2,1)S(1)}, u32[]{:S(2)}, u32[]{:S(2)}) collective-permute-start(bf16[384,384]{1,0:T(8,128)(2,1)S(1)} %get-tuple-element.44), channel_id=1, source_target_pairs={{0,8},{4,20},{8,0},{12,28},{16,24},{20,4},{24,16},{28,12},{1,9},{5... | collective-permute-start | bytes 884744 | tf_op jit(solution)/shard_map/ppermute | solution.py:194
  22.5 0.5 collective-permute-start.6
  23.0 1.3 %collective-permute-start.9 = (bf16[400,384]{1,0:T(8,128)(2,1)S(1)}, bf16[400,384]{1,0:T(8,128)(2,1)S(1)}, u32[]{:S(2)}, u32[]{:S(2)}) collective-permute-start(bf16[400,384]{1,0:T(8,128)(2,1)S(1)} %get-tuple-element.48), channel_id=1, source_target_pairs={{0,2},{1,3},{2,0},{3,1},{4,6},{5,7},{6,4},{7,5},{8,10},{9,11},{10,... | collective-permute-start | bytes 921608 | tf_op jit(solution)/shard_map/ppermute | solution.py:344
  24.3 1.5 %collective-permute-start.4 = (bf16[384,128]{1,0:T(8,128)(2,1)S(1)}, bf16[384,128]{1,0:T(8,128)(2,1)S(1)}, u32[]{:S(2)}, u32[]{:S(2)}) collective-permute-start(bf16[384,128]{1,0:T(8,128)(2,1)S(1)} %get-tuple-element.41), channel_id=1, source_target_pairs={{0,16},{4,20},{8,24},{12,28},{16,0},{20,4},{24,8},{28,12},{1,17},{... | collective-permute-start | bytes 294920 | tf_op jit(solution)/shard_map/ppermute | solution.py:383
  25.9 0.9 %constant_dynamic-update-slice_fusion.1 = (bf16[768,384]{1,0:T(8,128)(2,1)S(1)}, bf16[1536,384]{1,0:T(8,128)(2,1)}, bf16[768,384]{1,0:T(8,128)(2,1)S(1)}, bf16[1536,384]{1,0:T(8,128)(2,1)}) fusion(bf16[384,384]{1,0:T(8,128)(2,1)S(1)} %get-tuple-element.44, bf16[384,384]{1,0:T(8,128)(2,1)S(1)} %get-tuple-element.45), kind=kLoop, calls=%fused_computation.2 | loop fusion | bytes 1769472
  26.8 3.3 %collective-permute-done.4.got_ref = bf16[384,128]{1,0:T(8,128)(2,1)S(1)} collective-permute-done((bf16[384,128]{1,0:T(8,128)(2,1)S(1)}, bf16[384,128]{1,0:T(8,128)(2,1)S(1)}, u32[]{:S(2)}, u32[]{:S(2)}) %collective-permute-start.4) | collective-permute-done | bytes 98336 | tf_op jit(solution)/shard_map/ppermute | solution.py:383
  30.1 0.4 shard_map.97.grads_ref.refs_2_
  30.5 0.0 collective-permute-done.5.refs_0_
  30.5 0.4 collective-permute-done.6.refs_1_
  30.9 0.8 %constant_dynamic-update-slice_fusion = (bf16[768,384]{1,0:T(8,128)(2,1)S(1)}, bf16[1536,384]{1,0:T(8,128)(2,1)}) fusion(bf16[768,384]{1,0:T(8,128)(2,1)S(1)} %get-tuple-element.63, bf16[384,384]{1,0:T(8,128)(2,1)S(1)} %get-tuple-element.46, bf16[1536,384]{1,0:T(8,128)(2,1)} %get-tuple-element.64), kind=kLoop, calls=%fused_computation.1 | loop fusion | bytes 884736 | tf_op jit(solution)/shard_map/concatenate | solution.py:365
  31.7 1.5 %collective-permute-start.7 = (bf16[768,384]{1,0:T(8,128)(2,1)S(1)}, bf16[768,384]{1,0:T(8,128)(2,1)S(1)}, u32[]{:S(2)}, u32[]{:S(2)}) collective-permute-start(bf16[768,384]{1,0:T(8,128)(2,1)S(1)} %get-tuple-element.61.refs_1_), channel_id=1, source_target_pairs={{0,16},{4,12},{8,24},{12,4},{16,0},{20,28},{24,8},{28,20},{1,17},{... | collective-permute-start | bytes 1769480 | tf_op jit(solution)/shard_map/ppermute | solution.py:194
  33.2 0.8 %constant_dynamic-update-slice_fusion.8 = (bf16[1536,384]{1,0:T(8,128)(2,1)}, bf16[768,384]{1,0:T(8,128)(2,1)S(1)}) fusion(bf16[1536,384]{1,0:T(8,128)(2,1)} %get-tuple-element.66, bf16[384,384]{1,0:T(8,128)(2,1)S(1)} %get-tuple-element.47, bf16[768,384]{1,0:T(8,128)(2,1)S(1)} %get-tuple-element.65), kind=kLoop, calls=%fused_computation.9 | loop fusion | bytes 884736
  34.0 0.5 collective-permute-start.8
  34.5 1.2 %collective-permute-start.11 = (bf16[768,256]{1,0:T(8,128)(2,1)S(1)}, bf16[768,256]{1,0:T(8,128)(2,1)S(1)}, u32[]{:S(2)}, u32[]{:S(2)}) collective-permute-start(bf16[768,256]{1,0:T(8,128)(2,1)S(1)} %shard_map.97.grads_ref.refs_2_), channel_id=1, source_target_pairs={{0,1},{1,2},{2,3},{3,0},{4,5},{5,6},{6,7},{7,4},{8,9},{9,10},{10,1... | collective-permute-start | bytes 1179656 | tf_op jit(solution)/shard_map/ppermute | solution.py:412
  35.8 2.6 %collective-permute-start.12 = (bf16[768,256]{1,0:T(8,128)(2,1)S(1)}, bf16[768,256]{1,0:T(8,128)(2,1)S(1)}, u32[]{:S(2)}, u32[]{:S(2)}) collective-permute-start(bf16[768,256]{1,0:T(8,128)(2,1)S(1)} %shard_map.97.grads_ref.refs_2_), channel_id=1, source_target_pairs={{0,3},{1,0},{2,1},{3,2},{4,7},{5,4},{6,5},{7,6},{8,11},{9,8},{10,9... | collective-permute-start | bytes 1179656 | tf_op jit(solution)/shard_map/ppermute | solution.py:413
  38.4 0.3 collective-permute-done.9
  38.7 1.6 %collective-permute-start.10 = (bf16[384,384]{1,0:T(8,128)(2,1)S(1)}, bf16[384,384]{1,0:T(8,128)(2,1)S(1)}, u32[]{:S(2)}, u32[]{:S(2)}) collective-permute-start(bf16[384,384]{1,0:T(8,128)(2,1)S(1)} %shard_map.100), channel_id=1, source_target_pairs={{0,8},{4,20},{8,0},{12,28},{16,24},{20,4},{24,16},{28,12},{1,9},{5... | collective-permute-start | bytes 884744 | tf_op jit(solution)/shard_map/ppermute | solution.py:194
  40.2 2.6 %shard_map.98.refs_5_.total_ref = f32[1536,256]{1,0:T(8,128)S(1)} custom-call(bf16[6144,384]{1,0:T(8,128)(2,1)} %wq_ref.3, bf16[6144,384]{1,0:T(8,128)(2,1)} %wk_ref.3, bf16[768,256]{1,0:T(8,128)(2,1)S(1)} %shard_map.97.grads_ref.refs_2_), custom_call_target="tpu_custom_call" | custom-call | flops 603979776 | bytes 2359296 | tf_op jit(solution)/shard_map/pallas_call | solution.py:21
  42.8 5.5 %collective-permute-done.11.refs_3_ = bf16[768,256]{1,0:T(8,128)(2,1)S(1)} collective-permute-done((bf16[768,256]{1,0:T(8,128)(2,1)S(1)}, bf16[768,256]{1,0:T(8,128)(2,1)S(1)}, u32[]{:S(2)}, u32[]{:S(2)}) %collective-permute-start.11) | collective-permute-done | bytes 393248 | tf_op jit(solution)/shard_map/ppermute | solution.py:412
  48.3 7.7 %collective-permute-done.12.refs_4_ = bf16[768,256]{1,0:T(8,128)(2,1)S(1)} collective-permute-done((bf16[768,256]{1,0:T(8,128)(2,1)S(1)}, bf16[768,256]{1,0:T(8,128)(2,1)S(1)}, u32[]{:S(2)}, u32[]{:S(2)}) %collective-permute-start.12) | collective-permute-done | bytes 393248 | tf_op jit(solution)/shard_map/ppermute | solution.py:413
  56.0 0.0 collective-permute-done.10.refs_2_
  56.0 0.0 collective-permute-done.7.refs_0_
  56.0 0.0 collective-permute-done.8.refs_1_
  56.1 0.9 %constant_dynamic-update-slice_fusion.4.refs_0_ = bf16[1536,384]{1,0:T(8,128)(2,1)} fusion(bf16[1536,384]{1,0:T(8,128)(2,1)} %get-tuple-element.62, bf16[768,384]{1,0:T(8,128)(2,1)S(1)} %get-tuple-element.49), kind=kLoop, calls=%fused_computation.5 | loop fusion | bytes 1179648 | tf_op jit(solution)/shard_map/concatenate | solution.py:365
  56.9 0.0 collective-permute-start.13
  56.9 0.9 %constant_dynamic-update-slice_fusion.7.refs_3_ = bf16[1536,384]{1,0:T(8,128)(2,1)} fusion(bf16[1536,384]{1,0:T(8,128)(2,1)} %get-tuple-element.57, bf16[768,384]{1,0:T(8,128)(2,1)S(1)} %get-tuple-element.51), kind=kLoop, calls=%fused_computation.8 | loop fusion | bytes 1179648 | tf_op jit(solution)/shard_map/concatenate | solution.py:365
  57.8 0.5 collective-permute-start.14
  58.3 0.1 pad_maximum_fusion.refs_0_
  58.4 1.6 %collective-permute-start.15 = (bf16[768,384]{1,0:T(8,128)(2,1)S(1)}, bf16[768,384]{1,0:T(8,128)(2,1)S(1)}, u32[]{:S(2)}, u32[]{:S(2)}) collective-permute-start(bf16[768,384]{1,0:T(8,128)(2,1)S(1)} %pad_maximum_fusion.refs_0_), channel_id=1, source_target_pairs={{0,16},{4,12},{8,24},{12,4},{16,0},{20,28},{24,8},{28,20},{1,17},{... | collective-permute-start | bytes 1769480 | tf_op jit(solution)/shard_map/ppermute | solution.py:194
  60.0 0.7 collective-permute-start.16
  60.7 1.3 %collective-permute-start.17 = (bf16[768,256]{1,0:T(8,128)(2,1)S(1)}, bf16[768,256]{1,0:T(8,128)(2,1)S(1)}, u32[]{:S(2)}, u32[]{:S(2)}) collective-permute-start(bf16[768,256]{1,0:T(8,128)(2,1)S(1)} %get-tuple-element.52.refs_5_), channel_id=1, source_target_pairs={{2,1},{1,0},{6,5},{5,4},{10,9},{9,8},{14,13},{13,12},{18,17},{17,1... | collective-permute-start | bytes 1179656 | tf_op jit(solution)/shard_map/ppermute | solution.py:427
  62.0 0.0 copy-done.5
  62.0 0.0 copy-done.6
  62.0 0.1 pad_add_fusion.table_ref
  62.1 0.0 collective-permute-done.13.refs_1_
  62.1 0.0 collective-permute-start.18
  62.1 0.0 collective-permute-done.14.refs_4_
  62.1 4.2 %shard_map.102.refs_3_.total_ref = f32[1536,256]{1,0:T(8,128)S(1)} custom-call(s32[9]{0:T(128)S(1)} %pad_add_fusion.table_ref, f32[1536,256]{1,0:T(8,128)S(1)} %shard_map.98.refs_5_.total_ref, bf16[1536,384]{1,0:T(8,128)(2,1)} %constant_dynamic-update-slice_fusion.4.refs_0_, bf16[1536,384]{1,0:T(8,128)(2,1)} %collective-permute-done.13.refs_1_, ...), custom_call_target="tpu_custom_call" | custom-call | flops 1207959552 | bytes 3145728 | tf_op jit(solution)/shard_map/pallas_call | solution.py:21
  66.3 0.0 collective-permute-done.16.refs_1_
  66.3 7.5 %collective-permute-done.17.refs_2_ = bf16[768,256]{1,0:T(8,128)(2,1)S(1)} collective-permute-done((bf16[768,256]{1,0:T(8,128)(2,1)S(1)}, bf16[768,256]{1,0:T(8,128)(2,1)S(1)}, u32[]{:S(2)}, u32[]{:S(2)}) %collective-permute-start.17) | collective-permute-done | bytes 393248 | tf_op jit(solution)/shard_map/ppermute | solution.py:427
  73.8 0.0 collective-permute-done.15.refs_0_
  73.8 0.0 collective-permute-start.19
  73.8 0.0 collective-permute-done.18.refs_2_
  73.8 2.0 %collective-permute-done.19.refs_3_ = bf16[768,384]{1,0:T(8,128)(2,1)S(1)} collective-permute-done((bf16[768,384]{1,0:T(8,128)(2,1)S(1)}, bf16[768,384]{1,0:T(8,128)(2,1)S(1)}, u32[]{:S(2)}, u32[]{:S(2)}) %collective-permute-start.19) | collective-permute-done | bytes 589856 | tf_op jit(solution)/shard_map/ppermute | solution.py:194
  75.8 2.4 %shard_map.104 = bf16[1536,256]{1,0:T(8,128)(2,1)} custom-call(s32[9]{0:T(128)S(1)} %pad_add_fusion.table_ref, f32[1536,256]{1,0:T(8,128)S(1)} %shard_map.102.refs_3_.total_ref, bf16[768,384]{1,0:T(8,128)(2,1)S(1)} %pad_maximum_fusion.refs_0_, bf16[768,384]{1,0:T(8,128)(2,1)S(1)} %get-tuple-element.54.refs_1_, ...), custom_call_target="tpu_custom_call" | custom-call | flops 603979776 | bytes 3145728 | tf_op jit(solution)/shard_map/pallas_call | solution.py:21
  (13 shorter events, 0.1 us)
Async XLA Ops:
  0.0 1.4 %copy-start.4 = (f32[256,3]{0,1:T(4,128)S(1)}, f32[256,3]{0,1:T(4,128)}, u32[]{:S(2)}) copy-start(f32[256,3]{0,1:T(4,128)} %param.13) | copy-start | bytes 9220
  0.0 1.4 %copy-start = (bf16[256,384]{1,0:T(8,128)(2,1)S(1)}, bf16[256,384]{1,0:T(8,128)(2,1)}, u32[]{:S(2)}) copy-start(bf16[256,384]{1,0:T(8,128)(2,1)} %v_ref.5) | copy-start | bytes 589828
  0.0 1.4 %copy-start.1 = (bf16[256,384]{1,0:T(8,128)(2,1)S(1)}, bf16[256,384]{1,0:T(8,128)(2,1)}, u32[]{:S(2)}) copy-start(bf16[256,384]{1,0:T(8,128)(2,1)} %g_ref.5) | copy-start | bytes 589828
  0.0 1.5 %copy-start.2 = (bf16[256,384]{1,0:T(8,128)(2,1)S(1)}, bf16[256,384]{1,0:T(8,128)(2,1)}, u32[]{:S(2)}) copy-start(bf16[256,384]{1,0:T(8,128)(2,1)} %q_ref.3) | copy-start | bytes 589828
  0.0 1.6 %copy-start.3 = (bf16[256,384]{1,0:T(8,128)(2,1)S(1)}, bf16[256,384]{1,0:T(8,128)(2,1)}, u32[]{:S(2)}) copy-start(bf16[256,384]{1,0:T(8,128)(2,1)} %k_ref.3) | copy-start | bytes 589828
  2.5 5.3 %collective-permute-start = (bf16[784,128]{1,0:T(8,128)(2,1)S(1)}, bf16[784,128]{1,0:T(8,128)(2,1)S(1)}, u32[]{:S(2)}, u32[]{:S(2)}) collective-permute-start(bf16[784,128]{1,0:T(8,128)(2,1)S(1)} %get-tuple-element.32), channel_id=1, source_target_pairs={{0,4},{4,0},{8,12},{12,8},{16,20},{20,16},{24,28},{28,24},{1,5},{5... | collective-permute-start | bytes 602120 | tf_op jit(solution)/shard_map/ppermute | solution.py:383
  3.0 12.7 %collective-permute-start.2 = (bf16[384,384]{1,0:T(8,128)(2,1)S(1)}, bf16[384,384]{1,0:T(8,128)(2,1)S(1)}, u32[]{:S(2)}, u32[]{:S(2)}) collective-permute-start(bf16[384,384]{1,0:T(8,128)(2,1)S(1)} %get-tuple-element.31.token_ref), channel_id=1, source_target_pairs={{0,1},{1,2},{2,3},{3,0},{4,5},{5,6},{6,7},{7,4},{8,9},{9,10},{10,1... | collective-permute-start | bytes 884744 | tf_op jit(solution)/shard_map/ppermute | solution.py:344
  5.6 15.4 %collective-permute-start.3 = (bf16[384,384]{1,0:T(8,128)(2,1)S(1)}, bf16[384,384]{1,0:T(8,128)(2,1)S(1)}, u32[]{:S(2)}, u32[]{:S(2)}) collective-permute-start(bf16[384,384]{1,0:T(8,128)(2,1)S(1)} %get-tuple-element.40), channel_id=1, source_target_pairs={{0,3},{1,0},{2,1},{3,2},{4,7},{5,4},{6,5},{7,6},{8,11},{9,8},{10,9... | collective-permute-start | bytes 884744 | tf_op jit(solution)/shard_map/ppermute | solution.py:344
  7.8 7.0 %collective-permute-start.1 = (bf16[784,128]{1,0:T(8,128)(2,1)S(1)}, bf16[784,128]{1,0:T(8,128)(2,1)S(1)}, u32[]{:S(2)}, u32[]{:S(2)}) collective-permute-start(bf16[784,128]{1,0:T(8,128)(2,1)S(1)} %get-tuple-element.35), channel_id=1, source_target_pairs={{0,8},{4,12},{8,0},{12,4},{16,24},{20,28},{24,16},{28,20},{1,9},{5... | collective-permute-start | bytes 602120 | tf_op jit(solution)/shard_map/ppermute | solution.py:383
  21.0 9.5 %collective-permute-start.5 = (bf16[384,384]{1,0:T(8,128)(2,1)S(1)}, bf16[384,384]{1,0:T(8,128)(2,1)S(1)}, u32[]{:S(2)}, u32[]{:S(2)}) collective-permute-start(bf16[384,384]{1,0:T(8,128)(2,1)S(1)} %get-tuple-element.44), channel_id=1, source_target_pairs={{0,8},{4,20},{8,0},{12,28},{16,24},{20,4},{24,16},{28,12},{1,9},{5... | collective-permute-start | bytes 884744 | tf_op jit(solution)/shard_map/ppermute | solution.py:194
  22.5 8.4 %collective-permute-start.6 = (bf16[384,384]{1,0:T(8,128)(2,1)S(1)}, bf16[384,384]{1,0:T(8,128)(2,1)S(1)}, u32[]{:S(2)}, u32[]{:S(2)}) collective-permute-start(bf16[384,384]{1,0:T(8,128)(2,1)S(1)} %get-tuple-element.45), channel_id=1, source_target_pairs={{0,8},{4,20},{8,0},{12,28},{16,24},{20,4},{24,16},{28,12},{1,9},{5... | collective-permute-start | bytes 884744 | tf_op jit(solution)/shard_map/ppermute | solution.py:194
  23.0 15.6 %collective-permute-start.9 = (bf16[400,384]{1,0:T(8,128)(2,1)S(1)}, bf16[400,384]{1,0:T(8,128)(2,1)S(1)}, u32[]{:S(2)}, u32[]{:S(2)}) collective-permute-start(bf16[400,384]{1,0:T(8,128)(2,1)S(1)} %get-tuple-element.48), channel_id=1, source_target_pairs={{0,2},{1,3},{2,0},{3,1},{4,6},{5,7},{6,4},{7,5},{8,10},{9,11},{10,... | collective-permute-start | bytes 921608 | tf_op jit(solution)/shard_map/ppermute | solution.py:344
  24.3 5.7 %collective-permute-start.4 = (bf16[384,128]{1,0:T(8,128)(2,1)S(1)}, bf16[384,128]{1,0:T(8,128)(2,1)S(1)}, u32[]{:S(2)}, u32[]{:S(2)}) collective-permute-start(bf16[384,128]{1,0:T(8,128)(2,1)S(1)} %get-tuple-element.41), channel_id=1, source_target_pairs={{0,16},{4,20},{8,24},{12,28},{16,0},{20,4},{24,8},{28,12},{1,17},{... | collective-permute-start | bytes 294920 | tf_op jit(solution)/shard_map/ppermute | solution.py:383
  31.7 24.3 %collective-permute-start.7 = (bf16[768,384]{1,0:T(8,128)(2,1)S(1)}, bf16[768,384]{1,0:T(8,128)(2,1)S(1)}, u32[]{:S(2)}, u32[]{:S(2)}) collective-permute-start(bf16[768,384]{1,0:T(8,128)(2,1)S(1)} %get-tuple-element.61.refs_1_), channel_id=1, source_target_pairs={{0,16},{4,12},{8,24},{12,4},{16,0},{20,28},{24,8},{28,20},{1,17},{... | collective-permute-start | bytes 1769480 | tf_op jit(solution)/shard_map/ppermute | solution.py:194
  34.0 22.0 %collective-permute-start.8 = (bf16[768,384]{1,0:T(8,128)(2,1)S(1)}, bf16[768,384]{1,0:T(8,128)(2,1)S(1)}, u32[]{:S(2)}, u32[]{:S(2)}) collective-permute-start(bf16[768,384]{1,0:T(8,128)(2,1)S(1)} %get-tuple-element.58.refs_2_), channel_id=1, source_target_pairs={{0,16},{4,12},{8,24},{12,4},{16,0},{20,28},{24,8},{28,20},{1,17},{... | collective-permute-start | bytes 1769480 | tf_op jit(solution)/shard_map/ppermute | solution.py:194
  34.5 13.8 %collective-permute-start.11 = (bf16[768,256]{1,0:T(8,128)(2,1)S(1)}, bf16[768,256]{1,0:T(8,128)(2,1)S(1)}, u32[]{:S(2)}, u32[]{:S(2)}) collective-permute-start(bf16[768,256]{1,0:T(8,128)(2,1)S(1)} %shard_map.97.grads_ref.refs_2_), channel_id=1, source_target_pairs={{0,1},{1,2},{2,3},{3,0},{4,5},{5,6},{6,7},{7,4},{8,9},{9,10},{10,1... | collective-permute-start | bytes 1179656 | tf_op jit(solution)/shard_map/ppermute | solution.py:412
  35.8 20.3 %collective-permute-start.12 = (bf16[768,256]{1,0:T(8,128)(2,1)S(1)}, bf16[768,256]{1,0:T(8,128)(2,1)S(1)}, u32[]{:S(2)}, u32[]{:S(2)}) collective-permute-start(bf16[768,256]{1,0:T(8,128)(2,1)S(1)} %shard_map.97.grads_ref.refs_2_), channel_id=1, source_target_pairs={{0,3},{1,0},{2,1},{3,2},{4,7},{5,4},{6,5},{7,6},{8,11},{9,8},{10,9... | collective-permute-start | bytes 1179656 | tf_op jit(solution)/shard_map/ppermute | solution.py:413
  38.7 17.4 %collective-permute-start.10 = (bf16[384,384]{1,0:T(8,128)(2,1)S(1)}, bf16[384,384]{1,0:T(8,128)(2,1)S(1)}, u32[]{:S(2)}, u32[]{:S(2)}) collective-permute-start(bf16[384,384]{1,0:T(8,128)(2,1)S(1)} %shard_map.100), channel_id=1, source_target_pairs={{0,8},{4,20},{8,0},{12,28},{16,24},{20,4},{24,16},{28,12},{1,9},{5... | collective-permute-start | bytes 884744 | tf_op jit(solution)/shard_map/ppermute | solution.py:194
  56.9 5.1 %collective-permute-start.13 = (bf16[1536,384]{1,0:T(8,128)(2,1)}, bf16[1536,384]{1,0:T(8,128)(2,1)}, u32[]{:S(2)}, u32[]{:S(2)}) collective-permute-start(bf16[1536,384]{1,0:T(8,128)(2,1)} %constant_dynamic-update-slice_fusion.4.refs_0_), channel_id=1, source_target_pairs={{0,4},{4,0},{8,12},{12,8},{16,20},{20,16},{24,28},{28,24},{1,5},{5... | collective-permute-start | bytes 3538952 | tf_op jit(solution)/shard_map/ppermute | solution.py:194
  56.9 5.0 %copy-start.5 = (s32[8]{0:T(128)S(1)}, s32[8]{0:T(128)}, u32[]{:S(2)}) copy-start(s32[8]{0:T(128)} %constant.27.clone) | copy-start | bytes 100
  56.9 5.0 %copy-start.6 = (s32[8]{0:T(128)S(1)}, s32[8]{0:T(128)}, u32[]{:S(2)}) copy-start(s32[8]{0:T(128)} %constant.28.clone) | copy-start | bytes 100
  57.8 4.3 %collective-permute-start.14 = (bf16[1536,384]{1,0:T(8,128)(2,1)}, bf16[1536,384]{1,0:T(8,128)(2,1)}, u32[]{:S(2)}, u32[]{:S(2)}) collective-permute-start(bf16[1536,384]{1,0:T(8,128)(2,1)} %constant_dynamic-update-slice_fusion.7.refs_3_), channel_id=1, source_target_pairs={{0,4},{4,0},{8,12},{12,8},{16,20},{20,16},{24,28},{28,24},{1,5},{5... | collective-permute-start | bytes 3538952 | tf_op jit(solution)/shard_map/ppermute | solution.py:194
  58.4 15.4 %collective-permute-start.15 = (bf16[768,384]{1,0:T(8,128)(2,1)S(1)}, bf16[768,384]{1,0:T(8,128)(2,1)S(1)}, u32[]{:S(2)}, u32[]{:S(2)}) collective-permute-start(bf16[768,384]{1,0:T(8,128)(2,1)S(1)} %pad_maximum_fusion.refs_0_), channel_id=1, source_target_pairs={{0,16},{4,12},{8,24},{12,4},{16,0},{20,28},{24,8},{28,20},{1,17},{... | collective-permute-start | bytes 1769480 | tf_op jit(solution)/shard_map/ppermute | solution.py:194
  60.0 6.3 %collective-permute-start.16 = (bf16[768,256]{1,0:T(8,128)(2,1)S(1)}, bf16[768,256]{1,0:T(8,128)(2,1)S(1)}, u32[]{:S(2)}, u32[]{:S(2)}) collective-permute-start(bf16[768,256]{1,0:T(8,128)(2,1)S(1)} %get-tuple-element.50.refs_2_), channel_id=1, source_target_pairs={{1,2},{2,3},{5,6},{6,7},{9,10},{10,11},{13,14},{14,15},{17,18},{18... | collective-permute-start | bytes 1179656 | tf_op jit(solution)/shard_map/ppermute | solution.py:426
  60.7 13.1 %collective-permute-start.17 = (bf16[768,256]{1,0:T(8,128)(2,1)S(1)}, bf16[768,256]{1,0:T(8,128)(2,1)S(1)}, u32[]{:S(2)}, u32[]{:S(2)}) collective-permute-start(bf16[768,256]{1,0:T(8,128)(2,1)S(1)} %get-tuple-element.52.refs_5_), channel_id=1, source_target_pairs={{2,1},{1,0},{6,5},{5,4},{10,9},{9,8},{14,13},{13,12},{18,17},{17,1... | collective-permute-start | bytes 1179656 | tf_op jit(solution)/shard_map/ppermute | solution.py:427
  62.1 11.7 %collective-permute-start.18 = (bf16[768,384]{1,0:T(8,128)(2,1)S(1)}, bf16[768,384]{1,0:T(8,128)(2,1)S(1)}, u32[]{:S(2)}, u32[]{:S(2)}) collective-permute-start(bf16[768,384]{1,0:T(8,128)(2,1)S(1)} %pad_maximum_fusion.refs_0_), channel_id=1, source_target_pairs={{0,4},{4,0},{8,12},{12,8},{16,20},{20,16},{24,28},{28,24},{1,5},{5... | collective-permute-start | bytes 1769480 | tf_op jit(solution)/shard_map/ppermute | solution.py:194
  73.8 2.0 %collective-permute-start.19 = (bf16[768,384]{1,0:T(8,128)(2,1)S(1)}, bf16[768,384]{1,0:T(8,128)(2,1)S(1)}, u32[]{:S(2)}, u32[]{:S(2)}) collective-permute-start(bf16[768,384]{1,0:T(8,128)(2,1)S(1)} %get-tuple-element.54.refs_1_), channel_id=1, source_target_pairs={{0,4},{4,0},{8,12},{12,8},{16,20},{20,16},{24,28},{28,24},{1,5},{5... | collective-permute-start | bytes 1769480 | tf_op jit(solution)/shard_map/ppermute | solution.py:194

commit v5 on v4

--- a/solution.py
+++ b/solution.py
@@ -10,7 +10,9 @@
 F32 = jnp.float32
 BF16 = jnp.bfloat16
 VMEM_BYTES = 16 * 1024 * 1024
-EARLYC = False
+CUT = 592
+HOP = 624
+FAR = 1152
 
 
 def contract(a, b, left, right):
@@ -41,10 +43,6 @@
         in_specs=[pl.BlockSpec(memory_space=pl.ANY)] * (len(passed) + len(tokens)),
         out_specs=[pl.BlockSpec(memory_space=pl.ANY)] * len(passed),
     )
-
-
-def whole(shape):
-    return pl.BlockSpec(shape, lambda *_: (0,) * len(shape))
 
 
 def thirds(x):
@@ -208,18 +206,20 @@
     )
 
 
-def pack_kernel(share, shifts, wq_ref, wk_ref, *refs):
+def pack_kernel(share, plan, wq_ref, wk_ref, *refs):
     count, nseq = lax.axis_size("head"), lax.axis_size("seq")
     mine, my_seq = lax.axis_index("head"), lax.axis_index("seq")
-    outs, sems = refs[: len(shifts)], refs[len(shifts)]
+    odd = lax.rem(my_seq, 2)
+    outs, sems = refs[: len(plan)], refs[len(plan)]
     copies = []
-    for i, shift in enumerate(shifts):
-        block = lax.rem(mine + shift, count) * nseq + my_seq
-        rows = pl.ds(pl.multiple_of(block * share, 16), share)
+    for i, (even_shift, odd_shift, many) in enumerate(plan):
+        shift = even_shift + odd * (odd_shift - even_shift)
+        block = lax.rem(mine + shift, count) * nseq + my_seq // many * many
+        rows = pl.ds(pl.multiple_of(block * share, 16), many * share)
         for j, src in enumerate((wq_ref, wk_ref)):
             copies.append(
                 pltpu.make_async_copy(
-                    src.at[rows, :], outs[i].at[pl.ds(j * share, share), :], sems.at[i, j]
+                    src.at[rows, :], outs[i].at[pl.ds(j * many * share, many * share), :], sems.at[i, j]
                 )
             )
     for copy in copies:
@@ -228,29 +228,72 @@
         copy.wait()
 
 
-def pack_weights(w_query, w_key, shifts, share):
+def pack_weights(w_query, w_key, plan, share, pad=0):
     wide = w_query.shape[1]
     if share % 16:
         count, nseq = lax.axis_size("head"), lax.axis_size("seq")
-        blocks = [(lax.axis_index("head") + k) % count * nseq + lax.axis_index("seq") for k in shifts]
-        return [
-            jnp.concatenate(
-                [lax.dynamic_slice_in_dim(w, block * share, share, 0) for w in (w_query, w_key)]
+        mine, my_seq = lax.axis_index("head"), lax.axis_index("seq")
+        out = []
+        for even_shift, odd_shift, many in plan:
+            shift = jnp.where(my_seq % 2 == 1, odd_shift, even_shift)
+            start = ((mine + shift) % count * nseq + my_seq // many * many) * share
+            out.append(
+                jnp.concatenate(
+                    [lax.dynamic_slice_in_dim(w, start, many * share, 0) for w in (w_query, w_key)]
+                )
             )
-            for block in blocks
-        ]
+        return out
+    heights = [2 * many * share for _, _, many in plan]
+    heights[-1] += pad
     return call(
-        functools.partial(pack_kernel, share, shifts),
-        [
-            jax.ShapeDtypeStruct((2 * share + (16 if i == 2 else 0), wide), BF16)
-            for i in range(len(shifts))
-        ],
-        0, len(shifts) * share * wide * 8,
+        functools.partial(pack_kernel, share, tuple(plan)),
+        [jax.ShapeDtypeStruct((height, wide), BF16) for height in heights],
+        0, sum(heights) * wide * 4,
         *(pltpu.with_memory_space_constraint(w, pltpu.HBM) for w in (w_query, w_key)),
         in_specs=[pl.BlockSpec(memory_space=pl.ANY)] * 2,
-        out_specs=[pl.BlockSpec(memory_space=pltpu.VMEM)] * len(shifts),
-        scratch_shapes=[pltpu.SemaphoreType.DMA((len(shifts), 2))],
-    )
+        out_specs=[pl.BlockSpec(memory_space=pltpu.VMEM)] * len(plan),
+        scratch_shapes=[pltpu.SemaphoreType.DMA((len(plan), 2))],
+    )
+
+
+def join_kernel(groups, nargs, *refs):
+    for group, out_ref in zip(groups, refs[-len(groups) :]):
+        at = 0
+        for i, start, size in group:
+            out_ref[at : at + size, :] = refs[i][start : start + size, :]
+            at += size
+
+
+def join(*groups, tokens=()):
+    args, spec = [], []
+    for group in groups:
+        spec.append(tuple((place_in(args, x), start, size) for x, start, size in group))
+    return call(
+        functools.partial(join_kernel, tuple(spec), len(args)),
+        [jax.ShapeDtypeStruct((sum(size for _, _, size in group), args[0].shape[1]), BF16) for group in spec],
+        0, 0, *args, *tokens,
+        in_specs=[pl.BlockSpec(memory_space=pltpu.VMEM)] * len(args)
+        + [pl.BlockSpec(memory_space=pl.ANY)] * len(tokens),
+        out_specs=[pl.BlockSpec(memory_space=pltpu.VMEM)] * len(groups),
+    )
+
+
+def place_in(args, x):
+    for i, y in enumerate(args):
+        if y is x:
+            return i
+    args.append(x)
+    return len(args) - 1
+
+
+def rows_of(refs, low, high):
+    parts, at = [], 0
+    for ref in refs:
+        first, last = max(low, at), min(high, at + ref.shape[0])
+        if first < last:
+            parts.append(ref[first - at : last - at, :])
+        at += ref.shape[0]
+    return parts[0] if len(parts) == 1 else jnp.concatenate(parts)
 
 
 def row_block(weights, grads):
@@ -286,40 +329,115 @@
     )
 
 
-def add_kernel(counts, last, table_ref, total_ref, *refs):
-    out_ref, refs = refs[-1], list(refs[:-1])
-    groups = []
-    for nblocks, nother in counts:
-        blocks, refs = refs[:nblocks], refs[nblocks:]
-        others, refs = refs[:nother], refs[nother:]
-        grads = others[0][...]
-        if nother == 2:
-            grads = jnp.where(table_ref[0] == 1, others[1][...], grads)
-        groups.append((blocks, grads))
-    share = groups[0][0][0].shape[0]
-    nshares = table_ref.shape[0] - 1
+def relay_kernel(own_ref, lower_ref, upper_ref, token_ref, relay_ref, kept_ref, sent_ref):
+    mine, odd = lax.axis_index("head"), lax.rem(lax.axis_index("seq"), 2)
+
+    @pl.when(mine == 1)
+    def _():
+        relay_ref[...] = upper_ref[...]
+
+    @pl.when(mine == 2)
+    def _():
+        relay_ref[...] = lower_ref[...]
+
+    @pl.when((mine != 1) & (mine != 2))
+    def _():
+        relay_ref[...] = own_ref[...]
+
+    @pl.when(odd == 0)
+    def _():
+        kept_ref[...] = lower_ref[...]
+        sent_ref[...] = upper_ref[...]
+
+    @pl.when(odd == 1)
+    def _():
+        kept_ref[...] = upper_ref[...]
+        sent_ref[...] = lower_ref[...]
+
+
+def split_kernel(both_ref, token_ref, theirs_ref):
+    odd = lax.rem(lax.axis_index("seq"), 2)
+    share = theirs_ref.shape[0] // 2
+    for parity in range(2):
+
+        @pl.when(odd == parity)
+        def _():
+            for j in range(2):
+                at = (2 * j + 1 - parity) * share
+                theirs_ref[j * share : (j + 1) * share, :] = both_ref[at : at + share, :]
+
+
+def pick_kernel(both_ref, got_ref, out_ref):
+    odd = lax.rem(lax.axis_index("seq"), 2)
+    upper = lax.axis_index("head") // 2
+    share = out_ref.shape[0] // 2
+
+    @pl.when(odd + upper != 1)
+    def _():
+        out_ref[...] = got_ref[...]
+
+    for parity in range(2):
+
+        @pl.when((odd == parity) & (upper == 1 - parity))
+        def _():
+            for j in range(2):
+                at = (2 * j + parity) * share
+                out_ref[j * share : (j + 1) * share, :] = both_ref[at : at + share, :]
+
+
+def pair_kernel(table_ref, total_ref, *refs):
+    weights, (kept_ref, got_ref, out_ref, sent_ref) = refs[:-4], refs[-4:]
+    nblocks = table_ref.shape[0]
+    size = out_ref.shape[0] // nblocks
+    for j in range(nblocks):
+        block = rows_of(weights, 2 * size * j, 2 * size * (j + 1))
+        rows = pl.ds(pl.multiple_of(table_ref[j] * size, 16), size)
+        out_ref[rows, :] = total_ref[rows, :] + row_block(block, kept_ref[...])
+        sent_ref[rows, :] = row_block(block, got_ref[...]).astype(BF16)
+
+
+def pair_product(table, total, weights, kept, got):
+    chunk, span = total.shape
+    return call(
+        pair_kernel,
+        (jax.ShapeDtypeStruct((chunk, span), F32), jax.ShapeDtypeStruct((chunk, span), BF16)),
+        4 * chunk * span * kept.shape[0], chunk * span * 10,
+        table, total, *weights, kept, got,
+        in_specs=[pl.BlockSpec(memory_space=pltpu.SMEM)]
+        + [pl.BlockSpec(memory_space=pltpu.VMEM)] * (3 + len(weights)),
+        out_specs=[pl.BlockSpec(memory_space=pltpu.VMEM)] * 2,
+        vmem=24 * 1024 * 1024,
+    )
+
+
+def add_kernel(terms, plus, table_ref, total_ref, *refs):
+    args, out_ref = refs[:-1], refs[-1]
+    nshares = table_ref.shape[0]
     share = out_ref.shape[0] // nshares
     for j in range(nshares):
-        rows = pl.ds(pl.multiple_of(table_ref[1 + j] * share, 8), share)
+        rows = pl.ds(pl.multiple_of(table_ref[j] * share, 8), share)
         total = total_ref[rows, :]
-        for blocks, grads in groups:
-            at = 2 * share * j
-            for block in blocks:
-                if at < block.shape[0]:
-                    total = total + row_block(block[at : at + 2 * share], grads)
-                    break
-                at -= block.shape[0]
+        if plus is not None:
+            total = total + args[plus][rows, :].astype(F32)
+        for blocks, grads in terms:
+            weights = rows_of([args[i] for i in blocks], 2 * share * j, 2 * share * (j + 1))
+            total = total + row_block(weights, args[grads][...])
         out_ref[rows, :] = total.astype(out_ref.dtype)
 
 
-def add_product(table, total, terms, last):
+def add_product(table, total, terms, last, plus=None):
     chunk, span = total.shape
-    counts = tuple((len(blocks), len(others)) for blocks, others in terms)
-    args = [x for blocks, others in terms for x in (*blocks, *others)]
+    args = []
+
+    spec = tuple(
+        (tuple(place_in(args, x) for x in blocks), place_in(args, grads))
+        for blocks, grads in terms
+    )
+    plus = None if plus is None else place_in(args, plus)
     return call(
-        functools.partial(add_kernel, counts, last),
+        functools.partial(add_kernel, spec, plus),
         jax.ShapeDtypeStruct((chunk, span), BF16 if last else F32),
-        2 * len(terms) * chunk * span * args[-1].shape[0], chunk * span * 8,
+        2 * len(terms) * chunk * span * terms[0][1].shape[0], chunk * span * 8,
         table, total, *args,
         in_specs=[pl.BlockSpec(memory_space=pltpu.SMEM)]
         + [pl.BlockSpec(memory_space=pltpu.VMEM)] * (1 + len(args)),
@@ -340,8 +458,21 @@
 
     shifts = [1, nhead - 1] + list(range(2, nhead - 1))
     ring = {k: [(i, (i + k) % nhead) for i in range(nhead)] for k in shifts}
-    packed = pack_weights(w_query, w_key, shifts, share)
-    pieces = [lax.ppermute(p, "head", ring[k])[: 2 * share] for p, k in zip(packed, shifts)]
+    fast = nhead == 4 and nseq == 8
+    if fast:
+        packed = pack_weights(w_query, w_key, [(1, 3, 2), (2, 2, 2)], share)
+
+        def moves(even, odd):
+            return [
+                (i * nhead + j, i * nhead + k) for i in range(nseq) for j, k in (odd if i % 2 else even)
+            ]
+
+        axes = ("seq", "head")
+        first = lax.ppermute(packed[0], axes, moves(ring[1], ring[3]))
+        passing = lax.ppermute(packed[1], axes, moves([(0, 1), (1, 2)], [(3, 2), (2, 1)]))
+    else:
+        packed = pack_weights(w_query, w_key, [(k, k, 1) for k in shifts], share)
+        pieces = [lax.ppermute(p, "head", ring[k]) for p, k in zip(packed, shifts)]
 
     decay = log_decay.T
     sent, held, logs = call(
@@ -355,17 +486,6 @@
         decay, query_act, key_act, value_act, grad_output, packed[0],
         in_specs=[pl.BlockSpec(memory_space=pltpu.VMEM)] * 5 + [pl.BlockSpec(memory_space=pl.ANY)],
     )
-    nhops = len(share_order(nseq)[0]) + 1
-    holds = [[p] for p in pieces]
-    progress = [0] * len(pieces)
-
-    def advance(which):
-        for i in which:
-            if progress[i] < nhops:
-                held = holds[i][0] if progress[i] == 0 else jnp.concatenate(holds[i])
-                holds[i] = [held, share_hop(held, progress[i])]
-                progress[i] += 1
-
     local = call(
         functools.partial(local_kernel, nheads, width),
         jax.ShapeDtypeStruct((2 * rows, span), F32),
@@ -374,12 +494,6 @@
     )
     hop, enter = 1, None
     while True:
-        if 2 * hop >= nseq:
-            early = range(min(2, len(holds)))
-            sent, *firsts = gate([sent] + [holds[i][0] for i in early], [local])
-            for i in early:
-                holds[i][0] = firsts[i]
-            advance(early)
         got = lax.ppermute(sent, "seq", [(i, i ^ hop) for i in range(nseq)])
         if 2 * hop >= nseq:
             break
@@ -405,38 +519,68 @@
 
     even, odd = share_deltas(nseq)
     deltas = jnp.where(my_seq % 2 == 1, jnp.array(odd, jnp.int32), jnp.array(even, jnp.int32))
-    table = jnp.concatenate([(my_head >= 2).astype(jnp.int32)[None], deltas ^ my_seq])
+    table = deltas ^ my_seq
     total = own_product(w_query, w_key, both, chunk)
 
-    if nhead == 4 and nhops == 3:
+    if fast:
         p1 = lax.ppermute(both, "head", ring[1])
         p3 = lax.ppermute(both, "head", ring[3])
-        if EARLYC:
-            holds[0][1], holds[1][1], holds[2][0] = gate([holds[0][1], holds[1][1], holds[2][0]], [both])
-        else:
-            holds[0][1], holds[1][1] = gate([holds[0][1], holds[1][1]], [both])
-        advance([0, 1])
-        if not EARLYC:
-            (holds[2][0],) = gate([holds[2][0]], [holds[0][0], holds[1][0]])
-        advance([2])
-        holds[0][1], holds[1][1], holds[2][1], p1, p3 = gate(
-            [holds[0][1], holds[1][1], holds[2][1], p1, p3], [total]
-        )
-        advance([0, 1, 2])
-        up = lax.ppermute(p1, "head", [(1, 2), (2, 3)])
-        down = lax.ppermute(p3, "head", [(2, 1), (1, 0)])
-        total = add_product(table, total, [(holds[0], (p1,)), (holds[1], (p3,))], False)
-        holds[2][1], up, down = gate([holds[2][1], up, down], [total])
-        near, far = holds[2]
-        blocks = [near, far] + [share_hop(x, 2) for x in (near, far)]
-        return add_product(table, total, [(blocks, (down, up))], True)
+        one, two, cut = 2 * share, 4 * share, CUT
+        (first,) = gate([first], [both])
+        second = share_hop(first, 0)
+        sent = join(
+            ((first, 0, two), (second, 0, FAR - two)), ((second, FAR - two, 2 * two - FAR),),
+        )
+        blocks = [first, second] + [share_hop(x, 1) for x in sent]
+        (passing,) = gate([passing], [first])
+        passing = lax.ppermute(passing, axes, moves([(1, 2), (2, 3)], [(2, 1), (1, 0)]))
+        theirs = call(
+            split_kernel, jax.ShapeDtypeStruct((one, passing.shape[1]), BF16), 0, 0, passing, total,
+            in_specs=[pl.BlockSpec(memory_space=pltpu.VMEM), pl.BlockSpec(memory_space=pl.ANY)],
+            out_specs=pl.BlockSpec(memory_space=pltpu.VMEM),
+        )
+        theirs = lax.ppermute(
+            theirs, axes,
+            [(i * nhead + j, (i ^ 1) * nhead + j) for i in range(nseq) for j in range(nhead) if (j < 2) == (i % 2)],
+        )
+        third = call(
+            pick_kernel, jax.ShapeDtypeStruct(theirs.shape, BF16), 0, 0, passing, theirs,
+            in_specs=[pl.BlockSpec(memory_space=pltpu.VMEM)] * 2,
+            out_specs=pl.BlockSpec(memory_space=pltpu.VMEM),
+        )
+        fourth = share_hop(third, 0)
+        near, head_rows, tail_rows = join(
+            ((third, 0, one), (fourth, 0, one)),
+            ((third, 0, one), (fourth, 0, cut - one)),
+            ((fourth, cut - one, two - cut),),
+        )
+        far = [share_hop(x, 1) for x in (head_rows, tail_rows)]
+        relay, kept, handed = call(
+            relay_kernel, [jax.ShapeDtypeStruct(both.shape, BF16)] * 3, 0, 0, both, p1, p3, total,
+            in_specs=[pl.BlockSpec(memory_space=pltpu.VMEM)] * 3 + [pl.BlockSpec(memory_space=pl.ANY)],
+            out_specs=[pl.BlockSpec(memory_space=pltpu.VMEM)] * 3,
+        )
+        p2 = lax.ppermute(relay, "head", [(0, 2), (1, 0), (2, 3), (3, 1)])
+        got = share_hop(handed, 2)
+        total, handed = pair_product(table[: nseq // 2] // 2, total, blocks, kept, got)
+        got = share_hop(handed, 2)
+        far, far_head, far_tail = join(
+            ((far[0], 0, cut), (far[1], 0, two - cut)),
+            ((far[0], 0, cut), (far[1], 0, HOP - cut)),
+            ((far[1], HOP - cut, two - HOP),),
+            tokens=[p2, total],
+        )
+        term = (near, far, *(share_hop(x, 2) for x in (near, far_head, far_tail)))
+        return add_product(table, total, [(term, p2)], True, got)
 
     gathered = lax.all_gather(both, "head")
-    while min(progress) < nhops:
-        advance(range(len(pieces)))
     for i, k in enumerate(shifts):
+        held = [pieces[i]]
+        for number in range(len(share_order(nseq)[0]) + 1):
+            whole = held[0] if number == 0 else jnp.concatenate(held)
+            held = [whole, share_hop(whole, number)]
         grads = gathered[(my_head + nhead - k) % nhead]
-        total = add_product(table, total, [(holds[i], (grads,))], i == nhead - 2)
+        total = add_product(table, total, [(held, grads)], i == nhead - 2)
     return total
 
 

time: 78.4 us -> 74.9 us (0.955)
  waiting for transfers between devices: 36.3 us -> 30.3 us
  starting transfers between devices: 23.3 us -> 27.2 us
  local copies, waits for them, and re-layouts: 4.5 us -> 0.74 us
  Pallas kernels: 13.8 us -> 16.1 us
    ppermute x5, waiting for transfers between devices: 13.1 us -> 5.07 us  [the longest x1 2.89 us: shards(): p2 = lax.ppermute(relay, 'head', [(0, 2), (1, 0), (2, 3), (3, 1)])]
    ppermute x10 -> x11, waiting for transfers between devices: 2.39 us -> 9.23 us  [share_hop(): return lax.ppermute(held, 'seq', pairs)]
    ppermute x1, waiting for transfers between devices: 7.72 us -> 2.15 us  [shards(): p3 = lax.ppermute(both, 'head', ring[3])]
    ppermute x5, starting transfers between devices: 8.01 us -> 12.3 us  [the longest x1 3.71 us: shards(): p2 = lax.ppermute(relay, 'head', [(0, 2), (1, 0), (2, 3), (3, 1)])]
    concatenate x3 -> x0, local copies, waits for them, and re-layouts: 2.55 us -> none  [advance(): held = holds[i][0] if progress[i] == 0 else jnp.concatenate(holds[i])]
    pallas_call x14 -> x17, Pallas kernels: 13.8 us -> 16.1 us  [call(): pl.pallas_call(kernel, out_shape=out_shape, cost_estimate=pl.CostEstimate...]
    ppermute x1, starting transfers between devices: 2.6 us -> 0.49 us  [shards(): p3 = lax.ppermute(both, 'head', ring[3])]
    ppermute x10 -> x11, starting transfers between devices: 7.72 us -> 9.72 us  [share_hop(): return lax.ppermute(held, 'seq', pairs)]
  transfers between devices with their start and end apart: 20 -> 21, of which waited for: 9 -> 9; matrix products, arithmetic and copies ran while one was open for 5% -> 0% of each run, Pallas kernels for 12% -> 17%
where the time goes in v5:
time: 74.9 us; the launch traced here: 74.6 us
  waiting for transfers between devices  30.3 us (40%)
  starting transfers between devices  27.2 us (36%)
  Pallas kernels  16.1 us (21%)
    pallas_call x17, Pallas kernels, call(): pl.pallas_call(kernel, out_shape=out_shape, cost_estimate=pl.CostEstimate...  16.1 us
    ppermute x11, starting transfers between devices, share_hop(): return lax.ppermute(held, 'seq', pairs)  9.72 us
    ppermute x11, waiting for transfers between devices, share_hop(): return lax.ppermute(held, 'seq', pairs)  9.23 us
    ppermute x3, waiting for transfers between devices, shards(): got = lax.ppermute(sent, 'seq', [(i, i ^ hop) for i in range(nseq)])  9.03 us
    ppermute x1, waiting for transfers between devices, shards(): p1 = lax.ppermute(both, 'head', ring[1])  4.79 us
    ppermute x1, starting transfers between devices, shards(): p2 = lax.ppermute(relay, 'head', [(0, 2), (1, 0), (2, 3), (3, 1)])  3.71 us
    ppermute x1, starting transfers between devices, shards(): lax.ppermute(packed[1], axes, moves([(0, 1), (1, 2)], [(3, 2), (2, 1)]))  3.51 us
    ppermute x3, starting transfers between devices, shards(): got = lax.ppermute(sent, 'seq', [(i, i ^ hop) for i in range(nseq)])  3.15 us
  transfers between devices with their start and end apart: 21, of which 9 were waited for; matrix products, arithmetic and copies ran while one was open for 0% of the time, Pallas kernels for 17%

profile of v5, /device:TPU:0, one launch (start us, length us, event | category | flops | bytes accessed | tf_op | source)
XLA Modules:
  0.0 74.6 jit_solution(17415122731424899191)
XLA Ops:
  0.0 1.4 %shard_map.91 = (bf16[768,384]{1,0:T(8,128)(2,1)S(1)}, bf16[768,384]{1,0:T(8,128)(2,1)S(1)}) custom-call(bf16[6144,384]{1,0:T(8,128)(2,1)} %wq_ref.3, bf16[6144,384]{1,0:T(8,128)(2,1)} %wk_ref.3), custom_call_target="tpu_custom_call" | custom-call | bytes 2359296 | tf_op jit(solution)/shard_map/pallas_call | solution.py:23
  1.4 3.1 %collective-permute-start.3 = (bf16[768,384]{1,0:T(8,128)(2,1)S(1)}, bf16[768,384]{1,0:T(8,128)(2,1)S(1)}, u32[]{:S(2)}, u32[]{:S(2)}) collective-permute-start(bf16[768,384]{1,0:T(8,128)(2,1)S(1)} %get-tuple-element.30.token_ref), channel_id=1, source_target_pairs={{0,1},{1,2},{2,3},{3,0},{4,7},{5,4},{6,5},{7,6},{8,9},{9,10},{10,1... | collective-permute-start | bytes 1769480 | tf_op jit(solution)/shard_map/ppermute | solution.py:471
  4.5 3.5 %collective-permute-start.10 = (bf16[768,384]{1,0:T(8,128)(2,1)S(1)}, bf16[768,384]{1,0:T(8,128)(2,1)S(1)}, u32[]{:S(2)}, u32[]{:S(2)}) collective-permute-start(bf16[768,384]{1,0:T(8,128)(2,1)S(1)} %get-tuple-element.46), channel_id=1, source_target_pairs={{0,1},{1,2},{7,6},{6,5},{8,9},{9,10},{15,14},{14,13},{16,17},{17,1... | collective-permute-start | bytes 1769480 | tf_op jit(solution)/shard_map/ppermute | solution.py:472
  8.0 0.0 copy-done.1
  8.0 0.0 copy-done
  8.0 0.0 copy-done.3
  8.0 0.0 copy-done.2
  8.0 0.0 copy-done.4
  8.0 0.9 %shard_map.92 = (bf16[784,128]{1,0:T(8,128)(2,1)S(1)}, f32[768,128]{1,0:T(8,128)S(1)}, f32[24,128]{1,0:T(8,128)S(1)}) custom-call(f32[3,256]{1,0:T(4,128)S(1)} %bitcast.1, bf16[256,384]{1,0:T(8,128)(2,1)S(1)} %copy-done.2, bf16[256,384]{1,0:T(8,128)(2,1)S(1)} %copy-done.3, bf16[256,384]{1,0:T(8,128)(2,1)S(1)} %copy-done, bf16[256,384]{1,0:T(8,128)(2,1)S(1)} %copy-done.1, ...), custom_call_target="tpu_custom_call" | custom-call | flops 50331648 | bytes 786432 | tf_op jit(solution)/shard_map/pallas_call | solution.py:23
  8.9 0.1 collective-permute-start
  9.0 1.4 %collective-permute-done.got_ref = bf16[784,128]{1,0:T(8,128)(2,1)S(1)} collective-permute-done((bf16[784,128]{1,0:T(8,128)(2,1)S(1)}, bf16[784,128]{1,0:T(8,128)(2,1)S(1)}, u32[]{:S(2)}, u32[]{:S(2)}) %collective-permute-start) | collective-permute-done | bytes 200736 | tf_op jit(solution)/shard_map/ppermute | solution.py:497
  10.4 0.1 shard_map.93
  10.5 1.6 %collective-permute-start.1 = (bf16[784,128]{1,0:T(8,128)(2,1)S(1)}, bf16[784,128]{1,0:T(8,128)(2,1)S(1)}, u32[]{:S(2)}, u32[]{:S(2)}) collective-permute-start(bf16[784,128]{1,0:T(8,128)(2,1)S(1)} %get-tuple-element.34), channel_id=1, source_target_pairs={{0,8},{4,12},{8,0},{12,4},{16,24},{20,28},{24,16},{28,20},{1,9},{5... | collective-permute-start | bytes 602120 | tf_op jit(solution)/shard_map/ppermute | solution.py:497
  12.1 5.5 %collective-permute-done.1.got_ref = bf16[784,128]{1,0:T(8,128)(2,1)S(1)} collective-permute-done((bf16[784,128]{1,0:T(8,128)(2,1)S(1)}, bf16[784,128]{1,0:T(8,128)(2,1)S(1)}, u32[]{:S(2)}, u32[]{:S(2)}) %collective-permute-start.1) | collective-permute-done | bytes 200736 | tf_op jit(solution)/shard_map/ppermute | solution.py:497
  17.6 0.8 %shard_map.94 = (bf16[384,128]{1,0:T(8,128)(2,1)S(1)}, f32[768,128]{1,0:T(8,128)}, f32[24,128]{1,0:T(8,128)S(1)}, f32[768,128]{1,0:T(8,128)S(1)}) custom-call(bf16[784,128]{1,0:T(8,128)(2,1)S(1)} %collective-permute-done.1.got_ref, f32[768,128]{1,0:T(8,128)S(1)} %get-tuple-element.35.held_ref, f32[24,128]{1,0:T(8,128)S(1)} %get-tuple-element.36.logs_ref, ...), custom_call_target="tpu_custom_call" | custom-call | flops 491520 | bytes 786432 | tf_op jit(solution)/shard_map/pallas_call | solution.py:23
  18.4 1.5 %collective-permute-start.2 = (bf16[384,128]{1,0:T(8,128)(2,1)S(1)}, bf16[384,128]{1,0:T(8,128)(2,1)S(1)}, u32[]{:S(2)}, u32[]{:S(2)}) collective-permute-start(bf16[384,128]{1,0:T(8,128)(2,1)S(1)} %get-tuple-element.38), channel_id=1, source_target_pairs={{0,16},{4,20},{8,24},{12,28},{16,0},{20,4},{24,8},{28,12},{1,17},{... | collective-permute-start | bytes 294920 | tf_op jit(solution)/shard_map/ppermute | solution.py:497
  20.0 1.0 %shard_map.95.local_ref = f32[768,256]{1,0:T(8,128)S(1)} custom-call(f32[3,256]{1,0:T(4,128)S(1)} %bitcast.2, bf16[256,384]{1,0:T(8,128)(2,1)S(1)} %copy-done.2, bf16[256,384]{1,0:T(8,128)(2,1)S(1)} %copy-done.3, bf16[256,384]{1,0:T(8,128)(2,1)S(1)} %copy-done, bf16[256,384]{1,0:T(8,128)(2,1)S(1)} %copy-done.1), custom_call_target="tpu_custom_call" | custom-call | flops 150994944 | bytes 1572864 | tf_op jit(solution)/shard_map/pallas_call | solution.py:23
  21.0 2.1 %collective-permute-done.2.got_ref = bf16[384,128]{1,0:T(8,128)(2,1)S(1)} collective-permute-done((bf16[384,128]{1,0:T(8,128)(2,1)S(1)}, bf16[384,128]{1,0:T(8,128)(2,1)S(1)}, u32[]{:S(2)}, u32[]{:S(2)}) %collective-permute-start.2) | collective-permute-done | bytes 98336 | tf_op jit(solution)/shard_map/ppermute | solution.py:497
  23.1 0.4 shard_map.96.grads_ref.refs_1_.own_ref
  23.5 0.0 collective-permute-done.3.refs_0_
  23.5 1.6 %collective-permute-start.4 = (bf16[768,384]{1,0:T(8,128)(2,1)S(1)}, bf16[768,384]{1,0:T(8,128)(2,1)S(1)}, u32[]{:S(2)}, u32[]{:S(2)}) collective-permute-start(bf16[768,384]{1,0:T(8,128)(2,1)S(1)} %shard_map.98.refs_0_.refs_1_), channel_id=1, source_target_pairs={{0,8},{4,20},{8,0},{12,28},{16,24},{20,4},{24,16},{28,12},{1,9},{5... | collective-permute-start | bytes 1769480 | tf_op jit(solution)/shard_map/ppermute | solution.py:192
  25.1 0.0 collective-permute-done.10.refs_0_
  25.1 0.7 collective-permute-start.11
  25.8 7.7 %collective-permute-done.4.refs_1_ = bf16[768,384]{1,0:T(8,128)(2,1)S(1)} collective-permute-done((bf16[768,384]{1,0:T(8,128)(2,1)S(1)}, bf16[768,384]{1,0:T(8,128)(2,1)S(1)}, u32[]{:S(2)}, u32[]{:S(2)}) %collective-permute-start.4) | collective-permute-done | bytes 589856 | tf_op jit(solution)/shard_map/ppermute | solution.py:192
  33.5 1.0 %shard_map.99 = (bf16[1152,384]{1,0:T(8,128)(2,1)}, bf16[384,384]{1,0:T(8,128)(2,1)S(1)}) custom-call(bf16[768,384]{1,0:T(8,128)(2,1)S(1)} %shard_map.98.refs_0_.refs_1_, bf16[768,384]{1,0:T(8,128)(2,1)S(1)} %collective-permute-done.4.refs_1_), custom_call_target="tpu_custom_call" | custom-call | tf_op jit(solution)/shard_map/pallas_call | solution.py:23
  34.5 0.7 copy-done.5
  35.2 1.5 %collective-permute-start.5 = (bf16[1152,384]{1,0:T(8,128)(2,1)}, bf16[1152,384]{1,0:T(8,128)(2,1)}, u32[]{:S(2)}, u32[]{:S(2)}) collective-permute-start(bf16[1152,384]{1,0:T(8,128)(2,1)} %get-tuple-element.41), channel_id=1, source_target_pairs={{0,16},{4,12},{8,24},{12,4},{16,0},{20,28},{24,8},{28,20},{1,17},{... | collective-permute-start | bytes 2654216 | tf_op jit(solution)/shard_map/ppermute | solution.py:192
  36.7 0.5 collective-permute-start.8
  37.2 1.5 %collective-permute-start.7 = (bf16[768,256]{1,0:T(8,128)(2,1)S(1)}, bf16[768,256]{1,0:T(8,128)(2,1)}, u32[]{:S(2)}, u32[]{:S(2)}) collective-permute-start(bf16[768,256]{1,0:T(8,128)(2,1)S(1)} %shard_map.96.grads_ref.refs_1_.own_ref), channel_id=1, source_target_pairs={{0,1},{1,2},{2,3},{3,0},{4,5},{5,6},{6,7},{7,4},{8,9},{9,10},{10,1... | collective-permute-start | bytes 1179656 | tf_op jit(solution)/shard_map/ppermute | solution.py:526
  38.8 2.6 %shard_map.97.token_ref.total_ref = f32[1536,256]{1,0:T(8,128)S(1)} custom-call(bf16[6144,384]{1,0:T(8,128)(2,1)} %wq_ref.3, bf16[6144,384]{1,0:T(8,128)(2,1)} %wk_ref.3, bf16[768,256]{1,0:T(8,128)(2,1)S(1)} %shard_map.96.grads_ref.refs_1_.own_ref), custom_call_target="tpu_custom_call" | custom-call | flops 603979776 | bytes 2359296 | tf_op jit(solution)/shard_map/pallas_call | solution.py:23
  41.4 0.0 copy-start.6
  41.4 0.0 copy-start.7
  41.4 0.0 collective-permute-done.11.both_ref
  41.5 1.3 %collective-permute-start.12 = (bf16[384,384]{1,0:T(8,128)(2,1)S(1)}, bf16[384,384]{1,0:T(8,128)(2,1)S(1)}, u32[]{:S(2)}, u32[]{:S(2)}) collective-permute-start(bf16[384,384]{1,0:T(8,128)(2,1)S(1)} %shard_map.103), channel_id=1, source_target_pairs={{2,6},{3,7},{4,0},{5,1},{10,14},{11,15},{12,8},{13,9},{18,22},{19,... | collective-permute-start | bytes 884744 | tf_op jit(solution)/shard_map/ppermute | solution.py:542
  42.8 2.2 %collective-permute-done.12.got_ref = bf16[384,384]{1,0:T(8,128)(2,1)S(1)} collective-permute-done((bf16[384,384]{1,0:T(8,128)(2,1)S(1)}, bf16[384,384]{1,0:T(8,128)(2,1)S(1)}, u32[]{:S(2)}, u32[]{:S(2)}) %collective-permute-start.12) | collective-permute-done | bytes 294944 | tf_op jit(solution)/shard_map/ppermute | solution.py:542
  45.0 1.6 %collective-permute-start.13 = (bf16[384,384]{1,0:T(8,128)(2,1)S(1)}, bf16[384,384]{1,0:T(8,128)(2,1)}, u32[]{:S(2)}, u32[]{:S(2)}) collective-permute-start(bf16[384,384]{1,0:T(8,128)(2,1)S(1)} %shard_map.104.refs_0_), channel_id=1, source_target_pairs={{0,8},{4,20},{8,0},{12,28},{16,24},{20,4},{24,16},{28,12},{1,9},{5... | collective-permute-start | bytes 884744 | tf_op jit(solution)/shard_map/ppermute | solution.py:192
  46.6 2.2 %collective-permute-done.8.upper_ref = bf16[768,256]{1,0:T(8,128)(2,1)} collective-permute-done((bf16[768,256]{1,0:T(8,128)(2,1)S(1)}, bf16[768,256]{1,0:T(8,128)(2,1)}, u32[]{:S(2)}, u32[]{:S(2)}) %collective-permute-start.8) | collective-permute-done | bytes 393248 | tf_op jit(solution)/shard_map/ppermute | solution.py:527
  48.7 4.8 %collective-permute-done.7.lower_ref = bf16[768,256]{1,0:T(8,128)(2,1)} collective-permute-done((bf16[768,256]{1,0:T(8,128)(2,1)S(1)}, bf16[768,256]{1,0:T(8,128)(2,1)}, u32[]{:S(2)}, u32[]{:S(2)}) %collective-permute-start.7) | collective-permute-done | bytes 393248 | tf_op jit(solution)/shard_map/ppermute | solution.py:526
  53.5 1.2 %shard_map.100 = (bf16[768,256]{1,0:T(8,128)(2,1)S(1)}, bf16[768,256]{1,0:T(8,128)(2,1)S(1)}, bf16[768,256]{1,0:T(8,128)(2,1)S(1)}) custom-call(bf16[768,256]{1,0:T(8,128)(2,1)S(1)} %shard_map.96.grads_ref.refs_1_.own_ref, bf16[768,256]{1,0:T(8,128)(2,1)} %collective-permute-done.7.lower_ref, bf16[768,256]{1,0:T(8,128)(2,1)} %collective-permute-done.8.upper_ref, ...), custom_call_target="tpu_custom_call" | custom-call | tf_op jit(solution)/shard_map/pallas_call | solution.py:23
  54.7 0.1 collective-permute-start.9
  54.8 1.6 %collective-permute-start.6 = (bf16[384,384]{1,0:T(8,128)(2,1)}, bf16[384,384]{1,0:T(8,128)(2,1)S(1)}, u32[]{:S(2)}, u32[]{:S(2)}) collective-permute-start(bf16[384,384]{1,0:T(8,128)(2,1)} %copy-done.5), channel_id=1, source_target_pairs={{0,16},{4,12},{8,24},{12,4},{16,0},{20,28},{24,8},{28,20},{1,17},{... | collective-permute-start | bytes 884744 | tf_op jit(solution)/shard_map/ppermute | solution.py:192
  56.4 0.0 copy-done.6
  56.4 0.0 collective-permute-done.13.refs_1_
  56.4 1.1 %shard_map.105 = (bf16[768,384]{1,0:T(8,128)(2,1)S(1)}, bf16[592,384]{1,0:T(8,128)(2,1)S(1)}, bf16[176,384]{1,0:T(8,128)(2,1)S(1)}) custom-call(bf16[384,384]{1,0:T(8,128)(2,1)S(1)} %shard_map.104.refs_0_, bf16[384,384]{1,0:T(8,128)(2,1)} %collective-permute-done.13.refs_1_), custom_call_target="tpu_custom_call" | custom-call | tf_op jit(solution)/shard_map/pallas_call | solution.py:23
  57.5 0.6 collective-permute-start.14
  58.0 3.7 %collective-permute-start.16 = (bf16[768,256]{1,0:T(8,128)(2,1)S(1)}, bf16[768,256]{1,0:T(8,128)(2,1)S(1)}, u32[]{:S(2)}, u32[]{:S(2)}) collective-permute-start(bf16[768,256]{1,0:T(8,128)(2,1)S(1)} %get-tuple-element.50), channel_id=1, source_target_pairs={{0,2},{1,0},{2,3},{3,1},{4,6},{5,4},{6,7},{7,5},{8,10},{9,8},{10,1... | collective-permute-start | bytes 1179656 | tf_op jit(solution)/shard_map/ppermute | solution.py:563
  61.7 0.0 collective-permute-done.9.refs_5_
  61.8 0.0 collective-permute-done.6.refs_3_
  61.8 0.0 collective-permute-done.5.refs_2_
  61.8 3.0 %shard_map.101 = (f32[1536,256]{1,0:T(8,128)S(1)}, bf16[1536,256]{1,0:T(8,128)(2,1)S(1)}) custom-call(s32[4]{0:T(128)S(1)} %and_select_fusion.table_ref, f32[1536,256]{1,0:T(8,128)S(1)} %shard_map.97.token_ref.total_ref, bf16[768,384]{1,0:T(8,128)(2,1)S(1)} %shard_map.98.refs_0_.refs_1_, bf16[768,384]{1,0:T(8,128)(2,1)S(1)} %collective-permute-done.4.refs_1_, ...), custom_call_target="tpu_custom_call" | custom-call | flops 1207959552 | bytes 3932160 | tf_op jit(solution)/shard_map/pallas_call | solution.py:23
  64.8 0.1 collective-permute-start.20
  64.8 1.6 %collective-permute-start.15 = (bf16[176,384]{1,0:T(8,128)(2,1)S(1)}, bf16[176,384]{1,0:T(8,128)(2,1)S(1)}, u32[]{:S(2)}, u32[]{:S(2)}) collective-permute-start(bf16[176,384]{1,0:T(8,128)(2,1)S(1)} %get-tuple-element.49), channel_id=1, source_target_pairs={{0,16},{4,12},{8,24},{12,4},{16,0},{20,28},{24,8},{28,20},{1,17},{... | collective-permute-start | bytes 405512 | tf_op jit(solution)/shard_map/ppermute | solution.py:192
  66.4 0.6 collective-permute-start.17
  67.1 2.9 %collective-permute-done.16.refs_2_.refs_5_ = bf16[768,256]{1,0:T(8,128)(2,1)S(1)} collective-permute-done((bf16[768,256]{1,0:T(8,128)(2,1)S(1)}, bf16[768,256]{1,0:T(8,128)(2,1)S(1)}, u32[]{:S(2)}, u32[]{:S(2)}) %collective-permute-start.16) | collective-permute-done | bytes 393248 | tf_op jit(solution)/shard_map/ppermute | solution.py:563
  70.0 0.0 collective-permute-done.15.refs_1_
  70.0 0.0 collective-permute-done.14.refs_0_
  70.0 0.1 shard_map.106
  70.1 0.1 collective-permute-start.18
  70.1 0.5 collective-permute-start.19
  70.6 1.5 %collective-permute-done.19.refs_4_ = bf16[144,384]{1,0:T(8,128)(2,1)S(1)} collective-permute-done((bf16[144,384]{1,0:T(8,128)(2,1)S(1)}, bf16[144,384]{1,0:T(8,128)(2,1)S(1)}, u32[]{:S(2)}, u32[]{:S(2)}) %collective-permute-start.19) | collective-permute-done | bytes 110624 | tf_op jit(solution)/shard_map/ppermute | solution.py:192
  72.1 0.0 collective-permute-done.17.refs_2_
  72.1 0.0 collective-permute-done.18.refs_3_
  72.1 0.0 collective-permute-done.20.refs_6_
  72.1 2.4 %shard_map.107 = bf16[1536,256]{1,0:T(8,128)(2,1)} custom-call(s32[8]{0:T(128)S(1)} %fusion.table_ref, f32[1536,256]{1,0:T(8,128)S(1)} %get-tuple-element.45.refs_3_.total_ref, bf16[768,384]{1,0:T(8,128)(2,1)S(1)} %get-tuple-element.47.refs_0_, bf16[768,384]{1,0:T(8,128)(2,1)S(1)} %get-tuple-element.51.refs_1_, ...), custom_call_target="tpu_custom_call" | custom-call | flops 603979776 | bytes 3145728 | tf_op jit(solution)/shard_map/pallas_call | solution.py:23
  (13 shorter events, 0.1 us)
Async XLA Ops:
  0.0 8.0 %copy-start.1 = (bf16[256,384]{1,0:T(8,128)(2,1)S(1)}, bf16[256,384]{1,0:T(8,128)(2,1)}, u32[]{:S(2)}) copy-start(bf16[256,384]{1,0:T(8,128)(2,1)} %g_ref.5) | copy-start | bytes 589828
  0.0 8.0 %copy-start = (bf16[256,384]{1,0:T(8,128)(2,1)S(1)}, bf16[256,384]{1,0:T(8,128)(2,1)}, u32[]{:S(2)}) copy-start(bf16[256,384]{1,0:T(8,128)(2,1)} %v_ref.5) | copy-start | bytes 589828
  0.0 8.0 %copy-start.3 = (bf16[256,384]{1,0:T(8,128)(2,1)S(1)}, bf16[256,384]{1,0:T(8,128)(2,1)}, u32[]{:S(2)}) copy-start(bf16[256,384]{1,0:T(8,128)(2,1)} %k_ref.3) | copy-start | bytes 589828
  0.0 8.0 %copy-start.2 = (bf16[256,384]{1,0:T(8,128)(2,1)S(1)}, bf16[256,384]{1,0:T(8,128)(2,1)}, u32[]{:S(2)}) copy-start(bf16[256,384]{1,0:T(8,128)(2,1)} %q_ref.3) | copy-start | bytes 589828
  0.0 8.0 %copy-start.4 = (f32[256,3]{0,1:T(4,128)S(1)}, f32[256,3]{0,1:T(4,128)}, u32[]{:S(2)}) copy-start(f32[256,3]{0,1:T(4,128)} %param.13) | copy-start | bytes 9220
  1.4 22.1 %collective-permute-start.3 = (bf16[768,384]{1,0:T(8,128)(2,1)S(1)}, bf16[768,384]{1,0:T(8,128)(2,1)S(1)}, u32[]{:S(2)}, u32[]{:S(2)}) collective-permute-start(bf16[768,384]{1,0:T(8,128)(2,1)S(1)} %get-tuple-element.30.token_ref), channel_id=1, source_target_pairs={{0,1},{1,2},{2,3},{3,0},{4,7},{5,4},{6,5},{7,6},{8,9},{9,10},{10,1... | collective-permute-start | bytes 1769480 | tf_op jit(solution)/shard_map/ppermute | solution.py:471
  4.5 20.6 %collective-permute-start.10 = (bf16[768,384]{1,0:T(8,128)(2,1)S(1)}, bf16[768,384]{1,0:T(8,128)(2,1)S(1)}, u32[]{:S(2)}, u32[]{:S(2)}) collective-permute-start(bf16[768,384]{1,0:T(8,128)(2,1)S(1)} %get-tuple-element.46), channel_id=1, source_target_pairs={{0,1},{1,2},{7,6},{6,5},{8,9},{9,10},{15,14},{14,13},{16,17},{17,1... | collective-permute-start | bytes 1769480 | tf_op jit(solution)/shard_map/ppermute | solution.py:472
  8.9 1.5 %collective-permute-start = (bf16[784,128]{1,0:T(8,128)(2,1)S(1)}, bf16[784,128]{1,0:T(8,128)(2,1)S(1)}, u32[]{:S(2)}, u32[]{:S(2)}) collective-permute-start(bf16[784,128]{1,0:T(8,128)(2,1)S(1)} %get-tuple-element.31), channel_id=1, source_target_pairs={{0,4},{4,0},{8,12},{12,8},{16,20},{20,16},{24,28},{28,24},{1,5},{5... | collective-permute-start | bytes 602120 | tf_op jit(solution)/shard_map/ppermute | solution.py:497
  10.5 7.1 %collective-permute-start.1 = (bf16[784,128]{1,0:T(8,128)(2,1)S(1)}, bf16[784,128]{1,0:T(8,128)(2,1)S(1)}, u32[]{:S(2)}, u32[]{:S(2)}) collective-permute-start(bf16[784,128]{1,0:T(8,128)(2,1)S(1)} %get-tuple-element.34), channel_id=1, source_target_pairs={{0,8},{4,12},{8,0},{12,4},{16,24},{20,28},{24,16},{28,20},{1,9},{5... | collective-permute-start | bytes 602120 | tf_op jit(solution)/shard_map/ppermute | solution.py:497
  18.4 4.6 %collective-permute-start.2 = (bf16[384,128]{1,0:T(8,128)(2,1)S(1)}, bf16[384,128]{1,0:T(8,128)(2,1)S(1)}, u32[]{:S(2)}, u32[]{:S(2)}) collective-permute-start(bf16[384,128]{1,0:T(8,128)(2,1)S(1)} %get-tuple-element.38), channel_id=1, source_target_pairs={{0,16},{4,20},{8,24},{12,28},{16,0},{20,4},{24,8},{28,12},{1,17},{... | collective-permute-start | bytes 294920 | tf_op jit(solution)/shard_map/ppermute | solution.py:497
  23.5 9.9 %collective-permute-start.4 = (bf16[768,384]{1,0:T(8,128)(2,1)S(1)}, bf16[768,384]{1,0:T(8,128)(2,1)S(1)}, u32[]{:S(2)}, u32[]{:S(2)}) collective-permute-start(bf16[768,384]{1,0:T(8,128)(2,1)S(1)} %shard_map.98.refs_0_.refs_1_), channel_id=1, source_target_pairs={{0,8},{4,20},{8,0},{12,28},{16,24},{20,4},{24,16},{28,12},{1,9},{5... | collective-permute-start | bytes 1769480 | tf_op jit(solution)/shard_map/ppermute | solution.py:192
  25.1 16.3 %collective-permute-start.11 = (bf16[768,384]{1,0:T(8,128)(2,1)S(1)}, bf16[768,384]{1,0:T(8,128)(2,1)S(1)}, u32[]{:S(2)}, u32[]{:S(2)}) collective-permute-start(bf16[768,384]{1,0:T(8,128)(2,1)S(1)} %shard_map.102), channel_id=1, source_target_pairs={{1,2},{2,3},{6,5},{5,4},{9,10},{10,11},{14,13},{13,12},{17,18},{18... | collective-permute-start | bytes 1769480 | tf_op jit(solution)/shard_map/ppermute | solution.py:536
  34.5 0.7 copy-start.5
  35.2 26.6 %collective-permute-start.5 = (bf16[1152,384]{1,0:T(8,128)(2,1)}, bf16[1152,384]{1,0:T(8,128)(2,1)}, u32[]{:S(2)}, u32[]{:S(2)}) collective-permute-start(bf16[1152,384]{1,0:T(8,128)(2,1)} %get-tuple-element.41), channel_id=1, source_target_pairs={{0,16},{4,12},{8,24},{12,4},{16,0},{20,28},{24,8},{28,20},{1,17},{... | collective-permute-start | bytes 2654216 | tf_op jit(solution)/shard_map/ppermute | solution.py:192
  36.7 12.0 %collective-permute-start.8 = (bf16[768,256]{1,0:T(8,128)(2,1)S(1)}, bf16[768,256]{1,0:T(8,128)(2,1)}, u32[]{:S(2)}, u32[]{:S(2)}) collective-permute-start(bf16[768,256]{1,0:T(8,128)(2,1)S(1)} %shard_map.96.grads_ref.refs_1_.own_ref), channel_id=1, source_target_pairs={{0,3},{1,0},{2,1},{3,2},{4,7},{5,4},{6,5},{7,6},{8,11},{9,8},{10,9... | collective-permute-start | bytes 1179656 | tf_op jit(solution)/shard_map/ppermute | solution.py:527
  37.2 16.3 %collective-permute-start.7 = (bf16[768,256]{1,0:T(8,128)(2,1)S(1)}, bf16[768,256]{1,0:T(8,128)(2,1)}, u32[]{:S(2)}, u32[]{:S(2)}) collective-permute-start(bf16[768,256]{1,0:T(8,128)(2,1)S(1)} %shard_map.96.grads_ref.refs_1_.own_ref), channel_id=1, source_target_pairs={{0,1},{1,2},{2,3},{3,0},{4,5},{5,6},{6,7},{7,4},{8,9},{9,10},{10,1... | collective-permute-start | bytes 1179656 | tf_op jit(solution)/shard_map/ppermute | solution.py:526
  41.4 15.0 %copy-start.6 = (s32[8]{0:T(128)S(1)}, s32[8]{0:T(128)}, u32[]{:S(2)}) copy-start(s32[8]{0:T(128)} %constant.36.clone) | copy-start | bytes 100
  41.4 15.0 %copy-start.7 = (s32[8]{0:T(128)S(1)}, s32[8]{0:T(128)}, u32[]{:S(2)}) copy-start(s32[8]{0:T(128)} %constant.35.clone) | copy-start | bytes 100
  41.5 3.5 %collective-permute-start.12 = (bf16[384,384]{1,0:T(8,128)(2,1)S(1)}, bf16[384,384]{1,0:T(8,128)(2,1)S(1)}, u32[]{:S(2)}, u32[]{:S(2)}) collective-permute-start(bf16[384,384]{1,0:T(8,128)(2,1)S(1)} %shard_map.103), channel_id=1, source_target_pairs={{2,6},{3,7},{4,0},{5,1},{10,14},{11,15},{12,8},{13,9},{18,22},{19,... | collective-permute-start | bytes 884744 | tf_op jit(solution)/shard_map/ppermute | solution.py:542
  45.0 11.4 %collective-permute-start.13 = (bf16[384,384]{1,0:T(8,128)(2,1)S(1)}, bf16[384,384]{1,0:T(8,128)(2,1)}, u32[]{:S(2)}, u32[]{:S(2)}) collective-permute-start(bf16[384,384]{1,0:T(8,128)(2,1)S(1)} %shard_map.104.refs_0_), channel_id=1, source_target_pairs={{0,8},{4,20},{8,0},{12,28},{16,24},{20,4},{24,16},{28,12},{1,9},{5... | collective-permute-start | bytes 884744 | tf_op jit(solution)/shard_map/ppermute | solution.py:192
  54.7 7.1 %collective-permute-start.9 = (bf16[768,256]{1,0:T(8,128)(2,1)S(1)}, bf16[768,256]{1,0:T(8,128)(2,1)S(1)}, u32[]{:S(2)}, u32[]{:S(2)}) collective-permute-start(bf16[768,256]{1,0:T(8,128)(2,1)S(1)} %get-tuple-element.44), channel_id=1, source_target_pairs={{0,4},{4,0},{8,12},{12,8},{16,20},{20,16},{24,28},{28,24},{1,5},{5... | collective-permute-start | bytes 1179656 | tf_op jit(solution)/shard_map/ppermute | solution.py:192
  54.8 7.0 %collective-permute-start.6 = (bf16[384,384]{1,0:T(8,128)(2,1)}, bf16[384,384]{1,0:T(8,128)(2,1)S(1)}, u32[]{:S(2)}, u32[]{:S(2)}) collective-permute-start(bf16[384,384]{1,0:T(8,128)(2,1)} %copy-done.5), channel_id=1, source_target_pairs={{0,16},{4,12},{8,24},{12,4},{16,0},{20,28},{24,8},{28,20},{1,17},{... | collective-permute-start | bytes 884744 | tf_op jit(solution)/shard_map/ppermute | solution.py:192
  57.5 12.5 %collective-permute-start.14 = (bf16[592,384]{1,0:T(8,128)(2,1)S(1)}, bf16[592,384]{1,0:T(8,128)(2,1)S(1)}, u32[]{:S(2)}, u32[]{:S(2)}) collective-permute-start(bf16[592,384]{1,0:T(8,128)(2,1)S(1)} %get-tuple-element.48), channel_id=1, source_target_pairs={{0,16},{4,12},{8,24},{12,4},{16,0},{20,28},{24,8},{28,20},{1,17},{... | collective-permute-start | bytes 1363976 | tf_op jit(solution)/shard_map/ppermute | solution.py:192
  58.0 11.9 %collective-permute-start.16 = (bf16[768,256]{1,0:T(8,128)(2,1)S(1)}, bf16[768,256]{1,0:T(8,128)(2,1)S(1)}, u32[]{:S(2)}, u32[]{:S(2)}) collective-permute-start(bf16[768,256]{1,0:T(8,128)(2,1)S(1)} %get-tuple-element.50), channel_id=1, source_target_pairs={{0,2},{1,0},{2,3},{3,1},{4,6},{5,4},{6,7},{7,5},{8,10},{9,8},{10,1... | collective-permute-start | bytes 1179656 | tf_op jit(solution)/shard_map/ppermute | solution.py:563
  64.8 7.4 %collective-permute-start.20 = (bf16[1536,256]{1,0:T(8,128)(2,1)S(1)}, bf16[1536,256]{1,0:T(8,128)(2,1)S(1)}, u32[]{:S(2)}, u32[]{:S(2)}) collective-permute-start(bf16[1536,256]{1,0:T(8,128)(2,1)S(1)} %get-tuple-element.54), channel_id=1, source_target_pairs={{0,4},{4,0},{8,12},{12,8},{16,20},{20,16},{24,28},{28,24},{1,5},{5... | collective-permute-start | bytes 2359304 | tf_op jit(solution)/shard_map/ppermute | solution.py:192
  64.8 5.1 %collective-permute-start.15 = (bf16[176,384]{1,0:T(8,128)(2,1)S(1)}, bf16[176,384]{1,0:T(8,128)(2,1)S(1)}, u32[]{:S(2)}, u32[]{:S(2)}) collective-permute-start(bf16[176,384]{1,0:T(8,128)(2,1)S(1)} %get-tuple-element.49), channel_id=1, source_target_pairs={{0,16},{4,12},{8,24},{12,4},{16,0},{20,28},{24,8},{28,20},{1,17},{... | collective-permute-start | bytes 405512 | tf_op jit(solution)/shard_map/ppermute | solution.py:192
  66.4 5.7 %collective-permute-start.17 = (bf16[768,384]{1,0:T(8,128)(2,1)S(1)}, bf16[768,384]{1,0:T(8,128)(2,1)S(1)}, u32[]{:S(2)}, u32[]{:S(2)}) collective-permute-start(bf16[768,384]{1,0:T(8,128)(2,1)S(1)} %get-tuple-element.47.refs_0_), channel_id=1, source_target_pairs={{0,4},{4,0},{8,12},{12,8},{16,20},{20,16},{24,28},{28,24},{1,5},{5... | collective-permute-start | bytes 1769480 | tf_op jit(solution)/shard_map/ppermute | solution.py:192
  70.1 2.1 %collective-permute-start.18 = (bf16[624,384]{1,0:T(8,128)(2,1)S(1)}, bf16[624,384]{1,0:T(8,128)(2,1)S(1)}, u32[]{:S(2)}, u32[]{:S(2)}) collective-permute-start(bf16[624,384]{1,0:T(8,128)(2,1)S(1)} %get-tuple-element.52), channel_id=1, source_target_pairs={{0,4},{4,0},{8,12},{12,8},{16,20},{20,16},{24,28},{28,24},{1,5},{5... | collective-permute-start | bytes 1437704 | tf_op jit(solution)/shard_map/ppermute | solution.py:192
  70.1 2.0 %collective-permute-start.19 = (bf16[144,384]{1,0:T(8,128)(2,1)S(1)}, bf16[144,384]{1,0:T(8,128)(2,1)S(1)}, u32[]{:S(2)}, u32[]{:S(2)}) collective-permute-start(bf16[144,384]{1,0:T(8,128)(2,1)S(1)} %get-tuple-element.53), channel_id=1, source_target_pairs={{0,4},{4,0},{8,12},{12,8},{16,20},{20,16},{24,28},{28,24},{1,5},{5... | collective-permute-start | bytes 331784 | tf_op jit(solution)/shard_map/ppermute | solution.py:192

commit v6 on v5

--- a/solution.py
+++ b/solution.py
@@ -10,9 +10,8 @@
 F32 = jnp.float32
 BF16 = jnp.bfloat16
 VMEM_BYTES = 16 * 1024 * 1024
-CUT = 592
-HOP = 624
-FAR = 1152
+CUT = 144
+SPLIT = 1152
 
 
 def contract(a, b, left, right):
@@ -385,62 +384,77 @@
                 out_ref[j * share : (j + 1) * share, :] = both_ref[at : at + share, :]
 
 
-def pair_kernel(table_ref, total_ref, *refs):
-    weights, (kept_ref, got_ref, out_ref, sent_ref) = refs[:-4], refs[-4:]
+def pair_kernel(count, table_ref, total_ref, *refs):
+    weights, (kept_ref, got_ref), (out_ref, head_ref, tail_ref) = refs[:count], refs[count : count + 2], refs[count + 2 :]
     nblocks = table_ref.shape[0]
     size = out_ref.shape[0] // nblocks
+    split = head_ref.shape[0] // size
     for j in range(nblocks):
         block = rows_of(weights, 2 * size * j, 2 * size * (j + 1))
-        rows = pl.ds(pl.multiple_of(table_ref[j] * size, 16), size)
+        place = table_ref[j]
+        rows = pl.ds(pl.multiple_of(place * size, 16), size)
         out_ref[rows, :] = total_ref[rows, :] + row_block(block, kept_ref[...])
-        sent_ref[rows, :] = row_block(block, got_ref[...]).astype(BF16)
-
-
-def pair_product(table, total, weights, kept, got):
+        sent = row_block(block, got_ref[...]).astype(BF16)
+
+        @pl.when(place < split)
+        def _(sent=sent, place=place):
+            head_ref[pl.ds(pl.multiple_of(place * size, 16), size), :] = sent
+
+        @pl.when(place >= split)
+        def _(sent=sent, place=place):
+            tail_ref[pl.ds(pl.multiple_of((place - split) * size, 16), size), :] = sent
+
+
+def pair_product(table, total, weights, kept, got, split):
     chunk, span = total.shape
     return call(
-        pair_kernel,
-        (jax.ShapeDtypeStruct((chunk, span), F32), jax.ShapeDtypeStruct((chunk, span), BF16)),
+        functools.partial(pair_kernel, len(weights)),
+        (
+            jax.ShapeDtypeStruct((chunk, span), F32),
+            jax.ShapeDtypeStruct((split, span), BF16),
+            jax.ShapeDtypeStruct((chunk - split, span), BF16),
+        ),
         4 * chunk * span * kept.shape[0], chunk * span * 10,
         table, total, *weights, kept, got,
         in_specs=[pl.BlockSpec(memory_space=pltpu.SMEM)]
         + [pl.BlockSpec(memory_space=pltpu.VMEM)] * (3 + len(weights)),
-        out_specs=[pl.BlockSpec(memory_space=pltpu.VMEM)] * 2,
+        out_specs=[pl.BlockSpec(memory_space=pltpu.VMEM)] * 3,
         vmem=24 * 1024 * 1024,
     )
 
 
-def add_kernel(terms, plus, table_ref, total_ref, *refs):
+def add_kernel(blocks, base, low, high, plus, table_ref, total_ref, grads_ref, *refs):
     args, out_ref = refs[:-1], refs[-1]
     nshares = table_ref.shape[0]
     share = out_ref.shape[0] // nshares
     for j in range(nshares):
         rows = pl.ds(pl.multiple_of(table_ref[j] * share, 8), share)
         total = total_ref[rows, :]
-        if plus is not None:
-            total = total + args[plus][rows, :].astype(F32)
-        for blocks, grads in terms:
-            weights = rows_of([args[i] for i in blocks], 2 * share * j, 2 * share * (j + 1))
-            total = total + row_block(weights, args[grads][...])
+        if plus:
+            head, tail = (args[i] for i in plus)
+            split, place = head.shape[0] // share, table_ref[j]
+            from_head = head[pl.ds(pl.multiple_of(jnp.minimum(place, split - 1) * share, 16), share), :]
+            from_tail = tail[pl.ds(pl.multiple_of(jnp.maximum(place - split, 0) * share, 16), share), :]
+            total = total + jnp.where(place < split, from_head, from_tail).astype(F32)
+        if low <= j < high:
+            weights = rows_of([args[i] for i in blocks], 2 * share * (j - base), 2 * share * (j + 1 - base))
+            total = total + row_block(weights, grads_ref[...])
         out_ref[rows, :] = total.astype(out_ref.dtype)
 
 
-def add_product(table, total, terms, last, plus=None):
+def add_product(table, total, blocks, grads, last, plus=(), base=0, low=0, high=None):
     chunk, span = total.shape
     args = []
-
-    spec = tuple(
-        (tuple(place_in(args, x) for x in blocks), place_in(args, grads))
-        for blocks, grads in terms
-    )
-    plus = None if plus is None else place_in(args, plus)
+    blocks = tuple(place_in(args, x) for x in blocks)
+    plus = tuple(place_in(args, x) for x in plus)
+    high = table.shape[0] if high is None else high
     return call(
-        functools.partial(add_kernel, spec, plus),
+        functools.partial(add_kernel, blocks, base, low, high, plus),
         jax.ShapeDtypeStruct((chunk, span), BF16 if last else F32),
-        2 * len(terms) * chunk * span * terms[0][1].shape[0], chunk * span * 8,
-        table, total, *args,
+        2 * chunk * span * grads.shape[0], chunk * span * 8,
+        table, total, grads, *args,
         in_specs=[pl.BlockSpec(memory_space=pltpu.SMEM)]
-        + [pl.BlockSpec(memory_space=pltpu.VMEM)] * (1 + len(args)),
+        + [pl.BlockSpec(memory_space=pltpu.VMEM)] * (2 + len(args)),
         out_specs=pl.BlockSpec(memory_space=pltpu.VMEM),
         vmem=24 * 1024 * 1024,
     )
@@ -523,15 +537,14 @@
     total = own_product(w_query, w_key, both, chunk)
 
     if fast:
-        p1 = lax.ppermute(both, "head", ring[1])
-        p3 = lax.ppermute(both, "head", ring[3])
-        one, two, cut = 2 * share, 4 * share, CUT
+        one, two = 2 * share, 4 * share
         (first,) = gate([first], [both])
         second = share_hop(first, 0)
-        sent = join(
-            ((first, 0, two), (second, 0, FAR - two)), ((second, FAR - two, 2 * two - FAR),),
-        )
-        blocks = [first, second] + [share_hop(x, 1) for x in sent]
+        (near,) = join(((first, 0, two), (second, 0, two)))
+        blocks = [near, share_hop(near, 1)]
+        (ready,) = gate([both], [total, near])
+        p1 = lax.ppermute(ready, "head", ring[1])
+        p3 = lax.ppermute(ready, "head", ring[3])
         (passing,) = gate([passing], [first])
         passing = lax.ppermute(passing, axes, moves([(1, 2), (2, 3)], [(2, 1), (1, 0)]))
         theirs = call(
@@ -548,30 +561,23 @@
             in_specs=[pl.BlockSpec(memory_space=pltpu.VMEM)] * 2,
             out_specs=pl.BlockSpec(memory_space=pltpu.VMEM),
         )
-        fourth = share_hop(third, 0)
-        near, head_rows, tail_rows = join(
-            ((third, 0, one), (fourth, 0, one)),
-            ((third, 0, one), (fourth, 0, cut - one)),
-            ((fourth, cut - one, two - cut),),
-        )
-        far = [share_hop(x, 1) for x in (head_rows, tail_rows)]
+        fourth, fifth = share_hop(third, 0), share_hop(third, 1)
+        fourth, fifth = gate([fourth, fifth])
+        sixth = share_hop(fourth, 1)
+        (early,) = join(((third, 0, one), (fourth, 0, one), (fifth, 0, CUT)))
         relay, kept, handed = call(
-            relay_kernel, [jax.ShapeDtypeStruct(both.shape, BF16)] * 3, 0, 0, both, p1, p3, total,
+            relay_kernel, [jax.ShapeDtypeStruct(both.shape, BF16)] * 3, 0, 0, ready, p1, p3, total,
             in_specs=[pl.BlockSpec(memory_space=pltpu.VMEM)] * 3 + [pl.BlockSpec(memory_space=pl.ANY)],
             out_specs=[pl.BlockSpec(memory_space=pltpu.VMEM)] * 3,
         )
         p2 = lax.ppermute(relay, "head", [(0, 2), (1, 0), (2, 3), (3, 1)])
         got = share_hop(handed, 2)
-        total, handed = pair_product(table[: nseq // 2] // 2, total, blocks, kept, got)
-        got = share_hop(handed, 2)
-        far, far_head, far_tail = join(
-            ((far[0], 0, cut), (far[1], 0, two - cut)),
-            ((far[0], 0, cut), (far[1], 0, HOP - cut)),
-            ((far[1], HOP - cut, two - HOP),),
-            tokens=[p2, total],
-        )
-        term = (near, far, *(share_hop(x, 2) for x in (near, far_head, far_tail)))
-        return add_product(table, total, [(term, p2)], True, got)
+        total, *handed = pair_product(table[: nseq // 2] // 2, total, blocks, kept, got, SPLIT)
+        got = [share_hop(x, 2) for x in handed]
+        (late,) = join(((fifth, CUT, one - CUT), (sixth, 0, one)), tokens=[p2])
+        early, late = share_hop(early, 2), share_hop(late, 2)
+        total = add_product(table, total, (third, fourth, fifth, sixth, early), p2, False, high=6)
+        return add_product(table, total, (early, late), p2, True, plus=got, base=4, low=6)
 
     gathered = lax.all_gather(both, "head")
     for i, k in enumerate(shifts):
@@ -580,7 +586,7 @@
             whole = held[0] if number == 0 else jnp.concatenate(held)
             held = [whole, share_hop(whole, number)]
         grads = gathered[(my_head + nhead - k) % nhead]
-        total = add_product(table, total, [(held, grads)], i == nhead - 2)
+        total = add_product(table, total, held, grads, i == nhead - 2)
     return total
 
 

time: 74.9 us -> 73 us (0.975)
  starting transfers between devices: 27.2 us -> 24.9 us
  Pallas kernels: 16.1 us -> 17.9 us
    ppermute x2, waiting for transfers between devices: 6.94 us -> 10 us  [the longest x1 7.98 us: shards(): p1 = lax.ppermute(ready, 'head', ring[1])]
    ppermute x11 -> x10, waiting for transfers between devices: 9.23 us -> 6.19 us  [share_hop(): return lax.ppermute(held, 'seq', pairs)]
    ppermute x11 -> x10, starting transfers between devices: 9.72 us -> 6.93 us  [share_hop(): return lax.ppermute(held, 'seq', pairs)]
    ppermute x3, waiting for transfers between devices: 9.03 us -> 6.6 us  [shards(): got = lax.ppermute(sent, 'seq', [(i, i ^ hop) for i in range(nseq)])]
    pallas_call x17 -> x20, Pallas kernels: 16.1 us -> 17.9 us  [call(): pl.pallas_call(kernel, out_shape=out_shape, cost_estimate=pl.CostEstimate...]
    ppermute x3, starting transfers between devices: 3.15 us -> 4.73 us  [shards(): got = lax.ppermute(sent, 'seq', [(i, i ^ hop) for i in range(nseq)])]
    ppermute x1, waiting for transfers between devices: 0.01 us -> 1.53 us  [shards(): lax.ppermute(packed[1], axes, moves([(0, 1), (1, 2)], [(3, 2), (2, 1)]))]
    ppermute x1, starting transfers between devices: 3.51 us -> 2.28 us  [shards(): lax.ppermute(packed[1], axes, moves([(0, 1), (1, 2)], [(3, 2), (2, 1)]))]
  transfers between devices with their start and end apart: 21 -> 20, of which waited for: 9 -> 9; matrix products, arithmetic and copies ran while one was open for 0% -> 0% of each run, Pallas kernels for 17% -> 20%
where the time goes in v6:
time: 73 us; the launch traced here: 72.7 us
  waiting for transfers between devices  29.6 us (41%)
  starting transfers between devices  24.9 us (34%)
  Pallas kernels  17.9 us (25%)
    pallas_call x20, Pallas kernels, call(): pl.pallas_call(kernel, out_shape=out_shape, cost_estimate=pl.CostEstimate...  17.9 us
    ppermute x1, waiting for transfers between devices, shards(): p1 = lax.ppermute(ready, 'head', ring[1])  7.98 us
    ppermute x10, starting transfers between devices, share_hop(): return lax.ppermute(held, 'seq', pairs)  6.93 us
    ppermute x3, waiting for transfers between devices, shards(): got = lax.ppermute(sent, 'seq', [(i, i ^ hop) for i in range(nseq)])  6.6 us
    ppermute x10, waiting for transfers between devices, share_hop(): return lax.ppermute(held, 'seq', pairs)  6.19 us
    ppermute x3, starting transfers between devices, shards(): got = lax.ppermute(sent, 'seq', [(i, i ^ hop) for i in range(nseq)])  4.73 us
    ppermute x1, starting transfers between devices, shards(): p2 = lax.ppermute(relay, 'head', [(0, 2), (1, 0), (2, 3), (3, 1)])  3.81 us
    ppermute x1, starting transfers between devices, shards(): first = lax.ppermute(packed[0], axes, moves(ring[1], ring[3]))  3.09 us
  transfers between devices with their start and end apart: 20, of which 9 were waited for; matrix products, arithmetic and copies ran while one was open for 0% of the time, Pallas kernels for 20%

profile of v6, /device:TPU:0, one launch (start us, length us, event | category | flops | bytes accessed | tf_op | source)
XLA Modules:
  0.0 72.7 jit_solution(16200316746339650645)
XLA Ops:
  0.0 0.0 copy-start.1
  0.0 0.0 copy-start
  0.0 0.0 copy-start.3
  0.0 1.4 %shard_map.91 = (bf16[768,384]{1,0:T(8,128)(2,1)S(1)}, bf16[768,384]{1,0:T(8,128)(2,1)S(1)}) custom-call(bf16[6144,384]{1,0:T(8,128)(2,1)} %wq_ref.3, bf16[6144,384]{1,0:T(8,128)(2,1)} %wk_ref.3), custom_call_target="tpu_custom_call" | custom-call | bytes 2359296 | tf_op jit(solution)/shard_map/pallas_call | solution.py:22
  1.4 3.1 %collective-permute-start.3 = (bf16[768,384]{1,0:T(8,128)(2,1)S(1)}, bf16[768,384]{1,0:T(8,128)(2,1)S(1)}, u32[]{:S(2)}, u32[]{:S(2)}) collective-permute-start(bf16[768,384]{1,0:T(8,128)(2,1)S(1)} %get-tuple-element.25.token_ref), channel_id=1, source_target_pairs={{0,1},{1,2},{2,3},{3,0},{4,7},{5,4},{6,5},{7,6},{8,9},{9,10},{10,1... | collective-permute-start | bytes 1769480 | tf_op jit(solution)/shard_map/ppermute | solution.py:485
  4.5 0.0 copy-done.1
  4.5 0.0 copy-done
  4.5 0.0 copy-done.3
  4.5 0.0 copy-done.2
  4.5 0.0 copy-done.4
  4.5 0.9 %shard_map.92 = (bf16[784,128]{1,0:T(8,128)(2,1)S(1)}, f32[768,128]{1,0:T(8,128)S(1)}, f32[24,128]{1,0:T(8,128)S(1)}) custom-call(f32[3,256]{1,0:T(4,128)S(1)} %bitcast.1, bf16[256,384]{1,0:T(8,128)(2,1)S(1)} %copy-done.2, bf16[256,384]{1,0:T(8,128)(2,1)S(1)} %copy-done.3, bf16[256,384]{1,0:T(8,128)(2,1)S(1)} %copy-done, bf16[256,384]{1,0:T(8,128)(2,1)S(1)} %copy-done.1, ...), custom_call_target="tpu_custom_call" | custom-call | flops 50331648 | bytes 786432 | tf_op jit(solution)/shard_map/pallas_call | solution.py:22
  5.4 1.6 %collective-permute-start = (bf16[784,128]{1,0:T(8,128)(2,1)S(1)}, bf16[784,128]{1,0:T(8,128)(2,1)S(1)}, u32[]{:S(2)}, u32[]{:S(2)}) collective-permute-start(bf16[784,128]{1,0:T(8,128)(2,1)S(1)} %get-tuple-element.26), channel_id=1, source_target_pairs={{0,4},{4,0},{8,12},{12,8},{16,20},{20,16},{24,28},{28,24},{1,5},{5... | collective-permute-start | bytes 602120 | tf_op jit(solution)/shard_map/ppermute | solution.py:511
  7.0 1.1 %collective-permute-done.got_ref = bf16[784,128]{1,0:T(8,128)(2,1)S(1)} collective-permute-done((bf16[784,128]{1,0:T(8,128)(2,1)S(1)}, bf16[784,128]{1,0:T(8,128)(2,1)S(1)}, u32[]{:S(2)}, u32[]{:S(2)}) %collective-permute-start) | collective-permute-done | bytes 200736 | tf_op jit(solution)/shard_map/ppermute | solution.py:511
  8.1 0.1 shard_map.93
  8.2 1.6 %collective-permute-start.1 = (bf16[784,128]{1,0:T(8,128)(2,1)S(1)}, bf16[784,128]{1,0:T(8,128)(2,1)S(1)}, u32[]{:S(2)}, u32[]{:S(2)}) collective-permute-start(bf16[784,128]{1,0:T(8,128)(2,1)S(1)} %get-tuple-element.29), channel_id=1, source_target_pairs={{0,8},{4,12},{8,0},{12,4},{16,24},{20,28},{24,16},{28,20},{1,9},{5... | collective-permute-start | bytes 602120 | tf_op jit(solution)/shard_map/ppermute | solution.py:511
  9.8 2.3 %collective-permute-start.10 = (bf16[768,384]{1,0:T(8,128)(2,1)S(1)}, bf16[768,384]{1,0:T(8,128)(2,1)S(1)}, u32[]{:S(2)}, u32[]{:S(2)}) collective-permute-start(bf16[768,384]{1,0:T(8,128)(2,1)S(1)} %get-tuple-element.40), channel_id=1, source_target_pairs={{0,1},{1,2},{7,6},{6,5},{8,9},{9,10},{15,14},{14,13},{16,17},{17,1... | collective-permute-start | bytes 1769480 | tf_op jit(solution)/shard_map/ppermute | solution.py:486
  12.0 3.5 %collective-permute-done.1.got_ref = bf16[784,128]{1,0:T(8,128)(2,1)S(1)} collective-permute-done((bf16[784,128]{1,0:T(8,128)(2,1)S(1)}, bf16[784,128]{1,0:T(8,128)(2,1)S(1)}, u32[]{:S(2)}, u32[]{:S(2)}) %collective-permute-start.1) | collective-permute-done | bytes 200736 | tf_op jit(solution)/shard_map/ppermute | solution.py:511
  15.5 0.8 %shard_map.94 = (bf16[384,128]{1,0:T(8,128)(2,1)S(1)}, f32[768,128]{1,0:T(8,128)}, f32[24,128]{1,0:T(8,128)S(1)}, f32[768,128]{1,0:T(8,128)S(1)}) custom-call(bf16[784,128]{1,0:T(8,128)(2,1)S(1)} %collective-permute-done.1.got_ref, f32[768,128]{1,0:T(8,128)S(1)} %get-tuple-element.30.held_ref, f32[24,128]{1,0:T(8,128)S(1)} %get-tuple-element.31.logs_ref, ...), custom_call_target="tpu_custom_call" | custom-call | flops 491520 | bytes 786432 | tf_op jit(solution)/shard_map/pallas_call | solution.py:22
  16.3 1.5 %collective-permute-start.2 = (bf16[384,128]{1,0:T(8,128)(2,1)S(1)}, bf16[384,128]{1,0:T(8,128)(2,1)S(1)}, u32[]{:S(2)}, u32[]{:S(2)}) collective-permute-start(bf16[384,128]{1,0:T(8,128)(2,1)S(1)} %get-tuple-element.33), channel_id=1, source_target_pairs={{0,16},{4,20},{8,24},{12,28},{16,0},{20,4},{24,8},{28,12},{1,17},{... | collective-permute-start | bytes 294920 | tf_op jit(solution)/shard_map/ppermute | solution.py:511
  17.9 1.0 %shard_map.95.local_ref = f32[768,256]{1,0:T(8,128)S(1)} custom-call(f32[3,256]{1,0:T(4,128)S(1)} %bitcast.2, bf16[256,384]{1,0:T(8,128)(2,1)S(1)} %copy-done.2, bf16[256,384]{1,0:T(8,128)(2,1)S(1)} %copy-done.3, bf16[256,384]{1,0:T(8,128)(2,1)S(1)} %copy-done, bf16[256,384]{1,0:T(8,128)(2,1)S(1)} %copy-done.1), custom_call_target="tpu_custom_call" | custom-call | flops 150994944 | bytes 1572864 | tf_op jit(solution)/shard_map/pallas_call | solution.py:22
  18.9 2.1 %collective-permute-done.2.got_ref = bf16[384,128]{1,0:T(8,128)(2,1)S(1)} collective-permute-done((bf16[384,128]{1,0:T(8,128)(2,1)S(1)}, bf16[384,128]{1,0:T(8,128)(2,1)S(1)}, u32[]{:S(2)}, u32[]{:S(2)}) %collective-permute-start.2) | collective-permute-done | bytes 98336 | tf_op jit(solution)/shard_map/ppermute | solution.py:511
  21.0 0.4 shard_map.96.grads_ref.refs_1_.refs_0_
  21.4 0.0 collective-permute-done.3.refs_0_
  21.4 1.6 %collective-permute-start.4 = (bf16[768,384]{1,0:T(8,128)(2,1)S(1)}, bf16[768,384]{1,0:T(8,128)(2,1)S(1)}, u32[]{:S(2)}, u32[]{:S(2)}) collective-permute-start(bf16[768,384]{1,0:T(8,128)(2,1)S(1)} %shard_map.98.refs_0_.refs_1_), channel_id=1, source_target_pairs={{0,8},{4,20},{8,0},{12,28},{16,24},{20,4},{24,16},{28,12},{1,9},{5... | collective-permute-start | bytes 1769480 | tf_op jit(solution)/shard_map/ppermute | solution.py:191
  23.0 1.5 %collective-permute-done.10.refs_0_ = bf16[768,384]{1,0:T(8,128)(2,1)S(1)} collective-permute-done((bf16[768,384]{1,0:T(8,128)(2,1)S(1)}, bf16[768,384]{1,0:T(8,128)(2,1)S(1)}, u32[]{:S(2)}, u32[]{:S(2)}) %collective-permute-start.10) | collective-permute-done | bytes 589856 | tf_op jit(solution)/shard_map/ppermute | solution.py:486
  24.5 0.7 collective-permute-start.11
  25.2 6.2 %collective-permute-done.4.refs_1_ = bf16[768,384]{1,0:T(8,128)(2,1)S(1)} collective-permute-done((bf16[768,384]{1,0:T(8,128)(2,1)S(1)}, bf16[768,384]{1,0:T(8,128)(2,1)S(1)}, u32[]{:S(2)}, u32[]{:S(2)}) %collective-permute-start.4) | collective-permute-done | bytes 589856 | tf_op jit(solution)/shard_map/ppermute | solution.py:191
  31.4 0.1 shard_map.99.refs_2_.refs_0_
  31.5 1.6 %collective-permute-start.5 = (bf16[1536,384]{1,0:T(8,128)(2,1)S(1)}, bf16[1536,384]{1,0:T(8,128)(2,1)}, u32[]{:S(2)}, u32[]{:S(2)}) collective-permute-start(bf16[1536,384]{1,0:T(8,128)(2,1)S(1)} %shard_map.99.refs_2_.refs_0_), channel_id=1, source_target_pairs={{0,16},{4,12},{8,24},{12,4},{16,0},{20,28},{24,8},{28,20},{1,17},{... | collective-permute-start | bytes 3538952 | tf_op jit(solution)/shard_map/ppermute | solution.py:191
  33.1 2.6 %shard_map.97.refs_1_.token_ref.total_ref = f32[1536,256]{1,0:T(8,128)S(1)} custom-call(bf16[6144,384]{1,0:T(8,128)(2,1)} %wq_ref.3, bf16[6144,384]{1,0:T(8,128)(2,1)} %wk_ref.3, bf16[768,256]{1,0:T(8,128)(2,1)S(1)} %shard_map.96.grads_ref.refs_1_.refs_0_), custom_call_target="tpu_custom_call" | custom-call | flops 603979776 | bytes 2359296 | tf_op jit(solution)/shard_map/pallas_call | solution.py:22
  35.7 0.9 %collective-permute-start.7 = (bf16[768,256]{1,0:T(8,128)(2,1)S(1)}, bf16[768,256]{1,0:T(8,128)(2,1)}, u32[]{:S(2)}, u32[]{:S(2)}) collective-permute-start(bf16[768,256]{1,0:T(8,128)(2,1)S(1)} %shard_map.100.own_ref), channel_id=1, source_target_pairs={{0,3},{1,0},{2,1},{3,2},{4,7},{5,4},{6,5},{7,6},{8,11},{9,8},{10,9... | collective-permute-start | bytes 1179656 | tf_op jit(solution)/shard_map/ppermute | solution.py:547
  36.6 1.2 %collective-permute-start.6 = (bf16[768,256]{1,0:T(8,128)(2,1)S(1)}, bf16[768,256]{1,0:T(8,128)(2,1)}, u32[]{:S(2)}, u32[]{:S(2)}) collective-permute-start(bf16[768,256]{1,0:T(8,128)(2,1)S(1)} %shard_map.100.own_ref), channel_id=1, source_target_pairs={{0,1},{1,2},{2,3},{3,0},{4,5},{5,6},{6,7},{7,4},{8,9},{9,10},{10,1... | collective-permute-start | bytes 1179656 | tf_op jit(solution)/shard_map/ppermute | solution.py:546
  37.8 0.0 collective-permute-done.11.both_ref
  37.8 1.3 %collective-permute-start.12 = (bf16[384,384]{1,0:T(8,128)(2,1)S(1)}, bf16[384,384]{1,0:T(8,128)(2,1)S(1)}, u32[]{:S(2)}, u32[]{:S(2)}) collective-permute-start(bf16[384,384]{1,0:T(8,128)(2,1)S(1)} %shard_map.104), channel_id=1, source_target_pairs={{2,6},{3,7},{4,0},{5,1},{10,14},{11,15},{12,8},{13,9},{18,22},{19,... | collective-permute-start | bytes 884744 | tf_op jit(solution)/shard_map/ppermute | solution.py:555
  39.1 2.2 %collective-permute-done.12.got_ref = bf16[384,384]{1,0:T(8,128)(2,1)S(1)} collective-permute-done((bf16[384,384]{1,0:T(8,128)(2,1)S(1)}, bf16[384,384]{1,0:T(8,128)(2,1)S(1)}, u32[]{:S(2)}, u32[]{:S(2)}) %collective-permute-start.12) | collective-permute-done | bytes 294944 | tf_op jit(solution)/shard_map/ppermute | solution.py:555
  41.3 0.7 %shard_map.105.refs_0_ = bf16[384,384]{1,0:T(8,128)(2,1)} custom-call(bf16[768,384]{1,0:T(8,128)(2,1)S(1)} %collective-permute-done.11.both_ref, bf16[384,384]{1,0:T(8,128)(2,1)S(1)} %collective-permute-done.12.got_ref), custom_call_target="tpu_custom_call" | custom-call | tf_op jit(solution)/shard_map/pallas_call | solution.py:22
  42.0 0.5 collective-permute-start.14
  42.5 1.5 %collective-permute-start.13 = (bf16[384,384]{1,0:T(8,128)(2,1)}, bf16[384,384]{1,0:T(8,128)(2,1)}, u32[]{:S(2)}, u32[]{:S(2)}) collective-permute-start(bf16[384,384]{1,0:T(8,128)(2,1)} %shard_map.105.refs_0_), channel_id=1, source_target_pairs={{0,8},{4,20},{8,0},{12,28},{16,24},{20,4},{24,16},{28,12},{1,9},{5... | collective-permute-start | bytes 884744 | tf_op jit(solution)/shard_map/ppermute | solution.py:191
  44.1 2.0 %collective-permute-done.7.upper_ref = bf16[768,256]{1,0:T(8,128)(2,1)} collective-permute-done((bf16[768,256]{1,0:T(8,128)(2,1)S(1)}, bf16[768,256]{1,0:T(8,128)(2,1)}, u32[]{:S(2)}, u32[]{:S(2)}) %collective-permute-start.7) | collective-permute-done | bytes 393248 | tf_op jit(solution)/shard_map/ppermute | solution.py:547
  46.1 8.0 %collective-permute-done.6.lower_ref = bf16[768,256]{1,0:T(8,128)(2,1)} collective-permute-done((bf16[768,256]{1,0:T(8,128)(2,1)S(1)}, bf16[768,256]{1,0:T(8,128)(2,1)}, u32[]{:S(2)}, u32[]{:S(2)}) %collective-permute-start.6) | collective-permute-done | bytes 393248 | tf_op jit(solution)/shard_map/ppermute | solution.py:546
  54.1 1.2 %shard_map.101 = (bf16[768,256]{1,0:T(8,128)(2,1)S(1)}, bf16[768,256]{1,0:T(8,128)(2,1)S(1)}, bf16[768,256]{1,0:T(8,128)(2,1)S(1)}) custom-call(bf16[768,256]{1,0:T(8,128)(2,1)S(1)} %shard_map.100.own_ref, bf16[768,256]{1,0:T(8,128)(2,1)} %collective-permute-done.6.lower_ref, bf16[768,256]{1,0:T(8,128)(2,1)} %collective-permute-done.7.upper_ref, ...), custom_call_target="tpu_custom_call" | custom-call | tf_op jit(solution)/shard_map/pallas_call | solution.py:22
  55.3 0.1 collective-permute-start.8
  55.4 0.0 copy-done.5
  55.4 0.0 copy-done.6
  55.4 3.8 %collective-permute-start.9 = (bf16[768,256]{1,0:T(8,128)(2,1)S(1)}, bf16[768,256]{1,0:T(8,128)(2,1)S(1)}, u32[]{:S(2)}, u32[]{:S(2)}) collective-permute-start(bf16[768,256]{1,0:T(8,128)(2,1)S(1)} %get-tuple-element.39), channel_id=1, source_target_pairs={{0,2},{1,0},{2,3},{3,1},{4,6},{5,4},{6,7},{7,5},{8,10},{9,8},{10,1... | collective-permute-start | bytes 1179656 | tf_op jit(solution)/shard_map/ppermute | solution.py:573
  59.2 0.0 collective-permute-done.14.refs_1_
  59.2 0.0 collective-permute-done.13.refs_0_
  59.2 0.5 collective-permute-start.15
  59.7 1.1 %shard_map.107 = bf16[912,384]{1,0:T(8,128)(2,1)S(1)} custom-call(bf16[384,384]{1,0:T(8,128)(2,1)} %shard_map.105.refs_0_, bf16[384,384]{1,0:T(8,128)(2,1)} %get-tuple-element.41.refs_1_, bf16[384,384]{1,0:T(8,128)(2,1)S(1)} %get-tuple-element.42.refs_2_.refs_0_), custom_call_target="tpu_custom_call" | custom-call | tf_op jit(solution)/shard_map/pallas_call | solution.py:22
  60.8 0.1 collective-permute-start.16
  60.9 0.0 collective-permute-done.8.refs_3_
  60.9 0.0 collective-permute-done.5.refs_1_
  60.9 3.6 %shard_map.102 = (f32[1536,256]{1,0:T(8,128)S(1)}, bf16[1152,256]{1,0:T(8,128)(2,1)S(1)}, bf16[384,256]{1,0:T(8,128)(2,1)S(1)}) custom-call(s32[4]{0:T(128)S(1)} %and_select_fusion.table_ref, f32[1536,256]{1,0:T(8,128)S(1)} %shard_map.97.refs_1_.token_ref.total_ref, bf16[1536,384]{1,0:T(8,128)(2,1)S(1)} %shard_map.99.refs_2_.refs_0_, ...), custom_call_target="tpu_custom_call" | custom-call | flops 1207959552 | bytes 3932160 | tf_op jit(solution)/shard_map/pallas_call | solution.py:22
  64.6 0.6 collective-permute-start.18
  65.1 3.1 %collective-permute-done.9.grads_ref.refs_2_ = bf16[768,256]{1,0:T(8,128)(2,1)S(1)} collective-permute-done((bf16[768,256]{1,0:T(8,128)(2,1)S(1)}, bf16[768,256]{1,0:T(8,128)(2,1)S(1)}, u32[]{:S(2)}, u32[]{:S(2)}) %collective-permute-start.9) | collective-permute-done | bytes 393248 | tf_op jit(solution)/shard_map/ppermute | solution.py:573
  68.2 0.0 collective-permute-done.15.refs_3_.refs_1_
  68.3 0.1 collective-permute-start.17
  68.3 0.5 collective-permute-start.19
  68.8 0.0 collective-permute-done.16.refs_4_.refs_0_
  68.8 1.9 %shard_map.108.total_ref = f32[1536,256]{1,0:T(8,128)S(1)} custom-call(s32[8]{0:T(128)S(1)} %fusion.table_ref, f32[1536,256]{1,0:T(8,128)S(1)} %get-tuple-element.38.total_ref, bf16[768,256]{1,0:T(8,128)(2,1)S(1)} %collective-permute-done.9.grads_ref.refs_2_, bf16[384,384]{1,0:T(8,128)(2,1)} %shard_map.105.refs_0_, ...), custom_call_target="tpu_custom_call" | custom-call | flops 603979776 | bytes 3145728 | tf_op jit(solution)/shard_map/pallas_call | solution.py:22
  70.7 0.0 collective-permute-done.17.refs_1_
  70.8 0.0 collective-permute-done.19.refs_3_
  70.8 0.0 collective-permute-done.18.refs_2_
  70.8 1.9 %shard_map.110 = bf16[1536,256]{1,0:T(8,128)(2,1)} custom-call(s32[8]{0:T(128)S(1)} %fusion.table_ref, f32[1536,256]{1,0:T(8,128)S(1)} %shard_map.108.total_ref, bf16[768,256]{1,0:T(8,128)(2,1)S(1)} %collective-permute-done.9.grads_ref.refs_2_, bf16[912,384]{1,0:T(8,128)(2,1)S(1)} %collective-permute-done.16.refs_4_.refs_0_, ...), custom_call_target="tpu_custom_call" | custom-call | flops 603979776 | bytes 3145728 | tf_op jit(solution)/shard_map/pallas_call | solution.py:22
  (12 shorter events, 0.1 us)
Async XLA Ops:
  0.0 4.5 %copy-start.1 = (bf16[256,384]{1,0:T(8,128)(2,1)S(1)}, bf16[256,384]{1,0:T(8,128)(2,1)}, u32[]{:S(2)}) copy-start(bf16[256,384]{1,0:T(8,128)(2,1)} %g_ref.5) | copy-start | bytes 589828
  0.0 4.5 %copy-start = (bf16[256,384]{1,0:T(8,128)(2,1)S(1)}, bf16[256,384]{1,0:T(8,128)(2,1)}, u32[]{:S(2)}) copy-start(bf16[256,384]{1,0:T(8,128)(2,1)} %v_ref.5) | copy-start | bytes 589828
  0.0 4.5 %copy-start.3 = (bf16[256,384]{1,0:T(8,128)(2,1)S(1)}, bf16[256,384]{1,0:T(8,128)(2,1)}, u32[]{:S(2)}) copy-start(bf16[256,384]{1,0:T(8,128)(2,1)} %k_ref.3) | copy-start | bytes 589828
  0.0 4.5 %copy-start.2 = (bf16[256,384]{1,0:T(8,128)(2,1)S(1)}, bf16[256,384]{1,0:T(8,128)(2,1)}, u32[]{:S(2)}) copy-start(bf16[256,384]{1,0:T(8,128)(2,1)} %q_ref.3) | copy-start | bytes 589828
  0.0 4.5 %copy-start.4 = (f32[256,3]{0,1:T(4,128)S(1)}, f32[256,3]{0,1:T(4,128)}, u32[]{:S(2)}) copy-start(f32[256,3]{0,1:T(4,128)} %param.13) | copy-start | bytes 9220
  1.4 20.0 %collective-permute-start.3 = (bf16[768,384]{1,0:T(8,128)(2,1)S(1)}, bf16[768,384]{1,0:T(8,128)(2,1)S(1)}, u32[]{:S(2)}, u32[]{:S(2)}) collective-permute-start(bf16[768,384]{1,0:T(8,128)(2,1)S(1)} %get-tuple-element.25.token_ref), channel_id=1, source_target_pairs={{0,1},{1,2},{2,3},{3,0},{4,7},{5,4},{6,5},{7,6},{8,9},{9,10},{10,1... | collective-permute-start | bytes 1769480 | tf_op jit(solution)/shard_map/ppermute | solution.py:485
  5.4 2.7 %collective-permute-start = (bf16[784,128]{1,0:T(8,128)(2,1)S(1)}, bf16[784,128]{1,0:T(8,128)(2,1)S(1)}, u32[]{:S(2)}, u32[]{:S(2)}) collective-permute-start(bf16[784,128]{1,0:T(8,128)(2,1)S(1)} %get-tuple-element.26), channel_id=1, source_target_pairs={{0,4},{4,0},{8,12},{12,8},{16,20},{20,16},{24,28},{28,24},{1,5},{5... | collective-permute-start | bytes 602120 | tf_op jit(solution)/shard_map/ppermute | solution.py:511
  8.2 7.3 %collective-permute-start.1 = (bf16[784,128]{1,0:T(8,128)(2,1)S(1)}, bf16[784,128]{1,0:T(8,128)(2,1)S(1)}, u32[]{:S(2)}, u32[]{:S(2)}) collective-permute-start(bf16[784,128]{1,0:T(8,128)(2,1)S(1)} %get-tuple-element.29), channel_id=1, source_target_pairs={{0,8},{4,12},{8,0},{12,4},{16,24},{20,28},{24,16},{28,20},{1,9},{5... | collective-permute-start | bytes 602120 | tf_op jit(solution)/shard_map/ppermute | solution.py:511
  9.8 14.8 %collective-permute-start.10 = (bf16[768,384]{1,0:T(8,128)(2,1)S(1)}, bf16[768,384]{1,0:T(8,128)(2,1)S(1)}, u32[]{:S(2)}, u32[]{:S(2)}) collective-permute-start(bf16[768,384]{1,0:T(8,128)(2,1)S(1)} %get-tuple-element.40), channel_id=1, source_target_pairs={{0,1},{1,2},{7,6},{6,5},{8,9},{9,10},{15,14},{14,13},{16,17},{17,1... | collective-permute-start | bytes 1769480 | tf_op jit(solution)/shard_map/ppermute | solution.py:486
  16.3 4.6 %collective-permute-start.2 = (bf16[384,128]{1,0:T(8,128)(2,1)S(1)}, bf16[384,128]{1,0:T(8,128)(2,1)S(1)}, u32[]{:S(2)}, u32[]{:S(2)}) collective-permute-start(bf16[384,128]{1,0:T(8,128)(2,1)S(1)} %get-tuple-element.33), channel_id=1, source_target_pairs={{0,16},{4,20},{8,24},{12,28},{16,0},{20,4},{24,8},{28,12},{1,17},{... | collective-permute-start | bytes 294920 | tf_op jit(solution)/shard_map/ppermute | solution.py:511
  21.4 9.9 %collective-permute-start.4 = (bf16[768,384]{1,0:T(8,128)(2,1)S(1)}, bf16[768,384]{1,0:T(8,128)(2,1)S(1)}, u32[]{:S(2)}, u32[]{:S(2)}) collective-permute-start(bf16[768,384]{1,0:T(8,128)(2,1)S(1)} %shard_map.98.refs_0_.refs_1_), channel_id=1, source_target_pairs={{0,8},{4,20},{8,0},{12,28},{16,24},{20,4},{24,16},{28,12},{1,9},{5... | collective-permute-start | bytes 1769480 | tf_op jit(solution)/shard_map/ppermute | solution.py:191
  24.5 13.3 %collective-permute-start.11 = (bf16[768,384]{1,0:T(8,128)(2,1)S(1)}, bf16[768,384]{1,0:T(8,128)(2,1)S(1)}, u32[]{:S(2)}, u32[]{:S(2)}) collective-permute-start(bf16[768,384]{1,0:T(8,128)(2,1)S(1)} %shard_map.103), channel_id=1, source_target_pairs={{1,2},{2,3},{6,5},{5,4},{9,10},{10,11},{14,13},{13,12},{17,18},{18... | collective-permute-start | bytes 1769480 | tf_op jit(solution)/shard_map/ppermute | solution.py:549
  31.5 29.5 %collective-permute-start.5 = (bf16[1536,384]{1,0:T(8,128)(2,1)S(1)}, bf16[1536,384]{1,0:T(8,128)(2,1)}, u32[]{:S(2)}, u32[]{:S(2)}) collective-permute-start(bf16[1536,384]{1,0:T(8,128)(2,1)S(1)} %shard_map.99.refs_2_.refs_0_), channel_id=1, source_target_pairs={{0,16},{4,12},{8,24},{12,4},{16,0},{20,28},{24,8},{28,20},{1,17},{... | collective-permute-start | bytes 3538952 | tf_op jit(solution)/shard_map/ppermute | solution.py:191
  35.7 10.4 %collective-permute-start.7 = (bf16[768,256]{1,0:T(8,128)(2,1)S(1)}, bf16[768,256]{1,0:T(8,128)(2,1)}, u32[]{:S(2)}, u32[]{:S(2)}) collective-permute-start(bf16[768,256]{1,0:T(8,128)(2,1)S(1)} %shard_map.100.own_ref), channel_id=1, source_target_pairs={{0,3},{1,0},{2,1},{3,2},{4,7},{5,4},{6,5},{7,6},{8,11},{9,8},{10,9... | collective-permute-start | bytes 1179656 | tf_op jit(solution)/shard_map/ppermute | solution.py:547
  36.6 17.5 %collective-permute-start.6 = (bf16[768,256]{1,0:T(8,128)(2,1)S(1)}, bf16[768,256]{1,0:T(8,128)(2,1)}, u32[]{:S(2)}, u32[]{:S(2)}) collective-permute-start(bf16[768,256]{1,0:T(8,128)(2,1)S(1)} %shard_map.100.own_ref), channel_id=1, source_target_pairs={{0,1},{1,2},{2,3},{3,0},{4,5},{5,6},{6,7},{7,4},{8,9},{9,10},{10,1... | collective-permute-start | bytes 1179656 | tf_op jit(solution)/shard_map/ppermute | solution.py:546
  37.8 3.5 %collective-permute-start.12 = (bf16[384,384]{1,0:T(8,128)(2,1)S(1)}, bf16[384,384]{1,0:T(8,128)(2,1)S(1)}, u32[]{:S(2)}, u32[]{:S(2)}) collective-permute-start(bf16[384,384]{1,0:T(8,128)(2,1)S(1)} %shard_map.104), channel_id=1, source_target_pairs={{2,6},{3,7},{4,0},{5,1},{10,14},{11,15},{12,8},{13,9},{18,22},{19,... | collective-permute-start | bytes 884744 | tf_op jit(solution)/shard_map/ppermute | solution.py:555
  42.0 13.3 %copy-start.5 = (s32[8]{0:T(128)S(1)}, s32[8]{0:T(128)}, u32[]{:S(2)}) copy-start(s32[8]{0:T(128)} %constant.36.clone) | copy-start | bytes 100
  42.0 13.3 %copy-start.6 = (s32[8]{0:T(128)S(1)}, s32[8]{0:T(128)}, u32[]{:S(2)}) copy-start(s32[8]{0:T(128)} %constant.35.clone) | copy-start | bytes 100
  42.0 17.2 %collective-permute-start.14 = (bf16[384,384]{1,0:T(8,128)(2,1)}, bf16[384,384]{1,0:T(8,128)(2,1)S(1)}, u32[]{:S(2)}, u32[]{:S(2)}) collective-permute-start(bf16[384,384]{1,0:T(8,128)(2,1)} %shard_map.105.refs_0_), channel_id=1, source_target_pairs={{0,16},{4,12},{8,24},{12,4},{16,0},{20,28},{24,8},{28,20},{1,17},{... | collective-permute-start | bytes 884744 | tf_op jit(solution)/shard_map/ppermute | solution.py:191
  42.5 16.7 %collective-permute-start.13 = (bf16[384,384]{1,0:T(8,128)(2,1)}, bf16[384,384]{1,0:T(8,128)(2,1)}, u32[]{:S(2)}, u32[]{:S(2)}) collective-permute-start(bf16[384,384]{1,0:T(8,128)(2,1)} %shard_map.105.refs_0_), channel_id=1, source_target_pairs={{0,8},{4,20},{8,0},{12,28},{16,24},{20,4},{24,16},{28,12},{1,9},{5... | collective-permute-start | bytes 884744 | tf_op jit(solution)/shard_map/ppermute | solution.py:191
  55.3 5.7 %collective-permute-start.8 = (bf16[768,256]{1,0:T(8,128)(2,1)S(1)}, bf16[768,256]{1,0:T(8,128)(2,1)S(1)}, u32[]{:S(2)}, u32[]{:S(2)}) collective-permute-start(bf16[768,256]{1,0:T(8,128)(2,1)S(1)} %get-tuple-element.37), channel_id=1, source_target_pairs={{0,4},{4,0},{8,12},{12,8},{16,20},{20,16},{24,28},{28,24},{1,5},{5... | collective-permute-start | bytes 1179656 | tf_op jit(solution)/shard_map/ppermute | solution.py:191
  55.4 12.8 %collective-permute-start.9 = (bf16[768,256]{1,0:T(8,128)(2,1)S(1)}, bf16[768,256]{1,0:T(8,128)(2,1)S(1)}, u32[]{:S(2)}, u32[]{:S(2)}) collective-permute-start(bf16[768,256]{1,0:T(8,128)(2,1)S(1)} %get-tuple-element.39), channel_id=1, source_target_pairs={{0,2},{1,0},{2,3},{3,1},{4,6},{5,4},{6,7},{7,5},{8,10},{9,8},{10,1... | collective-permute-start | bytes 1179656 | tf_op jit(solution)/shard_map/ppermute | solution.py:573
  59.2 9.0 %collective-permute-start.15 = (bf16[384,384]{1,0:T(8,128)(2,1)}, bf16[384,384]{1,0:T(8,128)(2,1)S(1)}, u32[]{:S(2)}, u32[]{:S(2)}) collective-permute-start(bf16[384,384]{1,0:T(8,128)(2,1)} %get-tuple-element.41.refs_1_), channel_id=1, source_target_pairs={{0,16},{4,12},{8,24},{12,4},{16,0},{20,28},{24,8},{28,20},{1,17},{... | collective-permute-start | bytes 884744 | tf_op jit(solution)/shard_map/ppermute | solution.py:191
  60.8 8.0 %collective-permute-start.16 = (bf16[912,384]{1,0:T(8,128)(2,1)S(1)}, bf16[912,384]{1,0:T(8,128)(2,1)S(1)}, u32[]{:S(2)}, u32[]{:S(2)}) collective-permute-start(bf16[912,384]{1,0:T(8,128)(2,1)S(1)} %shard_map.107), channel_id=1, source_target_pairs={{0,4},{4,0},{8,12},{12,8},{16,20},{20,16},{24,28},{28,24},{1,5},{5... | collective-permute-start | bytes 2101256 | tf_op jit(solution)/shard_map/ppermute | solution.py:191
  64.6 6.2 %collective-permute-start.18 = (bf16[1152,256]{1,0:T(8,128)(2,1)S(1)}, bf16[1152,256]{1,0:T(8,128)(2,1)S(1)}, u32[]{:S(2)}, u32[]{:S(2)}) collective-permute-start(bf16[1152,256]{1,0:T(8,128)(2,1)S(1)} %get-tuple-element.43), channel_id=1, source_target_pairs={{0,4},{4,0},{8,12},{12,8},{16,20},{20,16},{24,28},{28,24},{1,5},{5... | collective-permute-start | bytes 1769480 | tf_op jit(solution)/shard_map/ppermute | solution.py:191
  68.3 2.5 %collective-permute-start.17 = (bf16[624,384]{1,0:T(8,128)(2,1)S(1)}, bf16[624,384]{1,0:T(8,128)(2,1)S(1)}, u32[]{:S(2)}, u32[]{:S(2)}) collective-permute-start(bf16[624,384]{1,0:T(8,128)(2,1)S(1)} %shard_map.109), channel_id=1, source_target_pairs={{0,4},{4,0},{8,12},{12,8},{16,20},{20,16},{24,28},{28,24},{1,5},{5... | collective-permute-start | bytes 1437704 | tf_op jit(solution)/shard_map/ppermute | solution.py:191
  68.3 2.4 %collective-permute-start.19 = (bf16[384,256]{1,0:T(8,128)(2,1)S(1)}, bf16[384,256]{1,0:T(8,128)(2,1)S(1)}, u32[]{:S(2)}, u32[]{:S(2)}) collective-permute-start(bf16[384,256]{1,0:T(8,128)(2,1)S(1)} %get-tuple-element.44), channel_id=1, source_target_pairs={{0,4},{4,0},{8,12},{12,8},{16,20},{20,16},{24,28},{28,24},{1,5},{5... | collective-permute-start | bytes 589832 | tf_op jit(solution)/shard_map/ppermute | solution.py:191

commit v7 on v6

--- a/solution.py
+++ b/solution.py
@@ -371,13 +371,13 @@
     upper = lax.axis_index("head") // 2
     share = out_ref.shape[0] // 2
 
-    @pl.when(odd + upper != 1)
+    @pl.when(odd != upper)
     def _():
         out_ref[...] = got_ref[...]
 
     for parity in range(2):
 
-        @pl.when((odd == parity) & (upper == 1 - parity))
+        @pl.when((odd == parity) & (upper == parity))
         def _():
             for j in range(2):
                 at = (2 * j + parity) * share
@@ -483,7 +483,7 @@
 
         axes = ("seq", "head")
         first = lax.ppermute(packed[0], axes, moves(ring[1], ring[3]))
-        passing = lax.ppermute(packed[1], axes, moves([(0, 1), (1, 2)], [(3, 2), (2, 1)]))
+        passing = lax.ppermute(packed[1], axes, moves([(3, 2), (2, 1)], [(0, 1), (1, 2)]))
     else:
         packed = pack_weights(w_query, w_key, [(k, k, 1) for k in shifts], share)
         pieces = [lax.ppermute(p, "head", ring[k]) for p, k in zip(packed, shifts)]
@@ -546,7 +546,7 @@
         p1 = lax.ppermute(ready, "head", ring[1])
         p3 = lax.ppermute(ready, "head", ring[3])
         (passing,) = gate([passing], [first])
-        passing = lax.ppermute(passing, axes, moves([(1, 2), (2, 3)], [(2, 1), (1, 0)]))
+        passing = lax.ppermute(passing, axes, moves([(2, 1), (1, 0)], [(1, 2), (2, 3)]))
         theirs = call(
             split_kernel, jax.ShapeDtypeStruct((one, passing.shape[1]), BF16), 0, 0, passing, total,
             in_specs=[pl.BlockSpec(memory_space=pltpu.VMEM), pl.BlockSpec(memory_space=pl.ANY)],
@@ -554,7 +554,7 @@
         )
         theirs = lax.ppermute(
             theirs, axes,
-            [(i * nhead + j, (i ^ 1) * nhead + j) for i in range(nseq) for j in range(nhead) if (j < 2) == (i % 2)],
+            [(i * nhead + j, (i ^ 1) * nhead + j) for i in range(nseq) for j in range(nhead) if (j >= 2) == (i % 2)],
         )
         third = call(
             pick_kernel, jax.ShapeDtypeStruct(theirs.shape, BF16), 0, 0, passing, theirs,

time: 73 us -> 71.1 us (0.974)
  starting transfers between devices: 24.9 us -> 23.6 us
    ppermute x1, waiting for transfers between devices: 2.03 us -> 5.58 us  [shards(): p3 = lax.ppermute(ready, 'head', ring[3])]
    ppermute x1, waiting for transfers between devices: 7.98 us -> 4.83 us  [shards(): p1 = lax.ppermute(ready, 'head', ring[1])]
    ppermute x3, waiting for transfers between devices: 6.6 us -> 8.2 us  [shards(): got = lax.ppermute(sent, 'seq', [(i, i ^ hop) for i in range(nseq)])]
    ppermute x2, waiting for transfers between devices: 1.53 us -> 0.01 us  [the longest x1 0.01 us: shards(): lax.ppermute(packed[1], axes, moves([(3, 2), (2, 1)], [(0, 1), (1, 2)]))]
    ppermute x1, starting transfers between devices: 3.81 us -> 2.48 us  [shards(): p2 = lax.ppermute(relay, 'head', [(0, 2), (1, 0), (2, 3), (3, 1)])]
    ppermute x1, waiting for transfers between devices: 2.18 us -> 1.17 us  [shards(): lax.ppermute(theirs, axes, [(i * nhead + j, (i ^ 1) * nhead + j) for i in...]
    ppermute x2, starting transfers between devices: 2.97 us -> 1.97 us  [the longest x1 1.28 us: shards(): lax.ppermute(passing, axes, moves([(2, 1), (1, 0)], [(1, 2), (2, 3)]))]
    ppermute x10, starting transfers between devices: 6.93 us -> 7.92 us  [share_hop(): return lax.ppermute(held, 'seq', pairs)]
  transfers between devices with their start and end apart: 20 -> 20, of which waited for: 9 -> 8; matrix products, arithmetic and copies ran while one was open for 0% -> 0% of each run, Pallas kernels for 20% -> 21%
where the time goes in v7:
time: 71.1 us; the launch traced here: 70.8 us
  waiting for transfers between devices  29 us (41%)
  starting transfers between devices  23.6 us (33%)
  Pallas kernels  17.9 us (25%)
    pallas_call x20, Pallas kernels, call(): pl.pallas_call(kernel, out_shape=out_shape, cost_estimate=pl.CostEstimate...  17.9 us
    ppermute x3, waiting for transfers between devices, shards(): got = lax.ppermute(sent, 'seq', [(i, i ^ hop) for i in range(nseq)])  8.2 us
    ppermute x10, starting transfers between devices, share_hop(): return lax.ppermute(held, 'seq', pairs)  7.92 us
    ppermute x10, waiting for transfers between devices, share_hop(): return lax.ppermute(held, 'seq', pairs)  7.12 us
    ppermute x1, waiting for transfers between devices, shards(): p3 = lax.ppermute(ready, 'head', ring[3])  5.58 us
    ppermute x1, waiting for transfers between devices, shards(): p1 = lax.ppermute(ready, 'head', ring[1])  4.83 us
    ppermute x3, starting transfers between devices, shards(): got = lax.ppermute(sent, 'seq', [(i, i ^ hop) for i in range(nseq)])  4.73 us
    ppermute x1, starting transfers between devices, shards(): first = lax.ppermute(packed[0], axes, moves(ring[1], ring[3]))  3.09 us
  transfers between devices with their start and end apart: 20, of which 8 were waited for; matrix products, arithmetic and copies ran while one was open for 0% of the time, Pallas kernels for 21%

profile of v7, /device:TPU:0, one launch (start us, length us, event | category | flops | bytes accessed | tf_op | source)
XLA Modules:
  0.0 70.8 jit_solution(12288544867476905657)
XLA Ops:
  0.0 0.0 copy-start.1
  0.0 0.0 copy-start
  0.0 0.0 copy-start.3
  0.0 1.4 %shard_map.91 = (bf16[768,384]{1,0:T(8,128)(2,1)S(1)}, bf16[768,384]{1,0:T(8,128)(2,1)S(1)}) custom-call(bf16[6144,384]{1,0:T(8,128)(2,1)} %wq_ref.3, bf16[6144,384]{1,0:T(8,128)(2,1)} %wk_ref.3), custom_call_target="tpu_custom_call" | custom-call | bytes 2359296 | tf_op jit(solution)/shard_map/pallas_call | solution.py:22
  1.4 3.1 %collective-permute-start.3 = (bf16[768,384]{1,0:T(8,128)(2,1)S(1)}, bf16[768,384]{1,0:T(8,128)(2,1)S(1)}, u32[]{:S(2)}, u32[]{:S(2)}) collective-permute-start(bf16[768,384]{1,0:T(8,128)(2,1)S(1)} %get-tuple-element.25.token_ref), channel_id=1, source_target_pairs={{0,1},{1,2},{2,3},{3,0},{4,7},{5,4},{6,5},{7,6},{8,9},{9,10},{10,1... | collective-permute-start | bytes 1769480 | tf_op jit(solution)/shard_map/ppermute | solution.py:485
  4.5 0.0 copy-done.1
  4.5 0.0 copy-done
  4.5 0.0 copy-done.3
  4.5 0.0 copy-done.2
  4.5 0.0 copy-done.4
  4.5 0.9 %shard_map.92 = (bf16[784,128]{1,0:T(8,128)(2,1)S(1)}, f32[768,128]{1,0:T(8,128)S(1)}, f32[24,128]{1,0:T(8,128)S(1)}) custom-call(f32[3,256]{1,0:T(4,128)S(1)} %bitcast.1, bf16[256,384]{1,0:T(8,128)(2,1)S(1)} %copy-done.2, bf16[256,384]{1,0:T(8,128)(2,1)S(1)} %copy-done.3, bf16[256,384]{1,0:T(8,128)(2,1)S(1)} %copy-done, bf16[256,384]{1,0:T(8,128)(2,1)S(1)} %copy-done.1, ...), custom_call_target="tpu_custom_call" | custom-call | flops 50331648 | bytes 786432 | tf_op jit(solution)/shard_map/pallas_call | solution.py:22
  5.4 1.6 %collective-permute-start = (bf16[784,128]{1,0:T(8,128)(2,1)S(1)}, bf16[784,128]{1,0:T(8,128)(2,1)S(1)}, u32[]{:S(2)}, u32[]{:S(2)}) collective-permute-start(bf16[784,128]{1,0:T(8,128)(2,1)S(1)} %get-tuple-element.26), channel_id=1, source_target_pairs={{0,4},{4,0},{8,12},{12,8},{16,20},{20,16},{24,28},{28,24},{1,5},{5... | collective-permute-start | bytes 602120 | tf_op jit(solution)/shard_map/ppermute | solution.py:511
  7.0 1.1 %collective-permute-done.got_ref = bf16[784,128]{1,0:T(8,128)(2,1)S(1)} collective-permute-done((bf16[784,128]{1,0:T(8,128)(2,1)S(1)}, bf16[784,128]{1,0:T(8,128)(2,1)S(1)}, u32[]{:S(2)}, u32[]{:S(2)}) %collective-permute-start) | collective-permute-done | bytes 200736 | tf_op jit(solution)/shard_map/ppermute | solution.py:511
  8.1 0.1 shard_map.93
  8.2 1.6 %collective-permute-start.1 = (bf16[784,128]{1,0:T(8,128)(2,1)S(1)}, bf16[784,128]{1,0:T(8,128)(2,1)S(1)}, u32[]{:S(2)}, u32[]{:S(2)}) collective-permute-start(bf16[784,128]{1,0:T(8,128)(2,1)S(1)} %get-tuple-element.29), channel_id=1, source_target_pairs={{0,8},{4,12},{8,0},{12,4},{16,24},{20,28},{24,16},{28,20},{1,9},{5... | collective-permute-start | bytes 602120 | tf_op jit(solution)/shard_map/ppermute | solution.py:511
  9.8 0.7 collective-permute-start.10
  10.4 5.1 %collective-permute-done.1.got_ref = bf16[784,128]{1,0:T(8,128)(2,1)S(1)} collective-permute-done((bf16[784,128]{1,0:T(8,128)(2,1)S(1)}, bf16[784,128]{1,0:T(8,128)(2,1)S(1)}, u32[]{:S(2)}, u32[]{:S(2)}) %collective-permute-start.1) | collective-permute-done | bytes 200736 | tf_op jit(solution)/shard_map/ppermute | solution.py:511
  15.5 0.8 %shard_map.94 = (bf16[384,128]{1,0:T(8,128)(2,1)S(1)}, f32[768,128]{1,0:T(8,128)}, f32[24,128]{1,0:T(8,128)S(1)}, f32[768,128]{1,0:T(8,128)S(1)}) custom-call(bf16[784,128]{1,0:T(8,128)(2,1)S(1)} %collective-permute-done.1.got_ref, f32[768,128]{1,0:T(8,128)S(1)} %get-tuple-element.30.held_ref, f32[24,128]{1,0:T(8,128)S(1)} %get-tuple-element.31.logs_ref, ...), custom_call_target="tpu_custom_call" | custom-call | flops 491520 | bytes 786432 | tf_op jit(solution)/shard_map/pallas_call | solution.py:22
  16.3 1.5 %collective-permute-start.2 = (bf16[384,128]{1,0:T(8,128)(2,1)S(1)}, bf16[384,128]{1,0:T(8,128)(2,1)S(1)}, u32[]{:S(2)}, u32[]{:S(2)}) collective-permute-start(bf16[384,128]{1,0:T(8,128)(2,1)S(1)} %get-tuple-element.33), channel_id=1, source_target_pairs={{0,16},{4,20},{8,24},{12,28},{16,0},{20,4},{24,8},{28,12},{1,17},{... | collective-permute-start | bytes 294920 | tf_op jit(solution)/shard_map/ppermute | solution.py:511
  17.9 1.0 %shard_map.95.local_ref = f32[768,256]{1,0:T(8,128)S(1)} custom-call(f32[3,256]{1,0:T(4,128)S(1)} %bitcast.2, bf16[256,384]{1,0:T(8,128)(2,1)S(1)} %copy-done.2, bf16[256,384]{1,0:T(8,128)(2,1)S(1)} %copy-done.3, bf16[256,384]{1,0:T(8,128)(2,1)S(1)} %copy-done, bf16[256,384]{1,0:T(8,128)(2,1)S(1)} %copy-done.1), custom_call_target="tpu_custom_call" | custom-call | flops 150994944 | bytes 1572864 | tf_op jit(solution)/shard_map/pallas_call | solution.py:22
  18.9 2.1 %collective-permute-done.2.got_ref = bf16[384,128]{1,0:T(8,128)(2,1)S(1)} collective-permute-done((bf16[384,128]{1,0:T(8,128)(2,1)S(1)}, bf16[384,128]{1,0:T(8,128)(2,1)S(1)}, u32[]{:S(2)}, u32[]{:S(2)}) %collective-permute-start.2) | collective-permute-done | bytes 98336 | tf_op jit(solution)/shard_map/ppermute | solution.py:511
  21.0 0.4 shard_map.96.grads_ref.refs_1_.refs_0_
  21.4 0.0 collective-permute-done.3.refs_0_
  21.4 1.6 %collective-permute-start.4 = (bf16[768,384]{1,0:T(8,128)(2,1)S(1)}, bf16[768,384]{1,0:T(8,128)(2,1)S(1)}, u32[]{:S(2)}, u32[]{:S(2)}) collective-permute-start(bf16[768,384]{1,0:T(8,128)(2,1)S(1)} %shard_map.98.refs_0_.refs_1_), channel_id=1, source_target_pairs={{0,8},{4,20},{8,0},{12,28},{16,24},{20,4},{24,16},{28,12},{1,9},{5... | collective-permute-start | bytes 1769480 | tf_op jit(solution)/shard_map/ppermute | solution.py:191
  23.0 0.0 collective-permute-done.10.refs_0_
  23.0 1.3 %collective-permute-start.11 = (bf16[768,384]{1,0:T(8,128)(2,1)S(1)}, bf16[768,384]{1,0:T(8,128)(2,1)S(1)}, u32[]{:S(2)}, u32[]{:S(2)}) collective-permute-start(bf16[768,384]{1,0:T(8,128)(2,1)S(1)} %shard_map.103), channel_id=1, source_target_pairs={{2,1},{1,0},{5,6},{6,7},{10,9},{9,8},{13,14},{14,15},{18,17},{17,1... | collective-permute-start | bytes 1769480 | tf_op jit(solution)/shard_map/ppermute | solution.py:549
  24.3 7.1 %collective-permute-done.4.refs_1_ = bf16[768,384]{1,0:T(8,128)(2,1)S(1)} collective-permute-done((bf16[768,384]{1,0:T(8,128)(2,1)S(1)}, bf16[768,384]{1,0:T(8,128)(2,1)S(1)}, u32[]{:S(2)}, u32[]{:S(2)}) %collective-permute-start.4) | collective-permute-done | bytes 589856 | tf_op jit(solution)/shard_map/ppermute | solution.py:191
  31.4 0.1 shard_map.99.refs_2_.refs_0_
  31.5 1.6 %collective-permute-start.5 = (bf16[1536,384]{1,0:T(8,128)(2,1)S(1)}, bf16[1536,384]{1,0:T(8,128)(2,1)}, u32[]{:S(2)}, u32[]{:S(2)}) collective-permute-start(bf16[1536,384]{1,0:T(8,128)(2,1)S(1)} %shard_map.99.refs_2_.refs_0_), channel_id=1, source_target_pairs={{0,16},{4,12},{8,24},{12,4},{16,0},{20,28},{24,8},{28,20},{1,17},{... | collective-permute-start | bytes 3538952 | tf_op jit(solution)/shard_map/ppermute | solution.py:191
  33.1 2.6 %shard_map.97.refs_1_.token_ref.total_ref = f32[1536,256]{1,0:T(8,128)S(1)} custom-call(bf16[6144,384]{1,0:T(8,128)(2,1)} %wq_ref.3, bf16[6144,384]{1,0:T(8,128)(2,1)} %wk_ref.3, bf16[768,256]{1,0:T(8,128)(2,1)S(1)} %shard_map.96.grads_ref.refs_1_.refs_0_), custom_call_target="tpu_custom_call" | custom-call | flops 603979776 | bytes 2359296 | tf_op jit(solution)/shard_map/pallas_call | solution.py:22
  35.7 1.3 %collective-permute-start.7 = (bf16[768,256]{1,0:T(8,128)(2,1)S(1)}, bf16[768,256]{1,0:T(8,128)(2,1)}, u32[]{:S(2)}, u32[]{:S(2)}) collective-permute-start(bf16[768,256]{1,0:T(8,128)(2,1)S(1)} %shard_map.100.own_ref), channel_id=1, source_target_pairs={{0,3},{1,0},{2,1},{3,2},{4,7},{5,4},{6,5},{7,6},{8,11},{9,8},{10,9... | collective-permute-start | bytes 1179656 | tf_op jit(solution)/shard_map/ppermute | solution.py:547
  37.0 0.8 %collective-permute-start.6 = (bf16[768,256]{1,0:T(8,128)(2,1)S(1)}, bf16[768,256]{1,0:T(8,128)(2,1)}, u32[]{:S(2)}, u32[]{:S(2)}) collective-permute-start(bf16[768,256]{1,0:T(8,128)(2,1)S(1)} %shard_map.100.own_ref), channel_id=1, source_target_pairs={{0,1},{1,2},{2,3},{3,0},{4,5},{5,6},{6,7},{7,4},{8,9},{9,10},{10,1... | collective-permute-start | bytes 1179656 | tf_op jit(solution)/shard_map/ppermute | solution.py:546
  37.8 0.0 collective-permute-done.11.both_ref
  37.8 1.3 %collective-permute-start.12 = (bf16[384,384]{1,0:T(8,128)(2,1)S(1)}, bf16[384,384]{1,0:T(8,128)(2,1)S(1)}, u32[]{:S(2)}, u32[]{:S(2)}) collective-permute-start(bf16[384,384]{1,0:T(8,128)(2,1)S(1)} %shard_map.104), channel_id=1, source_target_pairs={{0,4},{1,5},{6,2},{7,3},{8,12},{9,13},{14,10},{15,11},{16,20},{17,... | collective-permute-start | bytes 884744 | tf_op jit(solution)/shard_map/ppermute | solution.py:555
  39.1 1.2 %collective-permute-done.12.got_ref = bf16[384,384]{1,0:T(8,128)(2,1)S(1)} collective-permute-done((bf16[384,384]{1,0:T(8,128)(2,1)S(1)}, bf16[384,384]{1,0:T(8,128)(2,1)S(1)}, u32[]{:S(2)}, u32[]{:S(2)}) %collective-permute-start.12) | collective-permute-done | bytes 294944 | tf_op jit(solution)/shard_map/ppermute | solution.py:555
  40.3 0.7 %shard_map.105.refs_0_ = bf16[384,384]{1,0:T(8,128)(2,1)} custom-call(bf16[768,384]{1,0:T(8,128)(2,1)S(1)} %collective-permute-done.11.both_ref, bf16[384,384]{1,0:T(8,128)(2,1)S(1)} %collective-permute-done.12.got_ref), custom_call_target="tpu_custom_call" | custom-call | tf_op jit(solution)/shard_map/pallas_call | solution.py:22
  41.0 0.5 collective-permute-start.14
  41.6 1.5 %collective-permute-start.13 = (bf16[384,384]{1,0:T(8,128)(2,1)}, bf16[384,384]{1,0:T(8,128)(2,1)}, u32[]{:S(2)}, u32[]{:S(2)}) collective-permute-start(bf16[384,384]{1,0:T(8,128)(2,1)} %shard_map.105.refs_0_), channel_id=1, source_target_pairs={{0,8},{4,20},{8,0},{12,28},{16,24},{20,4},{24,16},{28,12},{1,9},{5... | collective-permute-start | bytes 884744 | tf_op jit(solution)/shard_map/ppermute | solution.py:191
  43.0 5.6 %collective-permute-done.7.upper_ref = bf16[768,256]{1,0:T(8,128)(2,1)} collective-permute-done((bf16[768,256]{1,0:T(8,128)(2,1)S(1)}, bf16[768,256]{1,0:T(8,128)(2,1)}, u32[]{:S(2)}, u32[]{:S(2)}) %collective-permute-start.7) | collective-permute-done | bytes 393248 | tf_op jit(solution)/shard_map/ppermute | solution.py:547
  48.6 4.8 %collective-permute-done.6.lower_ref = bf16[768,256]{1,0:T(8,128)(2,1)} collective-permute-done((bf16[768,256]{1,0:T(8,128)(2,1)S(1)}, bf16[768,256]{1,0:T(8,128)(2,1)}, u32[]{:S(2)}, u32[]{:S(2)}) %collective-permute-start.6) | collective-permute-done | bytes 393248 | tf_op jit(solution)/shard_map/ppermute | solution.py:546
  53.4 1.2 %shard_map.101 = (bf16[768,256]{1,0:T(8,128)(2,1)S(1)}, bf16[768,256]{1,0:T(8,128)(2,1)S(1)}, bf16[768,256]{1,0:T(8,128)(2,1)S(1)}) custom-call(bf16[768,256]{1,0:T(8,128)(2,1)S(1)} %shard_map.100.own_ref, bf16[768,256]{1,0:T(8,128)(2,1)} %collective-permute-done.6.lower_ref, bf16[768,256]{1,0:T(8,128)(2,1)} %collective-permute-done.7.upper_ref, ...), custom_call_target="tpu_custom_call" | custom-call | tf_op jit(solution)/shard_map/pallas_call | solution.py:22
  54.6 0.1 collective-permute-start.8
  54.7 0.0 copy-done.5
  54.7 0.0 copy-done.6
  54.8 2.5 %collective-permute-start.9 = (bf16[768,256]{1,0:T(8,128)(2,1)S(1)}, bf16[768,256]{1,0:T(8,128)(2,1)S(1)}, u32[]{:S(2)}, u32[]{:S(2)}) collective-permute-start(bf16[768,256]{1,0:T(8,128)(2,1)S(1)} %get-tuple-element.39), channel_id=1, source_target_pairs={{0,2},{1,0},{2,3},{3,1},{4,6},{5,4},{6,7},{7,5},{8,10},{9,8},{10,1... | collective-permute-start | bytes 1179656 | tf_op jit(solution)/shard_map/ppermute | solution.py:573
  57.2 0.0 collective-permute-done.14.refs_1_
  57.3 0.0 collective-permute-done.13.refs_0_
  57.3 1.5 %collective-permute-start.15 = (bf16[384,384]{1,0:T(8,128)(2,1)}, bf16[384,384]{1,0:T(8,128)(2,1)S(1)}, u32[]{:S(2)}, u32[]{:S(2)}) collective-permute-start(bf16[384,384]{1,0:T(8,128)(2,1)} %get-tuple-element.41.refs_1_), channel_id=1, source_target_pairs={{0,16},{4,12},{8,24},{12,4},{16,0},{20,28},{24,8},{28,20},{1,17},{... | collective-permute-start | bytes 884744 | tf_op jit(solution)/shard_map/ppermute | solution.py:191
  58.8 1.1 %shard_map.107 = bf16[912,384]{1,0:T(8,128)(2,1)S(1)} custom-call(bf16[384,384]{1,0:T(8,128)(2,1)} %shard_map.105.refs_0_, bf16[384,384]{1,0:T(8,128)(2,1)} %get-tuple-element.41.refs_1_, bf16[384,384]{1,0:T(8,128)(2,1)S(1)} %get-tuple-element.42.refs_2_.refs_0_), custom_call_target="tpu_custom_call" | custom-call | tf_op jit(solution)/shard_map/pallas_call | solution.py:22
  59.9 0.1 collective-permute-start.16
  60.0 0.0 collective-permute-done.8.refs_3_
  60.0 0.0 collective-permute-done.5.refs_1_
  60.0 3.6 %shard_map.102 = (f32[1536,256]{1,0:T(8,128)S(1)}, bf16[1152,256]{1,0:T(8,128)(2,1)S(1)}, bf16[384,256]{1,0:T(8,128)(2,1)S(1)}) custom-call(s32[4]{0:T(128)S(1)} %and_select_fusion.table_ref, f32[1536,256]{1,0:T(8,128)S(1)} %shard_map.97.refs_1_.token_ref.total_ref, bf16[1536,384]{1,0:T(8,128)(2,1)S(1)} %shard_map.99.refs_2_.refs_0_, ...), custom_call_target="tpu_custom_call" | custom-call | flops 1207959552 | bytes 3932160 | tf_op jit(solution)/shard_map/pallas_call | solution.py:22
  63.6 0.6 collective-permute-start.18
  64.2 2.1 %collective-permute-done.9.grads_ref.refs_2_ = bf16[768,256]{1,0:T(8,128)(2,1)S(1)} collective-permute-done((bf16[768,256]{1,0:T(8,128)(2,1)S(1)}, bf16[768,256]{1,0:T(8,128)(2,1)S(1)}, u32[]{:S(2)}, u32[]{:S(2)}) %collective-permute-start.9) | collective-permute-done | bytes 393248 | tf_op jit(solution)/shard_map/ppermute | solution.py:573
  66.3 0.0 collective-permute-done.15.refs_3_.refs_1_
  66.4 0.1 collective-permute-start.17
  66.4 0.5 collective-permute-start.19
  66.9 0.0 collective-permute-done.16.refs_4_.refs_0_
  66.9 1.9 %shard_map.108.total_ref = f32[1536,256]{1,0:T(8,128)S(1)} custom-call(s32[8]{0:T(128)S(1)} %fusion.table_ref, f32[1536,256]{1,0:T(8,128)S(1)} %get-tuple-element.38.total_ref, bf16[768,256]{1,0:T(8,128)(2,1)S(1)} %collective-permute-done.9.grads_ref.refs_2_, bf16[384,384]{1,0:T(8,128)(2,1)} %shard_map.105.refs_0_, ...), custom_call_target="tpu_custom_call" | custom-call | flops 603979776 | bytes 3145728 | tf_op jit(solution)/shard_map/pallas_call | solution.py:22
  68.8 0.0 collective-permute-done.17.refs_1_
  68.9 0.0 collective-permute-done.19.refs_3_
  68.9 0.0 collective-permute-done.18.refs_2_
  68.9 1.9 %shard_map.110 = bf16[1536,256]{1,0:T(8,128)(2,1)} custom-call(s32[8]{0:T(128)S(1)} %fusion.table_ref, f32[1536,256]{1,0:T(8,128)S(1)} %shard_map.108.total_ref, bf16[768,256]{1,0:T(8,128)(2,1)S(1)} %collective-permute-done.9.grads_ref.refs_2_, bf16[912,384]{1,0:T(8,128)(2,1)S(1)} %collective-permute-done.16.refs_4_.refs_0_, ...), custom_call_target="tpu_custom_call" | custom-call | flops 603979776 | bytes 3145728 | tf_op jit(solution)/shard_map/pallas_call | solution.py:22
  (12 shorter events, 0.1 us)
Async XLA Ops:
  0.0 4.5 %copy-start.1 = (bf16[256,384]{1,0:T(8,128)(2,1)S(1)}, bf16[256,384]{1,0:T(8,128)(2,1)}, u32[]{:S(2)}) copy-start(bf16[256,384]{1,0:T(8,128)(2,1)} %g_ref.5) | copy-start | bytes 589828
  0.0 4.5 %copy-start = (bf16[256,384]{1,0:T(8,128)(2,1)S(1)}, bf16[256,384]{1,0:T(8,128)(2,1)}, u32[]{:S(2)}) copy-start(bf16[256,384]{1,0:T(8,128)(2,1)} %v_ref.5) | copy-start | bytes 589828
  0.0 4.5 %copy-start.3 = (bf16[256,384]{1,0:T(8,128)(2,1)S(1)}, bf16[256,384]{1,0:T(8,128)(2,1)}, u32[]{:S(2)}) copy-start(bf16[256,384]{1,0:T(8,128)(2,1)} %k_ref.3) | copy-start | bytes 589828
  0.0 4.5 %copy-start.2 = (bf16[256,384]{1,0:T(8,128)(2,1)S(1)}, bf16[256,384]{1,0:T(8,128)(2,1)}, u32[]{:S(2)}) copy-start(bf16[256,384]{1,0:T(8,128)(2,1)} %q_ref.3) | copy-start | bytes 589828
  0.0 4.5 %copy-start.4 = (f32[256,3]{0,1:T(4,128)S(1)}, f32[256,3]{0,1:T(4,128)}, u32[]{:S(2)}) copy-start(f32[256,3]{0,1:T(4,128)} %param.13) | copy-start | bytes 9220
  1.4 20.0 %collective-permute-start.3 = (bf16[768,384]{1,0:T(8,128)(2,1)S(1)}, bf16[768,384]{1,0:T(8,128)(2,1)S(1)}, u32[]{:S(2)}, u32[]{:S(2)}) collective-permute-start(bf16[768,384]{1,0:T(8,128)(2,1)S(1)} %get-tuple-element.25.token_ref), channel_id=1, source_target_pairs={{0,1},{1,2},{2,3},{3,0},{4,7},{5,4},{6,5},{7,6},{8,9},{9,10},{10,1... | collective-permute-start | bytes 1769480 | tf_op jit(solution)/shard_map/ppermute | solution.py:485
  5.4 2.7 %collective-permute-start = (bf16[784,128]{1,0:T(8,128)(2,1)S(1)}, bf16[784,128]{1,0:T(8,128)(2,1)S(1)}, u32[]{:S(2)}, u32[]{:S(2)}) collective-permute-start(bf16[784,128]{1,0:T(8,128)(2,1)S(1)} %get-tuple-element.26), channel_id=1, source_target_pairs={{0,4},{4,0},{8,12},{12,8},{16,20},{20,16},{24,28},{28,24},{1,5},{5... | collective-permute-start | bytes 602120 | tf_op jit(solution)/shard_map/ppermute | solution.py:511
  8.2 7.3 %collective-permute-start.1 = (bf16[784,128]{1,0:T(8,128)(2,1)S(1)}, bf16[784,128]{1,0:T(8,128)(2,1)S(1)}, u32[]{:S(2)}, u32[]{:S(2)}) collective-permute-start(bf16[784,128]{1,0:T(8,128)(2,1)S(1)} %get-tuple-element.29), channel_id=1, source_target_pairs={{0,8},{4,12},{8,0},{12,4},{16,24},{20,28},{24,16},{28,20},{1,9},{5... | collective-permute-start | bytes 602120 | tf_op jit(solution)/shard_map/ppermute | solution.py:511
  9.8 13.2 %collective-permute-start.10 = (bf16[768,384]{1,0:T(8,128)(2,1)S(1)}, bf16[768,384]{1,0:T(8,128)(2,1)S(1)}, u32[]{:S(2)}, u32[]{:S(2)}) collective-permute-start(bf16[768,384]{1,0:T(8,128)(2,1)S(1)} %get-tuple-element.40), channel_id=1, source_target_pairs={{3,2},{2,1},{4,5},{5,6},{11,10},{10,9},{12,13},{13,14},{19,18},{18... | collective-permute-start | bytes 1769480 | tf_op jit(solution)/shard_map/ppermute | solution.py:486
  16.3 4.6 %collective-permute-start.2 = (bf16[384,128]{1,0:T(8,128)(2,1)S(1)}, bf16[384,128]{1,0:T(8,128)(2,1)S(1)}, u32[]{:S(2)}, u32[]{:S(2)}) collective-permute-start(bf16[384,128]{1,0:T(8,128)(2,1)S(1)} %get-tuple-element.33), channel_id=1, source_target_pairs={{0,16},{4,20},{8,24},{12,28},{16,0},{20,4},{24,8},{28,12},{1,17},{... | collective-permute-start | bytes 294920 | tf_op jit(solution)/shard_map/ppermute | solution.py:511
  21.4 9.9 %collective-permute-start.4 = (bf16[768,384]{1,0:T(8,128)(2,1)S(1)}, bf16[768,384]{1,0:T(8,128)(2,1)S(1)}, u32[]{:S(2)}, u32[]{:S(2)}) collective-permute-start(bf16[768,384]{1,0:T(8,128)(2,1)S(1)} %shard_map.98.refs_0_.refs_1_), channel_id=1, source_target_pairs={{0,8},{4,20},{8,0},{12,28},{16,24},{20,4},{24,16},{28,12},{1,9},{5... | collective-permute-start | bytes 1769480 | tf_op jit(solution)/shard_map/ppermute | solution.py:191
  23.0 14.8 %collective-permute-start.11 = (bf16[768,384]{1,0:T(8,128)(2,1)S(1)}, bf16[768,384]{1,0:T(8,128)(2,1)S(1)}, u32[]{:S(2)}, u32[]{:S(2)}) collective-permute-start(bf16[768,384]{1,0:T(8,128)(2,1)S(1)} %shard_map.103), channel_id=1, source_target_pairs={{2,1},{1,0},{5,6},{6,7},{10,9},{9,8},{13,14},{14,15},{18,17},{17,1... | collective-permute-start | bytes 1769480 | tf_op jit(solution)/shard_map/ppermute | solution.py:549
  31.5 28.5 %collective-permute-start.5 = (bf16[1536,384]{1,0:T(8,128)(2,1)S(1)}, bf16[1536,384]{1,0:T(8,128)(2,1)}, u32[]{:S(2)}, u32[]{:S(2)}) collective-permute-start(bf16[1536,384]{1,0:T(8,128)(2,1)S(1)} %shard_map.99.refs_2_.refs_0_), channel_id=1, source_target_pairs={{0,16},{4,12},{8,24},{12,4},{16,0},{20,28},{24,8},{28,20},{1,17},{... | collective-permute-start | bytes 3538952 | tf_op jit(solution)/shard_map/ppermute | solution.py:191
  35.7 12.9 %collective-permute-start.7 = (bf16[768,256]{1,0:T(8,128)(2,1)S(1)}, bf16[768,256]{1,0:T(8,128)(2,1)}, u32[]{:S(2)}, u32[]{:S(2)}) collective-permute-start(bf16[768,256]{1,0:T(8,128)(2,1)S(1)} %shard_map.100.own_ref), channel_id=1, source_target_pairs={{0,3},{1,0},{2,1},{3,2},{4,7},{5,4},{6,5},{7,6},{8,11},{9,8},{10,9... | collective-permute-start | bytes 1179656 | tf_op jit(solution)/shard_map/ppermute | solution.py:547
  37.0 16.5 %collective-permute-start.6 = (bf16[768,256]{1,0:T(8,128)(2,1)S(1)}, bf16[768,256]{1,0:T(8,128)(2,1)}, u32[]{:S(2)}, u32[]{:S(2)}) collective-permute-start(bf16[768,256]{1,0:T(8,128)(2,1)S(1)} %shard_map.100.own_ref), channel_id=1, source_target_pairs={{0,1},{1,2},{2,3},{3,0},{4,5},{5,6},{6,7},{7,4},{8,9},{9,10},{10,1... | collective-permute-start | bytes 1179656 | tf_op jit(solution)/shard_map/ppermute | solution.py:546
  37.8 2.5 %collective-permute-start.12 = (bf16[384,384]{1,0:T(8,128)(2,1)S(1)}, bf16[384,384]{1,0:T(8,128)(2,1)S(1)}, u32[]{:S(2)}, u32[]{:S(2)}) collective-permute-start(bf16[384,384]{1,0:T(8,128)(2,1)S(1)} %shard_map.104), channel_id=1, source_target_pairs={{0,4},{1,5},{6,2},{7,3},{8,12},{9,13},{14,10},{15,11},{16,20},{17,... | collective-permute-start | bytes 884744 | tf_op jit(solution)/shard_map/ppermute | solution.py:555
  41.0 13.7 %copy-start.5 = (s32[8]{0:T(128)S(1)}, s32[8]{0:T(128)}, u32[]{:S(2)}) copy-start(s32[8]{0:T(128)} %constant.36.clone) | copy-start | bytes 100
  41.0 13.7 %copy-start.6 = (s32[8]{0:T(128)S(1)}, s32[8]{0:T(128)}, u32[]{:S(2)}) copy-start(s32[8]{0:T(128)} %constant.35.clone) | copy-start | bytes 100
  41.0 16.2 %collective-permute-start.14 = (bf16[384,384]{1,0:T(8,128)(2,1)}, bf16[384,384]{1,0:T(8,128)(2,1)S(1)}, u32[]{:S(2)}, u32[]{:S(2)}) collective-permute-start(bf16[384,384]{1,0:T(8,128)(2,1)} %shard_map.105.refs_0_), channel_id=1, source_target_pairs={{0,16},{4,12},{8,24},{12,4},{16,0},{20,28},{24,8},{28,20},{1,17},{... | collective-permute-start | bytes 884744 | tf_op jit(solution)/shard_map/ppermute | solution.py:191
  41.6 15.7 %collective-permute-start.13 = (bf16[384,384]{1,0:T(8,128)(2,1)}, bf16[384,384]{1,0:T(8,128)(2,1)}, u32[]{:S(2)}, u32[]{:S(2)}) collective-permute-start(bf16[384,384]{1,0:T(8,128)(2,1)} %shard_map.105.refs_0_), channel_id=1, source_target_pairs={{0,8},{4,20},{8,0},{12,28},{16,24},{20,4},{24,16},{28,12},{1,9},{5... | collective-permute-start | bytes 884744 | tf_op jit(solution)/shard_map/ppermute | solution.py:191
  54.6 5.3 %collective-permute-start.8 = (bf16[768,256]{1,0:T(8,128)(2,1)S(1)}, bf16[768,256]{1,0:T(8,128)(2,1)S(1)}, u32[]{:S(2)}, u32[]{:S(2)}) collective-permute-start(bf16[768,256]{1,0:T(8,128)(2,1)S(1)} %get-tuple-element.37), channel_id=1, source_target_pairs={{0,4},{4,0},{8,12},{12,8},{16,20},{20,16},{24,28},{28,24},{1,5},{5... | collective-permute-start | bytes 1179656 | tf_op jit(solution)/shard_map/ppermute | solution.py:191
  54.8 11.5 %collective-permute-start.9 = (bf16[768,256]{1,0:T(8,128)(2,1)S(1)}, bf16[768,256]{1,0:T(8,128)(2,1)S(1)}, u32[]{:S(2)}, u32[]{:S(2)}) collective-permute-start(bf16[768,256]{1,0:T(8,128)(2,1)S(1)} %get-tuple-element.39), channel_id=1, source_target_pairs={{0,2},{1,0},{2,3},{3,1},{4,6},{5,4},{6,7},{7,5},{8,10},{9,8},{10,1... | collective-permute-start | bytes 1179656 | tf_op jit(solution)/shard_map/ppermute | solution.py:573
  57.3 9.1 %collective-permute-start.15 = (bf16[384,384]{1,0:T(8,128)(2,1)}, bf16[384,384]{1,0:T(8,128)(2,1)S(1)}, u32[]{:S(2)}, u32[]{:S(2)}) collective-permute-start(bf16[384,384]{1,0:T(8,128)(2,1)} %get-tuple-element.41.refs_1_), channel_id=1, source_target_pairs={{0,16},{4,12},{8,24},{12,4},{16,0},{20,28},{24,8},{28,20},{1,17},{... | collective-permute-start | bytes 884744 | tf_op jit(solution)/shard_map/ppermute | solution.py:191
  59.9 7.0 %collective-permute-start.16 = (bf16[912,384]{1,0:T(8,128)(2,1)S(1)}, bf16[912,384]{1,0:T(8,128)(2,1)S(1)}, u32[]{:S(2)}, u32[]{:S(2)}) collective-permute-start(bf16[912,384]{1,0:T(8,128)(2,1)S(1)} %shard_map.107), channel_id=1, source_target_pairs={{0,4},{4,0},{8,12},{12,8},{16,20},{20,16},{24,28},{28,24},{1,5},{5... | collective-permute-start | bytes 2101256 | tf_op jit(solution)/shard_map/ppermute | solution.py:191
  63.6 5.2 %collective-permute-start.18 = (bf16[1152,256]{1,0:T(8,128)(2,1)S(1)}, bf16[1152,256]{1,0:T(8,128)(2,1)S(1)}, u32[]{:S(2)}, u32[]{:S(2)}) collective-permute-start(bf16[1152,256]{1,0:T(8,128)(2,1)S(1)} %get-tuple-element.43), channel_id=1, source_target_pairs={{0,4},{4,0},{8,12},{12,8},{16,20},{20,16},{24,28},{28,24},{1,5},{5... | collective-permute-start | bytes 1769480 | tf_op jit(solution)/shard_map/ppermute | solution.py:191
  66.4 2.5 %collective-permute-start.17 = (bf16[624,384]{1,0:T(8,128)(2,1)S(1)}, bf16[624,384]{1,0:T(8,128)(2,1)S(1)}, u32[]{:S(2)}, u32[]{:S(2)}) collective-permute-start(bf16[624,384]{1,0:T(8,128)(2,1)S(1)} %shard_map.109), channel_id=1, source_target_pairs={{0,4},{4,0},{8,12},{12,8},{16,20},{20,16},{24,28},{28,24},{1,5},{5... | collective-permute-start | bytes 1437704 | tf_op jit(solution)/shard_map/ppermute | solution.py:191
  66.4 2.4 %collective-permute-start.19 = (bf16[384,256]{1,0:T(8,128)(2,1)S(1)}, bf16[384,256]{1,0:T(8,128)(2,1)S(1)}, u32[]{:S(2)}, u32[]{:S(2)}) collective-permute-start(bf16[384,256]{1,0:T(8,128)(2,1)S(1)} %get-tuple-element.44), channel_id=1, source_target_pairs={{0,4},{4,0},{8,12},{12,8},{16,20},{20,16},{24,28},{28,24},{1,5},{5... | collective-permute-start | bytes 589832 | tf_op jit(solution)/shard_map/ppermute | solution.py:191

commit v8 on v7

--- a/solution.py
+++ b/solution.py
@@ -296,8 +296,8 @@
 
 
 def row_block(weights, grads):
-    share, wide = weights.shape[0] // 2, weights.shape[1]
-    return contract(weights[:share], grads[:wide], 1, 0) + contract(weights[share:], grads[wide:], 1, 0)
+    share = weights.shape[0] // 2
+    return contract(jnp.concatenate([weights[:share], weights[share:]], axis=1), grads, 1, 0)
 
 
 def own_kernel(wq_ref, wk_ref, grads_ref, out_ref, near_q, near_k, sems):
@@ -389,12 +389,14 @@
     nblocks = table_ref.shape[0]
     size = out_ref.shape[0] // nblocks
     split = head_ref.shape[0] // size
+    span = out_ref.shape[1]
+    grads = jnp.concatenate([kept_ref[...], got_ref[...]], axis=1)
     for j in range(nblocks):
-        block = rows_of(weights, 2 * size * j, 2 * size * (j + 1))
+        both = row_block(rows_of(weights, 2 * size * j, 2 * size * (j + 1)), grads)
         place = table_ref[j]
         rows = pl.ds(pl.multiple_of(place * size, 16), size)
-        out_ref[rows, :] = total_ref[rows, :] + row_block(block, kept_ref[...])
-        sent = row_block(block, got_ref[...]).astype(BF16)
+        out_ref[rows, :] = total_ref[rows, :] + both[:, :span]
+        sent = both[:, span:].astype(BF16)
 
         @pl.when(place < split)
         def _(sent=sent, place=place):
@@ -542,7 +544,7 @@
         second = share_hop(first, 0)
         (near,) = join(((first, 0, two), (second, 0, two)))
         blocks = [near, share_hop(near, 1)]
-        (ready,) = gate([both], [total, near])
+        (ready,) = gate([both], [total])
         p1 = lax.ppermute(ready, "head", ring[1])
         p3 = lax.ppermute(ready, "head", ring[3])
         (passing,) = gate([passing], [first])

time: 71.1 us -> 70.9 us (level)
  transfers between devices with their start and end apart: 20 -> 20, of which waited for: 8 -> 8; matrix products, arithmetic and copies ran while one was open for 0% -> 0% of each run, Pallas kernels for 21% -> 20%
where the time goes in v8:
time: 70.9 us; the launch traced here: 70.6 us
  waiting for transfers between devices  29.4 us (41%)
  starting transfers between devices  23.6 us (33%)
  Pallas kernels  17.3 us (24%)
    pallas_call x20, Pallas kernels, call(): pl.pallas_call(kernel, out_shape=out_shape, cost_estimate=pl.CostEstimate...  17.3 us
    ppermute x3, waiting for transfers between devices, shards(): got = lax.ppermute(sent, 'seq', [(i, i ^ hop) for i in range(nseq)])  8.2 us
    ppermute x10, starting transfers between devices, share_hop(): return lax.ppermute(held, 'seq', pairs)  7.92 us
    ppermute x10, waiting for transfers between devices, share_hop(): return lax.ppermute(held, 'seq', pairs)  7.12 us
    ppermute x1, waiting for transfers between devices, shards(): p3 = lax.ppermute(ready, 'head', ring[3])  5.58 us
    ppermute x1, waiting for transfers between devices, shards(): p1 = lax.ppermute(ready, 'head', ring[1])  4.83 us
    ppermute x3, starting transfers between devices, shards(): got = lax.ppermute(sent, 'seq', [(i, i ^ hop) for i in range(nseq)])  4.73 us
    ppermute x1, starting transfers between devices, shards(): first = lax.ppermute(packed[0], axes, moves(ring[1], ring[3]))  3.09 us
  transfers between devices with their start and end apart: 20, of which 8 were waited for; matrix products, arithmetic and copies ran while one was open for 0% of the time, Pallas kernels for 20%

profile of v8, /device:TPU:0, one launch (start us, length us, event | category | flops | bytes accessed | tf_op | source)
XLA Modules:
  0.0 70.6 jit_solution(10544067468710301128)
XLA Ops:
  0.0 0.0 copy-start.1
  0.0 0.0 copy-start
  0.0 0.0 copy-start.3
  0.0 1.4 %shard_map.91 = (bf16[768,384]{1,0:T(8,128)(2,1)S(1)}, bf16[768,384]{1,0:T(8,128)(2,1)S(1)}) custom-call(bf16[6144,384]{1,0:T(8,128)(2,1)} %wq_ref.3, bf16[6144,384]{1,0:T(8,128)(2,1)} %wk_ref.3), custom_call_target="tpu_custom_call" | custom-call | bytes 2359296 | tf_op jit(solution)/shard_map/pallas_call | solution.py:22
  1.4 3.1 %collective-permute-start.3 = (bf16[768,384]{1,0:T(8,128)(2,1)S(1)}, bf16[768,384]{1,0:T(8,128)(2,1)S(1)}, u32[]{:S(2)}, u32[]{:S(2)}) collective-permute-start(bf16[768,384]{1,0:T(8,128)(2,1)S(1)} %get-tuple-element.25.token_ref), channel_id=1, source_target_pairs={{0,1},{1,2},{2,3},{3,0},{4,7},{5,4},{6,5},{7,6},{8,9},{9,10},{10,1... | collective-permute-start | bytes 1769480 | tf_op jit(solution)/shard_map/ppermute | solution.py:487
  4.5 0.0 copy-done.1
  4.5 0.0 copy-done
  4.5 0.0 copy-done.3
  4.5 0.0 copy-done.2
  4.5 0.0 copy-done.4
  4.5 0.9 %shard_map.92 = (bf16[784,128]{1,0:T(8,128)(2,1)S(1)}, f32[768,128]{1,0:T(8,128)S(1)}, f32[24,128]{1,0:T(8,128)S(1)}) custom-call(f32[3,256]{1,0:T(4,128)S(1)} %bitcast.1, bf16[256,384]{1,0:T(8,128)(2,1)S(1)} %copy-done.2, bf16[256,384]{1,0:T(8,128)(2,1)S(1)} %copy-done.3, bf16[256,384]{1,0:T(8,128)(2,1)S(1)} %copy-done, bf16[256,384]{1,0:T(8,128)(2,1)S(1)} %copy-done.1, ...), custom_call_target="tpu_custom_call" | custom-call | flops 50331648 | bytes 786432 | tf_op jit(solution)/shard_map/pallas_call | solution.py:22
  5.4 1.6 %collective-permute-start = (bf16[784,128]{1,0:T(8,128)(2,1)S(1)}, bf16[784,128]{1,0:T(8,128)(2,1)S(1)}, u32[]{:S(2)}, u32[]{:S(2)}) collective-permute-start(bf16[784,128]{1,0:T(8,128)(2,1)S(1)} %get-tuple-element.26), channel_id=1, source_target_pairs={{0,4},{4,0},{8,12},{12,8},{16,20},{20,16},{24,28},{28,24},{1,5},{5... | collective-permute-start | bytes 602120 | tf_op jit(solution)/shard_map/ppermute | solution.py:513
  7.0 1.1 %collective-permute-done.got_ref = bf16[784,128]{1,0:T(8,128)(2,1)S(1)} collective-permute-done((bf16[784,128]{1,0:T(8,128)(2,1)S(1)}, bf16[784,128]{1,0:T(8,128)(2,1)S(1)}, u32[]{:S(2)}, u32[]{:S(2)}) %collective-permute-start) | collective-permute-done | bytes 200736 | tf_op jit(solution)/shard_map/ppermute | solution.py:513
  8.1 0.1 shard_map.93
  8.2 1.6 %collective-permute-start.1 = (bf16[784,128]{1,0:T(8,128)(2,1)S(1)}, bf16[784,128]{1,0:T(8,128)(2,1)S(1)}, u32[]{:S(2)}, u32[]{:S(2)}) collective-permute-start(bf16[784,128]{1,0:T(8,128)(2,1)S(1)} %get-tuple-element.29), channel_id=1, source_target_pairs={{0,8},{4,12},{8,0},{12,4},{16,24},{20,28},{24,16},{28,20},{1,9},{5... | collective-permute-start | bytes 602120 | tf_op jit(solution)/shard_map/ppermute | solution.py:513
  9.8 0.7 collective-permute-start.10
  10.4 5.1 %collective-permute-done.1.got_ref = bf16[784,128]{1,0:T(8,128)(2,1)S(1)} collective-permute-done((bf16[784,128]{1,0:T(8,128)(2,1)S(1)}, bf16[784,128]{1,0:T(8,128)(2,1)S(1)}, u32[]{:S(2)}, u32[]{:S(2)}) %collective-permute-start.1) | collective-permute-done | bytes 200736 | tf_op jit(solution)/shard_map/ppermute | solution.py:513
  15.5 0.8 %shard_map.94 = (bf16[384,128]{1,0:T(8,128)(2,1)S(1)}, f32[768,128]{1,0:T(8,128)}, f32[24,128]{1,0:T(8,128)S(1)}, f32[768,128]{1,0:T(8,128)S(1)}) custom-call(bf16[784,128]{1,0:T(8,128)(2,1)S(1)} %collective-permute-done.1.got_ref, f32[768,128]{1,0:T(8,128)S(1)} %get-tuple-element.30.held_ref, f32[24,128]{1,0:T(8,128)S(1)} %get-tuple-element.31.logs_ref, ...), custom_call_target="tpu_custom_call" | custom-call | flops 491520 | bytes 786432 | tf_op jit(solution)/shard_map/pallas_call | solution.py:22
  16.3 1.5 %collective-permute-start.2 = (bf16[384,128]{1,0:T(8,128)(2,1)S(1)}, bf16[384,128]{1,0:T(8,128)(2,1)S(1)}, u32[]{:S(2)}, u32[]{:S(2)}) collective-permute-start(bf16[384,128]{1,0:T(8,128)(2,1)S(1)} %get-tuple-element.33), channel_id=1, source_target_pairs={{0,16},{4,20},{8,24},{12,28},{16,0},{20,4},{24,8},{28,12},{1,17},{... | collective-permute-start | bytes 294920 | tf_op jit(solution)/shard_map/ppermute | solution.py:513
  17.9 1.0 %shard_map.95.local_ref = f32[768,256]{1,0:T(8,128)S(1)} custom-call(f32[3,256]{1,0:T(4,128)S(1)} %bitcast.2, bf16[256,384]{1,0:T(8,128)(2,1)S(1)} %copy-done.2, bf16[256,384]{1,0:T(8,128)(2,1)S(1)} %copy-done.3, bf16[256,384]{1,0:T(8,128)(2,1)S(1)} %copy-done, bf16[256,384]{1,0:T(8,128)(2,1)S(1)} %copy-done.1), custom_call_target="tpu_custom_call" | custom-call | flops 150994944 | bytes 1572864 | tf_op jit(solution)/shard_map/pallas_call | solution.py:22
  18.9 2.1 %collective-permute-done.2.got_ref = bf16[384,128]{1,0:T(8,128)(2,1)S(1)} collective-permute-done((bf16[384,128]{1,0:T(8,128)(2,1)S(1)}, bf16[384,128]{1,0:T(8,128)(2,1)S(1)}, u32[]{:S(2)}, u32[]{:S(2)}) %collective-permute-start.2) | collective-permute-done | bytes 98336 | tf_op jit(solution)/shard_map/ppermute | solution.py:513
  21.0 0.4 shard_map.96.grads_ref.refs_1_.refs_0_
  21.4 0.0 collective-permute-done.3.refs_0_
  21.4 1.6 %collective-permute-start.4 = (bf16[768,384]{1,0:T(8,128)(2,1)S(1)}, bf16[768,384]{1,0:T(8,128)(2,1)S(1)}, u32[]{:S(2)}, u32[]{:S(2)}) collective-permute-start(bf16[768,384]{1,0:T(8,128)(2,1)S(1)} %shard_map.98.refs_0_.refs_1_), channel_id=1, source_target_pairs={{0,8},{4,20},{8,0},{12,28},{16,24},{20,4},{24,16},{28,12},{1,9},{5... | collective-permute-start | bytes 1769480 | tf_op jit(solution)/shard_map/ppermute | solution.py:191
  23.0 0.0 collective-permute-done.10.refs_0_
  23.0 1.3 %collective-permute-start.11 = (bf16[768,384]{1,0:T(8,128)(2,1)S(1)}, bf16[768,384]{1,0:T(8,128)(2,1)S(1)}, u32[]{:S(2)}, u32[]{:S(2)}) collective-permute-start(bf16[768,384]{1,0:T(8,128)(2,1)S(1)} %shard_map.103), channel_id=1, source_target_pairs={{2,1},{1,0},{5,6},{6,7},{10,9},{9,8},{13,14},{14,15},{18,17},{17,1... | collective-permute-start | bytes 1769480 | tf_op jit(solution)/shard_map/ppermute | solution.py:551
  24.3 7.1 %collective-permute-done.4.refs_1_ = bf16[768,384]{1,0:T(8,128)(2,1)S(1)} collective-permute-done((bf16[768,384]{1,0:T(8,128)(2,1)S(1)}, bf16[768,384]{1,0:T(8,128)(2,1)S(1)}, u32[]{:S(2)}, u32[]{:S(2)}) %collective-permute-start.4) | collective-permute-done | bytes 589856 | tf_op jit(solution)/shard_map/ppermute | solution.py:191
  31.4 0.1 shard_map.99.refs_0_
  31.5 1.6 %collective-permute-start.5 = (bf16[1536,384]{1,0:T(8,128)(2,1)S(1)}, bf16[1536,384]{1,0:T(8,128)(2,1)}, u32[]{:S(2)}, u32[]{:S(2)}) collective-permute-start(bf16[1536,384]{1,0:T(8,128)(2,1)S(1)} %shard_map.99.refs_0_), channel_id=1, source_target_pairs={{0,16},{4,12},{8,24},{12,4},{16,0},{20,28},{24,8},{28,20},{1,17},{... | collective-permute-start | bytes 3538952 | tf_op jit(solution)/shard_map/ppermute | solution.py:191
  33.1 2.6 %shard_map.97.refs_1_.token_ref.total_ref = f32[1536,256]{1,0:T(8,128)S(1)} custom-call(bf16[6144,384]{1,0:T(8,128)(2,1)} %wq_ref.3, bf16[6144,384]{1,0:T(8,128)(2,1)} %wk_ref.3, bf16[768,256]{1,0:T(8,128)(2,1)S(1)} %shard_map.96.grads_ref.refs_1_.refs_0_), custom_call_target="tpu_custom_call" | custom-call | flops 603979776 | bytes 2359296 | tf_op jit(solution)/shard_map/pallas_call | solution.py:22
  35.7 1.3 %collective-permute-start.7 = (bf16[768,256]{1,0:T(8,128)(2,1)S(1)}, bf16[768,256]{1,0:T(8,128)(2,1)}, u32[]{:S(2)}, u32[]{:S(2)}) collective-permute-start(bf16[768,256]{1,0:T(8,128)(2,1)S(1)} %shard_map.100.own_ref), channel_id=1, source_target_pairs={{0,3},{1,0},{2,1},{3,2},{4,7},{5,4},{6,5},{7,6},{8,11},{9,8},{10,9... | collective-permute-start | bytes 1179656 | tf_op jit(solution)/shard_map/ppermute | solution.py:549
  37.0 0.8 %collective-permute-start.6 = (bf16[768,256]{1,0:T(8,128)(2,1)S(1)}, bf16[768,256]{1,0:T(8,128)(2,1)}, u32[]{:S(2)}, u32[]{:S(2)}) collective-permute-start(bf16[768,256]{1,0:T(8,128)(2,1)S(1)} %shard_map.100.own_ref), channel_id=1, source_target_pairs={{0,1},{1,2},{2,3},{3,0},{4,5},{5,6},{6,7},{7,4},{8,9},{9,10},{10,1... | collective-permute-start | bytes 1179656 | tf_op jit(solution)/shard_map/ppermute | solution.py:548
  37.8 0.0 collective-permute-done.11.both_ref
  37.8 1.3 %collective-permute-start.12 = (bf16[384,384]{1,0:T(8,128)(2,1)S(1)}, bf16[384,384]{1,0:T(8,128)(2,1)S(1)}, u32[]{:S(2)}, u32[]{:S(2)}) collective-permute-start(bf16[384,384]{1,0:T(8,128)(2,1)S(1)} %shard_map.104), channel_id=1, source_target_pairs={{0,4},{1,5},{6,2},{7,3},{8,12},{9,13},{14,10},{15,11},{16,20},{17,... | collective-permute-start | bytes 884744 | tf_op jit(solution)/shard_map/ppermute | solution.py:557
  39.1 1.2 %collective-permute-done.12.got_ref = bf16[384,384]{1,0:T(8,128)(2,1)S(1)} collective-permute-done((bf16[384,384]{1,0:T(8,128)(2,1)S(1)}, bf16[384,384]{1,0:T(8,128)(2,1)S(1)}, u32[]{:S(2)}, u32[]{:S(2)}) %collective-permute-start.12) | collective-permute-done | bytes 294944 | tf_op jit(solution)/shard_map/ppermute | solution.py:557
  40.3 0.7 %shard_map.105.refs_0_ = bf16[384,384]{1,0:T(8,128)(2,1)} custom-call(bf16[768,384]{1,0:T(8,128)(2,1)S(1)} %collective-permute-done.11.both_ref, bf16[384,384]{1,0:T(8,128)(2,1)S(1)} %collective-permute-done.12.got_ref), custom_call_target="tpu_custom_call" | custom-call | tf_op jit(solution)/shard_map/pallas_call | solution.py:22
  41.0 0.5 collective-permute-start.14
  41.6 1.5 %collective-permute-start.13 = (bf16[384,384]{1,0:T(8,128)(2,1)}, bf16[384,384]{1,0:T(8,128)(2,1)}, u32[]{:S(2)}, u32[]{:S(2)}) collective-permute-start(bf16[384,384]{1,0:T(8,128)(2,1)} %shard_map.105.refs_0_), channel_id=1, source_target_pairs={{0,8},{4,20},{8,0},{12,28},{16,24},{20,4},{24,16},{28,12},{1,9},{5... | collective-permute-start | bytes 884744 | tf_op jit(solution)/shard_map/ppermute | solution.py:191
  43.0 5.6 %collective-permute-done.7.upper_ref = bf16[768,256]{1,0:T(8,128)(2,1)} collective-permute-done((bf16[768,256]{1,0:T(8,128)(2,1)S(1)}, bf16[768,256]{1,0:T(8,128)(2,1)}, u32[]{:S(2)}, u32[]{:S(2)}) %collective-permute-start.7) | collective-permute-done | bytes 393248 | tf_op jit(solution)/shard_map/ppermute | solution.py:549
  48.6 4.8 %collective-permute-done.6.lower_ref = bf16[768,256]{1,0:T(8,128)(2,1)} collective-permute-done((bf16[768,256]{1,0:T(8,128)(2,1)S(1)}, bf16[768,256]{1,0:T(8,128)(2,1)}, u32[]{:S(2)}, u32[]{:S(2)}) %collective-permute-start.6) | collective-permute-done | bytes 393248 | tf_op jit(solution)/shard_map/ppermute | solution.py:548
  53.4 1.2 %shard_map.101 = (bf16[768,256]{1,0:T(8,128)(2,1)S(1)}, bf16[768,256]{1,0:T(8,128)(2,1)S(1)}, bf16[768,256]{1,0:T(8,128)(2,1)S(1)}) custom-call(bf16[768,256]{1,0:T(8,128)(2,1)S(1)} %shard_map.100.own_ref, bf16[768,256]{1,0:T(8,128)(2,1)} %collective-permute-done.6.lower_ref, bf16[768,256]{1,0:T(8,128)(2,1)} %collective-permute-done.7.upper_ref, ...), custom_call_target="tpu_custom_call" | custom-call | tf_op jit(solution)/shard_map/pallas_call | solution.py:22
  54.6 0.1 collective-permute-start.8
  54.7 0.0 copy-done.5
  54.7 0.0 copy-done.6
  54.8 2.5 %collective-permute-start.9 = (bf16[768,256]{1,0:T(8,128)(2,1)S(1)}, bf16[768,256]{1,0:T(8,128)(2,1)S(1)}, u32[]{:S(2)}, u32[]{:S(2)}) collective-permute-start(bf16[768,256]{1,0:T(8,128)(2,1)S(1)} %get-tuple-element.39), channel_id=1, source_target_pairs={{0,2},{1,0},{2,3},{3,1},{4,6},{5,4},{6,7},{7,5},{8,10},{9,8},{10,1... | collective-permute-start | bytes 1179656 | tf_op jit(solution)/shard_map/ppermute | solution.py:575
  57.2 0.0 collective-permute-done.14.refs_1_
  57.3 0.0 collective-permute-done.13.refs_0_
  57.3 1.5 %collective-permute-start.15 = (bf16[384,384]{1,0:T(8,128)(2,1)}, bf16[384,384]{1,0:T(8,128)(2,1)S(1)}, u32[]{:S(2)}, u32[]{:S(2)}) collective-permute-start(bf16[384,384]{1,0:T(8,128)(2,1)} %get-tuple-element.41.refs_1_), channel_id=1, source_target_pairs={{0,16},{4,12},{8,24},{12,4},{16,0},{20,28},{24,8},{28,20},{1,17},{... | collective-permute-start | bytes 884744 | tf_op jit(solution)/shard_map/ppermute | solution.py:191
  58.8 1.1 %shard_map.107 = bf16[912,384]{1,0:T(8,128)(2,1)S(1)} custom-call(bf16[384,384]{1,0:T(8,128)(2,1)} %shard_map.105.refs_0_, bf16[384,384]{1,0:T(8,128)(2,1)} %get-tuple-element.41.refs_1_, bf16[384,384]{1,0:T(8,128)(2,1)S(1)} %get-tuple-element.42.refs_2_.refs_0_), custom_call_target="tpu_custom_call" | custom-call | tf_op jit(solution)/shard_map/pallas_call | solution.py:22
  59.9 0.1 collective-permute-start.16
  60.0 0.0 collective-permute-done.8.refs_3_
  60.0 0.0 collective-permute-done.5.refs_1_
  60.0 3.2 %shard_map.102 = (f32[1536,256]{1,0:T(8,128)S(1)}, bf16[1152,256]{1,0:T(8,128)(2,1)S(1)}, bf16[384,256]{1,0:T(8,128)(2,1)S(1)}) custom-call(s32[4]{0:T(128)S(1)} %and_select_fusion.table_ref, f32[1536,256]{1,0:T(8,128)S(1)} %shard_map.97.refs_1_.token_ref.total_ref, bf16[1536,384]{1,0:T(8,128)(2,1)S(1)} %shard_map.99.refs_0_, ...), custom_call_target="tpu_custom_call" | custom-call | flops 1207959552 | bytes 3932160 | tf_op jit(solution)/shard_map/pallas_call | solution.py:22
  63.2 0.6 collective-permute-start.18
  63.8 2.5 %collective-permute-done.9.grads_ref.refs_2_ = bf16[768,256]{1,0:T(8,128)(2,1)S(1)} collective-permute-done((bf16[768,256]{1,0:T(8,128)(2,1)S(1)}, bf16[768,256]{1,0:T(8,128)(2,1)S(1)}, u32[]{:S(2)}, u32[]{:S(2)}) %collective-permute-start.9) | collective-permute-done | bytes 393248 | tf_op jit(solution)/shard_map/ppermute | solution.py:575
  66.3 0.0 collective-permute-done.15.refs_3_.refs_1_
  66.4 0.1 collective-permute-start.17
  66.4 0.5 collective-permute-start.19
  66.9 0.0 collective-permute-done.16.refs_4_.refs_0_
  66.9 1.8 %shard_map.108.total_ref = f32[1536,256]{1,0:T(8,128)S(1)} custom-call(s32[8]{0:T(128)S(1)} %fusion.table_ref, f32[1536,256]{1,0:T(8,128)S(1)} %get-tuple-element.38.total_ref, bf16[768,256]{1,0:T(8,128)(2,1)S(1)} %collective-permute-done.9.grads_ref.refs_2_, bf16[384,384]{1,0:T(8,128)(2,1)} %shard_map.105.refs_0_, ...), custom_call_target="tpu_custom_call" | custom-call | flops 603979776 | bytes 3145728 | tf_op jit(solution)/shard_map/pallas_call | solution.py:22
  68.7 0.0 collective-permute-done.17.refs_1_
  68.7 0.0 collective-permute-done.19.refs_3_
  68.7 0.0 collective-permute-done.18.refs_2_
  68.7 1.9 %shard_map.110 = bf16[1536,256]{1,0:T(8,128)(2,1)} custom-call(s32[8]{0:T(128)S(1)} %fusion.table_ref, f32[1536,256]{1,0:T(8,128)S(1)} %shard_map.108.total_ref, bf16[768,256]{1,0:T(8,128)(2,1)S(1)} %collective-permute-done.9.grads_ref.refs_2_, bf16[912,384]{1,0:T(8,128)(2,1)S(1)} %collective-permute-done.16.refs_4_.refs_0_, ...), custom_call_target="tpu_custom_call" | custom-call | flops 603979776 | bytes 3145728 | tf_op jit(solution)/shard_map/pallas_call | solution.py:22
  (12 shorter events, 0.1 us)
Async XLA Ops:
  0.0 4.5 %copy-start.1 = (bf16[256,384]{1,0:T(8,128)(2,1)S(1)}, bf16[256,384]{1,0:T(8,128)(2,1)}, u32[]{:S(2)}) copy-start(bf16[256,384]{1,0:T(8,128)(2,1)} %g_ref.5) | copy-start | bytes 589828
  0.0 4.5 %copy-start = (bf16[256,384]{1,0:T(8,128)(2,1)S(1)}, bf16[256,384]{1,0:T(8,128)(2,1)}, u32[]{:S(2)}) copy-start(bf16[256,384]{1,0:T(8,128)(2,1)} %v_ref.5) | copy-start | bytes 589828
  0.0 4.5 %copy-start.3 = (bf16[256,384]{1,0:T(8,128)(2,1)S(1)}, bf16[256,384]{1,0:T(8,128)(2,1)}, u32[]{:S(2)}) copy-start(bf16[256,384]{1,0:T(8,128)(2,1)} %k_ref.3) | copy-start | bytes 589828
  0.0 4.5 %copy-start.2 = (bf16[256,384]{1,0:T(8,128)(2,1)S(1)}, bf16[256,384]{1,0:T(8,128)(2,1)}, u32[]{:S(2)}) copy-start(bf16[256,384]{1,0:T(8,128)(2,1)} %q_ref.3) | copy-start | bytes 589828
  0.0 4.5 %copy-start.4 = (f32[256,3]{0,1:T(4,128)S(1)}, f32[256,3]{0,1:T(4,128)}, u32[]{:S(2)}) copy-start(f32[256,3]{0,1:T(4,128)} %param.13) | copy-start | bytes 9220
  1.4 20.0 %collective-permute-start.3 = (bf16[768,384]{1,0:T(8,128)(2,1)S(1)}, bf16[768,384]{1,0:T(8,128)(2,1)S(1)}, u32[]{:S(2)}, u32[]{:S(2)}) collective-permute-start(bf16[768,384]{1,0:T(8,128)(2,1)S(1)} %get-tuple-element.25.token_ref), channel_id=1, source_target_pairs={{0,1},{1,2},{2,3},{3,0},{4,7},{5,4},{6,5},{7,6},{8,9},{9,10},{10,1... | collective-permute-start | bytes 1769480 | tf_op jit(solution)/shard_map/ppermute | solution.py:487
  5.4 2.7 %collective-permute-start = (bf16[784,128]{1,0:T(8,128)(2,1)S(1)}, bf16[784,128]{1,0:T(8,128)(2,1)S(1)}, u32[]{:S(2)}, u32[]{:S(2)}) collective-permute-start(bf16[784,128]{1,0:T(8,128)(2,1)S(1)} %get-tuple-element.26), channel_id=1, source_target_pairs={{0,4},{4,0},{8,12},{12,8},{16,20},{20,16},{24,28},{28,24},{1,5},{5... | collective-permute-start | bytes 602120 | tf_op jit(solution)/shard_map/ppermute | solution.py:513
  8.2 7.3 %collective-permute-start.1 = (bf16[784,128]{1,0:T(8,128)(2,1)S(1)}, bf16[784,128]{1,0:T(8,128)(2,1)S(1)}, u32[]{:S(2)}, u32[]{:S(2)}) collective-permute-start(bf16[784,128]{1,0:T(8,128)(2,1)S(1)} %get-tuple-element.29), channel_id=1, source_target_pairs={{0,8},{4,12},{8,0},{12,4},{16,24},{20,28},{24,16},{28,20},{1,9},{5... | collective-permute-start | bytes 602120 | tf_op jit(solution)/shard_map/ppermute | solution.py:513
  9.8 13.2 %collective-permute-start.10 = (bf16[768,384]{1,0:T(8,128)(2,1)S(1)}, bf16[768,384]{1,0:T(8,128)(2,1)S(1)}, u32[]{:S(2)}, u32[]{:S(2)}) collective-permute-start(bf16[768,384]{1,0:T(8,128)(2,1)S(1)} %get-tuple-element.40), channel_id=1, source_target_pairs={{3,2},{2,1},{4,5},{5,6},{11,10},{10,9},{12,13},{13,14},{19,18},{18... | collective-permute-start | bytes 1769480 | tf_op jit(solution)/shard_map/ppermute | solution.py:488
  16.3 4.6 %collective-permute-start.2 = (bf16[384,128]{1,0:T(8,128)(2,1)S(1)}, bf16[384,128]{1,0:T(8,128)(2,1)S(1)}, u32[]{:S(2)}, u32[]{:S(2)}) collective-permute-start(bf16[384,128]{1,0:T(8,128)(2,1)S(1)} %get-tuple-element.33), channel_id=1, source_target_pairs={{0,16},{4,20},{8,24},{12,28},{16,0},{20,4},{24,8},{28,12},{1,17},{... | collective-permute-start | bytes 294920 | tf_op jit(solution)/shard_map/ppermute | solution.py:513
  21.4 9.9 %collective-permute-start.4 = (bf16[768,384]{1,0:T(8,128)(2,1)S(1)}, bf16[768,384]{1,0:T(8,128)(2,1)S(1)}, u32[]{:S(2)}, u32[]{:S(2)}) collective-permute-start(bf16[768,384]{1,0:T(8,128)(2,1)S(1)} %shard_map.98.refs_0_.refs_1_), channel_id=1, source_target_pairs={{0,8},{4,20},{8,0},{12,28},{16,24},{20,4},{24,16},{28,12},{1,9},{5... | collective-permute-start | bytes 1769480 | tf_op jit(solution)/shard_map/ppermute | solution.py:191
  23.0 14.8 %collective-permute-start.11 = (bf16[768,384]{1,0:T(8,128)(2,1)S(1)}, bf16[768,384]{1,0:T(8,128)(2,1)S(1)}, u32[]{:S(2)}, u32[]{:S(2)}) collective-permute-start(bf16[768,384]{1,0:T(8,128)(2,1)S(1)} %shard_map.103), channel_id=1, source_target_pairs={{2,1},{1,0},{5,6},{6,7},{10,9},{9,8},{13,14},{14,15},{18,17},{17,1... | collective-permute-start | bytes 1769480 | tf_op jit(solution)/shard_map/ppermute | solution.py:551
  31.5 28.5 %collective-permute-start.5 = (bf16[1536,384]{1,0:T(8,128)(2,1)S(1)}, bf16[1536,384]{1,0:T(8,128)(2,1)}, u32[]{:S(2)}, u32[]{:S(2)}) collective-permute-start(bf16[1536,384]{1,0:T(8,128)(2,1)S(1)} %shard_map.99.refs_0_), channel_id=1, source_target_pairs={{0,16},{4,12},{8,24},{12,4},{16,0},{20,28},{24,8},{28,20},{1,17},{... | collective-permute-start | bytes 3538952 | tf_op jit(solution)/shard_map/ppermute | solution.py:191
  35.7 12.9 %collective-permute-start.7 = (bf16[768,256]{1,0:T(8,128)(2,1)S(1)}, bf16[768,256]{1,0:T(8,128)(2,1)}, u32[]{:S(2)}, u32[]{:S(2)}) collective-permute-start(bf16[768,256]{1,0:T(8,128)(2,1)S(1)} %shard_map.100.own_ref), channel_id=1, source_target_pairs={{0,3},{1,0},{2,1},{3,2},{4,7},{5,4},{6,5},{7,6},{8,11},{9,8},{10,9... | collective-permute-start | bytes 1179656 | tf_op jit(solution)/shard_map/ppermute | solution.py:549
  37.0 16.5 %collective-permute-start.6 = (bf16[768,256]{1,0:T(8,128)(2,1)S(1)}, bf16[768,256]{1,0:T(8,128)(2,1)}, u32[]{:S(2)}, u32[]{:S(2)}) collective-permute-start(bf16[768,256]{1,0:T(8,128)(2,1)S(1)} %shard_map.100.own_ref), channel_id=1, source_target_pairs={{0,1},{1,2},{2,3},{3,0},{4,5},{5,6},{6,7},{7,4},{8,9},{9,10},{10,1... | collective-permute-start | bytes 1179656 | tf_op jit(solution)/shard_map/ppermute | solution.py:548
  37.8 2.5 %collective-permute-start.12 = (bf16[384,384]{1,0:T(8,128)(2,1)S(1)}, bf16[384,384]{1,0:T(8,128)(2,1)S(1)}, u32[]{:S(2)}, u32[]{:S(2)}) collective-permute-start(bf16[384,384]{1,0:T(8,128)(2,1)S(1)} %shard_map.104), channel_id=1, source_target_pairs={{0,4},{1,5},{6,2},{7,3},{8,12},{9,13},{14,10},{15,11},{16,20},{17,... | collective-permute-start | bytes 884744 | tf_op jit(solution)/shard_map/ppermute | solution.py:557
  41.0 13.7 %copy-start.5 = (s32[8]{0:T(128)S(1)}, s32[8]{0:T(128)}, u32[]{:S(2)}) copy-start(s32[8]{0:T(128)} %constant.36.clone) | copy-start | bytes 100
  41.0 13.7 %copy-start.6 = (s32[8]{0:T(128)S(1)}, s32[8]{0:T(128)}, u32[]{:S(2)}) copy-start(s32[8]{0:T(128)} %constant.35.clone) | copy-start | bytes 100
  41.0 16.2 %collective-permute-start.14 = (bf16[384,384]{1,0:T(8,128)(2,1)}, bf16[384,384]{1,0:T(8,128)(2,1)S(1)}, u32[]{:S(2)}, u32[]{:S(2)}) collective-permute-start(bf16[384,384]{1,0:T(8,128)(2,1)} %shard_map.105.refs_0_), channel_id=1, source_target_pairs={{0,16},{4,12},{8,24},{12,4},{16,0},{20,28},{24,8},{28,20},{1,17},{... | collective-permute-start | bytes 884744 | tf_op jit(solution)/shard_map/ppermute | solution.py:191
  41.6 15.7 %collective-permute-start.13 = (bf16[384,384]{1,0:T(8,128)(2,1)}, bf16[384,384]{1,0:T(8,128)(2,1)}, u32[]{:S(2)}, u32[]{:S(2)}) collective-permute-start(bf16[384,384]{1,0:T(8,128)(2,1)} %shard_map.105.refs_0_), channel_id=1, source_target_pairs={{0,8},{4,20},{8,0},{12,28},{16,24},{20,4},{24,16},{28,12},{1,9},{5... | collective-permute-start | bytes 884744 | tf_op jit(solution)/shard_map/ppermute | solution.py:191
  54.6 5.3 %collective-permute-start.8 = (bf16[768,256]{1,0:T(8,128)(2,1)S(1)}, bf16[768,256]{1,0:T(8,128)(2,1)S(1)}, u32[]{:S(2)}, u32[]{:S(2)}) collective-permute-start(bf16[768,256]{1,0:T(8,128)(2,1)S(1)} %get-tuple-element.37), channel_id=1, source_target_pairs={{0,4},{4,0},{8,12},{12,8},{16,20},{20,16},{24,28},{28,24},{1,5},{5... | collective-permute-start | bytes 1179656 | tf_op jit(solution)/shard_map/ppermute | solution.py:191
  54.8 11.5 %collective-permute-start.9 = (bf16[768,256]{1,0:T(8,128)(2,1)S(1)}, bf16[768,256]{1,0:T(8,128)(2,1)S(1)}, u32[]{:S(2)}, u32[]{:S(2)}) collective-permute-start(bf16[768,256]{1,0:T(8,128)(2,1)S(1)} %get-tuple-element.39), channel_id=1, source_target_pairs={{0,2},{1,0},{2,3},{3,1},{4,6},{5,4},{6,7},{7,5},{8,10},{9,8},{10,1... | collective-permute-start | bytes 1179656 | tf_op jit(solution)/shard_map/ppermute | solution.py:575
  57.3 9.1 %collective-permute-start.15 = (bf16[384,384]{1,0:T(8,128)(2,1)}, bf16[384,384]{1,0:T(8,128)(2,1)S(1)}, u32[]{:S(2)}, u32[]{:S(2)}) collective-permute-start(bf16[384,384]{1,0:T(8,128)(2,1)} %get-tuple-element.41.refs_1_), channel_id=1, source_target_pairs={{0,16},{4,12},{8,24},{12,4},{16,0},{20,28},{24,8},{28,20},{1,17},{... | collective-permute-start | bytes 884744 | tf_op jit(solution)/shard_map/ppermute | solution.py:191
  59.9 7.0 %collective-permute-start.16 = (bf16[912,384]{1,0:T(8,128)(2,1)S(1)}, bf16[912,384]{1,0:T(8,128)(2,1)S(1)}, u32[]{:S(2)}, u32[]{:S(2)}) collective-permute-start(bf16[912,384]{1,0:T(8,128)(2,1)S(1)} %shard_map.107), channel_id=1, source_target_pairs={{0,4},{4,0},{8,12},{12,8},{16,20},{20,16},{24,28},{28,24},{1,5},{5... | collective-permute-start | bytes 2101256 | tf_op jit(solution)/shard_map/ppermute | solution.py:191
  63.2 5.5 %collective-permute-start.18 = (bf16[1152,256]{1,0:T(8,128)(2,1)S(1)}, bf16[1152,256]{1,0:T(8,128)(2,1)S(1)}, u32[]{:S(2)}, u32[]{:S(2)}) collective-permute-start(bf16[1152,256]{1,0:T(8,128)(2,1)S(1)} %get-tuple-element.43), channel_id=1, source_target_pairs={{0,4},{4,0},{8,12},{12,8},{16,20},{20,16},{24,28},{28,24},{1,5},{5... | collective-permute-start | bytes 1769480 | tf_op jit(solution)/shard_map/ppermute | solution.py:191
  66.4 2.4 %collective-permute-start.17 = (bf16[624,384]{1,0:T(8,128)(2,1)S(1)}, bf16[624,384]{1,0:T(8,128)(2,1)S(1)}, u32[]{:S(2)}, u32[]{:S(2)}) collective-permute-start(bf16[624,384]{1,0:T(8,128)(2,1)S(1)} %shard_map.109), channel_id=1, source_target_pairs={{0,4},{4,0},{8,12},{12,8},{16,20},{20,16},{24,28},{28,24},{1,5},{5... | collective-permute-start | bytes 1437704 | tf_op jit(solution)/shard_map/ppermute | solution.py:191
  66.4 2.3 %collective-permute-start.19 = (bf16[384,256]{1,0:T(8,128)(2,1)S(1)}, bf16[384,256]{1,0:T(8,128)(2,1)S(1)}, u32[]{:S(2)}, u32[]{:S(2)}) collective-permute-start(bf16[384,256]{1,0:T(8,128)(2,1)S(1)} %get-tuple-element.44), channel_id=1, source_target_pairs={{0,4},{4,0},{8,12},{12,8},{16,20},{20,16},{24,28},{28,24},{1,5},{5... | collective-permute-start | bytes 589832 | tf_op jit(solution)/shard_map/ppermute | solution.py:191

commit v9 on v8

--- a/solution.py
+++ b/solution.py
@@ -9,7 +9,7 @@
 
 F32 = jnp.float32
 BF16 = jnp.bfloat16
-VMEM_BYTES = 16 * 1024 * 1024
+VMEM_BYTES = 10 * 1024 * 1024
 CUT = 144
 SPLIT = 1152
 
@@ -416,12 +416,12 @@
             jax.ShapeDtypeStruct((split, span), BF16),
             jax.ShapeDtypeStruct((chunk - split, span), BF16),
         ),
-        4 * chunk * span * kept.shape[0], chunk * span * 10,
+        0, 0,
         table, total, *weights, kept, got,
         in_specs=[pl.BlockSpec(memory_space=pltpu.SMEM)]
         + [pl.BlockSpec(memory_space=pltpu.VMEM)] * (3 + len(weights)),
         out_specs=[pl.BlockSpec(memory_space=pltpu.VMEM)] * 3,
-        vmem=24 * 1024 * 1024,
+        vmem=14 * 1024 * 1024,
     )
 
 
@@ -458,7 +458,7 @@
         in_specs=[pl.BlockSpec(memory_space=pltpu.SMEM)]
         + [pl.BlockSpec(memory_space=pltpu.VMEM)] * (2 + len(args)),
         out_specs=pl.BlockSpec(memory_space=pltpu.VMEM),
-        vmem=24 * 1024 * 1024,
+        vmem=14 * 1024 * 1024,
     )
 
 

time: 70.9 us -> 70.9 us (level)
  no operation moved by 1% of the time
where the time goes in v9:
time: 70.9 us; the launch traced here: 70.5 us
  waiting for transfers between devices  29.3 us (41%)
  starting transfers between devices  23.6 us (33%)
  Pallas kernels  17.3 us (24%)
    pallas_call x20, Pallas kernels, call(): pl.pallas_call(kernel, out_shape=out_shape, cost_estimate=pl.CostEstimate...  17.3 us
    ppermute x3, waiting for transfers between devices, shards(): got = lax.ppermute(sent, 'seq', [(i, i ^ hop) for i in range(nseq)])  8.2 us
    ppermute x10, starting transfers between devices, share_hop(): return lax.ppermute(held, 'seq', pairs)  7.98 us
    ppermute x10, waiting for transfers between devices, share_hop(): return lax.ppermute(held, 'seq', pairs)  7.12 us
    ppermute x1, waiting for transfers between devices, shards(): p3 = lax.ppermute(ready, 'head', ring[3])  5.58 us
    ppermute x1, waiting for transfers between devices, shards(): p1 = lax.ppermute(ready, 'head', ring[1])  4.83 us
    ppermute x3, starting transfers between devices, shards(): got = lax.ppermute(sent, 'seq', [(i, i ^ hop) for i in range(nseq)])  4.73 us
    ppermute x1, starting transfers between devices, shards(): first = lax.ppermute(packed[0], axes, moves(ring[1], ring[3]))  3.09 us
  transfers between devices with their start and end apart: 20, of which 8 were waited for; matrix products, arithmetic and copies ran while one was open for 0% of the time, Pallas kernels for 20%

profile of v9, /device:TPU:0, one launch (start us, length us, event | category | flops | bytes accessed | tf_op | source)
XLA Modules:
  0.0 70.5 jit_solution(14030786767738335313)
XLA Ops:
  0.0 0.0 copy-start.1
  0.0 0.0 copy-start
  0.0 0.0 copy-start.3
  0.0 1.4 %shard_map.91 = (bf16[768,384]{1,0:T(8,128)(2,1)S(1)}, bf16[768,384]{1,0:T(8,128)(2,1)S(1)}) custom-call(bf16[6144,384]{1,0:T(8,128)(2,1)} %wq_ref.3, bf16[6144,384]{1,0:T(8,128)(2,1)} %wk_ref.3), custom_call_target="tpu_custom_call" | custom-call | bytes 2359296 | tf_op jit(solution)/shard_map/pallas_call | solution.py:22
  1.4 3.1 %collective-permute-start.3 = (bf16[768,384]{1,0:T(8,128)(2,1)S(1)}, bf16[768,384]{1,0:T(8,128)(2,1)S(1)}, u32[]{:S(2)}, u32[]{:S(2)}) collective-permute-start(bf16[768,384]{1,0:T(8,128)(2,1)S(1)} %get-tuple-element.25.token_ref), channel_id=1, source_target_pairs={{0,1},{1,2},{2,3},{3,0},{4,7},{5,4},{6,5},{7,6},{8,9},{9,10},{10,1... | collective-permute-start | bytes 1769480 | tf_op jit(solution)/shard_map/ppermute | solution.py:487
  4.5 0.0 copy-done.1
  4.5 0.0 copy-done
  4.5 0.0 copy-done.3
  4.5 0.0 copy-done.2
  4.5 0.0 copy-done.4
  4.5 0.9 %shard_map.92 = (bf16[784,128]{1,0:T(8,128)(2,1)S(1)}, f32[768,128]{1,0:T(8,128)S(1)}, f32[24,128]{1,0:T(8,128)S(1)}) custom-call(f32[3,256]{1,0:T(4,128)S(1)} %bitcast.1, bf16[256,384]{1,0:T(8,128)(2,1)S(1)} %copy-done.2, bf16[256,384]{1,0:T(8,128)(2,1)S(1)} %copy-done.3, bf16[256,384]{1,0:T(8,128)(2,1)S(1)} %copy-done, bf16[256,384]{1,0:T(8,128)(2,1)S(1)} %copy-done.1, ...), custom_call_target="tpu_custom_call" | custom-call | flops 50331648 | bytes 786432 | tf_op jit(solution)/shard_map/pallas_call | solution.py:22
  5.4 1.6 %collective-permute-start = (bf16[784,128]{1,0:T(8,128)(2,1)S(1)}, bf16[784,128]{1,0:T(8,128)(2,1)S(1)}, u32[]{:S(2)}, u32[]{:S(2)}) collective-permute-start(bf16[784,128]{1,0:T(8,128)(2,1)S(1)} %get-tuple-element.26), channel_id=1, source_target_pairs={{0,4},{4,0},{8,12},{12,8},{16,20},{20,16},{24,28},{28,24},{1,5},{5... | collective-permute-start | bytes 602120 | tf_op jit(solution)/shard_map/ppermute | solution.py:513
  7.0 1.1 %collective-permute-done.got_ref = bf16[784,128]{1,0:T(8,128)(2,1)S(1)} collective-permute-done((bf16[784,128]{1,0:T(8,128)(2,1)S(1)}, bf16[784,128]{1,0:T(8,128)(2,1)S(1)}, u32[]{:S(2)}, u32[]{:S(2)}) %collective-permute-start) | collective-permute-done | bytes 200736 | tf_op jit(solution)/shard_map/ppermute | solution.py:513
  8.1 0.1 shard_map.93
  8.2 1.6 %collective-permute-start.1 = (bf16[784,128]{1,0:T(8,128)(2,1)S(1)}, bf16[784,128]{1,0:T(8,128)(2,1)S(1)}, u32[]{:S(2)}, u32[]{:S(2)}) collective-permute-start(bf16[784,128]{1,0:T(8,128)(2,1)S(1)} %get-tuple-element.29), channel_id=1, source_target_pairs={{0,8},{4,12},{8,0},{12,4},{16,24},{20,28},{24,16},{28,20},{1,9},{5... | collective-permute-start | bytes 602120 | tf_op jit(solution)/shard_map/ppermute | solution.py:513
  9.8 0.7 collective-permute-start.10
  10.4 5.1 %collective-permute-done.1.got_ref = bf16[784,128]{1,0:T(8,128)(2,1)S(1)} collective-permute-done((bf16[784,128]{1,0:T(8,128)(2,1)S(1)}, bf16[784,128]{1,0:T(8,128)(2,1)S(1)}, u32[]{:S(2)}, u32[]{:S(2)}) %collective-permute-start.1) | collective-permute-done | bytes 200736 | tf_op jit(solution)/shard_map/ppermute | solution.py:513
  15.5 0.8 %shard_map.94 = (bf16[384,128]{1,0:T(8,128)(2,1)S(1)}, f32[768,128]{1,0:T(8,128)}, f32[24,128]{1,0:T(8,128)S(1)}, f32[768,128]{1,0:T(8,128)S(1)}) custom-call(bf16[784,128]{1,0:T(8,128)(2,1)S(1)} %collective-permute-done.1.got_ref, f32[768,128]{1,0:T(8,128)S(1)} %get-tuple-element.30.held_ref, f32[24,128]{1,0:T(8,128)S(1)} %get-tuple-element.31.logs_ref, ...), custom_call_target="tpu_custom_call" | custom-call | flops 491520 | bytes 786432 | tf_op jit(solution)/shard_map/pallas_call | solution.py:22
  16.3 1.5 %collective-permute-start.2 = (bf16[384,128]{1,0:T(8,128)(2,1)S(1)}, bf16[384,128]{1,0:T(8,128)(2,1)S(1)}, u32[]{:S(2)}, u32[]{:S(2)}) collective-permute-start(bf16[384,128]{1,0:T(8,128)(2,1)S(1)} %get-tuple-element.33), channel_id=1, source_target_pairs={{0,16},{4,20},{8,24},{12,28},{16,0},{20,4},{24,8},{28,12},{1,17},{... | collective-permute-start | bytes 294920 | tf_op jit(solution)/shard_map/ppermute | solution.py:513
  17.9 1.0 %shard_map.95.local_ref = f32[768,256]{1,0:T(8,128)S(1)} custom-call(f32[3,256]{1,0:T(4,128)S(1)} %bitcast.2, bf16[256,384]{1,0:T(8,128)(2,1)S(1)} %copy-done.2, bf16[256,384]{1,0:T(8,128)(2,1)S(1)} %copy-done.3, bf16[256,384]{1,0:T(8,128)(2,1)S(1)} %copy-done, bf16[256,384]{1,0:T(8,128)(2,1)S(1)} %copy-done.1), custom_call_target="tpu_custom_call" | custom-call | flops 150994944 | bytes 1572864 | tf_op jit(solution)/shard_map/pallas_call | solution.py:22
  18.9 2.1 %collective-permute-done.2.got_ref = bf16[384,128]{1,0:T(8,128)(2,1)S(1)} collective-permute-done((bf16[384,128]{1,0:T(8,128)(2,1)S(1)}, bf16[384,128]{1,0:T(8,128)(2,1)S(1)}, u32[]{:S(2)}, u32[]{:S(2)}) %collective-permute-start.2) | collective-permute-done | bytes 98336 | tf_op jit(solution)/shard_map/ppermute | solution.py:513
  21.0 0.4 shard_map.96.grads_ref.refs_1_.refs_0_
  21.4 0.0 collective-permute-done.3.refs_0_
  21.4 1.6 %collective-permute-start.4 = (bf16[768,384]{1,0:T(8,128)(2,1)S(1)}, bf16[768,384]{1,0:T(8,128)(2,1)S(1)}, u32[]{:S(2)}, u32[]{:S(2)}) collective-permute-start(bf16[768,384]{1,0:T(8,128)(2,1)S(1)} %shard_map.98.refs_0_.refs_1_), channel_id=1, source_target_pairs={{0,8},{4,20},{8,0},{12,28},{16,24},{20,4},{24,16},{28,12},{1,9},{5... | collective-permute-start | bytes 1769480 | tf_op jit(solution)/shard_map/ppermute | solution.py:191
  23.0 0.0 collective-permute-done.10.refs_0_
  23.0 1.3 %collective-permute-start.11 = (bf16[768,384]{1,0:T(8,128)(2,1)S(1)}, bf16[768,384]{1,0:T(8,128)(2,1)S(1)}, u32[]{:S(2)}, u32[]{:S(2)}) collective-permute-start(bf16[768,384]{1,0:T(8,128)(2,1)S(1)} %shard_map.103), channel_id=1, source_target_pairs={{2,1},{1,0},{5,6},{6,7},{10,9},{9,8},{13,14},{14,15},{18,17},{17,1... | collective-permute-start | bytes 1769480 | tf_op jit(solution)/shard_map/ppermute | solution.py:551
  24.3 7.1 %collective-permute-done.4.refs_1_ = bf16[768,384]{1,0:T(8,128)(2,1)S(1)} collective-permute-done((bf16[768,384]{1,0:T(8,128)(2,1)S(1)}, bf16[768,384]{1,0:T(8,128)(2,1)S(1)}, u32[]{:S(2)}, u32[]{:S(2)}) %collective-permute-start.4) | collective-permute-done | bytes 589856 | tf_op jit(solution)/shard_map/ppermute | solution.py:191
  31.4 0.1 shard_map.99.refs_0_
  31.5 1.6 %collective-permute-start.5 = (bf16[1536,384]{1,0:T(8,128)(2,1)S(1)}, bf16[1536,384]{1,0:T(8,128)(2,1)}, u32[]{:S(2)}, u32[]{:S(2)}) collective-permute-start(bf16[1536,384]{1,0:T(8,128)(2,1)S(1)} %shard_map.99.refs_0_), channel_id=1, source_target_pairs={{0,16},{4,12},{8,24},{12,4},{16,0},{20,28},{24,8},{28,20},{1,17},{... | collective-permute-start | bytes 3538952 | tf_op jit(solution)/shard_map/ppermute | solution.py:191
  33.1 2.6 %shard_map.97.refs_1_.token_ref.total_ref = f32[1536,256]{1,0:T(8,128)S(1)} custom-call(bf16[6144,384]{1,0:T(8,128)(2,1)} %wq_ref.3, bf16[6144,384]{1,0:T(8,128)(2,1)} %wk_ref.3, bf16[768,256]{1,0:T(8,128)(2,1)S(1)} %shard_map.96.grads_ref.refs_1_.refs_0_), custom_call_target="tpu_custom_call" | custom-call | flops 603979776 | bytes 2359296 | tf_op jit(solution)/shard_map/pallas_call | solution.py:22
  35.7 1.3 %collective-permute-start.7 = (bf16[768,256]{1,0:T(8,128)(2,1)S(1)}, bf16[768,256]{1,0:T(8,128)(2,1)}, u32[]{:S(2)}, u32[]{:S(2)}) collective-permute-start(bf16[768,256]{1,0:T(8,128)(2,1)S(1)} %shard_map.100.own_ref), channel_id=1, source_target_pairs={{0,3},{1,0},{2,1},{3,2},{4,7},{5,4},{6,5},{7,6},{8,11},{9,8},{10,9... | collective-permute-start | bytes 1179656 | tf_op jit(solution)/shard_map/ppermute | solution.py:549
  37.0 0.8 %collective-permute-start.6 = (bf16[768,256]{1,0:T(8,128)(2,1)S(1)}, bf16[768,256]{1,0:T(8,128)(2,1)}, u32[]{:S(2)}, u32[]{:S(2)}) collective-permute-start(bf16[768,256]{1,0:T(8,128)(2,1)S(1)} %shard_map.100.own_ref), channel_id=1, source_target_pairs={{0,1},{1,2},{2,3},{3,0},{4,5},{5,6},{6,7},{7,4},{8,9},{9,10},{10,1... | collective-permute-start | bytes 1179656 | tf_op jit(solution)/shard_map/ppermute | solution.py:548
  37.8 0.0 collective-permute-done.11.both_ref
  37.8 1.3 %collective-permute-start.12 = (bf16[384,384]{1,0:T(8,128)(2,1)S(1)}, bf16[384,384]{1,0:T(8,128)(2,1)S(1)}, u32[]{:S(2)}, u32[]{:S(2)}) collective-permute-start(bf16[384,384]{1,0:T(8,128)(2,1)S(1)} %shard_map.104), channel_id=1, source_target_pairs={{0,4},{1,5},{6,2},{7,3},{8,12},{9,13},{14,10},{15,11},{16,20},{17,... | collective-permute-start | bytes 884744 | tf_op jit(solution)/shard_map/ppermute | solution.py:557
  39.1 1.2 %collective-permute-done.12.got_ref = bf16[384,384]{1,0:T(8,128)(2,1)S(1)} collective-permute-done((bf16[384,384]{1,0:T(8,128)(2,1)S(1)}, bf16[384,384]{1,0:T(8,128)(2,1)S(1)}, u32[]{:S(2)}, u32[]{:S(2)}) %collective-permute-start.12) | collective-permute-done | bytes 294944 | tf_op jit(solution)/shard_map/ppermute | solution.py:557
  40.3 0.7 %shard_map.105.refs_0_ = bf16[384,384]{1,0:T(8,128)(2,1)} custom-call(bf16[768,384]{1,0:T(8,128)(2,1)S(1)} %collective-permute-done.11.both_ref, bf16[384,384]{1,0:T(8,128)(2,1)S(1)} %collective-permute-done.12.got_ref), custom_call_target="tpu_custom_call" | custom-call | tf_op jit(solution)/shard_map/pallas_call | solution.py:22
  41.0 0.5 collective-permute-start.14
  41.6 1.5 %collective-permute-start.13 = (bf16[384,384]{1,0:T(8,128)(2,1)}, bf16[384,384]{1,0:T(8,128)(2,1)}, u32[]{:S(2)}, u32[]{:S(2)}) collective-permute-start(bf16[384,384]{1,0:T(8,128)(2,1)} %shard_map.105.refs_0_), channel_id=1, source_target_pairs={{0,8},{4,20},{8,0},{12,28},{16,24},{20,4},{24,16},{28,12},{1,9},{5... | collective-permute-start | bytes 884744 | tf_op jit(solution)/shard_map/ppermute | solution.py:191
  43.0 5.6 %collective-permute-done.7.upper_ref = bf16[768,256]{1,0:T(8,128)(2,1)} collective-permute-done((bf16[768,256]{1,0:T(8,128)(2,1)S(1)}, bf16[768,256]{1,0:T(8,128)(2,1)}, u32[]{:S(2)}, u32[]{:S(2)}) %collective-permute-start.7) | collective-permute-done | bytes 393248 | tf_op jit(solution)/shard_map/ppermute | solution.py:549
  48.6 4.8 %collective-permute-done.6.lower_ref = bf16[768,256]{1,0:T(8,128)(2,1)} collective-permute-done((bf16[768,256]{1,0:T(8,128)(2,1)S(1)}, bf16[768,256]{1,0:T(8,128)(2,1)}, u32[]{:S(2)}, u32[]{:S(2)}) %collective-permute-start.6) | collective-permute-done | bytes 393248 | tf_op jit(solution)/shard_map/ppermute | solution.py:548
  53.4 1.2 %shard_map.101 = (bf16[768,256]{1,0:T(8,128)(2,1)S(1)}, bf16[768,256]{1,0:T(8,128)(2,1)S(1)}, bf16[768,256]{1,0:T(8,128)(2,1)S(1)}) custom-call(bf16[768,256]{1,0:T(8,128)(2,1)S(1)} %shard_map.100.own_ref, bf16[768,256]{1,0:T(8,128)(2,1)} %collective-permute-done.6.lower_ref, bf16[768,256]{1,0:T(8,128)(2,1)} %collective-permute-done.7.upper_ref, ...), custom_call_target="tpu_custom_call" | custom-call | tf_op jit(solution)/shard_map/pallas_call | solution.py:22
  54.6 0.1 collective-permute-start.8
  54.7 2.5 %collective-permute-start.9 = (bf16[768,256]{1,0:T(8,128)(2,1)S(1)}, bf16[768,256]{1,0:T(8,128)(2,1)S(1)}, u32[]{:S(2)}, u32[]{:S(2)}) collective-permute-start(bf16[768,256]{1,0:T(8,128)(2,1)S(1)} %get-tuple-element.39), channel_id=1, source_target_pairs={{0,2},{1,0},{2,3},{3,1},{4,6},{5,4},{6,7},{7,5},{8,10},{9,8},{10,1... | collective-permute-start | bytes 1179656 | tf_op jit(solution)/shard_map/ppermute | solution.py:575
  57.2 0.0 copy-done.5
  57.2 0.0 copy-done.6
  57.2 0.0 collective-permute-done.14.refs_1_
  57.2 0.0 collective-permute-done.13.refs_0_
  57.3 1.6 %collective-permute-start.15 = (bf16[384,384]{1,0:T(8,128)(2,1)}, bf16[384,384]{1,0:T(8,128)(2,1)S(1)}, u32[]{:S(2)}, u32[]{:S(2)}) collective-permute-start(bf16[384,384]{1,0:T(8,128)(2,1)} %get-tuple-element.41.refs_1_), channel_id=1, source_target_pairs={{0,16},{4,12},{8,24},{12,4},{16,0},{20,28},{24,8},{28,20},{1,17},{... | collective-permute-start | bytes 884744 | tf_op jit(solution)/shard_map/ppermute | solution.py:191
  58.8 1.1 %shard_map.107 = bf16[912,384]{1,0:T(8,128)(2,1)S(1)} custom-call(bf16[384,384]{1,0:T(8,128)(2,1)} %shard_map.105.refs_0_, bf16[384,384]{1,0:T(8,128)(2,1)} %get-tuple-element.41.refs_1_, bf16[384,384]{1,0:T(8,128)(2,1)S(1)} %get-tuple-element.42.refs_2_.refs_0_), custom_call_target="tpu_custom_call" | custom-call | tf_op jit(solution)/shard_map/pallas_call | solution.py:22
  60.0 0.1 collective-permute-start.16
  60.0 0.0 collective-permute-done.8.refs_3_
  60.1 0.0 collective-permute-done.5.refs_1_
  60.1 3.2 %shard_map.102 = (f32[1536,256]{1,0:T(8,128)S(1)}, bf16[1152,256]{1,0:T(8,128)(2,1)S(1)}, bf16[384,256]{1,0:T(8,128)(2,1)S(1)}) custom-call(s32[4]{0:T(128)S(1)} %and_select_fusion.table_ref, f32[1536,256]{1,0:T(8,128)S(1)} %shard_map.97.refs_1_.token_ref.total_ref, bf16[1536,384]{1,0:T(8,128)(2,1)S(1)} %shard_map.99.refs_0_, ...), custom_call_target="tpu_custom_call" | custom-call | tf_op jit(solution)/shard_map/pallas_call | solution.py:22
  63.3 0.6 collective-permute-start.18
  63.9 2.4 %collective-permute-done.9.grads_ref.refs_2_ = bf16[768,256]{1,0:T(8,128)(2,1)S(1)} collective-permute-done((bf16[768,256]{1,0:T(8,128)(2,1)S(1)}, bf16[768,256]{1,0:T(8,128)(2,1)S(1)}, u32[]{:S(2)}, u32[]{:S(2)}) %collective-permute-start.9) | collective-permute-done | bytes 393248 | tf_op jit(solution)/shard_map/ppermute | solution.py:575
  66.2 0.0 collective-permute-done.15.refs_3_.refs_1_
  66.3 0.1 collective-permute-start.17
  66.4 0.5 collective-permute-start.19
  66.9 0.0 collective-permute-done.16.refs_4_.refs_0_
  66.9 1.8 %shard_map.108.total_ref = f32[1536,256]{1,0:T(8,128)S(1)} custom-call(s32[8]{0:T(128)S(1)} %fusion.table_ref, f32[1536,256]{1,0:T(8,128)S(1)} %get-tuple-element.38.total_ref, bf16[768,256]{1,0:T(8,128)(2,1)S(1)} %collective-permute-done.9.grads_ref.refs_2_, bf16[384,384]{1,0:T(8,128)(2,1)} %shard_map.105.refs_0_, ...), custom_call_target="tpu_custom_call" | custom-call | flops 603979776 | bytes 3145728 | tf_op jit(solution)/shard_map/pallas_call | solution.py:22
  68.6 0.0 collective-permute-done.17.refs_1_
  68.6 0.0 collective-permute-done.19.refs_3_
  68.7 0.0 collective-permute-done.18.refs_2_
  68.7 1.9 %shard_map.110 = bf16[1536,256]{1,0:T(8,128)(2,1)} custom-call(s32[8]{0:T(128)S(1)} %fusion.table_ref, f32[1536,256]{1,0:T(8,128)S(1)} %shard_map.108.total_ref, bf16[768,256]{1,0:T(8,128)(2,1)S(1)} %collective-permute-done.9.grads_ref.refs_2_, bf16[912,384]{1,0:T(8,128)(2,1)S(1)} %collective-permute-done.16.refs_4_.refs_0_, ...), custom_call_target="tpu_custom_call" | custom-call | flops 603979776 | bytes 3145728 | tf_op jit(solution)/shard_map/pallas_call | solution.py:22
  (12 shorter events, 0.1 us)
Async XLA Ops:
  0.0 4.5 %copy-start.1 = (bf16[256,384]{1,0:T(8,128)(2,1)S(1)}, bf16[256,384]{1,0:T(8,128)(2,1)}, u32[]{:S(2)}) copy-start(bf16[256,384]{1,0:T(8,128)(2,1)} %g_ref.5) | copy-start | bytes 589828
  0.0 4.5 %copy-start = (bf16[256,384]{1,0:T(8,128)(2,1)S(1)}, bf16[256,384]{1,0:T(8,128)(2,1)}, u32[]{:S(2)}) copy-start(bf16[256,384]{1,0:T(8,128)(2,1)} %v_ref.5) | copy-start | bytes 589828
  0.0 4.5 %copy-start.3 = (bf16[256,384]{1,0:T(8,128)(2,1)S(1)}, bf16[256,384]{1,0:T(8,128)(2,1)}, u32[]{:S(2)}) copy-start(bf16[256,384]{1,0:T(8,128)(2,1)} %k_ref.3) | copy-start | bytes 589828
  0.0 4.5 %copy-start.2 = (bf16[256,384]{1,0:T(8,128)(2,1)S(1)}, bf16[256,384]{1,0:T(8,128)(2,1)}, u32[]{:S(2)}) copy-start(bf16[256,384]{1,0:T(8,128)(2,1)} %q_ref.3) | copy-start | bytes 589828
  0.0 4.5 %copy-start.4 = (f32[256,3]{0,1:T(4,128)S(1)}, f32[256,3]{0,1:T(4,128)}, u32[]{:S(2)}) copy-start(f32[256,3]{0,1:T(4,128)} %param.13) | copy-start | bytes 9220
  1.4 20.0 %collective-permute-start.3 = (bf16[768,384]{1,0:T(8,128)(2,1)S(1)}, bf16[768,384]{1,0:T(8,128)(2,1)S(1)}, u32[]{:S(2)}, u32[]{:S(2)}) collective-permute-start(bf16[768,384]{1,0:T(8,128)(2,1)S(1)} %get-tuple-element.25.token_ref), channel_id=1, source_target_pairs={{0,1},{1,2},{2,3},{3,0},{4,7},{5,4},{6,5},{7,6},{8,9},{9,10},{10,1... | collective-permute-start | bytes 1769480 | tf_op jit(solution)/shard_map/ppermute | solution.py:487
  5.4 2.7 %collective-permute-start = (bf16[784,128]{1,0:T(8,128)(2,1)S(1)}, bf16[784,128]{1,0:T(8,128)(2,1)S(1)}, u32[]{:S(2)}, u32[]{:S(2)}) collective-permute-start(bf16[784,128]{1,0:T(8,128)(2,1)S(1)} %get-tuple-element.26), channel_id=1, source_target_pairs={{0,4},{4,0},{8,12},{12,8},{16,20},{20,16},{24,28},{28,24},{1,5},{5... | collective-permute-start | bytes 602120 | tf_op jit(solution)/shard_map/ppermute | solution.py:513
  8.2 7.3 %collective-permute-start.1 = (bf16[784,128]{1,0:T(8,128)(2,1)S(1)}, bf16[784,128]{1,0:T(8,128)(2,1)S(1)}, u32[]{:S(2)}, u32[]{:S(2)}) collective-permute-start(bf16[784,128]{1,0:T(8,128)(2,1)S(1)} %get-tuple-element.29), channel_id=1, source_target_pairs={{0,8},{4,12},{8,0},{12,4},{16,24},{20,28},{24,16},{28,20},{1,9},{5... | collective-permute-start | bytes 602120 | tf_op jit(solution)/shard_map/ppermute | solution.py:513
  9.8 13.2 %collective-permute-start.10 = (bf16[768,384]{1,0:T(8,128)(2,1)S(1)}, bf16[768,384]{1,0:T(8,128)(2,1)S(1)}, u32[]{:S(2)}, u32[]{:S(2)}) collective-permute-start(bf16[768,384]{1,0:T(8,128)(2,1)S(1)} %get-tuple-element.40), channel_id=1, source_target_pairs={{3,2},{2,1},{4,5},{5,6},{11,10},{10,9},{12,13},{13,14},{19,18},{18... | collective-permute-start | bytes 1769480 | tf_op jit(solution)/shard_map/ppermute | solution.py:488
  16.3 4.6 %collective-permute-start.2 = (bf16[384,128]{1,0:T(8,128)(2,1)S(1)}, bf16[384,128]{1,0:T(8,128)(2,1)S(1)}, u32[]{:S(2)}, u32[]{:S(2)}) collective-permute-start(bf16[384,128]{1,0:T(8,128)(2,1)S(1)} %get-tuple-element.33), channel_id=1, source_target_pairs={{0,16},{4,20},{8,24},{12,28},{16,0},{20,4},{24,8},{28,12},{1,17},{... | collective-permute-start | bytes 294920 | tf_op jit(solution)/shard_map/ppermute | solution.py:513
  21.4 9.9 %collective-permute-start.4 = (bf16[768,384]{1,0:T(8,128)(2,1)S(1)}, bf16[768,384]{1,0:T(8,128)(2,1)S(1)}, u32[]{:S(2)}, u32[]{:S(2)}) collective-permute-start(bf16[768,384]{1,0:T(8,128)(2,1)S(1)} %shard_map.98.refs_0_.refs_1_), channel_id=1, source_target_pairs={{0,8},{4,20},{8,0},{12,28},{16,24},{20,4},{24,16},{28,12},{1,9},{5... | collective-permute-start | bytes 1769480 | tf_op jit(solution)/shard_map/ppermute | solution.py:191
  23.0 14.8 %collective-permute-start.11 = (bf16[768,384]{1,0:T(8,128)(2,1)S(1)}, bf16[768,384]{1,0:T(8,128)(2,1)S(1)}, u32[]{:S(2)}, u32[]{:S(2)}) collective-permute-start(bf16[768,384]{1,0:T(8,128)(2,1)S(1)} %shard_map.103), channel_id=1, source_target_pairs={{2,1},{1,0},{5,6},{6,7},{10,9},{9,8},{13,14},{14,15},{18,17},{17,1... | collective-permute-start | bytes 1769480 | tf_op jit(solution)/shard_map/ppermute | solution.py:551
  31.5 28.6 %collective-permute-start.5 = (bf16[1536,384]{1,0:T(8,128)(2,1)S(1)}, bf16[1536,384]{1,0:T(8,128)(2,1)}, u32[]{:S(2)}, u32[]{:S(2)}) collective-permute-start(bf16[1536,384]{1,0:T(8,128)(2,1)S(1)} %shard_map.99.refs_0_), channel_id=1, source_target_pairs={{0,16},{4,12},{8,24},{12,4},{16,0},{20,28},{24,8},{28,20},{1,17},{... | collective-permute-start | bytes 3538952 | tf_op jit(solution)/shard_map/ppermute | solution.py:191
  35.7 12.9 %collective-permute-start.7 = (bf16[768,256]{1,0:T(8,128)(2,1)S(1)}, bf16[768,256]{1,0:T(8,128)(2,1)}, u32[]{:S(2)}, u32[]{:S(2)}) collective-permute-start(bf16[768,256]{1,0:T(8,128)(2,1)S(1)} %shard_map.100.own_ref), channel_id=1, source_target_pairs={{0,3},{1,0},{2,1},{3,2},{4,7},{5,4},{6,5},{7,6},{8,11},{9,8},{10,9... | collective-permute-start | bytes 1179656 | tf_op jit(solution)/shard_map/ppermute | solution.py:549
  37.0 16.5 %collective-permute-start.6 = (bf16[768,256]{1,0:T(8,128)(2,1)S(1)}, bf16[768,256]{1,0:T(8,128)(2,1)}, u32[]{:S(2)}, u32[]{:S(2)}) collective-permute-start(bf16[768,256]{1,0:T(8,128)(2,1)S(1)} %shard_map.100.own_ref), channel_id=1, source_target_pairs={{0,1},{1,2},{2,3},{3,0},{4,5},{5,6},{6,7},{7,4},{8,9},{9,10},{10,1... | collective-permute-start | bytes 1179656 | tf_op jit(solution)/shard_map/ppermute | solution.py:548
  37.8 2.5 %collective-permute-start.12 = (bf16[384,384]{1,0:T(8,128)(2,1)S(1)}, bf16[384,384]{1,0:T(8,128)(2,1)S(1)}, u32[]{:S(2)}, u32[]{:S(2)}) collective-permute-start(bf16[384,384]{1,0:T(8,128)(2,1)S(1)} %shard_map.104), channel_id=1, source_target_pairs={{0,4},{1,5},{6,2},{7,3},{8,12},{9,13},{14,10},{15,11},{16,20},{17,... | collective-permute-start | bytes 884744 | tf_op jit(solution)/shard_map/ppermute | solution.py:557
  41.0 16.2 %copy-start.5 = (s32[8]{0:T(128)S(1)}, s32[8]{0:T(128)}, u32[]{:S(2)}) copy-start(s32[8]{0:T(128)} %constant.36.clone) | copy-start | bytes 100
  41.0 16.2 %copy-start.6 = (s32[8]{0:T(128)S(1)}, s32[8]{0:T(128)}, u32[]{:S(2)}) copy-start(s32[8]{0:T(128)} %constant.35.clone) | copy-start | bytes 100
  41.0 16.2 %collective-permute-start.14 = (bf16[384,384]{1,0:T(8,128)(2,1)}, bf16[384,384]{1,0:T(8,128)(2,1)S(1)}, u32[]{:S(2)}, u32[]{:S(2)}) collective-permute-start(bf16[384,384]{1,0:T(8,128)(2,1)} %shard_map.105.refs_0_), channel_id=1, source_target_pairs={{0,16},{4,12},{8,24},{12,4},{16,0},{20,28},{24,8},{28,20},{1,17},{... | collective-permute-start | bytes 884744 | tf_op jit(solution)/shard_map/ppermute | solution.py:191
  41.6 15.7 %collective-permute-start.13 = (bf16[384,384]{1,0:T(8,128)(2,1)}, bf16[384,384]{1,0:T(8,128)(2,1)}, u32[]{:S(2)}, u32[]{:S(2)}) collective-permute-start(bf16[384,384]{1,0:T(8,128)(2,1)} %shard_map.105.refs_0_), channel_id=1, source_target_pairs={{0,8},{4,20},{8,0},{12,28},{16,24},{20,4},{24,16},{28,12},{1,9},{5... | collective-permute-start | bytes 884744 | tf_op jit(solution)/shard_map/ppermute | solution.py:191
  54.6 5.4 %collective-permute-start.8 = (bf16[768,256]{1,0:T(8,128)(2,1)S(1)}, bf16[768,256]{1,0:T(8,128)(2,1)S(1)}, u32[]{:S(2)}, u32[]{:S(2)}) collective-permute-start(bf16[768,256]{1,0:T(8,128)(2,1)S(1)} %get-tuple-element.37), channel_id=1, source_target_pairs={{0,4},{4,0},{8,12},{12,8},{16,20},{20,16},{24,28},{28,24},{1,5},{5... | collective-permute-start | bytes 1179656 | tf_op jit(solution)/shard_map/ppermute | solution.py:191
  54.7 11.5 %collective-permute-start.9 = (bf16[768,256]{1,0:T(8,128)(2,1)S(1)}, bf16[768,256]{1,0:T(8,128)(2,1)S(1)}, u32[]{:S(2)}, u32[]{:S(2)}) collective-permute-start(bf16[768,256]{1,0:T(8,128)(2,1)S(1)} %get-tuple-element.39), channel_id=1, source_target_pairs={{0,2},{1,0},{2,3},{3,1},{4,6},{5,4},{6,7},{7,5},{8,10},{9,8},{10,1... | collective-permute-start | bytes 1179656 | tf_op jit(solution)/shard_map/ppermute | solution.py:575
  57.3 9.0 %collective-permute-start.15 = (bf16[384,384]{1,0:T(8,128)(2,1)}, bf16[384,384]{1,0:T(8,128)(2,1)S(1)}, u32[]{:S(2)}, u32[]{:S(2)}) collective-permute-start(bf16[384,384]{1,0:T(8,128)(2,1)} %get-tuple-element.41.refs_1_), channel_id=1, source_target_pairs={{0,16},{4,12},{8,24},{12,4},{16,0},{20,28},{24,8},{28,20},{1,17},{... | collective-permute-start | bytes 884744 | tf_op jit(solution)/shard_map/ppermute | solution.py:191
  60.0 6.9 %collective-permute-start.16 = (bf16[912,384]{1,0:T(8,128)(2,1)S(1)}, bf16[912,384]{1,0:T(8,128)(2,1)S(1)}, u32[]{:S(2)}, u32[]{:S(2)}) collective-permute-start(bf16[912,384]{1,0:T(8,128)(2,1)S(1)} %shard_map.107), channel_id=1, source_target_pairs={{0,4},{4,0},{8,12},{12,8},{16,20},{20,16},{24,28},{28,24},{1,5},{5... | collective-permute-start | bytes 2101256 | tf_op jit(solution)/shard_map/ppermute | solution.py:191
  63.3 5.4 %collective-permute-start.18 = (bf16[1152,256]{1,0:T(8,128)(2,1)S(1)}, bf16[1152,256]{1,0:T(8,128)(2,1)S(1)}, u32[]{:S(2)}, u32[]{:S(2)}) collective-permute-start(bf16[1152,256]{1,0:T(8,128)(2,1)S(1)} %get-tuple-element.43), channel_id=1, source_target_pairs={{0,4},{4,0},{8,12},{12,8},{16,20},{20,16},{24,28},{28,24},{1,5},{5... | collective-permute-start | bytes 1769480 | tf_op jit(solution)/shard_map/ppermute | solution.py:191
  66.3 2.3 %collective-permute-start.17 = (bf16[624,384]{1,0:T(8,128)(2,1)S(1)}, bf16[624,384]{1,0:T(8,128)(2,1)S(1)}, u32[]{:S(2)}, u32[]{:S(2)}) collective-permute-start(bf16[624,384]{1,0:T(8,128)(2,1)S(1)} %shard_map.109), channel_id=1, source_target_pairs={{0,4},{4,0},{8,12},{12,8},{16,20},{20,16},{24,28},{28,24},{1,5},{5... | collective-permute-start | bytes 1437704 | tf_op jit(solution)/shard_map/ppermute | solution.py:191
  66.4 2.3 %collective-permute-start.19 = (bf16[384,256]{1,0:T(8,128)(2,1)S(1)}, bf16[384,256]{1,0:T(8,128)(2,1)S(1)}, u32[]{:S(2)}, u32[]{:S(2)}) collective-permute-start(bf16[384,256]{1,0:T(8,128)(2,1)S(1)} %get-tuple-element.44), channel_id=1, source_target_pairs={{0,4},{4,0},{8,12},{12,8},{16,20},{20,16},{24,28},{28,24},{1,5},{5... | collective-permute-start | bytes 589832 | tf_op jit(solution)/shard_map/ppermute | solution.py:191

commit v10 on v9

--- a/solution.py
+++ b/solution.py
@@ -328,30 +328,21 @@
     )
 
 
-def relay_kernel(own_ref, lower_ref, upper_ref, token_ref, relay_ref, kept_ref, sent_ref):
+def relay_kernel(own_ref, handed_ref, kept_ref, relay_ref):
     mine, odd = lax.axis_index("head"), lax.rem(lax.axis_index("seq"), 2)
-
-    @pl.when(mine == 1)
+    inner = (mine == 1) | (mine == 2)
+
+    @pl.when(inner & (mine + odd == 2))
     def _():
-        relay_ref[...] = upper_ref[...]
-
-    @pl.when(mine == 2)
+        relay_ref[...] = kept_ref[...]
+
+    @pl.when(inner & (mine + odd != 2))
     def _():
-        relay_ref[...] = lower_ref[...]
-
-    @pl.when((mine != 1) & (mine != 2))
+        relay_ref[...] = handed_ref[...]
+
+    @pl.when(jnp.logical_not(inner))
     def _():
         relay_ref[...] = own_ref[...]
-
-    @pl.when(odd == 0)
-    def _():
-        kept_ref[...] = lower_ref[...]
-        sent_ref[...] = upper_ref[...]
-
-    @pl.when(odd == 1)
-    def _():
-        kept_ref[...] = upper_ref[...]
-        sent_ref[...] = lower_ref[...]
 
 
 def split_kernel(both_ref, token_ref, theirs_ref):
@@ -545,8 +536,8 @@
         (near,) = join(((first, 0, two), (second, 0, two)))
         blocks = [near, share_hop(near, 1)]
         (ready,) = gate([both], [total])
-        p1 = lax.ppermute(ready, "head", ring[1])
-        p3 = lax.ppermute(ready, "head", ring[3])
+        handed = lax.ppermute(ready, axes, moves(ring[3], ring[1]))
+        kept = lax.ppermute(ready, axes, moves(ring[1], ring[3]))
         (passing,) = gate([passing], [first])
         passing = lax.ppermute(passing, axes, moves([(2, 1), (1, 0)], [(1, 2), (2, 3)]))
         theirs = call(
@@ -567,10 +558,11 @@
         fourth, fifth = gate([fourth, fifth])
         sixth = share_hop(fourth, 1)
         (early,) = join(((third, 0, one), (fourth, 0, one), (fifth, 0, CUT)))
-        relay, kept, handed = call(
-            relay_kernel, [jax.ShapeDtypeStruct(both.shape, BF16)] * 3, 0, 0, ready, p1, p3, total,
-            in_specs=[pl.BlockSpec(memory_space=pltpu.VMEM)] * 3 + [pl.BlockSpec(memory_space=pl.ANY)],
-            out_specs=[pl.BlockSpec(memory_space=pltpu.VMEM)] * 3,
+        handed, kept = gate([handed, kept], [total])
+        relay = call(
+            relay_kernel, jax.ShapeDtypeStruct(both.shape, BF16), 0, 0, ready, handed, kept,
+            in_specs=[pl.BlockSpec(memory_space=pltpu.VMEM)] * 3,
+            out_specs=pl.BlockSpec(memory_space=pltpu.VMEM),
         )
         p2 = lax.ppermute(relay, "head", [(0, 2), (1, 0), (2, 3), (3, 1)])
         got = share_hop(handed, 2)

time: 70.9 us -> 70.7 us (level)
  waiting for transfers between devices: 29.3 us -> 28.2 us
  starting transfers between devices: 23.6 us -> 24.6 us
    ppermute x1, starting transfers between devices: 2.48 us -> 0.61 us  [shards(): p2 = lax.ppermute(relay, 'head', [(0, 2), (1, 0), (2, 3), (3, 1)])]
    ppermute x2, waiting for transfers between devices: 10.4 us -> 8.56 us  [the longest x1 4.45 us: shards(): kept = lax.ppermute(ready, axes, moves(ring[1], ring[3]))]
    ppermute x2, starting transfers between devices: 2.08 us -> 3.88 us  [the longest x1 2.88 us: shards(): handed = lax.ppermute(ready, axes, moves(ring[3], ring[1]))]
    ppermute x10, starting transfers between devices: 7.98 us -> 8.99 us  [share_hop(): return lax.ppermute(held, 'seq', pairs)]
    ppermute x1, waiting for transfers between devices: 2.39 us -> 3.18 us  [shards(): p2 = lax.ppermute(relay, 'head', [(0, 2), (1, 0), (2, 3), (3, 1)])]
    pallas_call x20 -> x21, Pallas kernels: 17.3 us -> 17.3 us  [call(): pl.pallas_call(kernel, out_shape=out_shape, cost_estimate=pl.CostEstimate...]
where the time goes in v10:
time: 70.7 us; the launch traced here: 70.4 us
  waiting for transfers between devices  28.2 us (40%)
  starting transfers between devices  24.6 us (35%)
  Pallas kernels  17.3 us (24%)
    pallas_call x21, Pallas kernels, call(): pl.pallas_call(kernel, out_shape=out_shape, cost_estimate=pl.CostEstimate...  17.3 us
    ppermute x10, starting transfers between devices, share_hop(): return lax.ppermute(held, 'seq', pairs)  8.99 us
    ppermute x3, waiting for transfers between devices, shards(): got = lax.ppermute(sent, 'seq', [(i, i ^ hop) for i in range(nseq)])  8.2 us
    ppermute x10, waiting for transfers between devices, share_hop(): return lax.ppermute(held, 'seq', pairs)  7.12 us
    ppermute x3, starting transfers between devices, shards(): got = lax.ppermute(sent, 'seq', [(i, i ^ hop) for i in range(nseq)])  4.73 us
    ppermute x1, waiting for transfers between devices, shards(): kept = lax.ppermute(ready, axes, moves(ring[1], ring[3]))  4.45 us
    ppermute x1, waiting for transfers between devices, shards(): handed = lax.ppermute(ready, axes, moves(ring[3], ring[1]))  4.11 us
    ppermute x1, waiting for transfers between devices, shards(): p2 = lax.ppermute(relay, 'head', [(0, 2), (1, 0), (2, 3), (3, 1)])  3.18 us
  transfers between devices with their start and end apart: 20, of which 8 were waited for; matrix products, arithmetic and copies ran while one was open for 0% of the time, Pallas kernels for 20%

profile of v10, /device:TPU:0, one launch (start us, length us, event | category | flops | bytes accessed | tf_op | source)
XLA Modules:
  0.0 70.4 jit_solution(5562772726161433089)
XLA Ops:
  0.0 0.0 copy-start.1
  0.0 0.0 copy-start
  0.0 0.0 copy-start.3
  0.0 1.4 %shard_map.91 = (bf16[768,384]{1,0:T(8,128)(2,1)S(1)}, bf16[768,384]{1,0:T(8,128)(2,1)S(1)}) custom-call(bf16[6144,384]{1,0:T(8,128)(2,1)} %wq_ref.3, bf16[6144,384]{1,0:T(8,128)(2,1)} %wk_ref.3), custom_call_target="tpu_custom_call" | custom-call | bytes 2359296 | tf_op jit(solution)/shard_map/pallas_call | solution.py:22
  1.4 3.1 %collective-permute-start.3 = (bf16[768,384]{1,0:T(8,128)(2,1)S(1)}, bf16[768,384]{1,0:T(8,128)(2,1)S(1)}, u32[]{:S(2)}, u32[]{:S(2)}) collective-permute-start(bf16[768,384]{1,0:T(8,128)(2,1)S(1)} %get-tuple-element.24.token_ref), channel_id=1, source_target_pairs={{0,1},{1,2},{2,3},{3,0},{4,7},{5,4},{6,5},{7,6},{8,9},{9,10},{10,1... | collective-permute-start | bytes 1769480 | tf_op jit(solution)/shard_map/ppermute | solution.py:478
  4.5 0.0 copy-done.1
  4.5 0.0 copy-done
  4.5 0.0 copy-done.3
  4.5 0.0 copy-done.2
  4.5 0.0 copy-done.4
  4.5 0.9 %shard_map.92 = (bf16[784,128]{1,0:T(8,128)(2,1)S(1)}, f32[768,128]{1,0:T(8,128)S(1)}, f32[24,128]{1,0:T(8,128)S(1)}) custom-call(f32[3,256]{1,0:T(4,128)S(1)} %bitcast.1, bf16[256,384]{1,0:T(8,128)(2,1)S(1)} %copy-done.2, bf16[256,384]{1,0:T(8,128)(2,1)S(1)} %copy-done.3, bf16[256,384]{1,0:T(8,128)(2,1)S(1)} %copy-done, bf16[256,384]{1,0:T(8,128)(2,1)S(1)} %copy-done.1, ...), custom_call_target="tpu_custom_call" | custom-call | flops 50331648 | bytes 786432 | tf_op jit(solution)/shard_map/pallas_call | solution.py:22
  5.4 1.6 %collective-permute-start = (bf16[784,128]{1,0:T(8,128)(2,1)S(1)}, bf16[784,128]{1,0:T(8,128)(2,1)S(1)}, u32[]{:S(2)}, u32[]{:S(2)}) collective-permute-start(bf16[784,128]{1,0:T(8,128)(2,1)S(1)} %get-tuple-element.25), channel_id=1, source_target_pairs={{0,4},{4,0},{8,12},{12,8},{16,20},{20,16},{24,28},{28,24},{1,5},{5... | collective-permute-start | bytes 602120 | tf_op jit(solution)/shard_map/ppermute | solution.py:504
  7.0 1.1 %collective-permute-done.got_ref = bf16[784,128]{1,0:T(8,128)(2,1)S(1)} collective-permute-done((bf16[784,128]{1,0:T(8,128)(2,1)S(1)}, bf16[784,128]{1,0:T(8,128)(2,1)S(1)}, u32[]{:S(2)}, u32[]{:S(2)}) %collective-permute-start) | collective-permute-done | bytes 200736 | tf_op jit(solution)/shard_map/ppermute | solution.py:504
  8.1 0.1 shard_map.93
  8.2 1.6 %collective-permute-start.1 = (bf16[784,128]{1,0:T(8,128)(2,1)S(1)}, bf16[784,128]{1,0:T(8,128)(2,1)S(1)}, u32[]{:S(2)}, u32[]{:S(2)}) collective-permute-start(bf16[784,128]{1,0:T(8,128)(2,1)S(1)} %get-tuple-element.28), channel_id=1, source_target_pairs={{0,8},{4,12},{8,0},{12,4},{16,24},{20,28},{24,16},{28,20},{1,9},{5... | collective-permute-start | bytes 602120 | tf_op jit(solution)/shard_map/ppermute | solution.py:504
  9.8 0.7 collective-permute-start.10
  10.4 5.1 %collective-permute-done.1.got_ref = bf16[784,128]{1,0:T(8,128)(2,1)S(1)} collective-permute-done((bf16[784,128]{1,0:T(8,128)(2,1)S(1)}, bf16[784,128]{1,0:T(8,128)(2,1)S(1)}, u32[]{:S(2)}, u32[]{:S(2)}) %collective-permute-start.1) | collective-permute-done | bytes 200736 | tf_op jit(solution)/shard_map/ppermute | solution.py:504
  15.5 0.8 %shard_map.94 = (bf16[384,128]{1,0:T(8,128)(2,1)S(1)}, f32[768,128]{1,0:T(8,128)}, f32[24,128]{1,0:T(8,128)S(1)}, f32[768,128]{1,0:T(8,128)S(1)}) custom-call(bf16[784,128]{1,0:T(8,128)(2,1)S(1)} %collective-permute-done.1.got_ref, f32[768,128]{1,0:T(8,128)S(1)} %get-tuple-element.29.held_ref, f32[24,128]{1,0:T(8,128)S(1)} %get-tuple-element.30.logs_ref, ...), custom_call_target="tpu_custom_call" | custom-call | flops 491520 | bytes 786432 | tf_op jit(solution)/shard_map/pallas_call | solution.py:22
  16.3 1.5 %collective-permute-start.2 = (bf16[384,128]{1,0:T(8,128)(2,1)S(1)}, bf16[384,128]{1,0:T(8,128)(2,1)S(1)}, u32[]{:S(2)}, u32[]{:S(2)}) collective-permute-start(bf16[384,128]{1,0:T(8,128)(2,1)S(1)} %get-tuple-element.32), channel_id=1, source_target_pairs={{0,16},{4,20},{8,24},{12,28},{16,0},{20,4},{24,8},{28,12},{1,17},{... | collective-permute-start | bytes 294920 | tf_op jit(solution)/shard_map/ppermute | solution.py:504
  17.9 1.0 %shard_map.95.local_ref = f32[768,256]{1,0:T(8,128)S(1)} custom-call(f32[3,256]{1,0:T(4,128)S(1)} %bitcast.2, bf16[256,384]{1,0:T(8,128)(2,1)S(1)} %copy-done.2, bf16[256,384]{1,0:T(8,128)(2,1)S(1)} %copy-done.3, bf16[256,384]{1,0:T(8,128)(2,1)S(1)} %copy-done, bf16[256,384]{1,0:T(8,128)(2,1)S(1)} %copy-done.1), custom_call_target="tpu_custom_call" | custom-call | flops 150994944 | bytes 1572864 | tf_op jit(solution)/shard_map/pallas_call | solution.py:22
  18.9 2.1 %collective-permute-done.2.got_ref = bf16[384,128]{1,0:T(8,128)(2,1)S(1)} collective-permute-done((bf16[384,128]{1,0:T(8,128)(2,1)S(1)}, bf16[384,128]{1,0:T(8,128)(2,1)S(1)}, u32[]{:S(2)}, u32[]{:S(2)}) %collective-permute-start.2) | collective-permute-done | bytes 98336 | tf_op jit(solution)/shard_map/ppermute | solution.py:504
  21.0 0.4 shard_map.96.grads_ref.refs_1_.refs_0_
  21.4 0.0 collective-permute-done.3.refs_0_
  21.4 1.6 %collective-permute-start.4 = (bf16[768,384]{1,0:T(8,128)(2,1)S(1)}, bf16[768,384]{1,0:T(8,128)(2,1)S(1)}, u32[]{:S(2)}, u32[]{:S(2)}) collective-permute-start(bf16[768,384]{1,0:T(8,128)(2,1)S(1)} %shard_map.98.refs_0_.refs_1_), channel_id=1, source_target_pairs={{0,8},{4,20},{8,0},{12,28},{16,24},{20,4},{24,16},{28,12},{1,9},{5... | collective-permute-start | bytes 1769480 | tf_op jit(solution)/shard_map/ppermute | solution.py:191
  23.0 0.0 collective-permute-done.10.refs_0_
  23.0 1.3 %collective-permute-start.11 = (bf16[768,384]{1,0:T(8,128)(2,1)S(1)}, bf16[768,384]{1,0:T(8,128)(2,1)S(1)}, u32[]{:S(2)}, u32[]{:S(2)}) collective-permute-start(bf16[768,384]{1,0:T(8,128)(2,1)S(1)} %shard_map.104), channel_id=1, source_target_pairs={{2,1},{1,0},{5,6},{6,7},{10,9},{9,8},{13,14},{14,15},{18,17},{17,1... | collective-permute-start | bytes 1769480 | tf_op jit(solution)/shard_map/ppermute | solution.py:542
  24.3 7.1 %collective-permute-done.4.refs_1_ = bf16[768,384]{1,0:T(8,128)(2,1)S(1)} collective-permute-done((bf16[768,384]{1,0:T(8,128)(2,1)S(1)}, bf16[768,384]{1,0:T(8,128)(2,1)S(1)}, u32[]{:S(2)}, u32[]{:S(2)}) %collective-permute-start.4) | collective-permute-done | bytes 589856 | tf_op jit(solution)/shard_map/ppermute | solution.py:191
  31.4 0.1 shard_map.99.refs_0_
  31.5 1.6 %collective-permute-start.5 = (bf16[1536,384]{1,0:T(8,128)(2,1)S(1)}, bf16[1536,384]{1,0:T(8,128)(2,1)}, u32[]{:S(2)}, u32[]{:S(2)}) collective-permute-start(bf16[1536,384]{1,0:T(8,128)(2,1)S(1)} %shard_map.99.refs_0_), channel_id=1, source_target_pairs={{0,16},{4,12},{8,24},{12,4},{16,0},{20,28},{24,8},{28,20},{1,17},{... | collective-permute-start | bytes 3538952 | tf_op jit(solution)/shard_map/ppermute | solution.py:191
  33.1 2.6 %shard_map.97.refs_1_.refs_2_.total_ref.token_ref = f32[1536,256]{1,0:T(8,128)S(1)} custom-call(bf16[6144,384]{1,0:T(8,128)(2,1)} %wq_ref.3, bf16[6144,384]{1,0:T(8,128)(2,1)} %wk_ref.3, bf16[768,256]{1,0:T(8,128)(2,1)S(1)} %shard_map.96.grads_ref.refs_1_.refs_0_), custom_call_target="tpu_custom_call" | custom-call | flops 603979776 | bytes 2359296 | tf_op jit(solution)/shard_map/pallas_call | solution.py:22
  35.7 1.0 %collective-permute-start.7 = (bf16[768,256]{1,0:T(8,128)(2,1)S(1)}, bf16[768,256]{1,0:T(8,128)(2,1)}, u32[]{:S(2)}, u32[]{:S(2)}) collective-permute-start(bf16[768,256]{1,0:T(8,128)(2,1)S(1)} %shard_map.100.own_ref), channel_id=1, source_target_pairs={{0,1},{1,2},{2,3},{3,0},{4,7},{5,4},{6,5},{7,6},{8,9},{9,10},{10,1... | collective-permute-start | bytes 1179656 | tf_op jit(solution)/shard_map/ppermute | solution.py:540
  36.7 2.9 %collective-permute-start.6 = (bf16[768,256]{1,0:T(8,128)(2,1)S(1)}, bf16[768,256]{1,0:T(8,128)(2,1)}, u32[]{:S(2)}, u32[]{:S(2)}) collective-permute-start(bf16[768,256]{1,0:T(8,128)(2,1)S(1)} %shard_map.100.own_ref), channel_id=1, source_target_pairs={{0,3},{1,0},{2,1},{3,2},{4,5},{5,6},{6,7},{7,4},{8,11},{9,8},{10,9... | collective-permute-start | bytes 1179656 | tf_op jit(solution)/shard_map/ppermute | solution.py:539
  39.6 0.0 collective-permute-done.11.both_ref
  39.6 1.3 %collective-permute-start.12 = (bf16[384,384]{1,0:T(8,128)(2,1)S(1)}, bf16[384,384]{1,0:T(8,128)(2,1)S(1)}, u32[]{:S(2)}, u32[]{:S(2)}) collective-permute-start(bf16[384,384]{1,0:T(8,128)(2,1)S(1)} %shard_map.105), channel_id=1, source_target_pairs={{0,4},{1,5},{6,2},{7,3},{8,12},{9,13},{14,10},{15,11},{16,20},{17,... | collective-permute-start | bytes 884744 | tf_op jit(solution)/shard_map/ppermute | solution.py:548
  40.9 1.2 %collective-permute-done.12.got_ref = bf16[384,384]{1,0:T(8,128)(2,1)S(1)} collective-permute-done((bf16[384,384]{1,0:T(8,128)(2,1)S(1)}, bf16[384,384]{1,0:T(8,128)(2,1)S(1)}, u32[]{:S(2)}, u32[]{:S(2)}) %collective-permute-start.12) | collective-permute-done | bytes 294944 | tf_op jit(solution)/shard_map/ppermute | solution.py:548
  42.1 0.7 %shard_map.106.refs_0_ = bf16[384,384]{1,0:T(8,128)(2,1)} custom-call(bf16[768,384]{1,0:T(8,128)(2,1)S(1)} %collective-permute-done.11.both_ref, bf16[384,384]{1,0:T(8,128)(2,1)S(1)} %collective-permute-done.12.got_ref), custom_call_target="tpu_custom_call" | custom-call | tf_op jit(solution)/shard_map/pallas_call | solution.py:22
  42.8 0.5 collective-permute-start.14
  43.3 1.5 %collective-permute-start.13 = (bf16[384,384]{1,0:T(8,128)(2,1)}, bf16[384,384]{1,0:T(8,128)(2,1)}, u32[]{:S(2)}, u32[]{:S(2)}) collective-permute-start(bf16[384,384]{1,0:T(8,128)(2,1)} %shard_map.106.refs_0_), channel_id=1, source_target_pairs={{0,8},{4,20},{8,0},{12,28},{16,24},{20,4},{24,16},{28,12},{1,9},{5... | collective-permute-start | bytes 884744 | tf_op jit(solution)/shard_map/ppermute | solution.py:191
  44.8 4.4 %collective-permute-done.7.refs_1_ = bf16[768,256]{1,0:T(8,128)(2,1)} collective-permute-done((bf16[768,256]{1,0:T(8,128)(2,1)S(1)}, bf16[768,256]{1,0:T(8,128)(2,1)}, u32[]{:S(2)}, u32[]{:S(2)}) %collective-permute-start.7) | collective-permute-done | bytes 393248 | tf_op jit(solution)/shard_map/ppermute | solution.py:540
  49.3 4.1 %collective-permute-done.6.refs_0_ = bf16[768,256]{1,0:T(8,128)(2,1)} collective-permute-done((bf16[768,256]{1,0:T(8,128)(2,1)S(1)}, bf16[768,256]{1,0:T(8,128)(2,1)}, u32[]{:S(2)}, u32[]{:S(2)}) %collective-permute-start.6) | collective-permute-done | bytes 393248 | tf_op jit(solution)/shard_map/ppermute | solution.py:539
  53.4 0.0 collective-permute-start.8
  53.4 1.1 %shard_map.103 = bf16[768,256]{1,0:T(8,128)(2,1)S(1)} custom-call(bf16[768,256]{1,0:T(8,128)(2,1)S(1)} %shard_map.100.own_ref, bf16[768,256]{1,0:T(8,128)(2,1)} %get-tuple-element.36.handed_ref, bf16[768,256]{1,0:T(8,128)(2,1)} %get-tuple-element.35.refs_2_.kept_ref), custom_call_target="tpu_custom_call" | custom-call | tf_op jit(solution)/shard_map/pallas_call | solution.py:22
  54.5 0.6 collective-permute-start.9
  55.2 0.0 copy-done.5
  55.2 0.0 copy-done.6
  55.2 0.0 collective-permute-done.14.refs_1_
  55.2 0.0 collective-permute-done.13.refs_0_
  55.2 2.3 %collective-permute-start.15 = (bf16[384,384]{1,0:T(8,128)(2,1)}, bf16[384,384]{1,0:T(8,128)(2,1)S(1)}, u32[]{:S(2)}, u32[]{:S(2)}) collective-permute-start(bf16[384,384]{1,0:T(8,128)(2,1)} %get-tuple-element.39.refs_1_), channel_id=1, source_target_pairs={{0,16},{4,12},{8,24},{12,4},{16,0},{20,28},{24,8},{28,20},{1,17},{... | collective-permute-start | bytes 884744 | tf_op jit(solution)/shard_map/ppermute | solution.py:191
  57.5 1.1 %shard_map.108 = bf16[912,384]{1,0:T(8,128)(2,1)S(1)} custom-call(bf16[384,384]{1,0:T(8,128)(2,1)} %shard_map.106.refs_0_, bf16[384,384]{1,0:T(8,128)(2,1)} %get-tuple-element.39.refs_1_, bf16[384,384]{1,0:T(8,128)(2,1)S(1)} %get-tuple-element.40.refs_2_.refs_0_), custom_call_target="tpu_custom_call" | custom-call | tf_op jit(solution)/shard_map/pallas_call | solution.py:22
  58.6 0.9 %collective-permute-start.16 = (bf16[912,384]{1,0:T(8,128)(2,1)S(1)}, bf16[912,384]{1,0:T(8,128)(2,1)S(1)}, u32[]{:S(2)}, u32[]{:S(2)}) collective-permute-start(bf16[912,384]{1,0:T(8,128)(2,1)S(1)} %shard_map.108), channel_id=1, source_target_pairs={{0,4},{4,0},{8,12},{12,8},{16,20},{20,16},{24,28},{28,24},{1,5},{5... | collective-permute-start | bytes 2101256 | tf_op jit(solution)/shard_map/ppermute | solution.py:191
  59.5 0.0 collective-permute-done.8.refs_3_
  59.5 0.0 collective-permute-done.5.refs_1_
  59.5 3.3 %shard_map.102 = (f32[1536,256]{1,0:T(8,128)S(1)}, bf16[1152,256]{1,0:T(8,128)(2,1)S(1)}, bf16[384,256]{1,0:T(8,128)(2,1)S(1)}) custom-call(s32[4]{0:T(128)S(1)} %and_select_fusion.table_ref, f32[1536,256]{1,0:T(8,128)S(1)} %shard_map.97.refs_1_.refs_2_.total_ref.token_ref, bf16[1536,384]{1,0:T(8,128)(2,1)S(1)} %shard_map.99.refs_0_, ...), custom_call_target="tpu_custom_call" | custom-call | tf_op jit(solution)/shard_map/pallas_call | solution.py:22
  62.9 0.1 collective-permute-start.18
  62.9 3.2 %collective-permute-done.9.grads_ref.refs_2_ = bf16[768,256]{1,0:T(8,128)(2,1)S(1)} collective-permute-done((bf16[768,256]{1,0:T(8,128)(2,1)S(1)}, bf16[768,256]{1,0:T(8,128)(2,1)S(1)}, u32[]{:S(2)}, u32[]{:S(2)}) %collective-permute-start.9) | collective-permute-done | bytes 393248 | tf_op jit(solution)/shard_map/ppermute | solution.py:567
  66.1 0.0 collective-permute-done.15.refs_3_.refs_1_
  66.2 0.1 collective-permute-start.17
  66.3 0.5 collective-permute-start.19
  66.8 0.0 collective-permute-done.16.refs_4_.refs_0_
  66.8 1.8 %shard_map.109.total_ref = f32[1536,256]{1,0:T(8,128)S(1)} custom-call(s32[8]{0:T(128)S(1)} %fusion.table_ref, f32[1536,256]{1,0:T(8,128)S(1)} %get-tuple-element.37.total_ref, bf16[768,256]{1,0:T(8,128)(2,1)S(1)} %collective-permute-done.9.grads_ref.refs_2_, bf16[384,384]{1,0:T(8,128)(2,1)} %shard_map.106.refs_0_, ...), custom_call_target="tpu_custom_call" | custom-call | flops 603979776 | bytes 3145728 | tf_op jit(solution)/shard_map/pallas_call | solution.py:22
  68.5 0.0 collective-permute-done.17.refs_1_
  68.5 0.0 collective-permute-done.19.refs_3_
  68.5 0.0 collective-permute-done.18.refs_2_
  68.6 1.9 %shard_map.111 = bf16[1536,256]{1,0:T(8,128)(2,1)} custom-call(s32[8]{0:T(128)S(1)} %fusion.table_ref, f32[1536,256]{1,0:T(8,128)S(1)} %shard_map.109.total_ref, bf16[768,256]{1,0:T(8,128)(2,1)S(1)} %collective-permute-done.9.grads_ref.refs_2_, bf16[912,384]{1,0:T(8,128)(2,1)S(1)} %collective-permute-done.16.refs_4_.refs_0_, ...), custom_call_target="tpu_custom_call" | custom-call | flops 603979776 | bytes 3145728 | tf_op jit(solution)/shard_map/pallas_call | solution.py:22
  (13 shorter events, 0.1 us)
Async XLA Ops:
  0.0 4.5 %copy-start.1 = (bf16[256,384]{1,0:T(8,128)(2,1)S(1)}, bf16[256,384]{1,0:T(8,128)(2,1)}, u32[]{:S(2)}) copy-start(bf16[256,384]{1,0:T(8,128)(2,1)} %g_ref.5) | copy-start | bytes 589828
  0.0 4.5 %copy-start = (bf16[256,384]{1,0:T(8,128)(2,1)S(1)}, bf16[256,384]{1,0:T(8,128)(2,1)}, u32[]{:S(2)}) copy-start(bf16[256,384]{1,0:T(8,128)(2,1)} %v_ref.5) | copy-start | bytes 589828
  0.0 4.5 %copy-start.3 = (bf16[256,384]{1,0:T(8,128)(2,1)S(1)}, bf16[256,384]{1,0:T(8,128)(2,1)}, u32[]{:S(2)}) copy-start(bf16[256,384]{1,0:T(8,128)(2,1)} %k_ref.3) | copy-start | bytes 589828
  0.0 4.5 %copy-start.2 = (bf16[256,384]{1,0:T(8,128)(2,1)S(1)}, bf16[256,384]{1,0:T(8,128)(2,1)}, u32[]{:S(2)}) copy-start(bf16[256,384]{1,0:T(8,128)(2,1)} %q_ref.3) | copy-start | bytes 589828
  0.0 4.5 %copy-start.4 = (f32[256,3]{0,1:T(4,128)S(1)}, f32[256,3]{0,1:T(4,128)}, u32[]{:S(2)}) copy-start(f32[256,3]{0,1:T(4,128)} %param.13) | copy-start | bytes 9220
  1.4 20.0 %collective-permute-start.3 = (bf16[768,384]{1,0:T(8,128)(2,1)S(1)}, bf16[768,384]{1,0:T(8,128)(2,1)S(1)}, u32[]{:S(2)}, u32[]{:S(2)}) collective-permute-start(bf16[768,384]{1,0:T(8,128)(2,1)S(1)} %get-tuple-element.24.token_ref), channel_id=1, source_target_pairs={{0,1},{1,2},{2,3},{3,0},{4,7},{5,4},{6,5},{7,6},{8,9},{9,10},{10,1... | collective-permute-start | bytes 1769480 | tf_op jit(solution)/shard_map/ppermute | solution.py:478
  5.4 2.7 %collective-permute-start = (bf16[784,128]{1,0:T(8,128)(2,1)S(1)}, bf16[784,128]{1,0:T(8,128)(2,1)S(1)}, u32[]{:S(2)}, u32[]{:S(2)}) collective-permute-start(bf16[784,128]{1,0:T(8,128)(2,1)S(1)} %get-tuple-element.25), channel_id=1, source_target_pairs={{0,4},{4,0},{8,12},{12,8},{16,20},{20,16},{24,28},{28,24},{1,5},{5... | collective-permute-start | bytes 602120 | tf_op jit(solution)/shard_map/ppermute | solution.py:504
  8.2 7.3 %collective-permute-start.1 = (bf16[784,128]{1,0:T(8,128)(2,1)S(1)}, bf16[784,128]{1,0:T(8,128)(2,1)S(1)}, u32[]{:S(2)}, u32[]{:S(2)}) collective-permute-start(bf16[784,128]{1,0:T(8,128)(2,1)S(1)} %get-tuple-element.28), channel_id=1, source_target_pairs={{0,8},{4,12},{8,0},{12,4},{16,24},{20,28},{24,16},{28,20},{1,9},{5... | collective-permute-start | bytes 602120 | tf_op jit(solution)/shard_map/ppermute | solution.py:504
  9.8 13.2 %collective-permute-start.10 = (bf16[768,384]{1,0:T(8,128)(2,1)S(1)}, bf16[768,384]{1,0:T(8,128)(2,1)S(1)}, u32[]{:S(2)}, u32[]{:S(2)}) collective-permute-start(bf16[768,384]{1,0:T(8,128)(2,1)S(1)} %get-tuple-element.38), channel_id=1, source_target_pairs={{3,2},{2,1},{4,5},{5,6},{11,10},{10,9},{12,13},{13,14},{19,18},{18... | collective-permute-start | bytes 1769480 | tf_op jit(solution)/shard_map/ppermute | solution.py:479
  16.3 4.6 %collective-permute-start.2 = (bf16[384,128]{1,0:T(8,128)(2,1)S(1)}, bf16[384,128]{1,0:T(8,128)(2,1)S(1)}, u32[]{:S(2)}, u32[]{:S(2)}) collective-permute-start(bf16[384,128]{1,0:T(8,128)(2,1)S(1)} %get-tuple-element.32), channel_id=1, source_target_pairs={{0,16},{4,20},{8,24},{12,28},{16,0},{20,4},{24,8},{28,12},{1,17},{... | collective-permute-start | bytes 294920 | tf_op jit(solution)/shard_map/ppermute | solution.py:504
  21.4 9.9 %collective-permute-start.4 = (bf16[768,384]{1,0:T(8,128)(2,1)S(1)}, bf16[768,384]{1,0:T(8,128)(2,1)S(1)}, u32[]{:S(2)}, u32[]{:S(2)}) collective-permute-start(bf16[768,384]{1,0:T(8,128)(2,1)S(1)} %shard_map.98.refs_0_.refs_1_), channel_id=1, source_target_pairs={{0,8},{4,20},{8,0},{12,28},{16,24},{20,4},{24,16},{28,12},{1,9},{5... | collective-permute-start | bytes 1769480 | tf_op jit(solution)/shard_map/ppermute | solution.py:191
  23.0 16.6 %collective-permute-start.11 = (bf16[768,384]{1,0:T(8,128)(2,1)S(1)}, bf16[768,384]{1,0:T(8,128)(2,1)S(1)}, u32[]{:S(2)}, u32[]{:S(2)}) collective-permute-start(bf16[768,384]{1,0:T(8,128)(2,1)S(1)} %shard_map.104), channel_id=1, source_target_pairs={{2,1},{1,0},{5,6},{6,7},{10,9},{9,8},{13,14},{14,15},{18,17},{17,1... | collective-permute-start | bytes 1769480 | tf_op jit(solution)/shard_map/ppermute | solution.py:542
  31.5 28.1 %collective-permute-start.5 = (bf16[1536,384]{1,0:T(8,128)(2,1)S(1)}, bf16[1536,384]{1,0:T(8,128)(2,1)}, u32[]{:S(2)}, u32[]{:S(2)}) collective-permute-start(bf16[1536,384]{1,0:T(8,128)(2,1)S(1)} %shard_map.99.refs_0_), channel_id=1, source_target_pairs={{0,16},{4,12},{8,24},{12,4},{16,0},{20,28},{24,8},{28,20},{1,17},{... | collective-permute-start | bytes 3538952 | tf_op jit(solution)/shard_map/ppermute | solution.py:191
  35.7 13.6 %collective-permute-start.7 = (bf16[768,256]{1,0:T(8,128)(2,1)S(1)}, bf16[768,256]{1,0:T(8,128)(2,1)}, u32[]{:S(2)}, u32[]{:S(2)}) collective-permute-start(bf16[768,256]{1,0:T(8,128)(2,1)S(1)} %shard_map.100.own_ref), channel_id=1, source_target_pairs={{0,1},{1,2},{2,3},{3,0},{4,7},{5,4},{6,5},{7,6},{8,9},{9,10},{10,1... | collective-permute-start | bytes 1179656 | tf_op jit(solution)/shard_map/ppermute | solution.py:540
  36.7 16.7 %collective-permute-start.6 = (bf16[768,256]{1,0:T(8,128)(2,1)S(1)}, bf16[768,256]{1,0:T(8,128)(2,1)}, u32[]{:S(2)}, u32[]{:S(2)}) collective-permute-start(bf16[768,256]{1,0:T(8,128)(2,1)S(1)} %shard_map.100.own_ref), channel_id=1, source_target_pairs={{0,3},{1,0},{2,1},{3,2},{4,5},{5,6},{6,7},{7,4},{8,11},{9,8},{10,9... | collective-permute-start | bytes 1179656 | tf_op jit(solution)/shard_map/ppermute | solution.py:539
  39.6 2.5 %collective-permute-start.12 = (bf16[384,384]{1,0:T(8,128)(2,1)S(1)}, bf16[384,384]{1,0:T(8,128)(2,1)S(1)}, u32[]{:S(2)}, u32[]{:S(2)}) collective-permute-start(bf16[384,384]{1,0:T(8,128)(2,1)S(1)} %shard_map.105), channel_id=1, source_target_pairs={{0,4},{1,5},{6,2},{7,3},{8,12},{9,13},{14,10},{15,11},{16,20},{17,... | collective-permute-start | bytes 884744 | tf_op jit(solution)/shard_map/ppermute | solution.py:548
  42.8 12.3 %collective-permute-start.14 = (bf16[384,384]{1,0:T(8,128)(2,1)}, bf16[384,384]{1,0:T(8,128)(2,1)S(1)}, u32[]{:S(2)}, u32[]{:S(2)}) collective-permute-start(bf16[384,384]{1,0:T(8,128)(2,1)} %shard_map.106.refs_0_), channel_id=1, source_target_pairs={{0,16},{4,12},{8,24},{12,4},{16,0},{20,28},{24,8},{28,20},{1,17},{... | collective-permute-start | bytes 884744 | tf_op jit(solution)/shard_map/ppermute | solution.py:191
  43.3 11.8 %collective-permute-start.13 = (bf16[384,384]{1,0:T(8,128)(2,1)}, bf16[384,384]{1,0:T(8,128)(2,1)}, u32[]{:S(2)}, u32[]{:S(2)}) collective-permute-start(bf16[384,384]{1,0:T(8,128)(2,1)} %shard_map.106.refs_0_), channel_id=1, source_target_pairs={{0,8},{4,20},{8,0},{12,28},{16,24},{20,4},{24,16},{28,12},{1,9},{5... | collective-permute-start | bytes 884744 | tf_op jit(solution)/shard_map/ppermute | solution.py:191
  44.8 10.3 %copy-start.5 = (s32[8]{0:T(128)S(1)}, s32[8]{0:T(128)}, u32[]{:S(2)}) copy-start(s32[8]{0:T(128)} %constant.36.clone) | copy-start | bytes 100
  44.8 10.3 %copy-start.6 = (s32[8]{0:T(128)S(1)}, s32[8]{0:T(128)}, u32[]{:S(2)}) copy-start(s32[8]{0:T(128)} %constant.35.clone) | copy-start | bytes 100
  53.4 6.1 %collective-permute-start.8 = (bf16[768,256]{1,0:T(8,128)(2,1)}, bf16[768,256]{1,0:T(8,128)(2,1)S(1)}, u32[]{:S(2)}, u32[]{:S(2)}) collective-permute-start(bf16[768,256]{1,0:T(8,128)(2,1)} %get-tuple-element.36.handed_ref), channel_id=1, source_target_pairs={{0,4},{4,0},{8,12},{12,8},{16,20},{20,16},{24,28},{28,24},{1,5},{5... | collective-permute-start | bytes 1179656 | tf_op jit(solution)/shard_map/ppermute | solution.py:191
  54.5 11.6 %collective-permute-start.9 = (bf16[768,256]{1,0:T(8,128)(2,1)S(1)}, bf16[768,256]{1,0:T(8,128)(2,1)S(1)}, u32[]{:S(2)}, u32[]{:S(2)}) collective-permute-start(bf16[768,256]{1,0:T(8,128)(2,1)S(1)} %shard_map.103), channel_id=1, source_target_pairs={{0,2},{1,0},{2,3},{3,1},{4,6},{5,4},{6,7},{7,5},{8,10},{9,8},{10,1... | collective-permute-start | bytes 1179656 | tf_op jit(solution)/shard_map/ppermute | solution.py:567
  55.2 10.9 %collective-permute-start.15 = (bf16[384,384]{1,0:T(8,128)(2,1)}, bf16[384,384]{1,0:T(8,128)(2,1)S(1)}, u32[]{:S(2)}, u32[]{:S(2)}) collective-permute-start(bf16[384,384]{1,0:T(8,128)(2,1)} %get-tuple-element.39.refs_1_), channel_id=1, source_target_pairs={{0,16},{4,12},{8,24},{12,4},{16,0},{20,28},{24,8},{28,20},{1,17},{... | collective-permute-start | bytes 884744 | tf_op jit(solution)/shard_map/ppermute | solution.py:191
  58.6 8.2 %collective-permute-start.16 = (bf16[912,384]{1,0:T(8,128)(2,1)S(1)}, bf16[912,384]{1,0:T(8,128)(2,1)S(1)}, u32[]{:S(2)}, u32[]{:S(2)}) collective-permute-start(bf16[912,384]{1,0:T(8,128)(2,1)S(1)} %shard_map.108), channel_id=1, source_target_pairs={{0,4},{4,0},{8,12},{12,8},{16,20},{20,16},{24,28},{28,24},{1,5},{5... | collective-permute-start | bytes 2101256 | tf_op jit(solution)/shard_map/ppermute | solution.py:191
  62.9 5.7 %collective-permute-start.18 = (bf16[1152,256]{1,0:T(8,128)(2,1)S(1)}, bf16[1152,256]{1,0:T(8,128)(2,1)S(1)}, u32[]{:S(2)}, u32[]{:S(2)}) collective-permute-start(bf16[1152,256]{1,0:T(8,128)(2,1)S(1)} %get-tuple-element.41), channel_id=1, source_target_pairs={{0,4},{4,0},{8,12},{12,8},{16,20},{20,16},{24,28},{28,24},{1,5},{5... | collective-permute-start | bytes 1769480 | tf_op jit(solution)/shard_map/ppermute | solution.py:191
  66.2 2.3 %collective-permute-start.17 = (bf16[624,384]{1,0:T(8,128)(2,1)S(1)}, bf16[624,384]{1,0:T(8,128)(2,1)S(1)}, u32[]{:S(2)}, u32[]{:S(2)}) collective-permute-start(bf16[624,384]{1,0:T(8,128)(2,1)S(1)} %shard_map.110), channel_id=1, source_target_pairs={{0,4},{4,0},{8,12},{12,8},{16,20},{20,16},{24,28},{28,24},{1,5},{5... | collective-permute-start | bytes 1437704 | tf_op jit(solution)/shard_map/ppermute | solution.py:191
  66.3 2.3 %collective-permute-start.19 = (bf16[384,256]{1,0:T(8,128)(2,1)S(1)}, bf16[384,256]{1,0:T(8,128)(2,1)S(1)}, u32[]{:S(2)}, u32[]{:S(2)}) collective-permute-start(bf16[384,256]{1,0:T(8,128)(2,1)S(1)} %get-tuple-element.42), channel_id=1, source_target_pairs={{0,4},{4,0},{8,12},{12,8},{16,20},{20,16},{24,28},{28,24},{1,5},{5... | collective-permute-start | bytes 589832 | tf_op jit(solution)/shard_map/ppermute | solution.py:191

commit v11 on v10

--- a/solution.py
+++ b/solution.py
@@ -10,7 +10,7 @@
 F32 = jnp.float32
 BF16 = jnp.bfloat16
 VMEM_BYTES = 10 * 1024 * 1024
-CUT = 144
+CUT = 160
 SPLIT = 1152
 
 

time: 70.7 us -> 70.7 us (level)
  no operation moved by 1% of the time
where the time goes in v11:
time: 70.7 us; the launch traced here: 70.4 us
  waiting for transfers between devices  28.2 us (40%)
  starting transfers between devices  24.6 us (35%)
  Pallas kernels  17.3 us (24%)
    pallas_call x21, Pallas kernels, call(): pl.pallas_call(kernel, out_shape=out_shape, cost_estimate=pl.CostEstimate...  17.3 us
    ppermute x10, starting transfers between devices, share_hop(): return lax.ppermute(held, 'seq', pairs)  8.99 us
    ppermute x3, waiting for transfers between devices, shards(): got = lax.ppermute(sent, 'seq', [(i, i ^ hop) for i in range(nseq)])  8.2 us
    ppermute x10, waiting for transfers between devices, share_hop(): return lax.ppermute(held, 'seq', pairs)  7.12 us
    ppermute x3, starting transfers between devices, shards(): got = lax.ppermute(sent, 'seq', [(i, i ^ hop) for i in range(nseq)])  4.73 us
    ppermute x1, waiting for transfers between devices, shards(): kept = lax.ppermute(ready, axes, moves(ring[1], ring[3]))  4.45 us
    ppermute x1, waiting for transfers between devices, shards(): handed = lax.ppermute(ready, axes, moves(ring[3], ring[1]))  4.11 us
    ppermute x1, waiting for transfers between devices, shards(): p2 = lax.ppermute(relay, 'head', [(0, 2), (1, 0), (2, 3), (3, 1)])  3.18 us
  transfers between devices with their start and end apart: 20, of which 8 were waited for; matrix products, arithmetic and copies ran while one was open for 0% of the time, Pallas kernels for 20%

profile of v11, /device:TPU:0, one launch (start us, length us, event | category | flops | bytes accessed | tf_op | source)
XLA Modules:
  0.0 70.4 jit_solution(5269888407767843023)
XLA Ops:
  0.0 0.0 copy-start.1
  0.0 0.0 copy-start
  0.0 0.0 copy-start.3
  0.0 1.4 %shard_map.91 = (bf16[768,384]{1,0:T(8,128)(2,1)S(1)}, bf16[768,384]{1,0:T(8,128)(2,1)S(1)}) custom-call(bf16[6144,384]{1,0:T(8,128)(2,1)} %wq_ref.3, bf16[6144,384]{1,0:T(8,128)(2,1)} %wk_ref.3), custom_call_target="tpu_custom_call" | custom-call | bytes 2359296 | tf_op jit(solution)/shard_map/pallas_call | solution.py:22
  1.4 3.1 %collective-permute-start.3 = (bf16[768,384]{1,0:T(8,128)(2,1)S(1)}, bf16[768,384]{1,0:T(8,128)(2,1)S(1)}, u32[]{:S(2)}, u32[]{:S(2)}) collective-permute-start(bf16[768,384]{1,0:T(8,128)(2,1)S(1)} %get-tuple-element.24.token_ref), channel_id=1, source_target_pairs={{0,1},{1,2},{2,3},{3,0},{4,7},{5,4},{6,5},{7,6},{8,9},{9,10},{10,1... | collective-permute-start | bytes 1769480 | tf_op jit(solution)/shard_map/ppermute | solution.py:478
  4.5 0.0 copy-done.1
  4.5 0.0 copy-done
  4.5 0.0 copy-done.3
  4.5 0.0 copy-done.2
  4.5 0.0 copy-done.4
  4.5 0.9 %shard_map.92 = (bf16[784,128]{1,0:T(8,128)(2,1)S(1)}, f32[768,128]{1,0:T(8,128)S(1)}, f32[24,128]{1,0:T(8,128)S(1)}) custom-call(f32[3,256]{1,0:T(4,128)S(1)} %bitcast.1, bf16[256,384]{1,0:T(8,128)(2,1)S(1)} %copy-done.2, bf16[256,384]{1,0:T(8,128)(2,1)S(1)} %copy-done.3, bf16[256,384]{1,0:T(8,128)(2,1)S(1)} %copy-done, bf16[256,384]{1,0:T(8,128)(2,1)S(1)} %copy-done.1, ...), custom_call_target="tpu_custom_call" | custom-call | flops 50331648 | bytes 786432 | tf_op jit(solution)/shard_map/pallas_call | solution.py:22
  5.4 1.6 %collective-permute-start = (bf16[784,128]{1,0:T(8,128)(2,1)S(1)}, bf16[784,128]{1,0:T(8,128)(2,1)S(1)}, u32[]{:S(2)}, u32[]{:S(2)}) collective-permute-start(bf16[784,128]{1,0:T(8,128)(2,1)S(1)} %get-tuple-element.25), channel_id=1, source_target_pairs={{0,4},{4,0},{8,12},{12,8},{16,20},{20,16},{24,28},{28,24},{1,5},{5... | collective-permute-start | bytes 602120 | tf_op jit(solution)/shard_map/ppermute | solution.py:504
  7.0 1.1 %collective-permute-done.got_ref = bf16[784,128]{1,0:T(8,128)(2,1)S(1)} collective-permute-done((bf16[784,128]{1,0:T(8,128)(2,1)S(1)}, bf16[784,128]{1,0:T(8,128)(2,1)S(1)}, u32[]{:S(2)}, u32[]{:S(2)}) %collective-permute-start) | collective-permute-done | bytes 200736 | tf_op jit(solution)/shard_map/ppermute | solution.py:504
  8.1 0.1 shard_map.93
  8.2 1.6 %collective-permute-start.1 = (bf16[784,128]{1,0:T(8,128)(2,1)S(1)}, bf16[784,128]{1,0:T(8,128)(2,1)S(1)}, u32[]{:S(2)}, u32[]{:S(2)}) collective-permute-start(bf16[784,128]{1,0:T(8,128)(2,1)S(1)} %get-tuple-element.28), channel_id=1, source_target_pairs={{0,8},{4,12},{8,0},{12,4},{16,24},{20,28},{24,16},{28,20},{1,9},{5... | collective-permute-start | bytes 602120 | tf_op jit(solution)/shard_map/ppermute | solution.py:504
  9.8 0.7 collective-permute-start.10
  10.4 5.1 %collective-permute-done.1.got_ref = bf16[784,128]{1,0:T(8,128)(2,1)S(1)} collective-permute-done((bf16[784,128]{1,0:T(8,128)(2,1)S(1)}, bf16[784,128]{1,0:T(8,128)(2,1)S(1)}, u32[]{:S(2)}, u32[]{:S(2)}) %collective-permute-start.1) | collective-permute-done | bytes 200736 | tf_op jit(solution)/shard_map/ppermute | solution.py:504
  15.5 0.8 %shard_map.94 = (bf16[384,128]{1,0:T(8,128)(2,1)S(1)}, f32[768,128]{1,0:T(8,128)}, f32[24,128]{1,0:T(8,128)S(1)}, f32[768,128]{1,0:T(8,128)S(1)}) custom-call(bf16[784,128]{1,0:T(8,128)(2,1)S(1)} %collective-permute-done.1.got_ref, f32[768,128]{1,0:T(8,128)S(1)} %get-tuple-element.29.held_ref, f32[24,128]{1,0:T(8,128)S(1)} %get-tuple-element.30.logs_ref, ...), custom_call_target="tpu_custom_call" | custom-call | flops 491520 | bytes 786432 | tf_op jit(solution)/shard_map/pallas_call | solution.py:22
  16.3 1.5 %collective-permute-start.2 = (bf16[384,128]{1,0:T(8,128)(2,1)S(1)}, bf16[384,128]{1,0:T(8,128)(2,1)S(1)}, u32[]{:S(2)}, u32[]{:S(2)}) collective-permute-start(bf16[384,128]{1,0:T(8,128)(2,1)S(1)} %get-tuple-element.32), channel_id=1, source_target_pairs={{0,16},{4,20},{8,24},{12,28},{16,0},{20,4},{24,8},{28,12},{1,17},{... | collective-permute-start | bytes 294920 | tf_op jit(solution)/shard_map/ppermute | solution.py:504
  17.9 1.0 %shard_map.95.local_ref = f32[768,256]{1,0:T(8,128)S(1)} custom-call(f32[3,256]{1,0:T(4,128)S(1)} %bitcast.2, bf16[256,384]{1,0:T(8,128)(2,1)S(1)} %copy-done.2, bf16[256,384]{1,0:T(8,128)(2,1)S(1)} %copy-done.3, bf16[256,384]{1,0:T(8,128)(2,1)S(1)} %copy-done, bf16[256,384]{1,0:T(8,128)(2,1)S(1)} %copy-done.1), custom_call_target="tpu_custom_call" | custom-call | flops 150994944 | bytes 1572864 | tf_op jit(solution)/shard_map/pallas_call | solution.py:22
  18.9 2.1 %collective-permute-done.2.got_ref = bf16[384,128]{1,0:T(8,128)(2,1)S(1)} collective-permute-done((bf16[384,128]{1,0:T(8,128)(2,1)S(1)}, bf16[384,128]{1,0:T(8,128)(2,1)S(1)}, u32[]{:S(2)}, u32[]{:S(2)}) %collective-permute-start.2) | collective-permute-done | bytes 98336 | tf_op jit(solution)/shard_map/ppermute | solution.py:504
  21.0 0.4 shard_map.96.grads_ref.refs_1_.refs_0_
  21.4 0.0 collective-permute-done.3.refs_0_
  21.4 1.6 %collective-permute-start.4 = (bf16[768,384]{1,0:T(8,128)(2,1)S(1)}, bf16[768,384]{1,0:T(8,128)(2,1)S(1)}, u32[]{:S(2)}, u32[]{:S(2)}) collective-permute-start(bf16[768,384]{1,0:T(8,128)(2,1)S(1)} %shard_map.98.refs_0_.refs_1_), channel_id=1, source_target_pairs={{0,8},{4,20},{8,0},{12,28},{16,24},{20,4},{24,16},{28,12},{1,9},{5... | collective-permute-start | bytes 1769480 | tf_op jit(solution)/shard_map/ppermute | solution.py:191
  23.0 0.0 collective-permute-done.10.refs_0_
  23.0 1.3 %collective-permute-start.11 = (bf16[768,384]{1,0:T(8,128)(2,1)S(1)}, bf16[768,384]{1,0:T(8,128)(2,1)S(1)}, u32[]{:S(2)}, u32[]{:S(2)}) collective-permute-start(bf16[768,384]{1,0:T(8,128)(2,1)S(1)} %shard_map.104), channel_id=1, source_target_pairs={{2,1},{1,0},{5,6},{6,7},{10,9},{9,8},{13,14},{14,15},{18,17},{17,1... | collective-permute-start | bytes 1769480 | tf_op jit(solution)/shard_map/ppermute | solution.py:542
  24.3 7.1 %collective-permute-done.4.refs_1_ = bf16[768,384]{1,0:T(8,128)(2,1)S(1)} collective-permute-done((bf16[768,384]{1,0:T(8,128)(2,1)S(1)}, bf16[768,384]{1,0:T(8,128)(2,1)S(1)}, u32[]{:S(2)}, u32[]{:S(2)}) %collective-permute-start.4) | collective-permute-done | bytes 589856 | tf_op jit(solution)/shard_map/ppermute | solution.py:191
  31.4 0.1 shard_map.99.refs_0_
  31.5 1.6 %collective-permute-start.5 = (bf16[1536,384]{1,0:T(8,128)(2,1)S(1)}, bf16[1536,384]{1,0:T(8,128)(2,1)}, u32[]{:S(2)}, u32[]{:S(2)}) collective-permute-start(bf16[1536,384]{1,0:T(8,128)(2,1)S(1)} %shard_map.99.refs_0_), channel_id=1, source_target_pairs={{0,16},{4,12},{8,24},{12,4},{16,0},{20,28},{24,8},{28,20},{1,17},{... | collective-permute-start | bytes 3538952 | tf_op jit(solution)/shard_map/ppermute | solution.py:191
  33.1 2.6 %shard_map.97.refs_1_.refs_2_.total_ref.token_ref = f32[1536,256]{1,0:T(8,128)S(1)} custom-call(bf16[6144,384]{1,0:T(8,128)(2,1)} %wq_ref.3, bf16[6144,384]{1,0:T(8,128)(2,1)} %wk_ref.3, bf16[768,256]{1,0:T(8,128)(2,1)S(1)} %shard_map.96.grads_ref.refs_1_.refs_0_), custom_call_target="tpu_custom_call" | custom-call | flops 603979776 | bytes 2359296 | tf_op jit(solution)/shard_map/pallas_call | solution.py:22
  35.7 1.0 %collective-permute-start.7 = (bf16[768,256]{1,0:T(8,128)(2,1)S(1)}, bf16[768,256]{1,0:T(8,128)(2,1)}, u32[]{:S(2)}, u32[]{:S(2)}) collective-permute-start(bf16[768,256]{1,0:T(8,128)(2,1)S(1)} %shard_map.100.own_ref), channel_id=1, source_target_pairs={{0,1},{1,2},{2,3},{3,0},{4,7},{5,4},{6,5},{7,6},{8,9},{9,10},{10,1... | collective-permute-start | bytes 1179656 | tf_op jit(solution)/shard_map/ppermute | solution.py:540
  36.7 2.9 %collective-permute-start.6 = (bf16[768,256]{1,0:T(8,128)(2,1)S(1)}, bf16[768,256]{1,0:T(8,128)(2,1)}, u32[]{:S(2)}, u32[]{:S(2)}) collective-permute-start(bf16[768,256]{1,0:T(8,128)(2,1)S(1)} %shard_map.100.own_ref), channel_id=1, source_target_pairs={{0,3},{1,0},{2,1},{3,2},{4,5},{5,6},{6,7},{7,4},{8,11},{9,8},{10,9... | collective-permute-start | bytes 1179656 | tf_op jit(solution)/shard_map/ppermute | solution.py:539
  39.6 0.0 collective-permute-done.11.both_ref
  39.6 1.3 %collective-permute-start.12 = (bf16[384,384]{1,0:T(8,128)(2,1)S(1)}, bf16[384,384]{1,0:T(8,128)(2,1)S(1)}, u32[]{:S(2)}, u32[]{:S(2)}) collective-permute-start(bf16[384,384]{1,0:T(8,128)(2,1)S(1)} %shard_map.105), channel_id=1, source_target_pairs={{0,4},{1,5},{6,2},{7,3},{8,12},{9,13},{14,10},{15,11},{16,20},{17,... | collective-permute-start | bytes 884744 | tf_op jit(solution)/shard_map/ppermute | solution.py:548
  40.9 1.2 %collective-permute-done.12.got_ref = bf16[384,384]{1,0:T(8,128)(2,1)S(1)} collective-permute-done((bf16[384,384]{1,0:T(8,128)(2,1)S(1)}, bf16[384,384]{1,0:T(8,128)(2,1)S(1)}, u32[]{:S(2)}, u32[]{:S(2)}) %collective-permute-start.12) | collective-permute-done | bytes 294944 | tf_op jit(solution)/shard_map/ppermute | solution.py:548
  42.1 0.7 %shard_map.106.refs_0_ = bf16[384,384]{1,0:T(8,128)(2,1)} custom-call(bf16[768,384]{1,0:T(8,128)(2,1)S(1)} %collective-permute-done.11.both_ref, bf16[384,384]{1,0:T(8,128)(2,1)S(1)} %collective-permute-done.12.got_ref), custom_call_target="tpu_custom_call" | custom-call | tf_op jit(solution)/shard_map/pallas_call | solution.py:22
  42.8 0.5 collective-permute-start.14
  43.3 1.5 %collective-permute-start.13 = (bf16[384,384]{1,0:T(8,128)(2,1)}, bf16[384,384]{1,0:T(8,128)(2,1)}, u32[]{:S(2)}, u32[]{:S(2)}) collective-permute-start(bf16[384,384]{1,0:T(8,128)(2,1)} %shard_map.106.refs_0_), channel_id=1, source_target_pairs={{0,8},{4,20},{8,0},{12,28},{16,24},{20,4},{24,16},{28,12},{1,9},{5... | collective-permute-start | bytes 884744 | tf_op jit(solution)/shard_map/ppermute | solution.py:191
  44.8 4.4 %collective-permute-done.7.refs_1_ = bf16[768,256]{1,0:T(8,128)(2,1)} collective-permute-done((bf16[768,256]{1,0:T(8,128)(2,1)S(1)}, bf16[768,256]{1,0:T(8,128)(2,1)}, u32[]{:S(2)}, u32[]{:S(2)}) %collective-permute-start.7) | collective-permute-done | bytes 393248 | tf_op jit(solution)/shard_map/ppermute | solution.py:540
  49.3 4.1 %collective-permute-done.6.refs_0_ = bf16[768,256]{1,0:T(8,128)(2,1)} collective-permute-done((bf16[768,256]{1,0:T(8,128)(2,1)S(1)}, bf16[768,256]{1,0:T(8,128)(2,1)}, u32[]{:S(2)}, u32[]{:S(2)}) %collective-permute-start.6) | collective-permute-done | bytes 393248 | tf_op jit(solution)/shard_map/ppermute | solution.py:539
  53.4 0.0 collective-permute-start.8
  53.4 1.1 %shard_map.103 = bf16[768,256]{1,0:T(8,128)(2,1)S(1)} custom-call(bf16[768,256]{1,0:T(8,128)(2,1)S(1)} %shard_map.100.own_ref, bf16[768,256]{1,0:T(8,128)(2,1)} %get-tuple-element.36.handed_ref, bf16[768,256]{1,0:T(8,128)(2,1)} %get-tuple-element.35.refs_2_.kept_ref), custom_call_target="tpu_custom_call" | custom-call | tf_op jit(solution)/shard_map/pallas_call | solution.py:22
  54.5 0.6 collective-permute-start.9
  55.2 0.0 copy-done.5
  55.2 0.0 copy-done.6
  55.2 0.0 collective-permute-done.14.refs_1_
  55.2 0.0 collective-permute-done.13.refs_0_
  55.2 2.3 %collective-permute-start.15 = (bf16[384,384]{1,0:T(8,128)(2,1)}, bf16[384,384]{1,0:T(8,128)(2,1)S(1)}, u32[]{:S(2)}, u32[]{:S(2)}) collective-permute-start(bf16[384,384]{1,0:T(8,128)(2,1)} %get-tuple-element.39.refs_1_), channel_id=1, source_target_pairs={{0,16},{4,12},{8,24},{12,4},{16,0},{20,28},{24,8},{28,20},{1,17},{... | collective-permute-start | bytes 884744 | tf_op jit(solution)/shard_map/ppermute | solution.py:191
  57.5 1.1 %shard_map.108 = bf16[928,384]{1,0:T(8,128)(2,1)S(1)} custom-call(bf16[384,384]{1,0:T(8,128)(2,1)} %shard_map.106.refs_0_, bf16[384,384]{1,0:T(8,128)(2,1)} %get-tuple-element.39.refs_1_, bf16[384,384]{1,0:T(8,128)(2,1)S(1)} %get-tuple-element.40.refs_2_.refs_0_), custom_call_target="tpu_custom_call" | custom-call | tf_op jit(solution)/shard_map/pallas_call | solution.py:22
  58.6 0.9 %collective-permute-start.16 = (bf16[928,384]{1,0:T(8,128)(2,1)S(1)}, bf16[928,384]{1,0:T(8,128)(2,1)S(1)}, u32[]{:S(2)}, u32[]{:S(2)}) collective-permute-start(bf16[928,384]{1,0:T(8,128)(2,1)S(1)} %shard_map.108), channel_id=1, source_target_pairs={{0,4},{4,0},{8,12},{12,8},{16,20},{20,16},{24,28},{28,24},{1,5},{5... | collective-permute-start | bytes 2138120 | tf_op jit(solution)/shard_map/ppermute | solution.py:191
  59.5 0.0 collective-permute-done.8.refs_3_
  59.5 0.0 collective-permute-done.5.refs_1_
  59.5 3.3 %shard_map.102 = (f32[1536,256]{1,0:T(8,128)S(1)}, bf16[1152,256]{1,0:T(8,128)(2,1)S(1)}, bf16[384,256]{1,0:T(8,128)(2,1)S(1)}) custom-call(s32[4]{0:T(128)S(1)} %and_select_fusion.table_ref, f32[1536,256]{1,0:T(8,128)S(1)} %shard_map.97.refs_1_.refs_2_.total_ref.token_ref, bf16[1536,384]{1,0:T(8,128)(2,1)S(1)} %shard_map.99.refs_0_, ...), custom_call_target="tpu_custom_call" | custom-call | tf_op jit(solution)/shard_map/pallas_call | solution.py:22
  62.9 0.1 collective-permute-start.18
  62.9 3.2 %collective-permute-done.9.grads_ref.refs_2_ = bf16[768,256]{1,0:T(8,128)(2,1)S(1)} collective-permute-done((bf16[768,256]{1,0:T(8,128)(2,1)S(1)}, bf16[768,256]{1,0:T(8,128)(2,1)S(1)}, u32[]{:S(2)}, u32[]{:S(2)}) %collective-permute-start.9) | collective-permute-done | bytes 393248 | tf_op jit(solution)/shard_map/ppermute | solution.py:567
  66.1 0.0 collective-permute-done.15.refs_3_.refs_1_
  66.2 0.1 collective-permute-start.17
  66.3 0.5 collective-permute-start.19
  66.8 0.0 collective-permute-done.16.refs_4_.refs_0_
  66.8 1.8 %shard_map.109.total_ref = f32[1536,256]{1,0:T(8,128)S(1)} custom-call(s32[8]{0:T(128)S(1)} %fusion.table_ref, f32[1536,256]{1,0:T(8,128)S(1)} %get-tuple-element.37.total_ref, bf16[768,256]{1,0:T(8,128)(2,1)S(1)} %collective-permute-done.9.grads_ref.refs_2_, bf16[384,384]{1,0:T(8,128)(2,1)} %shard_map.106.refs_0_, ...), custom_call_target="tpu_custom_call" | custom-call | flops 603979776 | bytes 3145728 | tf_op jit(solution)/shard_map/pallas_call | solution.py:22
  68.5 0.0 collective-permute-done.17.refs_1_
  68.5 0.0 collective-permute-done.19.refs_3_
  68.5 0.0 collective-permute-done.18.refs_2_
  68.6 1.9 %shard_map.111 = bf16[1536,256]{1,0:T(8,128)(2,1)} custom-call(s32[8]{0:T(128)S(1)} %fusion.table_ref, f32[1536,256]{1,0:T(8,128)S(1)} %shard_map.109.total_ref, bf16[768,256]{1,0:T(8,128)(2,1)S(1)} %collective-permute-done.9.grads_ref.refs_2_, bf16[928,384]{1,0:T(8,128)(2,1)S(1)} %collective-permute-done.16.refs_4_.refs_0_, ...), custom_call_target="tpu_custom_call" | custom-call | flops 603979776 | bytes 3145728 | tf_op jit(solution)/shard_map/pallas_call | solution.py:22
  (13 shorter events, 0.1 us)
Async XLA Ops:
  0.0 4.5 %copy-start.1 = (bf16[256,384]{1,0:T(8,128)(2,1)S(1)}, bf16[256,384]{1,0:T(8,128)(2,1)}, u32[]{:S(2)}) copy-start(bf16[256,384]{1,0:T(8,128)(2,1)} %g_ref.5) | copy-start | bytes 589828
  0.0 4.5 %copy-start = (bf16[256,384]{1,0:T(8,128)(2,1)S(1)}, bf16[256,384]{1,0:T(8,128)(2,1)}, u32[]{:S(2)}) copy-start(bf16[256,384]{1,0:T(8,128)(2,1)} %v_ref.5) | copy-start | bytes 589828
  0.0 4.5 %copy-start.3 = (bf16[256,384]{1,0:T(8,128)(2,1)S(1)}, bf16[256,384]{1,0:T(8,128)(2,1)}, u32[]{:S(2)}) copy-start(bf16[256,384]{1,0:T(8,128)(2,1)} %k_ref.3) | copy-start | bytes 589828
  0.0 4.5 %copy-start.2 = (bf16[256,384]{1,0:T(8,128)(2,1)S(1)}, bf16[256,384]{1,0:T(8,128)(2,1)}, u32[]{:S(2)}) copy-start(bf16[256,384]{1,0:T(8,128)(2,1)} %q_ref.3) | copy-start | bytes 589828
  0.0 4.5 %copy-start.4 = (f32[256,3]{0,1:T(4,128)S(1)}, f32[256,3]{0,1:T(4,128)}, u32[]{:S(2)}) copy-start(f32[256,3]{0,1:T(4,128)} %param.13) | copy-start | bytes 9220
  1.4 20.0 %collective-permute-start.3 = (bf16[768,384]{1,0:T(8,128)(2,1)S(1)}, bf16[768,384]{1,0:T(8,128)(2,1)S(1)}, u32[]{:S(2)}, u32[]{:S(2)}) collective-permute-start(bf16[768,384]{1,0:T(8,128)(2,1)S(1)} %get-tuple-element.24.token_ref), channel_id=1, source_target_pairs={{0,1},{1,2},{2,3},{3,0},{4,7},{5,4},{6,5},{7,6},{8,9},{9,10},{10,1... | collective-permute-start | bytes 1769480 | tf_op jit(solution)/shard_map/ppermute | solution.py:478
  5.4 2.7 %collective-permute-start = (bf16[784,128]{1,0:T(8,128)(2,1)S(1)}, bf16[784,128]{1,0:T(8,128)(2,1)S(1)}, u32[]{:S(2)}, u32[]{:S(2)}) collective-permute-start(bf16[784,128]{1,0:T(8,128)(2,1)S(1)} %get-tuple-element.25), channel_id=1, source_target_pairs={{0,4},{4,0},{8,12},{12,8},{16,20},{20,16},{24,28},{28,24},{1,5},{5... | collective-permute-start | bytes 602120 | tf_op jit(solution)/shard_map/ppermute | solution.py:504
  8.2 7.3 %collective-permute-start.1 = (bf16[784,128]{1,0:T(8,128)(2,1)S(1)}, bf16[784,128]{1,0:T(8,128)(2,1)S(1)}, u32[]{:S(2)}, u32[]{:S(2)}) collective-permute-start(bf16[784,128]{1,0:T(8,128)(2,1)S(1)} %get-tuple-element.28), channel_id=1, source_target_pairs={{0,8},{4,12},{8,0},{12,4},{16,24},{20,28},{24,16},{28,20},{1,9},{5... | collective-permute-start | bytes 602120 | tf_op jit(solution)/shard_map/ppermute | solution.py:504
  9.8 13.2 %collective-permute-start.10 = (bf16[768,384]{1,0:T(8,128)(2,1)S(1)}, bf16[768,384]{1,0:T(8,128)(2,1)S(1)}, u32[]{:S(2)}, u32[]{:S(2)}) collective-permute-start(bf16[768,384]{1,0:T(8,128)(2,1)S(1)} %get-tuple-element.38), channel_id=1, source_target_pairs={{3,2},{2,1},{4,5},{5,6},{11,10},{10,9},{12,13},{13,14},{19,18},{18... | collective-permute-start | bytes 1769480 | tf_op jit(solution)/shard_map/ppermute | solution.py:479
  16.3 4.6 %collective-permute-start.2 = (bf16[384,128]{1,0:T(8,128)(2,1)S(1)}, bf16[384,128]{1,0:T(8,128)(2,1)S(1)}, u32[]{:S(2)}, u32[]{:S(2)}) collective-permute-start(bf16[384,128]{1,0:T(8,128)(2,1)S(1)} %get-tuple-element.32), channel_id=1, source_target_pairs={{0,16},{4,20},{8,24},{12,28},{16,0},{20,4},{24,8},{28,12},{1,17},{... | collective-permute-start | bytes 294920 | tf_op jit(solution)/shard_map/ppermute | solution.py:504
  21.4 9.9 %collective-permute-start.4 = (bf16[768,384]{1,0:T(8,128)(2,1)S(1)}, bf16[768,384]{1,0:T(8,128)(2,1)S(1)}, u32[]{:S(2)}, u32[]{:S(2)}) collective-permute-start(bf16[768,384]{1,0:T(8,128)(2,1)S(1)} %shard_map.98.refs_0_.refs_1_), channel_id=1, source_target_pairs={{0,8},{4,20},{8,0},{12,28},{16,24},{20,4},{24,16},{28,12},{1,9},{5... | collective-permute-start | bytes 1769480 | tf_op jit(solution)/shard_map/ppermute | solution.py:191
  23.0 16.6 %collective-permute-start.11 = (bf16[768,384]{1,0:T(8,128)(2,1)S(1)}, bf16[768,384]{1,0:T(8,128)(2,1)S(1)}, u32[]{:S(2)}, u32[]{:S(2)}) collective-permute-start(bf16[768,384]{1,0:T(8,128)(2,1)S(1)} %shard_map.104), channel_id=1, source_target_pairs={{2,1},{1,0},{5,6},{6,7},{10,9},{9,8},{13,14},{14,15},{18,17},{17,1... | collective-permute-start | bytes 1769480 | tf_op jit(solution)/shard_map/ppermute | solution.py:542
  31.5 28.1 %collective-permute-start.5 = (bf16[1536,384]{1,0:T(8,128)(2,1)S(1)}, bf16[1536,384]{1,0:T(8,128)(2,1)}, u32[]{:S(2)}, u32[]{:S(2)}) collective-permute-start(bf16[1536,384]{1,0:T(8,128)(2,1)S(1)} %shard_map.99.refs_0_), channel_id=1, source_target_pairs={{0,16},{4,12},{8,24},{12,4},{16,0},{20,28},{24,8},{28,20},{1,17},{... | collective-permute-start | bytes 3538952 | tf_op jit(solution)/shard_map/ppermute | solution.py:191
  35.7 13.6 %collective-permute-start.7 = (bf16[768,256]{1,0:T(8,128)(2,1)S(1)}, bf16[768,256]{1,0:T(8,128)(2,1)}, u32[]{:S(2)}, u32[]{:S(2)}) collective-permute-start(bf16[768,256]{1,0:T(8,128)(2,1)S(1)} %shard_map.100.own_ref), channel_id=1, source_target_pairs={{0,1},{1,2},{2,3},{3,0},{4,7},{5,4},{6,5},{7,6},{8,9},{9,10},{10,1... | collective-permute-start | bytes 1179656 | tf_op jit(solution)/shard_map/ppermute | solution.py:540
  36.7 16.7 %collective-permute-start.6 = (bf16[768,256]{1,0:T(8,128)(2,1)S(1)}, bf16[768,256]{1,0:T(8,128)(2,1)}, u32[]{:S(2)}, u32[]{:S(2)}) collective-permute-start(bf16[768,256]{1,0:T(8,128)(2,1)S(1)} %shard_map.100.own_ref), channel_id=1, source_target_pairs={{0,3},{1,0},{2,1},{3,2},{4,5},{5,6},{6,7},{7,4},{8,11},{9,8},{10,9... | collective-permute-start | bytes 1179656 | tf_op jit(solution)/shard_map/ppermute | solution.py:539
  39.6 2.5 %collective-permute-start.12 = (bf16[384,384]{1,0:T(8,128)(2,1)S(1)}, bf16[384,384]{1,0:T(8,128)(2,1)S(1)}, u32[]{:S(2)}, u32[]{:S(2)}) collective-permute-start(bf16[384,384]{1,0:T(8,128)(2,1)S(1)} %shard_map.105), channel_id=1, source_target_pairs={{0,4},{1,5},{6,2},{7,3},{8,12},{9,13},{14,10},{15,11},{16,20},{17,... | collective-permute-start | bytes 884744 | tf_op jit(solution)/shard_map/ppermute | solution.py:548
  42.8 12.3 %collective-permute-start.14 = (bf16[384,384]{1,0:T(8,128)(2,1)}, bf16[384,384]{1,0:T(8,128)(2,1)S(1)}, u32[]{:S(2)}, u32[]{:S(2)}) collective-permute-start(bf16[384,384]{1,0:T(8,128)(2,1)} %shard_map.106.refs_0_), channel_id=1, source_target_pairs={{0,16},{4,12},{8,24},{12,4},{16,0},{20,28},{24,8},{28,20},{1,17},{... | collective-permute-start | bytes 884744 | tf_op jit(solution)/shard_map/ppermute | solution.py:191
  43.3 11.8 %collective-permute-start.13 = (bf16[384,384]{1,0:T(8,128)(2,1)}, bf16[384,384]{1,0:T(8,128)(2,1)}, u32[]{:S(2)}, u32[]{:S(2)}) collective-permute-start(bf16[384,384]{1,0:T(8,128)(2,1)} %shard_map.106.refs_0_), channel_id=1, source_target_pairs={{0,8},{4,20},{8,0},{12,28},{16,24},{20,4},{24,16},{28,12},{1,9},{5... | collective-permute-start | bytes 884744 | tf_op jit(solution)/shard_map/ppermute | solution.py:191
  44.8 10.3 %copy-start.5 = (s32[8]{0:T(128)S(1)}, s32[8]{0:T(128)}, u32[]{:S(2)}) copy-start(s32[8]{0:T(128)} %constant.36.clone) | copy-start | bytes 100
  44.8 10.3 %copy-start.6 = (s32[8]{0:T(128)S(1)}, s32[8]{0:T(128)}, u32[]{:S(2)}) copy-start(s32[8]{0:T(128)} %constant.35.clone) | copy-start | bytes 100
  53.4 6.1 %collective-permute-start.8 = (bf16[768,256]{1,0:T(8,128)(2,1)}, bf16[768,256]{1,0:T(8,128)(2,1)S(1)}, u32[]{:S(2)}, u32[]{:S(2)}) collective-permute-start(bf16[768,256]{1,0:T(8,128)(2,1)} %get-tuple-element.36.handed_ref), channel_id=1, source_target_pairs={{0,4},{4,0},{8,12},{12,8},{16,20},{20,16},{24,28},{28,24},{1,5},{5... | collective-permute-start | bytes 1179656 | tf_op jit(solution)/shard_map/ppermute | solution.py:191
  54.5 11.6 %collective-permute-start.9 = (bf16[768,256]{1,0:T(8,128)(2,1)S(1)}, bf16[768,256]{1,0:T(8,128)(2,1)S(1)}, u32[]{:S(2)}, u32[]{:S(2)}) collective-permute-start(bf16[768,256]{1,0:T(8,128)(2,1)S(1)} %shard_map.103), channel_id=1, source_target_pairs={{0,2},{1,0},{2,3},{3,1},{4,6},{5,4},{6,7},{7,5},{8,10},{9,8},{10,1... | collective-permute-start | bytes 1179656 | tf_op jit(solution)/shard_map/ppermute | solution.py:567
  55.2 10.9 %collective-permute-start.15 = (bf16[384,384]{1,0:T(8,128)(2,1)}, bf16[384,384]{1,0:T(8,128)(2,1)S(1)}, u32[]{:S(2)}, u32[]{:S(2)}) collective-permute-start(bf16[384,384]{1,0:T(8,128)(2,1)} %get-tuple-element.39.refs_1_), channel_id=1, source_target_pairs={{0,16},{4,12},{8,24},{12,4},{16,0},{20,28},{24,8},{28,20},{1,17},{... | collective-permute-start | bytes 884744 | tf_op jit(solution)/shard_map/ppermute | solution.py:191
  58.6 8.2 %collective-permute-start.16 = (bf16[928,384]{1,0:T(8,128)(2,1)S(1)}, bf16[928,384]{1,0:T(8,128)(2,1)S(1)}, u32[]{:S(2)}, u32[]{:S(2)}) collective-permute-start(bf16[928,384]{1,0:T(8,128)(2,1)S(1)} %shard_map.108), channel_id=1, source_target_pairs={{0,4},{4,0},{8,12},{12,8},{16,20},{20,16},{24,28},{28,24},{1,5},{5... | collective-permute-start | bytes 2138120 | tf_op jit(solution)/shard_map/ppermute | solution.py:191
  62.9 5.7 %collective-permute-start.18 = (bf16[1152,256]{1,0:T(8,128)(2,1)S(1)}, bf16[1152,256]{1,0:T(8,128)(2,1)S(1)}, u32[]{:S(2)}, u32[]{:S(2)}) collective-permute-start(bf16[1152,256]{1,0:T(8,128)(2,1)S(1)} %get-tuple-element.41), channel_id=1, source_target_pairs={{0,4},{4,0},{8,12},{12,8},{16,20},{20,16},{24,28},{28,24},{1,5},{5... | collective-permute-start | bytes 1769480 | tf_op jit(solution)/shard_map/ppermute | solution.py:191
  66.2 2.3 %collective-permute-start.17 = (bf16[608,384]{1,0:T(8,128)(2,1)S(1)}, bf16[608,384]{1,0:T(8,128)(2,1)S(1)}, u32[]{:S(2)}, u32[]{:S(2)}) collective-permute-start(bf16[608,384]{1,0:T(8,128)(2,1)S(1)} %shard_map.110), channel_id=1, source_target_pairs={{0,4},{4,0},{8,12},{12,8},{16,20},{20,16},{24,28},{28,24},{1,5},{5... | collective-permute-start | bytes 1400840 | tf_op jit(solution)/shard_map/ppermute | solution.py:191
  66.3 2.3 %collective-permute-start.19 = (bf16[384,256]{1,0:T(8,128)(2,1)S(1)}, bf16[384,256]{1,0:T(8,128)(2,1)S(1)}, u32[]{:S(2)}, u32[]{:S(2)}) collective-permute-start(bf16[384,256]{1,0:T(8,128)(2,1)S(1)} %get-tuple-element.42), channel_id=1, source_target_pairs={{0,4},{4,0},{8,12},{12,8},{16,20},{20,16},{24,28},{28,24},{1,5},{5... | collective-permute-start | bytes 589832 | tf_op jit(solution)/shard_map/ppermute | solution.py:191
